TPU v7x, 32 devices: a whole 2x2x4 slice. The times are simulated.
32 devices in a mesh: section: 2 (over core), wide: 4 (over y, x), narrow: 4 (over z).
Axes of the slice: x: 2, y: 2, z: 4, core: 2. Of those that a mesh axis runs over, the one named last changes fastest.
Arguments:
- hidden_in: bfloat16 [2, 1024, 3072], P(None, 'wide', 'narrow'), may hold values from -64 to 64
- row_kind: int32 [2, 1024], replicated, may hold values from 0 to 3, as said below
- positions: int32 [3, 2, 1024], replicated, may hold values from 0 to 44, as said below
- timesteps: int32 [2], replicated, may hold values from 0 to 999
- stale_cache: bfloat16 [2, 2, 1024, 48, 128], P('section', None, 'narrow', 'wide'), may hold values from -8 to 8
- w_qkv: bfloat16 [2, 3072, 9216], P('section', 'narrow', 'wide'), may hold values from -0.109375 to 0.109375
- qk_norm: float32 [2, 4, 64], P('section'), may hold values from -6 to 6, as said below
- w_out: bfloat16 [2, 3072, 3072], P('section', 'wide', 'narrow'), may hold values from -0.109375 to 0.109375
- ada_weight: bfloat16 [2, 2, 512, 6, 3072], P('section', None, None, None, 'narrow'), may hold values from -0.25 to 0.25
- w_up: bfloat16 [2, 3072, 12288], P('section', 'narrow', 'wide'), may hold values from -0.109375 to 0.109375
- w_down: bfloat16 [2, 12288, 3072], P('section', 'wide', 'narrow'), may hold values from -0.0546875 to 0.0546875
Outputs:
- layer_out: bfloat16 [2, 2, 1024, 3072], P('section', None, 'wide', 'narrow')
- new_cache: bfloat16 [2, 2, 1024, 48, 128], P('section', None, 'narrow', 'wide')
Inputs may be any that keep to these rules, and one draw needn't show every extreme that they name: `row_kind`: kind is 2 times the request (0 or 1) plus 1 for a text row. In each patch the rows of request 0 come first and those of request 1 follow, each request holding 1024/4 rows or more; text rows stand only in patch 0, as the first 128 rows of each request's block. `positions`: rows 0, 1, 2 are frame (below 13), height (below 30) and width (below 45); text rows have all three zero. `qk_norm`: rows are query gain, query bias, key gain, key bias; gains lie in 0.6 to 1.4.
All inputs are finite; a program needn't handle non-finite values.
Results may differ from a plain program's by a relative error of at most 0.019.
Values may be sent and summed in bfloat16 or wider, within the bound.
No kernel may reach another device: no remote copies, remote signals or barrier semaphores. Data moves between devices by JAX's collectives and lax.ppermute only.
A program may use at most 128 MiB of HBM per device.

v0:
```python
import jax
import jax.numpy as jnp
from jax import lax
from jax.sharding import PartitionSpec as P

EPS_ROW = 1e-05
EPS_HEAD = 1e-06
NEG_FILL = -1e30


def passed_along(value, axis, by):
    devices = lax.axis_size(axis)
    pairs = [(i, i + by) for i in range(devices) if 0 <= i + by < devices]
    return lax.ppermute(value, axis, pairs)


def time_features(timesteps, feature_count):
    half_count = feature_count // 2
    frequency = jnp.exp(-jnp.log(10000.0) * jnp.arange(half_count, dtype=jnp.float32) / half_count)
    angle = timesteps.astype(jnp.float32)[:, None] * frequency[None, :]
    return jnp.concatenate([jnp.cos(angle), jnp.sin(angle)], axis=1)


def rotary_angles(row_positions, head_dim):
    dim_frame = head_dim // 4
    dim_plane = head_dim // 8 * 3
    pieces = []
    for axis_pos, span_dims in ((0, dim_frame), (1, dim_plane), (2, dim_plane)):
        frequency = 10000.0 ** (-jnp.arange(0, span_dims, 2, dtype=jnp.float32) / span_dims)
        pieces.append(row_positions[axis_pos].astype(jnp.float32)[:, None] * frequency[None, :])
    return jnp.concatenate(pieces, axis=1)


def rotate(values, angles):
    row_count, head_count, head_dim = values.shape
    paired = values.reshape(row_count, head_count, head_dim // 2, 2)
    former = paired[..., 0]
    latter = paired[..., 1]
    cosine = jnp.cos(angles)[:, None, :]
    sine = jnp.sin(angles)[:, None, :]
    turned = jnp.stack([former * cosine - latter * sine, latter * cosine + former * sine], axis=-1)
    return turned.reshape(row_count, head_count, head_dim)


def head_norm(values, gain, offset):
    center = values - jnp.mean(values, axis=-1, keepdims=True)
    spread = jnp.mean(center * center, axis=-1, keepdims=True)
    return center * lax.rsqrt(spread + EPS_HEAD) * gain + offset


def select_rows(table, kinds):
    match = (kinds[:, None] == jnp.arange(4, dtype=jnp.int32)[None, :]).astype(jnp.float32)
    return jnp.sum(match[:, :, None, None] * table[None], axis=1)


def partial_softmax(queries, query_req, keys_flat, key_req, head_dim):
    scores = jnp.einsum(
        "qhd,khd->qhk", queries, keys_flat[..., :head_dim], preferred_element_type=jnp.float32
    )
    scores = scores * head_dim ** (-0.5)
    allowed = (query_req[:, None] == key_req[None, :])[:, None, :]
    masked = jnp.where(allowed, scores, NEG_FILL)
    top = jnp.max(masked, axis=2)
    weights = jnp.where(allowed, jnp.exp(masked - top[..., None]), 0.0)
    total = jnp.sum(weights, axis=2)
    accum = jnp.einsum(
        "qhk,khd->qhd",
        weights.astype(jnp.bfloat16),
        keys_flat[..., head_dim:],
        preferred_element_type=jnp.float32,
    )
    return (top, total, accum)


def combine_parts(former, latter):
    top = jnp.maximum(former[0], latter[0])
    factor_b = jnp.exp(latter[0] - top)
    total = latter[1] * factor_b
    accum = latter[2] * factor_b[..., None]
    return (top, total, accum)


def per_device(
    hidden_in,
    row_kind,
    positions,
    timesteps,
    stale_cache,
    w_qkv,
    qk_norm,
    w_out,
    ada_weight,
    w_up,
    w_down,
):
    n_wide = lax.axis_size("wide")
    n_narrow = lax.axis_size("narrow")
    n_section = lax.axis_size("section")
    wide_idx = lax.axis_index("wide")
    narrow_idx = lax.axis_index("narrow")
    section_idx = lax.axis_index("section")
    patch_count, rows_a, feat_a = hidden_in.shape
    total_rows = rows_a * n_wide
    rows_b = total_rows // n_narrow
    heads_local = stale_cache.shape[3]
    head_dim = stale_cache.shape[4] // 2
    model_width = feat_a * n_narrow
    zero_index = jnp.zeros((), jnp.int32)
    activated = jax.nn.silu(time_features(timesteps, ada_weight.shape[2])).astype(jnp.bfloat16)
    modulation = jnp.einsum(
        "re,kesd->krsd", activated, ada_weight[0], preferred_element_type=jnp.float32
    )
    tables = modulation.reshape(2, 4, 3, feat_a)
    norms = qk_norm[0]
    qkv_block = w_qkv[0]
    out_block = w_out[0]
    up_block = w_up[0]
    down_block = w_down[0]

    def normalize(values):
        moments = lax.psum((jnp.sum(values, axis=1), jnp.sum(values * values, axis=1)), "narrow")
        row_mean = moments[0] / model_width
        variance = moments[1] / model_width - row_mean * row_mean
        return (values - row_mean[:, None]) * lax.rsqrt(variance + EPS_ROW)[:, None]

    outputs = jnp.zeros((1, patch_count, rows_a, feat_a), jnp.bfloat16)
    cache_now = stale_cache
    arriving = jnp.zeros((rows_a, feat_a), jnp.bfloat16)
    step_total = patch_count + n_section - 1
    for step_index in range(step_total):
        patch_index = step_index - section_idx
        is_live = (patch_index >= 0) & (patch_index < patch_count)
        patch_slot = jnp.clip(patch_index, 0, patch_count - 1)
        layer_in = jnp.where(
            section_idx == 0, hidden_in[min(step_index, patch_count - 1)], arriving
        )
        x_in = layer_in.astype(jnp.float32)
        kinds_a = lax.dynamic_slice(row_kind, (patch_slot, wide_idx * rows_a), (1, rows_a))[0]
        kinds_b = lax.dynamic_slice(row_kind, (patch_slot, narrow_idx * rows_b), (1, rows_b))[0]
        positions_b = lax.dynamic_slice(
            positions, (zero_index, patch_slot, narrow_idx * rows_b), (3, 1, rows_b)
        )[:, 0]
        first_mod = select_rows(tables[0], kinds_a)
        entry_rows = (normalize(x_in) * (1.0 + first_mod[:, 1]) + first_mod[:, 0]).astype(
            jnp.bfloat16
        )
        qkv_terms = jnp.dot(
            lax.all_gather(entry_rows, "wide", axis=0, tiled=True),
            qkv_block,
            preferred_element_type=jnp.float32,
        )
        qkv = (
            lax.psum_scatter(
                qkv_terms.astype(jnp.bfloat16), "narrow", scatter_dimension=0, tiled=True
            )
            .astype(jnp.float32)
            .reshape(rows_b, heads_local, 3, head_dim)
        )
        angles = rotary_angles(positions_b, head_dim)
        queries = rotate(head_norm(qkv[:, :, 0], norms[0], norms[1]), angles).astype(jnp.bfloat16)
        fresh_keys = rotate(head_norm(qkv[:, :, 1], norms[2], norms[3]), angles).astype(
            jnp.bfloat16
        )
        fresh_values = qkv[:, :, 2].astype(jnp.bfloat16)
        fresh_pairs = jnp.concatenate([fresh_keys, fresh_values], axis=-1)
        cache_updated = lax.dynamic_update_slice(
            cache_now,
            fresh_pairs[None, None],
            (zero_index, patch_slot, zero_index, zero_index, zero_index),
        )
        local_pairs = cache_updated[0]
        query_req = kinds_b // 2
        start_carry = (
            jnp.full((rows_b, heads_local), NEG_FILL, jnp.float32),
            jnp.zeros((rows_b, heads_local), jnp.float32),
            jnp.zeros((rows_b, heads_local, head_dim), jnp.float32),
        )
        piece = lax.all_gather(local_pairs, "narrow", axis=1, tiled=True)
        count = piece.shape[1]
        key_req = (row_kind // 2).reshape(-1)
        keys_flat = piece.reshape(patch_count * count, heads_local, 2 * head_dim)
        top_all, total_all, accum_all = combine_parts(
            start_carry, partial_softmax(queries, query_req, keys_flat, key_req, head_dim)
        )
        attended = (
            (accum_all / total_all[..., None])
            .reshape(rows_b, heads_local * head_dim)
            .astype(jnp.bfloat16)
        )
        proj_terms = jnp.dot(
            lax.all_gather(attended, "narrow", axis=0, tiled=True),
            out_block,
            preferred_element_type=jnp.float32,
        )
        projected = lax.psum_scatter(
            proj_terms.astype(jnp.bfloat16), "wide", scatter_dimension=0, tiled=True
        ).astype(jnp.float32)
        after_attn = x_in + first_mod[:, 2] * projected
        second_mod = select_rows(tables[1], kinds_a)
        entry_second = (normalize(after_attn) * (1.0 + second_mod[:, 1]) + second_mod[:, 0]).astype(
            jnp.bfloat16
        )
        up_terms = jnp.dot(
            lax.all_gather(entry_second, "wide", axis=0, tiled=True),
            up_block,
            preferred_element_type=jnp.float32,
        )
        up_sum = lax.psum_scatter(
            up_terms.astype(jnp.bfloat16), "narrow", scatter_dimension=0, tiled=True
        ).astype(jnp.float32)
        hidden_act = jax.nn.gelu(up_sum, approximate=True).astype(jnp.bfloat16)
        down_terms = jnp.dot(
            lax.all_gather(hidden_act, "narrow", axis=0, tiled=True),
            down_block,
            preferred_element_type=jnp.float32,
        )
        down_sum = lax.psum_scatter(
            down_terms.astype(jnp.bfloat16), "wide", scatter_dimension=0, tiled=True
        ).astype(jnp.float32)
        layer_result = (after_attn + second_mod[:, 2] * down_sum).astype(jnp.bfloat16)
        written = lax.dynamic_update_slice(
            outputs, layer_result[None, None], (zero_index, patch_slot, zero_index, zero_index)
        )
        outputs = jnp.where(is_live, written, outputs)
        cache_now = jnp.where(is_live, cache_updated, cache_now)
        if step_index + 1 < step_total:
            arriving = passed_along(layer_result, "section", 1)
    return (outputs, cache_now)


def solution(mesh):
    in_specs = (
        P(None, "wide", "narrow"),
        P(),
        P(),
        P(),
        P("section", None, "narrow", "wide", None),
        P("section", "narrow", "wide"),
        P("section", None, None),
        P("section", "wide", "narrow"),
        P("section", None, None, None, "narrow"),
        P("section", "narrow", "wide"),
        P("section", "wide", "narrow"),
    )
    out_specs = (P("section", None, "wide", "narrow"), P("section", None, "narrow", "wide", None))
    return jax.shard_map(
        per_device, mesh=mesh, in_specs=in_specs, out_specs=out_specs, check_vma=False
    )
```

profile of v0, /device:TPU:0, one launch (start us, length us, event | category | flops | bytes accessed | tf_op | source)
XLA Modules:
  0.0 2294.2 jit_solution(12155450396828680348)
XLA Ops:
  12.7 5.0 fusion.101
  23.8 13.9 all-reduce.5
  38.4 22.5 multiply_reduce_fusion.1
  63.4 29.4 %all-gather.19.cloned.1.call-done = bf16[1024,768]{1,0:T(8,128)(2,1)} async-done(((bf16[256,768]{1,0:T(8,128)(2,1)}), bf16[1024,768]{1,0:T(8,128)(2,1)}) %all-gather.19.cloned.1.call-update) | async-done | bytes 1572880 | tf_op jit(solution)/shard_map/all_gather | solution.py:148
  92.7 7.3 convolution_convert_fusion.2
  110.7 74.8 %reduce-scatter.13.cloned.1.call-done = bf16[256,2304]{1,0:T(8,128)(2,1)} async-done(((bf16[1024,2304]{1,0:T(8,128)(2,1)}), bf16[256,2304]{1,0:T(8,128)(2,1)}) %reduce-scatter.13.cloned.1.call-update) | async-done | bytes 1179664 | tf_op jit(solution)/shard_map/reduce_scatter | solution.py:153
  225.0 106.8 %all-gather.43.cloned.1.call-done = bf16[1,2,1024,12,128]{4,2,3,1,0:T(8,128)(2,1)} async-done(((bf16[1,2,256,12,128]{4,2,3,1,0:T(8,128)(2,1)}), bf16[1,2,1024,12,128]{4,2,3,1,0:T(8,128)(2,1)}) %all-gather.43.cloned.1.call-update) | async-done | bytes 6291472 | tf_op jit(solution)/shard_map/all_gather | solution.py:178
  331.8 16.2 copy.60
  348.0 11.2 reshape.804
  359.2 12.1 fusion
  371.3 11.7 fusion.3
  383.0 11.9 fusion.112
  395.0 36.0 %all-gather.21.cloned.1.call-done = bf16[1024,768]{0,1:T(8,128)(2,1)} async-done(((bf16[256,768]{0,1:T(8,128)(2,1)}), bf16[1024,768]{0,1:T(8,128)(2,1)}) %all-gather.21.cloned.1.call-update) | async-done | bytes 1572880 | tf_op jit(solution)/shard_map/all_gather | solution.py:191
  431.0 4.3 convolution_convert_fusion.8
  435.4 29.3 %reduce-scatter.15.cloned.1.call-done = bf16[256,768]{1,0:T(8,128)(2,1)} async-done(((bf16[1024,768]{1,0:T(8,128)(2,1)}), bf16[256,768]{1,0:T(8,128)(2,1)}) %reduce-scatter.15.cloned.1.call-update) | async-done | bytes 393232 | tf_op jit(solution)/shard_map/reduce_scatter | solution.py:195
  467.6 12.4 all-reduce.4
  483.5 28.1 %all-gather.23.cloned.1.call-done = bf16[1024,768]{1,0:T(8,128)(2,1)} async-done(((bf16[256,768]{1,0:T(8,128)(2,1)}), bf16[1024,768]{1,0:T(8,128)(2,1)}) %all-gather.23.cloned.1.call-update) | async-done | bytes 1572880 | tf_op jit(solution)/shard_map/all_gather | solution.py:204
  511.7 9.1 convolution_convert_fusion.5
  520.8 110.8 %reduce-scatter.17.cloned.1.call-done = bf16[256,3072]{1,0:T(8,128)(2,1)} async-done(((bf16[1024,3072]{1,0:T(8,128)(2,1)}), bf16[256,3072]{1,0:T(8,128)(2,1)}) %reduce-scatter.17.cloned.1.call-update) | async-done | bytes 1572880 | tf_op jit(solution)/shard_map/reduce_scatter | solution.py:208
  631.7 3.7 fusion.37
  635.4 116.0 %all-gather.25.cloned.1.call-done = bf16[1024,3072]{1,0:T(8,128)(2,1)} async-done(((bf16[256,3072]{1,0:T(8,128)(2,1)}), bf16[1024,3072]{1,0:T(8,128)(2,1)}) %all-gather.25.cloned.1.call-update) | async-done | bytes 6291472 | tf_op jit(solution)/shard_map/all_gather | solution.py:213
  751.4 9.4 fusion.59
  760.9 29.3 %reduce-scatter.19.cloned.1.call-done = bf16[256,768]{1,0:T(8,128)(2,1)} async-done(((bf16[1024,768]{1,0:T(8,128)(2,1)}), bf16[256,768]{1,0:T(8,128)(2,1)}) %reduce-scatter.19.cloned.1.call-update) | async-done | bytes 393232 | tf_op jit(solution)/shard_map/reduce_scatter | solution.py:217
  796.5 12.4 all-reduce.3
  812.2 28.3 %all-gather.27.cloned.1.call-done = bf16[1024,768]{1,0:T(8,128)(2,1)} async-done(((bf16[256,768]{1,0:T(8,128)(2,1)}), bf16[1024,768]{1,0:T(8,128)(2,1)}) %all-gather.27.cloned.1.call-update) | async-done | bytes 1572880 | tf_op jit(solution)/shard_map/all_gather | solution.py:148
  840.5 7.3 convolution_convert_fusion.1
  853.5 79.8 %reduce-scatter.21.cloned.1.call-done = bf16[256,2304]{1,0:T(8,128)(2,1)} async-done(((bf16[1024,2304]{1,0:T(8,128)(2,1)}), bf16[256,2304]{1,0:T(8,128)(2,1)}) %reduce-scatter.21.cloned.1.call-update) | async-done | bytes 1179664 | tf_op jit(solution)/shard_map/reduce_scatter | solution.py:153
  968.8 110.9 %all-gather.45.cloned.1.call-done = bf16[1,2,1024,12,128]{4,2,3,1,0:T(8,128)(2,1)} async-done(((bf16[1,2,256,12,128]{4,2,3,1,0:T(8,128)(2,1)}), bf16[1,2,1024,12,128]{4,2,3,1,0:T(8,128)(2,1)}) %all-gather.45.cloned.1.call-update) | async-done | bytes 6291472 | tf_op jit(solution)/shard_map/all_gather | solution.py:178
  1079.7 16.2 copy.65
  1095.9 11.2 reshape.807
  1107.1 12.2 fusion.1
  1119.3 11.7 fusion.5
  1131.0 11.9 fusion.122
  1142.9 36.0 %all-gather.29.cloned.1.call-done = bf16[1024,768]{0,1:T(8,128)(2,1)} async-done(((bf16[256,768]{0,1:T(8,128)(2,1)}), bf16[1024,768]{0,1:T(8,128)(2,1)}) %all-gather.29.cloned.1.call-update) | async-done | bytes 1572880 | tf_op jit(solution)/shard_map/all_gather | solution.py:191
  1178.9 4.3 convolution_convert_fusion.7
  1183.3 29.3 %reduce-scatter.23.cloned.1.call-done = bf16[256,768]{1,0:T(8,128)(2,1)} async-done(((bf16[1024,768]{1,0:T(8,128)(2,1)}), bf16[256,768]{1,0:T(8,128)(2,1)}) %reduce-scatter.23.cloned.1.call-update) | async-done | bytes 393232 | tf_op jit(solution)/shard_map/reduce_scatter | solution.py:195
  1215.6 12.4 all-reduce.2
  1231.3 28.3 %all-gather.31.cloned.1.call-done = bf16[1024,768]{1,0:T(8,128)(2,1)} async-done(((bf16[256,768]{1,0:T(8,128)(2,1)}), bf16[1024,768]{1,0:T(8,128)(2,1)}) %all-gather.31.cloned.1.call-update) | async-done | bytes 1572880 | tf_op jit(solution)/shard_map/all_gather | solution.py:204
  1259.6 9.1 convolution_convert_fusion.4
  1268.9 110.7 %reduce-scatter.25.cloned.1.call-done = bf16[256,3072]{1,0:T(8,128)(2,1)} async-done(((bf16[1024,3072]{1,0:T(8,128)(2,1)}), bf16[256,3072]{1,0:T(8,128)(2,1)}) %reduce-scatter.25.cloned.1.call-update) | async-done | bytes 1572880 | tf_op jit(solution)/shard_map/reduce_scatter | solution.py:208
  1379.6 3.6 fusion.43
  1383.3 116.0 %all-gather.33.cloned.1.call-done = bf16[1024,3072]{1,0:T(8,128)(2,1)} async-done(((bf16[256,3072]{1,0:T(8,128)(2,1)}), bf16[1024,3072]{1,0:T(8,128)(2,1)}) %all-gather.33.cloned.1.call-update) | async-done | bytes 6291472 | tf_op jit(solution)/shard_map/all_gather | solution.py:213
  1499.3 9.4 fusion.62
  1508.7 29.3 %reduce-scatter.27.cloned.1.call-done = bf16[256,768]{1,0:T(8,128)(2,1)} async-done(((bf16[1024,768]{1,0:T(8,128)(2,1)}), bf16[256,768]{1,0:T(8,128)(2,1)}) %reduce-scatter.27.cloned.1.call-update) | async-done | bytes 393232 | tf_op jit(solution)/shard_map/reduce_scatter | solution.py:217
  1545.1 12.4 all-reduce.1
  1560.8 28.3 %all-gather.35.cloned.1.call-done = bf16[1024,768]{1,0:T(8,128)(2,1)} async-done(((bf16[256,768]{1,0:T(8,128)(2,1)}), bf16[1024,768]{1,0:T(8,128)(2,1)}) %all-gather.35.cloned.1.call-update) | async-done | bytes 1572880 | tf_op jit(solution)/shard_map/all_gather | solution.py:148
  1589.1 7.3 convolution_convert_fusion
  1600.4 81.4 %reduce-scatter.29.cloned.1.call-done = bf16[256,2304]{1,0:T(8,128)(2,1)} async-done(((bf16[1024,2304]{1,0:T(8,128)(2,1)}), bf16[256,2304]{1,0:T(8,128)(2,1)}) %reduce-scatter.29.cloned.1.call-update) | async-done | bytes 1179664 | tf_op jit(solution)/shard_map/reduce_scatter | solution.py:153
  1717.1 111.1 %all-gather.47.cloned.1.call-done = bf16[1,2,1024,12,128]{4,2,3,1,0:T(8,128)(2,1)} async-done(((bf16[1,2,256,12,128]{4,2,3,1,0:T(8,128)(2,1)}), bf16[1,2,1024,12,128]{4,2,3,1,0:T(8,128)(2,1)}) %all-gather.47.cloned.1.call-update) | async-done | bytes 6291472 | tf_op jit(solution)/shard_map/all_gather | solution.py:178
  1828.2 16.2 copy.69
  1844.4 11.2 reshape.810
  1855.6 12.2 fusion.2
  1867.8 11.7 fusion.7
  1879.5 11.9 fusion.132
  1891.5 36.0 %all-gather.37.cloned.1.call-done = bf16[1024,768]{0,1:T(8,128)(2,1)} async-done(((bf16[256,768]{0,1:T(8,128)(2,1)}), bf16[1024,768]{0,1:T(8,128)(2,1)}) %all-gather.37.cloned.1.call-update) | async-done | bytes 1572880 | tf_op jit(solution)/shard_map/all_gather | solution.py:191
  1927.5 4.3 convolution_convert_fusion.6
  1931.9 29.3 %reduce-scatter.31.cloned.1.call-done = bf16[256,768]{1,0:T(8,128)(2,1)} async-done(((bf16[1024,768]{1,0:T(8,128)(2,1)}), bf16[256,768]{1,0:T(8,128)(2,1)}) %reduce-scatter.31.cloned.1.call-update) | async-done | bytes 393232 | tf_op jit(solution)/shard_map/reduce_scatter | solution.py:195
  1963.6 11.6 all-reduce
  1977.9 28.3 %all-gather.39.cloned.1.call-done = bf16[1024,768]{1,0:T(8,128)(2,1)} async-done(((bf16[256,768]{1,0:T(8,128)(2,1)}), bf16[1024,768]{1,0:T(8,128)(2,1)}) %all-gather.39.cloned.1.call-update) | async-done | bytes 1572880 | tf_op jit(solution)/shard_map/all_gather | solution.py:204
  2006.2 9.1 convolution_convert_fusion.3
  2015.6 110.6 %reduce-scatter.33.cloned.1.call-done = bf16[256,3072]{1,0:T(8,128)(2,1)} async-done(((bf16[1024,3072]{1,0:T(8,128)(2,1)}), bf16[256,3072]{1,0:T(8,128)(2,1)}) %reduce-scatter.33.cloned.1.call-update) | async-done | bytes 1572880 | tf_op jit(solution)/shard_map/reduce_scatter | solution.py:208
  2129.9 116.0 %all-gather.41.cloned.1.call-done = bf16[1024,3072]{1,0:T(8,128)(2,1)} async-done(((bf16[256,3072]{1,0:T(8,128)(2,1)}), bf16[1024,3072]{1,0:T(8,128)(2,1)}) %all-gather.41.cloned.1.call-update) | async-done | bytes 6291472 | tf_op jit(solution)/shard_map/all_gather | solution.py:213
  2245.8 9.4 fusion.65
  2258.0 26.6 %reduce-scatter.35.cloned.1.call-done = bf16[256,768]{1,0:T(8,128)(2,1)} async-done(((bf16[1024,768]{1,0:T(8,128)(2,1)}), bf16[256,768]{1,0:T(8,128)(2,1)}) %reduce-scatter.35.cloned.1.call-update) | async-done | bytes 393232 | tf_op jit(solution)/shard_map/reduce_scatter | solution.py:217
  (245 shorter events, 192.9 us)
Async XLA Ops:
  7.2 85.6 %copy-start = (bf16[1,768,2304]{2,1,0:T(8,128)(2,1)S(1)}, bf16[1,768,2304]{2,1,0:T(8,128)(2,1)}, u32[]{:S(2)}) copy-start(bf16[1,768,2304]{2,1,0:T(8,128)(2,1)} %param.16) | copy-start | bytes 10616836
  7.2 85.5 %all-gather.19.cloned.1.call-start = ((), (), s32[]{:S(2)}) async-start(), calls=%async_computation.12 | async-start | bytes 1966080 | tf_op jit(solution)/shard_map/all_gather | solution.py:148
  38.4 23.9 %copy-start.7 = (bf16[2,256,768]{2,1,0:T(8,128)(2,1)S(1)}, bf16[2,256,768]{2,1,0:T(8,128)(2,1)}, u32[]{:S(2)}) copy-start(bf16[2,256,768]{2,1,0:T(8,128)(2,1)} %param.11) | copy-start | bytes 2359300
  60.9 1.4 copy-start.6
  63.3 122.2 %reduce-scatter.13.cloned.1.call-start = ((), (), s32[]{:S(2)}) async-start(), calls=%async_computation.13 | async-start | bytes 5898240 | tf_op jit(solution)/shard_map/reduce_scatter | solution.py:153
  100.0 0.7 copy-start.29
  100.1 231.7 %all-gather.43.cloned.1.call-start = ((), (), s32[]{:S(2)}) async-start(), calls=%async_computation.36 | async-start | bytes 7864320 | tf_op jit(solution)/shard_map/all_gather | solution.py:178
  187.8 1.7 copy-start.1
  191.8 0.8 copy-start.21
  191.8 0.8 copy-start.19
  199.5 3.5 copy-start.23
  199.5 3.5 copy-start.24
  215.8 215.2 %all-gather.21.cloned.1.call-start = ((), (), s32[]{:S(2)}) async-start(), calls=%async_computation.14 | async-start | bytes 1966080 | tf_op jit(solution)/shard_map/all_gather | solution.py:191
  359.2 12.2 copy-start.16
  371.3 11.7 copy-start.11
  394.9 69.7 %reduce-scatter.15.cloned.1.call-start = ((), (), s32[]{:S(2)}) async-start(), calls=%async_computation.15 | async-start | bytes 1966080 | tf_op jit(solution)/shard_map/reduce_scatter | solution.py:195
  435.3 76.3 %all-gather.23.cloned.1.call-start = ((), (), s32[]{:S(2)}) async-start(), calls=%async_computation.16 | async-start | bytes 1966080 | tf_op jit(solution)/shard_map/all_gather | solution.py:204
  483.3 148.3 %reduce-scatter.17.cloned.1.call-start = ((), (), s32[]{:S(2)}) async-start(), calls=%async_computation.17 | async-start | bytes 7864320 | tf_op jit(solution)/shard_map/reduce_scatter | solution.py:208
  520.8 230.7 %all-gather.25.cloned.1.call-start = ((), (), s32[]{:S(2)}) async-start(), calls=%async_computation.18 | async-start | bytes 7864320 | tf_op jit(solution)/shard_map/all_gather | solution.py:213
  635.4 154.8 %reduce-scatter.19.cloned.1.call-start = ((), (), s32[]{:S(2)}) async-start(), calls=%async_computation.19 | async-start | bytes 1966080 | tf_op jit(solution)/shard_map/reduce_scatter | solution.py:217
  760.8 79.7 %all-gather.27.cloned.1.call-start = ((), (), s32[]{:S(2)}) async-start(), calls=%async_computation.20 | async-start | bytes 1966080 | tf_op jit(solution)/shard_map/all_gather | solution.py:148
  790.2 4.9 copy-start.8
  791.9 4.6 copy-start.13
  791.9 3.1 collective-permute-start
  812.2 121.1 %reduce-scatter.21.cloned.1.call-start = ((), (), s32[]{:S(2)}) async-start(), calls=%async_computation.21 | async-start | bytes 5898240 | tf_op jit(solution)/shard_map/reduce_scatter | solution.py:153
  847.8 231.9 %all-gather.45.cloned.1.call-start = ((), (), s32[]{:S(2)}) async-start(), calls=%async_computation.37 | async-start | bytes 7864320 | tf_op jit(solution)/shard_map/all_gather | solution.py:178
  851.1 1.2 copy-start.4
  935.6 1.7 copy-start.2
  939.6 0.8 copy-start.22
  939.6 0.8 copy-start.20
  947.3 3.5 copy-start.27
  947.3 3.5 copy-start.28
  963.7 215.3 %all-gather.29.cloned.1.call-start = ((), (), s32[]{:S(2)}) async-start(), calls=%async_computation.22 | async-start | bytes 1966080 | tf_op jit(solution)/shard_map/all_gather | solution.py:191
  1107.1 12.2 copy-start.15
  1119.2 11.7 copy-start.12
  1142.9 69.7 %reduce-scatter.23.cloned.1.call-start = ((), (), s32[]{:S(2)}) async-start(), calls=%async_computation.23 | async-start | bytes 1966080 | tf_op jit(solution)/shard_map/reduce_scatter | solution.py:195
  1183.3 76.3 %all-gather.31.cloned.1.call-start = ((), (), s32[]{:S(2)}) async-start(), calls=%async_computation.24 | async-start | bytes 1966080 | tf_op jit(solution)/shard_map/all_gather | solution.py:204
  1231.3 148.3 %reduce-scatter.25.cloned.1.call-start = ((), (), s32[]{:S(2)}) async-start(), calls=%async_computation.25 | async-start | bytes 7864320 | tf_op jit(solution)/shard_map/reduce_scatter | solution.py:208
  1268.7 230.6 %all-gather.33.cloned.1.call-start = ((), (), s32[]{:S(2)}) async-start(), calls=%async_computation.26 | async-start | bytes 7864320 | tf_op jit(solution)/shard_map/all_gather | solution.py:213
  1383.2 154.8 %reduce-scatter.27.cloned.1.call-start = ((), (), s32[]{:S(2)}) async-start(), calls=%async_computation.27 | async-start | bytes 1966080 | tf_op jit(solution)/shard_map/reduce_scatter | solution.py:217
  1508.7 80.4 %all-gather.35.cloned.1.call-start = ((), (), s32[]{:S(2)}) async-start(), calls=%async_computation.28 | async-start | bytes 1966080 | tf_op jit(solution)/shard_map/all_gather | solution.py:148
  1538.0 5.7 copy-start.9
  1540.6 3.1 collective-permute-start.1
  1560.7 121.1 %reduce-scatter.29.cloned.1.call-start = ((), (), s32[]{:S(2)}) async-start(), calls=%async_computation.29 | async-start | bytes 5898240 | tf_op jit(solution)/shard_map/reduce_scatter | solution.py:153
  1596.4 231.8 %all-gather.47.cloned.1.call-start = ((), (), s32[]{:S(2)}) async-start(), calls=%async_computation.38 | async-start | bytes 7864320 | tf_op jit(solution)/shard_map/all_gather | solution.py:178
  1598.1 1.2 copy-start.5
  1684.2 1.7 copy-start.3
  1688.2 0.8 copy-start.18
  1688.2 0.8 copy-start.17
  1695.9 3.5 copy-start.25
  1695.9 3.5 copy-start.26
  1712.2 215.3 %all-gather.37.cloned.1.call-start = ((), (), s32[]{:S(2)}) async-start(), calls=%async_computation.30 | async-start | bytes 1966080 | tf_op jit(solution)/shard_map/all_gather | solution.py:191
  1855.6 12.2 copy-start.14
  1867.8 11.7 copy-start.10
  1891.4 69.7 %reduce-scatter.31.cloned.1.call-start = ((), (), s32[]{:S(2)}) async-start(), calls=%async_computation.31 | async-start | bytes 1966080 | tf_op jit(solution)/shard_map/reduce_scatter | solution.py:195
  1931.8 74.4 %all-gather.39.cloned.1.call-start = ((), (), s32[]{:S(2)}) async-start(), calls=%async_computation.32 | async-start | bytes 1966080 | tf_op jit(solution)/shard_map/all_gather | solution.py:204
  1977.8 148.3 %reduce-scatter.33.cloned.1.call-start = ((), (), s32[]{:S(2)}) async-start(), calls=%async_computation.33 | async-start | bytes 7864320 | tf_op jit(solution)/shard_map/reduce_scatter | solution.py:208
  2015.3 230.6 %all-gather.41.cloned.1.call-start = ((), (), s32[]{:S(2)}) async-start(), calls=%async_computation.34 | async-start | bytes 7864320 | tf_op jit(solution)/shard_map/all_gather | solution.py:213
  2129.8 154.8 %reduce-scatter.35.cloned.1.call-start = ((), (), s32[]{:S(2)}) async-start(), calls=%async_computation.35 | async-start | bytes 1966080 | tf_op jit(solution)/shard_map/reduce_scatter | solution.py:217
Sparse Core Ops, SparseCore 0:
  63.4 29.2 all-gather.18
  100.2 85.2 reduce-scatter.12
  215.9 115.8 all-gather.42
  395.1 35.8 all-gather.20
  435.5 29.1 reduce-scatter.14
  483.4 28.2 all-gather.22
  520.9 110.7 reduce-scatter.16
  635.5 115.8 all-gather.24
  760.9 29.1 reduce-scatter.18
  812.3 28.1 all-gather.26
  848.0 85.2 reduce-scatter.20
  963.8 115.8 all-gather.44
  1143.0 35.8 all-gather.28
  1183.4 29.1 reduce-scatter.22
  1231.4 28.1 all-gather.30
  1268.8 110.7 reduce-scatter.24
  1383.4 115.8 all-gather.32
  1508.8 29.1 reduce-scatter.26
  1560.9 28.1 all-gather.34
  1596.6 85.2 reduce-scatter.28
  1712.3 115.8 all-gather.46
  1891.6 35.8 all-gather.36
  1931.9 29.1 reduce-scatter.30
  1978.0 28.1 all-gather.38
  2015.4 110.7 reduce-scatter.32
  2129.9 115.8 all-gather.40
  2255.4 29.1 reduce-scatter.34
where the time goes:
time: 2300 us; the launch traced here: 2290 us
  waiting for transfers between devices  1700 us (74%)
  other arithmetic  175 us (8%)
  matrix products  167 us (7%)
  local copies, waits for them, and re-layouts  155 us (7%)
  blocking collectives  75 us (3%)
    all_gather x3, waiting for transfers between devices, per_device(): lax.all_gather(hidden_act, 'narrow', axis=0, tiled=True)  348 us
    reduce_scatter x3, waiting for transfers between devices, per_device(): lax.psum_scatter(up_terms.astype(jnp.bfloat16), 'narrow', scatter_dimensi...  332 us
    all_gather x3, waiting for transfers between devices, per_device(): piece = lax.all_gather(local_pairs, 'narrow', axis=1, tiled=True)  329 us
    reduce_scatter x3, waiting for transfers between devices, per_device(): lax.psum_scatter(qkv_terms.astype(jnp.bfloat16), 'narrow', scatter_dimens...  236 us
    all_gather x3, waiting for transfers between devices, per_device(): lax.all_gather(attended, 'narrow', axis=0, tiled=True)  108 us
    reduce_scatter x3, waiting for transfers between devices, per_device(): lax.psum_scatter(proj_terms.astype(jnp.bfloat16), 'wide', scatter_dimensi...  87.8 us
    all_gather x3, waiting for transfers between devices, per_device(): lax.all_gather(entry_rows, 'wide', axis=0, tiled=True)  86 us
    reduce_scatter x3, waiting for transfers between devices, per_device(): lax.psum_scatter(down_terms.astype(jnp.bfloat16), 'wide', scatter_dimensi...  85.1 us
  transfers between devices with their start and end apart: 29, of which 29 were waited for; matrix products, arithmetic and copies ran while one was open for 2% of the time, Pallas kernels for 0%

commit v1 on v0

v1 whole, which is shorter than its diff:
```python
import functools

import jax
import jax.numpy as jnp
from jax import lax
from jax.experimental import pallas as pl
from jax.experimental.pallas import tpu as pltpu
from jax.sharding import PartitionSpec as P

EPS_ROW = 1e-05
EPS_HEAD = 1e-06
FAR = -1e30
LOG2E = 1.4426950408889634
BF = jnp.bfloat16
F32 = jnp.float32


def time_features(timesteps, feature_count):
    half_count = feature_count // 2
    frequency = jnp.exp(-jnp.log(10000.0) * jnp.arange(half_count, dtype=F32) / half_count)
    angle = timesteps.astype(F32)[:, None] * frequency[None, :]
    return jnp.concatenate([jnp.cos(angle), jnp.sin(angle)], axis=1)


def rotary_tables(row_positions, head_dim):
    dim_frame = head_dim // 4
    dim_plane = head_dim // 8 * 3
    pieces = []
    for axis_pos, span_dims in ((0, dim_frame), (1, dim_plane), (2, dim_plane)):
        frequency = 10000.0 ** (-jnp.arange(0, span_dims, 2, dtype=F32) / span_dims)
        pieces.append(row_positions[axis_pos].astype(F32)[:, None] * jnp.repeat(frequency, 2)[None, :])
    angles = jnp.concatenate(pieces, axis=1)
    sign = jnp.where(jnp.arange(head_dim) % 2 == 0, -1.0, 1.0).astype(F32)
    cosine = jnp.cos(angles)
    sine = jnp.sin(angles) * sign[None, :]
    return jnp.concatenate([cosine, cosine], axis=1), jnp.concatenate([sine, sine], axis=1)


def prepare_kernel(heads, head_dim, qkv_ref, cos_ref, sin_ref, kind_ref, norm_ref, q_ref, pair_ref):
    pair = 2 * head_dim
    rows = qkv_ref.shape[0]
    lane = lax.broadcasted_iota(jnp.int32, (rows, pair), 1)
    first = lane < head_dim
    even = lane % 2 == 0
    request = kind_ref[...] // 2
    mask_part = jnp.where(lane == head_dim + request, 1.0, 0.0)
    cosine = cos_ref[...]
    sine = sin_ref[...]
    gain = norm_ref[0:1, :]
    bias = norm_ref[1:2, :]
    for h in range(heads):
        base = 3 * head_dim * h
        both = qkv_ref[:, base : base + pair].astype(F32)
        key_value = qkv_ref[:, base + head_dim : base + head_dim + pair].astype(F32)
        mean_q = jnp.sum(jnp.where(first, both, 0.0), axis=1, keepdims=True) / head_dim
        mean_k = jnp.sum(jnp.where(first, 0.0, both), axis=1, keepdims=True) / head_dim
        center = both - jnp.where(first, mean_q, mean_k)
        square = center * center
        var_q = jnp.sum(jnp.where(first, square, 0.0), axis=1, keepdims=True) / head_dim
        var_k = jnp.sum(jnp.where(first, 0.0, square), axis=1, keepdims=True) / head_dim
        scale = jnp.where(first, lax.rsqrt(var_q + EPS_HEAD), lax.rsqrt(var_k + EPS_HEAD))
        normed = center * scale * gain + bias
        swapped = jnp.where(even, pltpu.roll(normed, pair - 1, 1), pltpu.roll(normed, 1, 1))
        turned = normed * cosine + swapped * sine
        q_ref[h] = jnp.where(first, turned, mask_part).astype(BF)
        pair_ref[h] = jnp.where(first, pltpu.roll(turned, head_dim, 1), key_value).astype(BF)


def prepare(qkv, cosine, sine, kinds, norm_rows, heads, head_dim):
    rows, width = qkv.shape
    block = min(256, rows)
    pair = 2 * head_dim
    return pl.pallas_call(
        functools.partial(prepare_kernel, heads, head_dim),
        grid=(rows // block,),
        in_specs=[
            pl.BlockSpec((block, width), lambda i: (i, 0)),
            pl.BlockSpec((block, pair), lambda i: (i, 0)),
            pl.BlockSpec((block, pair), lambda i: (i, 0)),
            pl.BlockSpec((block, 1), lambda i: (i, 0)),
            pl.BlockSpec((2, pair), lambda i: (0, 0)),
        ],
        out_specs=[
            pl.BlockSpec((heads, block, pair), lambda i: (0, i, 0)),
            pl.BlockSpec((heads, block, pair), lambda i: (0, i, 0)),
        ],
        out_shape=[
            jax.ShapeDtypeStruct((heads, rows, pair), BF),
            jax.ShapeDtypeStruct((heads, rows, pair), BF),
        ],
        compiler_params=pltpu.CompilerParams(vmem_limit_bytes=48 * 1024 * 1024),
        name="prepare",
    )(qkv, cosine, sine, kinds[:, None], norm_rows)


def attend_kernel(heads, head_dim, q_ref, own_ref, other_ref, own_mask_ref, other_mask_ref, out_ref):
    pair = 2 * head_dim
    keys_count = own_ref.shape[1]
    lane = lax.broadcasted_iota(jnp.int32, (keys_count, pair), 1)
    first = lane < head_dim
    one = jnp.where(lane == 0, 1.0, 0.0).astype(BF)
    factor = LOG2E * head_dim ** (-0.5)
    pieces = []
    for h in range(heads):
        queries = q_ref[h]
        own = own_ref[h]
        other = other_ref[h]
        contract = (((1,), (1,)), ((), ()))
        scores_a = lax.dot_general(
            queries, jnp.where(first, own, own_mask_ref[...]), contract, preferred_element_type=F32
        )
        scores_b = lax.dot_general(
            queries, jnp.where(first, other, other_mask_ref[...]), contract, preferred_element_type=F32
        )
        top = jnp.maximum(
            jnp.max(scores_a, axis=1, keepdims=True), jnp.max(scores_b, axis=1, keepdims=True)
        )
        weights_a = jnp.exp2((scores_a - top) * factor).astype(BF)
        weights_b = jnp.exp2((scores_b - top) * factor).astype(BF)
        mixed = jnp.dot(weights_a, jnp.where(first, one, own), preferred_element_type=F32)
        mixed += jnp.dot(weights_b, jnp.where(first, one, other), preferred_element_type=F32)
        pieces.append(mixed[:, head_dim:] / mixed[:, 0:1])
    out_ref[...] = jnp.concatenate(pieces, axis=1).astype(BF)


def attend(queries, own, other, own_mask, other_mask, head_dim):
    heads, rows, pair = queries.shape
    keys_count = own.shape[1]
    block = min(256, rows)
    whole = pl.BlockSpec((heads, keys_count, pair), lambda i: (0, 0, 0))
    mask = pl.BlockSpec((keys_count, pair), lambda i: (0, 0))
    return pl.pallas_call(
        functools.partial(attend_kernel, heads, head_dim),
        grid=(rows // block,),
        in_specs=[pl.BlockSpec((heads, block, pair), lambda i: (0, i, 0)), whole, whole, mask, mask],
        out_specs=pl.BlockSpec((block, heads * head_dim), lambda i: (i, 0)),
        out_shape=jax.ShapeDtypeStruct((rows, heads * head_dim), BF),
        compiler_params=pltpu.CompilerParams(vmem_limit_bytes=48 * 1024 * 1024),
        name="attend",
    )(queries, own, other, own_mask, other_mask)


def key_mask(kinds, head_dim):
    lane = jnp.arange(2 * head_dim)[None, :]
    foreign = (lane >= head_dim) & (lane < head_dim + 2) & (lane - head_dim != (kinds // 2)[:, None])
    return jnp.where(foreign, FAR, 0.0).astype(BF)


def pick(table, kinds, part):
    column = kinds[:, None]
    low = jnp.where(column == 0, table[0, part][None], table[1, part][None])
    high = jnp.where(column == 2, table[2, part][None], table[3, part][None])
    return jnp.where(column < 2, low, high)


def exchange(blocks, axis):
    n = lax.axis_size(axis)
    me = lax.axis_index(axis)
    got = jnp.zeros_like(blocks)
    got = lax.dynamic_update_slice_in_dim(
        got, lax.dynamic_slice_in_dim(blocks, me, 1, 0), me, 0
    )
    for step in range(1, n):
        there = (me + step) % n
        back = (me + n - step) % n
        block = lax.dynamic_slice_in_dim(blocks, there, 1, 0)
        block = lax.ppermute(block, axis, [(i, (i + step) % n) for i in range(n)])
        got = lax.dynamic_update_slice_in_dim(got, block, back, 0)
    return got


def per_device(
    hidden_in,
    row_kind,
    positions,
    timesteps,
    stale_cache,
    w_qkv,
    qk_norm,
    w_out,
    ada_weight,
    w_up,
    w_down,
):
    n_wide = lax.axis_size("wide")
    n_narrow = lax.axis_size("narrow")
    wide_idx = lax.axis_index("wide")
    narrow_idx = lax.axis_index("narrow")
    section = lax.axis_index("section")
    patch_count, rows_a, feat_a = hidden_in.shape
    total_rows = rows_a * n_wide
    rows_b = total_rows // n_narrow
    heads_local = stale_cache.shape[3]
    pair = stale_cache.shape[4]
    head_dim = pair // 2
    model_width = feat_a * n_narrow
    by_heads = heads_local % n_narrow == 0
    heads = heads_local // n_narrow if by_heads else heads_local
    lead = section == 0

    def swap(value):
        return lax.ppermute(value, "section", [(0, 1), (1, 0)])

    def both_layers(own):
        other = swap(own)
        return (jnp.where(lead, own, other), jnp.where(lead, other, own))

    qkv_weights = both_layers(w_qkv[0])
    out_weights = both_layers(w_out[0])
    up_weights = both_layers(w_up[0])
    down_weights = both_layers(w_down[0])
    norm_rows = both_layers(qk_norm[0])

    activated = jax.nn.silu(time_features(timesteps, ada_weight.shape[2])).astype(BF)
    modulation = jnp.einsum("re,kesd->krsd", activated, ada_weight[0], preferred_element_type=F32)
    tables = both_layers(modulation.reshape(2, 4, 3, feat_a))

    kinds = lax.dynamic_slice_in_dim(row_kind, section, 1, 0)[0]
    kinds_other = lax.dynamic_slice_in_dim(row_kind, 1 - section, 1, 0)[0]
    own_mask = key_mask(kinds, head_dim)
    other_mask = key_mask(kinds_other, head_dim)
    kinds_a = lax.dynamic_slice_in_dim(kinds, wide_idx * rows_a, rows_a)
    places = lax.dynamic_slice_in_dim(positions, section, 1, 1)[:, 0]
    kinds_q = kinds
    if not by_heads:
        places = lax.dynamic_slice_in_dim(places, narrow_idx * rows_b, rows_b, 1)
        kinds_q = lax.dynamic_slice_in_dim(kinds, narrow_idx * rows_b, rows_b)
    cosine, sine = rotary_tables(places, head_dim)

    def to_heads(rows_part):
        if by_heads:
            blocks = rows_part.reshape(rows_b, n_narrow, heads, pair).transpose(1, 2, 0, 3)
            return exchange(blocks, "narrow").transpose(1, 0, 2, 3).reshape(heads, total_rows, pair)
        return lax.all_gather(rows_part.transpose(1, 0, 2), "narrow", axis=1, tiled=True)

    def to_rows(pairs):
        if by_heads:
            blocks = pairs.reshape(heads, n_narrow, rows_b, pair).transpose(1, 0, 2, 3)
            return exchange(blocks, "narrow").transpose(2, 0, 1, 3).reshape(rows_b, heads_local, pair)
        return pairs.transpose(1, 0, 2)

    stale = to_heads(stale_cache[0, 1])

    def normalize(values):
        moments = lax.psum(
            jnp.stack([jnp.sum(values, axis=1), jnp.sum(values * values, axis=1)]), "narrow"
        )
        row_mean = moments[0] / model_width
        variance = moments[1] / model_width - row_mean * row_mean
        return (values - row_mean[:, None]) * lax.rsqrt(variance + EPS_ROW)[:, None]

    layer_in = lax.dynamic_slice_in_dim(hidden_in, section, 1, 0)[0]
    results = []
    caches = []
    for layer in range(2):
        table = tables[layer]
        x_in = layer_in.astype(F32)
        entry = normalize(x_in) * (1.0 + pick(table[0], kinds_a, 1)) + pick(table[0], kinds_a, 0)
        qkv_terms = jnp.dot(
            lax.all_gather(entry.astype(BF), "wide", axis=0, tiled=True),
            qkv_weights[layer],
            preferred_element_type=F32,
        ).astype(BF)
        qkv = lax.psum_scatter(
            qkv_terms, "narrow", scatter_dimension=1 if by_heads else 0, tiled=True
        )
        norms = norm_rows[layer]
        norm_pair = jnp.stack(
            [jnp.concatenate([norms[0], norms[2]]), jnp.concatenate([norms[1], norms[3]])]
        )
        queries, fresh = prepare(qkv, cosine, sine, kinds_q, norm_pair, heads, head_dim)
        caches.append(to_rows(fresh))
        if not by_heads:
            fresh = lax.all_gather(fresh, "narrow", axis=1, tiled=True)
        if layer == 0:
            other = jnp.where(lead, stale, swap(fresh))
        else:
            other = swap(jnp.where(lead, fresh, stale))
        attended = attend(queries, fresh, other, own_mask, other_mask, head_dim)
        attended = lax.all_gather(attended, "narrow", axis=1 if by_heads else 0, tiled=True)
        proj_terms = jnp.dot(attended, out_weights[layer], preferred_element_type=F32).astype(BF)
        projected = lax.psum_scatter(proj_terms, "wide", scatter_dimension=0, tiled=True)
        after = x_in + pick(table[0], kinds_a, 2) * projected.astype(F32)
        entry = normalize(after) * (1.0 + pick(table[1], kinds_a, 1)) + pick(table[1], kinds_a, 0)
        up_terms = jnp.dot(
            lax.all_gather(entry.astype(BF), "wide", axis=0, tiled=True),
            up_weights[layer],
            preferred_element_type=F32,
        ).astype(BF)
        up_sum = lax.psum_scatter(up_terms, "narrow", scatter_dimension=0, tiled=True)
        inner = jax.nn.gelu(up_sum.astype(F32), approximate=True).astype(BF)
        down_terms = jnp.dot(
            lax.all_gather(inner, "narrow", axis=0, tiled=True),
            down_weights[layer],
            preferred_element_type=F32,
        ).astype(BF)
        down_sum = lax.psum_scatter(down_terms, "wide", scatter_dimension=0, tiled=True)
        layer_in = (after + pick(table[1], kinds_a, 2) * down_sum.astype(F32)).astype(BF)
        results.append(layer_in)

    def by_layer(parts):
        got = swap(jnp.where(lead, parts[1], parts[0]))
        kept = jnp.where(lead, parts[0], parts[1])
        return jnp.stack([jnp.where(lead, kept, got), jnp.where(lead, got, kept)])[None]

    return (by_layer(results), by_layer(caches))


def solution(mesh):
    in_specs = (
        P(None, "wide", "narrow"),
        P(),
        P(),
        P(),
        P("section", None, "narrow", "wide", None),
        P("section", "narrow", "wide"),
        P("section", None, None),
        P("section", "wide", "narrow"),
        P("section", None, None, None, "narrow"),
        P("section", "narrow", "wide"),
        P("section", "wide", "narrow"),
    )
    out_specs = (P("section", None, "wide", "narrow"), P("section", None, "narrow", "wide", None))
    return jax.shard_map(
        per_device, mesh=mesh, in_specs=in_specs, out_specs=out_specs, check_vma=False
    )
```

time: 2300 us -> 1180 us (0.51)
  waiting for transfers between devices: 1700 us -> 925 us
  other arithmetic: 175 us -> 31.6 us
  local copies, waits for them, and re-layouts: 155 us -> 19.9 us
  matrix products: 167 us -> 70.7 us
  Pallas kernels: 0 us -> 38.5 us
  blocking collectives: 75 us -> 48.5 us
    all_gather x15 -> x8, waiting for transfers between devices: 956 us -> 411 us  [the longest x2 223 us: per_device(): lax.all_gather(inner, 'narrow', axis=0, tiled=True)]
    reduce_scatter x12 -> x6, waiting for transfers between devices: 741 us -> 311 us  [the longest x2 222 us: per_device(): lax.psum_scatter(up_terms, 'narrow', scatter_dimension=0, tiled=True)]
    unnamed x27 -> x18, waiting for transfers between devices: 0.44 us -> 169 us
    dot_general x18 -> x8, matrix products: 162 us -> 65.6 us  [the longest x2 20.1 us: per_device(): jnp.dot(lax.all_gather(inner, 'narrow', axis=0, tiled=True), down_weights...]
    reduce_sum x10 -> x0, other arithmetic: 60.3 us -> none  [the longest x3 35 us: partial_softmax(): total = jnp.sum(weights, axis=2)]
    all_gather x3 -> x0, local copies, waits for them, and re-layouts: 48.6 us -> none  [per_device(): piece = lax.all_gather(local_pairs, 'narrow', axis=1, tiled=True)]
    pallas_call x0 -> x4, Pallas kernels: none -> 38.5 us  [the longest x2 22 us: attend(): pl.pallas_call(functools.partial(attend_kernel, heads, head_dim), grid=(r...]
    reshape x3 -> x0, local copies, waits for them, and re-layouts: 33.5 us -> none  [per_device(): keys_flat = piece.reshape(patch_count * count, heads_local, 2 * head_dim)]
  transfers between devices with their start and end apart: 29 -> 35, of which waited for: 29 -> 23; matrix products, arithmetic and copies ran while one was open for 2% -> 2% of each run, Pallas kernels for 0% -> 1%
where the time goes in v1:
time: 1180 us; the launch traced here: 1170 us
  waiting for transfers between devices  925 us (78%)
  matrix products  70.7 us (6%)
  blocking collectives  48.5 us (4%)
  Pallas kernels  38.5 us (3%)
  other arithmetic  31.6 us (3%)
  starting transfers between devices  20.5 us (2%)
  local copies, waits for them, and re-layouts  19.9 us (2%)
  between operations  14.9 us (1%)
    all_gather x2, waiting for transfers between devices, per_device(): lax.all_gather(inner, 'narrow', axis=0, tiled=True)  223 us
    reduce_scatter x2, waiting for transfers between devices, per_device(): lax.psum_scatter(up_terms, 'narrow', scatter_dimension=0, tiled=True)  222 us
    unnamed x18, waiting for transfers between devices  169 us
    all_gather x4, waiting for transfers between devices, per_device(): lax.all_gather(entry.astype(BF), 'wide', axis=0, tiled=True)  114 us
    all_gather x2, waiting for transfers between devices, per_device(): lax.all_gather(attended, 'narrow', axis=1 if by_heads else 0, tiled=True)  73.1 us
    reduce_scatter x2, waiting for transfers between devices, per_device(): lax.psum_scatter(proj_terms, 'wide', scatter_dimension=0, tiled=True)  58.8 us
    psum x4, blocking collectives, normalize(): lax.psum(jnp.stack([jnp.sum(values, axis=1), jnp.sum(values * values, axi...  48.5 us
    reduce_scatter x2, waiting for transfers between devices, per_device(): lax.psum_scatter(down_terms, 'wide', scatter_dimension=0, tiled=True)  30.1 us
  transfers between devices with their start and end apart: 35, of which 23 were waited for; matrix products, arithmetic and copies ran while one was open for 2% of the time, Pallas kernels for 1%

profile of v1, /device:TPU:0, one launch (start us, length us, event | category | flops | bytes accessed | tf_op | source)
XLA Modules:
  0.0 1169.4 jit_solution(9258117394250500189)
XLA Ops:
  8.0 5.1 fusion.40
  14.1 13.4 %psum.28 = f32[2,256]{1,0:T(2,128)S(1)} all-reduce(f32[2,256]{1,0:T(2,128)S(1)} %pad_maximum_fusion.4), channel_id=1, replica_groups=mesh['section'=2,'wide'=4,'narrow'=4] {'narrow'}, use_global_device_ids=true, to_apply=%region_2.3 | all-reduce | flops 512 | bytes 4096 | tf_op jit(solution)/shard_map/psum | solution.py:245
  29.1 1.9 fusion.50
  31.1 29.3 %all-gather.9.cloned.1.call-done = bf16[1024,768]{1,0:T(8,128)(2,1)} async-done(((bf16[256,768]{1,0:T(8,128)(2,1)}), bf16[1024,768]{1,0:T(8,128)(2,1)}) %all-gather.9.cloned.1.call-update) | async-done | bytes 1572880 | tf_op jit(solution)/shard_map/all_gather | solution.py:260
  60.4 8.5 fusion.2
  71.4 1.5 collective-permute-start.3
  72.8 2.4 collective-permute-start.4
  75.3 1.6 collective-permute-start.5
  77.8 2.4 sine_multiply_fusion
  82.7 83.9 %reduce-scatter.25.cloned.1.call-done = bf16[576,1024]{1,0:T(8,128)(2,1)} async-done(((bf16[2304,1024]{1,0:T(8,128)(2,1)}), bf16[576,1024]{1,0:T(8,128)(2,1)}) %reduce-scatter.25.cloned.1.call-update) | async-done | bytes 1179664
  166.6 1.7 copy.66.qkv_ref
  168.3 8.5 prepare.2
  177.9 1.1 select_convert_fusion
  183.9 11.6 attend.2
  196.5 1.1 collective-permute-start.7
  197.6 2.8 collective-permute-done.7
  200.4 35.4 %all-gather.11.cloned.1.call-done = bf16[1024,768]{0,1:T(8,128)(2,1)} async-done(((bf16[1024,192]{0,1:T(8,128)(2,1)}), bf16[1024,768]{0,1:T(8,128)(2,1)}) %all-gather.11.cloned.1.call-update) | async-done | bytes 1572880 | tf_op jit(solution)/shard_map/all_gather | solution.py:280
  235.8 4.3 convolution_convert_fusion.5
  240.5 29.7 %reduce-scatter.13.cloned.1.call-done = bf16[256,768]{1,0:T(8,128)(2,1)} async-done(((bf16[1024,768]{1,0:T(8,128)(2,1)}), bf16[256,768]{1,0:T(8,128)(2,1)}) %reduce-scatter.13.cloned.1.call-update) | async-done | bytes 393232 | tf_op jit(solution)/shard_map/reduce_scatter | solution.py:282
  270.2 1.4 fusion.78
  271.6 11.7 psum.29
  283.3 1.8 add_convert_fusion.3
  285.5 28.1 %all-gather.13.cloned.1.call-done = bf16[1024,768]{1,0:T(8,128)(2,1)} async-done(((bf16[256,768]{1,0:T(8,128)(2,1)}), bf16[1024,768]{1,0:T(8,128)(2,1)}) %all-gather.13.cloned.1.call-update) | async-done | bytes 1572880 | tf_op jit(solution)/shard_map/all_gather | solution.py:286
  313.6 9.1 convolution_convert_fusion.3
  322.7 111.0 %reduce-scatter.15.cloned.1.call-done = bf16[256,3072]{1,0:T(8,128)(2,1)} async-done(((bf16[1024,3072]{1,0:T(8,128)(2,1)}), bf16[256,3072]{1,0:T(8,128)(2,1)}) %reduce-scatter.15.cloned.1.call-update) | async-done | bytes 1572880 | tf_op jit(solution)/shard_map/reduce_scatter | solution.py:290
  433.7 3.6 fusion.23
  437.5 8.2 collective-permute-done.9
  445.8 107.6 %all-gather.15.cloned.1.call-done = bf16[1024,3072]{1,0:T(8,128)(2,1)} async-done(((bf16[256,3072]{1,0:T(8,128)(2,1)}), bf16[1024,3072]{1,0:T(8,128)(2,1)}) %all-gather.15.cloned.1.call-update) | async-done | bytes 6291472 | tf_op jit(solution)/shard_map/all_gather | solution.py:293
  553.4 9.4 fusion.30
  563.0 30.1 %reduce-scatter.17.cloned.1.call-done = bf16[256,768]{1,0:T(8,128)(2,1)} async-done(((bf16[1024,768]{1,0:T(8,128)(2,1)}), bf16[256,768]{1,0:T(8,128)(2,1)}) %reduce-scatter.17.cloned.1.call-update) | async-done | bytes 393232 | tf_op jit(solution)/shard_map/reduce_scatter | solution.py:297
  593.1 1.4 convert_reduce_fusion
  594.5 11.7 %psum.30 = f32[2,256]{1,0:T(2,128)S(1)} all-reduce(f32[2,256]{1,0:T(2,128)S(1)} %pad_maximum_fusion.6), channel_id=1, replica_groups=mesh['section'=2,'wide'=4,'narrow'=4] {'narrow'}, use_global_device_ids=true, to_apply=%region_12.13 | all-reduce | flops 512 | bytes 4096 | tf_op jit(solution)/shard_map/psum | solution.py:245
  606.3 1.9 fusion.55
  608.2 28.3 %all-gather.17.cloned.1.call-done = bf16[1024,768]{1,0:T(8,128)(2,1)} async-done(((bf16[256,768]{1,0:T(8,128)(2,1)}), bf16[1024,768]{1,0:T(8,128)(2,1)}) %all-gather.17.cloned.1.call-update) | async-done | bytes 1572880 | tf_op jit(solution)/shard_map/all_gather | solution.py:260
  636.5 9.5 fusion.3
  646.9 84.6 %reduce-scatter.27.cloned.1.call-done = bf16[576,1024]{1,0:T(8,128)(2,1)} async-done(((bf16[2304,1024]{1,0:T(8,128)(2,1)}), bf16[576,1024]{1,0:T(8,128)(2,1)}) %reduce-scatter.27.cloned.1.call-update) | async-done | bytes 1179664
  731.6 1.7 copy.68.qkv_ref
  733.3 1.0 copy-done.1
  734.3 7.9 prepare.3
  742.2 1.3 bitcast_select_fusion.2
  743.6 2.3 collective-permute-done.10.other_ref
  745.9 10.4 attend.3
  757.4 37.7 %all-gather.19.cloned.1.call-done = bf16[1024,768]{0,1:T(8,128)(2,1)} async-done(((bf16[1024,192]{0,1:T(8,128)(2,1)}), bf16[1024,768]{0,1:T(8,128)(2,1)}) %all-gather.19.cloned.1.call-update) | async-done | bytes 1572880 | tf_op jit(solution)/shard_map/all_gather | solution.py:280
  795.1 4.3 convolution_convert_fusion.4
  800.2 29.2 %reduce-scatter.19.cloned.1.call-done = bf16[256,768]{1,0:T(8,128)(2,1)} async-done(((bf16[1024,768]{1,0:T(8,128)(2,1)}), bf16[256,768]{1,0:T(8,128)(2,1)}) %reduce-scatter.19.cloned.1.call-update) | async-done | bytes 393232 | tf_op jit(solution)/shard_map/reduce_scatter | solution.py:282
  829.4 1.4 fusion.77
  830.8 11.7 psum.31
  842.5 1.8 add_convert_fusion.1
  844.4 28.3 %all-gather.21.cloned.1.call-done = bf16[1024,768]{1,0:T(8,128)(2,1)} async-done(((bf16[256,768]{1,0:T(8,128)(2,1)}), bf16[1024,768]{1,0:T(8,128)(2,1)}) %all-gather.21.cloned.1.call-update) | async-done | bytes 1572880 | tf_op jit(solution)/shard_map/all_gather | solution.py:286
  872.7 9.8 convolution_convert_fusion.2
  882.6 110.8 %reduce-scatter.21.cloned.1.call-done = bf16[256,3072]{1,0:T(8,128)(2,1)} async-done(((bf16[1024,3072]{1,0:T(8,128)(2,1)}), bf16[256,3072]{1,0:T(8,128)(2,1)}) %reduce-scatter.21.cloned.1.call-update) | async-done | bytes 1572880 | tf_op jit(solution)/shard_map/reduce_scatter | solution.py:290
  993.4 3.6 fusion.29
  997.3 115.8 %all-gather.23.cloned.1.call-done = bf16[1024,3072]{1,0:T(8,128)(2,1)} async-done(((bf16[256,3072]{1,0:T(8,128)(2,1)}), bf16[1024,3072]{1,0:T(8,128)(2,1)}) %all-gather.23.cloned.1.call-update) | async-done | bytes 6291472 | tf_op jit(solution)/shard_map/all_gather | solution.py:293
  1113.1 10.7 fusion.33
  1123.8 1.2 dynamic-slice_bitcast_fusion.3
  1125.9 3.0 collective-permute-start.14
  1130.0 4.8 collective-permute-done.12
  1134.8 6.2 collective-permute-done.13
  1141.1 2.0 collective-permute-start.15
  1143.2 3.4 collective-permute-start.16
  1147.5 4.3 collective-permute-done.15
  1151.7 5.8 collective-permute-done.16
  1158.0 1.4 broadcast_select_fusion
  1160.3 1.3 maximum_bitcast_fusion
  (192 shorter events, 25.5 us)
Async XLA Ops:
  7.2 53.2 %all-gather.9.cloned.1.call-start = ((), (), s32[]{:S(2)}) async-start(), calls=%async_computation.8 | async-start | bytes 1966080 | tf_op jit(solution)/shard_map/all_gather | solution.py:260
  8.0 5.7 copy-start.9
  8.0 19.5 %copy-start.20 = (s32[2,1024]{1,0:T(2,128)S(1)}, s32[2,1024]{1,0:T(2,128)}, u32[]{:S(2)}) copy-start(s32[2,1024]{1,0:T(2,128)} %param.12) | copy-start | bytes 24580
  13.2 14.4 %collective-permute-start = (f32[2,4,3,768]{3,0,2,1:T(2,128)S(1)}, f32[2,4,3,768]{3,0,2,1:T(2,128)S(1)}, u32[]{:S(2)}, u32[]{:S(2)}) collective-permute-start(f32[2,4,3,768]{3,0,2,1:T(2,128)S(1)} %bitcast.210), channel_id=1, source_target_pairs={{0,16},{16,0},{1,17},{17,1},{2,18},{18,2},{3,19},{19,3},{4,20},{20... | collective-permute-start | bytes 221192 | tf_op jit(solution)/shard_map/ppermute | solution.py:202
  13.7 46.7 %collective-permute-start.1 = (bf16[768,2304]{1,0:T(8,128)(2,1)}, bf16[768,2304]{1,0:T(8,128)(2,1)}, u32[]{:S(2)}, u32[]{:S(2)}) collective-permute-start(bf16[768,2304]{1,0:T(8,128)(2,1)} %bitcast.11), channel_id=1, source_target_pairs={{0,16},{16,0},{1,17},{17,1},{2,18},{18,2},{3,19},{19,3},{4,20},{20... | collective-permute-start | bytes 10616840 | tf_op jit(solution)/shard_map/ppermute | solution.py:202
  31.0 135.6 %reduce-scatter.25.cloned.1.call-start = ((), (), s32[]{:S(2)}) async-start(), calls=%async_computation.22 | async-start | bytes 5898240
  68.9 0.7 copy-start.22
  68.9 1.6 copy-start.12
  68.9 8.4 copy-start.21
  68.9 166.9 %all-gather.11.cloned.1.call-start = ((), (), s32[]{:S(2)}) async-start(), calls=%async_computation.9 | async-start | bytes 1966080 | tf_op jit(solution)/shard_map/all_gather | solution.py:280
  69.5 12.4 %collective-permute-start.2 = (f32[4,64]{1,0:T(4,128)S(1)}, f32[4,64]{1,0:T(4,128)S(1)}, u32[]{:S(2)}, u32[]{:S(2)}) collective-permute-start(f32[4,64]{1,0:T(4,128)S(1)} %bitcast.242), channel_id=1, source_target_pairs={{0,16},{16,0},{1,17},{17,1},{2,18},{18,2},{3,19},{19,3},{4,20},{20... | collective-permute-start | bytes 3080 | tf_op jit(solution)/shard_map/ppermute | solution.py:202
  70.5 9.7 copy-start.11
  71.4 108.7 %collective-permute-start.3 = (bf16[1,3,256,128]{3,2,0,1:T(8,128)(2,1)}, bf16[1,3,256,128]{3,2,0,1:T(8,128)(2,1)}, u32[]{:S(2)}, u32[]{:S(2)}) collective-permute-start(bf16[1,3,256,128]{3,2,0,1:T(8,128)(2,1)} %get-tuple-element.88), channel_id=1, source_target_pairs={{0,1},{1,2},{2,3},{3,0},{4,5},{5,6},{6,7},{7,4},{8,9},{9,10},{10,1... | collective-permute-start | bytes 589832 | tf_op jit(solution)/shard_map/ppermute | solution.py:167
  72.8 108.2 %collective-permute-start.4 = (bf16[1,3,256,128]{3,2,0,1:T(8,128)(2,1)S(1)}, bf16[1,3,256,128]{3,2,0,1:T(8,128)(2,1)}, u32[]{:S(2)}, u32[]{:S(2)}) collective-permute-start(bf16[1,3,256,128]{3,2,0,1:T(8,128)(2,1)S(1)} %get-tuple-element.87), channel_id=1, source_target_pairs={{0,2},{1,3},{2,0},{3,1},{4,6},{5,7},{6,4},{7,5},{8,10},{9,11},{10,... | collective-permute-start | bytes 589832 | tf_op jit(solution)/shard_map/ppermute | solution.py:167
  75.3 106.8 %collective-permute-start.5 = (bf16[1,3,256,128]{3,2,0,1:T(8,128)(2,1)S(1)}, bf16[1,3,256,128]{3,2,0,1:T(8,128)(2,1)}, u32[]{:S(2)}, u32[]{:S(2)}) collective-permute-start(bf16[1,3,256,128]{3,2,0,1:T(8,128)(2,1)S(1)} %get-tuple-element.86), channel_id=1, source_target_pairs={{0,3},{1,0},{2,1},{3,2},{4,7},{5,4},{6,5},{7,6},{8,11},{9,8},{10,9... | collective-permute-start | bytes 589832 | tf_op jit(solution)/shard_map/ppermute | solution.py:167
  80.5 98.4 %copy-start = (f32[1024,128]{1,0:T(8,128)}, f32[1024,128]{1,0:T(8,128)S(1)}, u32[]{:S(2)}) copy-start(f32[1024,128]{1,0:T(8,128)S(1)} %get-tuple-element.129.sin_ref) | copy-start | bytes 1572868
  176.9 0.9 copy-start.4
  177.7 6.1 copy-start.5
  177.7 5.3 collective-permute-start.6
  179.0 16.5 %copy-start.2 = (bf16[1024,128]{1,0:T(8,128)(2,1)}, bf16[1024,128]{1,0:T(8,128)(2,1)S(1)}, u32[]{:S(2)}) copy-start(bf16[1024,128]{1,0:T(8,128)(2,1)S(1)} %get-tuple-element.121.own_mask_ref) | copy-start | bytes 786436
  183.0 0.9 copy-start.8
  196.4 73.7 %reduce-scatter.13.cloned.1.call-start = ((), (), s32[]{:S(2)}) async-start(), calls=%async_computation.10 | async-start | bytes 1966080 | tf_op jit(solution)/shard_map/reduce_scatter | solution.py:282
  196.5 43.9 %copy-start.15 = (f32[1,4,3,768]{3,0,2,1:T(1,128)S(1)}, f32[1,4,3,768]{3,0,2,1:T(1,128)}, u32[]{:S(2)}) copy-start(f32[1,4,3,768]{3,0,2,1:T(1,128)} %get-tuple-element.127) | copy-start | bytes 110596
  196.5 73.7 %copy-start.10 = (bf16[2,256,768]{2,1,0:T(8,128)(2,1)S(1)}, bf16[2,256,768]{2,1,0:T(8,128)(2,1)}, u32[]{:S(2)}) copy-start(bf16[2,256,768]{2,1,0:T(8,128)(2,1)} %param.11) | copy-start | bytes 2359300
  196.5 73.7 %copy-start.16 = (f32[768]{0:T(1024)S(1)}, f32[768]{0:T(1024)}, u32[]{:S(2)}) copy-start(f32[768]{0:T(1024)} %get-tuple-element.52) | copy-start | bytes 9220
  196.5 73.7 %copy-start.17 = (f32[768]{0:T(1024)S(1)}, f32[768]{0:T(1024)}, u32[]{:S(2)}) copy-start(f32[768]{0:T(1024)} %get-tuple-element.61) | copy-start | bytes 9220
  196.5 73.7 %copy-start.18 = (f32[768]{0:T(1024)S(1)}, f32[768]{0:T(1024)}, u32[]{:S(2)}) copy-start(f32[768]{0:T(1024)} %get-tuple-element.62) | copy-start | bytes 9220
  196.5 73.6 %copy-start.19 = (f32[768]{0:T(1024)S(1)}, f32[768]{0:T(1024)}, u32[]{:S(2)}) copy-start(f32[768]{0:T(1024)} %get-tuple-element.63) | copy-start | bytes 9220
  196.5 3.9 collective-permute-start.7
  240.2 73.4 %all-gather.13.cloned.1.call-start = ((), (), s32[]{:S(2)}) async-start(), calls=%async_computation.11 | async-start | bytes 1966080 | tf_op jit(solution)/shard_map/all_gather | solution.py:286
  240.2 45.2 %collective-permute-start.8 = (bf16[768,3072]{1,0:T(8,128)(2,1)}, bf16[768,3072]{1,0:T(8,128)(2,1)}, u32[]{:S(2)}, u32[]{:S(2)}) collective-permute-start(bf16[768,3072]{1,0:T(8,128)(2,1)} %bitcast.243), channel_id=1, source_target_pairs={{0,16},{16,0},{1,17},{17,1},{2,18},{18,2},{3,19},{19,3},{4,20},{20... | collective-permute-start | bytes 14155784 | tf_op jit(solution)/shard_map/ppermute | solution.py:202
  285.2 148.6 %reduce-scatter.15.cloned.1.call-start = ((), (), s32[]{:S(2)}) async-start(), calls=%async_computation.12 | async-start | bytes 7864320 | tf_op jit(solution)/shard_map/reduce_scatter | solution.py:290
  322.6 230.8 %all-gather.15.cloned.1.call-start = ((), (), s32[]{:S(2)}) async-start(), calls=%async_computation.13 | async-start | bytes 7864320 | tf_op jit(solution)/shard_map/all_gather | solution.py:293
  437.4 155.7 %reduce-scatter.17.cloned.1.call-start = ((), (), s32[]{:S(2)}) async-start(), calls=%async_computation.14 | async-start | bytes 1966080 | tf_op jit(solution)/shard_map/reduce_scatter | solution.py:297
  437.4 125.4 %copy-start.14 = (f32[1,4,3,768]{3,0,2,1:T(1,128)S(1)}, f32[1,4,3,768]{3,0,2,1:T(1,128)}, u32[]{:S(2)}) copy-start(f32[1,4,3,768]{3,0,2,1:T(1,128)} %get-tuple-element.92) | copy-start | bytes 110596
  437.4 8.3 collective-permute-start.9
  562.8 73.7 %all-gather.17.cloned.1.call-start = ((), (), s32[]{:S(2)}) async-start(), calls=%async_computation.15 | async-start | bytes 1966080 | tf_op jit(solution)/shard_map/all_gather | solution.py:260
  594.5 51.6 %copy-start.6 = (bf16[256,768]{1,0:T(8,128)(2,1)}, bf16[256,768]{1,0:T(8,128)(2,1)S(1)}, u32[]{:S(2)}) copy-start(bf16[256,768]{1,0:T(8,128)(2,1)S(1)} %get-tuple-element.70) | copy-start | bytes 1179652
  608.2 123.4 %reduce-scatter.27.cloned.1.call-start = ((), (), s32[]{:S(2)}) async-start(), calls=%async_computation.23 | async-start | bytes 5898240
  646.1 0.6 copy-start.25
  646.1 0.7 copy-start.26
  646.1 0.8 copy-start.23
  646.1 0.8 copy-start.24
  646.1 148.9 %all-gather.19.cloned.1.call-start = ((), (), s32[]{:S(2)}) async-start(), calls=%async_computation.16 | async-start | bytes 1966080 | tf_op jit(solution)/shard_map/all_gather | solution.py:280
  733.3 1.0 copy-start.1
  734.3 11.6 copy-start.3
  742.2 52.8 %copy-start.27 = (bf16[1,768,768]{2,1,0:T(8,128)(2,1)S(1)}, bf16[1,768,768]{2,1,0:T(8,128)(2,1)}, u32[]{:S(2)}) copy-start(bf16[1,768,768]{2,1,0:T(8,128)(2,1)} %param.18) | copy-start | bytes 3538948
  743.5 2.4 collective-permute-start.10
  757.3 42.2 %copy-start.13 = (f32[1,4,3,768]{3,0,2,1:T(1,128)S(1)}, f32[1,4,3,768]{3,0,2,1:T(1,128)}, u32[]{:S(2)}) copy-start(f32[1,4,3,768]{3,0,2,1:T(1,128)} %get-tuple-element.91) | copy-start | bytes 110596
  757.3 72.0 %copy-start.7 = (bf16[256,768]{1,0:T(8,128)(2,1)S(1)}, bf16[256,768]{1,0:T(8,128)(2,1)}, u32[]{:S(2)}) copy-start(bf16[256,768]{1,0:T(8,128)(2,1)} %copy-done.6) | copy-start | bytes 1179652
  757.3 72.0 %reduce-scatter.19.cloned.1.call-start = ((), (), s32[]{:S(2)}) async-start(), calls=%async_computation.17 | async-start | bytes 1966080 | tf_op jit(solution)/shard_map/reduce_scatter | solution.py:282
  799.4 73.3 %all-gather.21.cloned.1.call-start = ((), (), s32[]{:S(2)}) async-start(), calls=%async_computation.18 | async-start | bytes 1966080 | tf_op jit(solution)/shard_map/all_gather | solution.py:286
  844.3 149.1 %reduce-scatter.21.cloned.1.call-start = ((), (), s32[]{:S(2)}) async-start(), calls=%async_computation.19 | async-start | bytes 7864320 | tf_op jit(solution)/shard_map/reduce_scatter | solution.py:290
  882.5 230.6 %all-gather.23.cloned.1.call-start = ((), (), s32[]{:S(2)}) async-start(), calls=%async_computation.20 | async-start | bytes 7864320 | tf_op jit(solution)/shard_map/all_gather | solution.py:293
  997.1 160.9 %reduce-scatter.23.cloned.1.call-start = ((), (), s32[]{:S(2)}) async-start(), calls=%async_computation.21 | async-start | bytes 1966080 | tf_op jit(solution)/shard_map/reduce_scatter | solution.py:297
  1125.0 9.8 collective-permute-start.12
  1125.1 15.9 %collective-permute-start.13 = (bf16[1,3,256,128]{3,2,0,1:T(8,128)(2,1)S(1)}, bf16[1,3,256,128]{3,2,0,1:T(8,128)(2,1)S(1)}, u32[]{:S(2)}, u32[]{:S(2)}) collective-permute-start(bf16[1,3,256,128]{3,2,0,1:T(8,128)(2,1)S(1)} %get-tuple-element.81), channel_id=1, source_target_pairs={{0,2},{1,3},{2,0},{3,1},{4,6},{5,7},{6,4},{7,5},{8,10},{9,11},{10,... | collective-permute-start | bytes 589832 | tf_op jit(solution)/shard_map/ppermute | solution.py:167
  1125.9 17.2 %collective-permute-start.14 = (bf16[1,3,256,128]{3,2,0,1:T(8,128)(2,1)S(1)}, bf16[1,3,256,128]{3,2,0,1:T(8,128)(2,1)S(1)}, u32[]{:S(2)}, u32[]{:S(2)}) collective-permute-start(bf16[1,3,256,128]{3,2,0,1:T(8,128)(2,1)S(1)} %get-tuple-element.80), channel_id=1, source_target_pairs={{0,3},{1,0},{2,1},{3,2},{4,7},{5,4},{6,5},{7,6},{8,11},{9,8},{10,9... | collective-permute-start | bytes 589832 | tf_op jit(solution)/shard_map/ppermute | solution.py:167
  1141.1 10.6 collective-permute-start.15
  1143.2 14.4 %collective-permute-start.16 = (bf16[1,3,256,128]{3,2,0,1:T(8,128)(2,1)S(1)}, bf16[1,3,256,128]{3,2,0,1:T(8,128)(2,1)S(1)}, u32[]{:S(2)}, u32[]{:S(2)}) collective-permute-start(bf16[1,3,256,128]{3,2,0,1:T(8,128)(2,1)S(1)} %get-tuple-element.84), channel_id=1, source_target_pairs={{0,2},{1,3},{2,0},{3,1},{4,6},{5,7},{6,4},{7,5},{8,10},{9,11},{10,... | collective-permute-start | bytes 589832 | tf_op jit(solution)/shard_map/ppermute | solution.py:167
  1146.6 11.0 collective-permute-start.17
  1157.8 2.4 collective-permute-start.18
  1159.4 2.2 collective-permute-start.11
Sparse Core Ops, SparseCore 0:
  31.2 29.1 all-gather.8
  69.0 97.5 reduce-scatter.24
  196.5 39.2 all-gather.10
  240.3 29.8 reduce-scatter.12
  285.3 28.2 all-gather.12
  322.8 110.9 reduce-scatter.14
  437.5 115.8 all-gather.14
  562.9 30.0 reduce-scatter.16
  608.3 28.1 all-gather.16
  646.3 85.2 reduce-scatter.26
  757.4 37.5 all-gather.18
  799.5 29.7 reduce-scatter.18
  844.5 28.2 all-gather.20
  882.6 110.7 reduce-scatter.20
  997.2 115.8 all-gather.22
  1124.0 29.1 reduce-scatter.22

commit v2 on v1

--- a/solution.py
+++ b/solution.py
@@ -182,6 +182,165 @@
     w_up,
     w_down,
 ):
+    operands = (
+        hidden_in,
+        row_kind,
+        positions,
+        timesteps,
+        stale_cache,
+        w_qkv[0],
+        qk_norm[0],
+        w_out[0],
+        ada_weight[0],
+        w_up[0],
+        w_down[0],
+    )
+    if stale_cache.shape[3] % lax.axis_size("narrow") == 0:
+        return features_whole(*operands)
+    return features_split(*operands)
+
+
+def swap(value):
+    return lax.ppermute(value, "section", [(0, 1), (1, 0)])
+
+
+def by_layer(parts, lead):
+    got = swap(jnp.where(lead, parts[1], parts[0]))
+    kept = jnp.where(lead, parts[0], parts[1])
+    return jnp.stack([jnp.where(lead, kept, got), jnp.where(lead, got, kept)])[None]
+
+
+def norm_pairs(norms):
+    return jnp.stack([jnp.concatenate([norms[0], norms[2]]), jnp.concatenate([norms[1], norms[3]])])
+
+
+def modulate(values, table, kinds):
+    return (values * (1.0 + pick(table, kinds, 1)) + pick(table, kinds, 0)).astype(BF)
+
+
+def row_norm(values):
+    center = values - jnp.mean(values, axis=1, keepdims=True)
+    variance = jnp.mean(center * center, axis=1, keepdims=True)
+    return center * lax.rsqrt(variance + EPS_ROW)
+
+
+def features_whole(
+    hidden_in,
+    row_kind,
+    positions,
+    timesteps,
+    stale_cache,
+    w_qkv,
+    qk_norm,
+    w_out,
+    ada_weight,
+    w_up,
+    w_down,
+):
+    n_wide = lax.axis_size("wide")
+    n_narrow = lax.axis_size("narrow")
+    wide_idx = lax.axis_index("wide")
+    narrow_idx = lax.axis_index("narrow")
+    section = lax.axis_index("section")
+    lead = section == 0
+    _, rows_a, feat_a = hidden_in.shape
+    total_rows = rows_a * n_wide
+    rows_b = total_rows // n_narrow
+    rows_c = rows_a // n_narrow
+    heads_local = stale_cache.shape[3]
+    heads = heads_local // n_narrow
+    pair = stale_cache.shape[4]
+    head_dim = pair // 2
+    model_width = feat_a * n_narrow
+    both = ("wide", "narrow")
+
+    def weights_for(own, axis):
+        parts = jnp.stack(jnp.split(own, n_narrow, axis))
+        got = exchange(parts, "narrow")
+        joined = jnp.concatenate([got[i] for i in range(n_narrow)], axis=1 - axis)
+        other = swap(joined)
+        return (jnp.where(lead, joined, other), jnp.where(lead, other, joined))
+
+    def to_rows_c(block):
+        got = exchange(block.reshape(n_narrow, rows_c, feat_a), "narrow")
+        return got.transpose(1, 0, 2).reshape(rows_c, model_width)
+
+    def from_rows_c(block):
+        got = exchange(block.reshape(rows_c, n_narrow, feat_a).transpose(1, 0, 2), "narrow")
+        return got.reshape(rows_a, feat_a)
+
+    activated = jax.nn.silu(time_features(timesteps, ada_weight.shape[1])).astype(BF)
+    modulation = jnp.einsum("re,kesd->krsd", activated, ada_weight, preferred_element_type=F32)
+    modulation = lax.all_gather(modulation.reshape(2, 4, 3, feat_a), ("section", "narrow"), axis=0)
+    tables = modulation.reshape(2, n_narrow, 2, 4, 3, feat_a).transpose(0, 2, 3, 4, 1, 5)
+    tables = tables.reshape(2, 2, 4, 3, model_width)
+
+    qkv_weights = weights_for(w_qkv, 1)
+    out_weights = weights_for(w_out, 0)
+    up_weights = weights_for(w_up, 1)
+    down_weights = weights_for(w_down, 0)
+    own_norms = qk_norm
+    other_norms = swap(qk_norm)
+    norm_rows = (jnp.where(lead, own_norms, other_norms), jnp.where(lead, other_norms, own_norms))
+
+    kinds = lax.dynamic_slice_in_dim(row_kind, section, 1, 0)[0]
+    kinds_other = lax.dynamic_slice_in_dim(row_kind, 1 - section, 1, 0)[0]
+    own_mask = key_mask(kinds, head_dim)
+    other_mask = key_mask(kinds_other, head_dim)
+    kinds_c = lax.dynamic_slice_in_dim(kinds, wide_idx * rows_a + narrow_idx * rows_c, rows_c)
+    places = lax.dynamic_slice_in_dim(positions, section, 1, 1)[:, 0]
+    cosine, sine = rotary_tables(places, head_dim)
+
+    blocks = stale_cache[0, 1].reshape(rows_b, n_narrow, heads, pair).transpose(1, 2, 0, 3)
+    stale = exchange(blocks, "narrow").transpose(1, 0, 2, 3).reshape(heads, total_rows, pair)
+
+    layer_in = to_rows_c(lax.dynamic_slice_in_dim(hidden_in, section, 1, 0)[0])
+    results = []
+    caches = []
+    for layer in range(2):
+        table = tables[layer]
+        x_in = layer_in.astype(F32)
+        entry = modulate(row_norm(x_in), table[0], kinds_c)
+        entry = lax.all_gather(entry, both, axis=0, tiled=True)
+        qkv = jnp.dot(entry, qkv_weights[layer], preferred_element_type=F32).astype(BF)
+        queries, fresh = prepare(
+            qkv, cosine, sine, kinds, norm_pairs(norm_rows[layer]), heads, head_dim
+        )
+        blocks = fresh.reshape(heads, n_narrow, rows_b, pair).transpose(1, 0, 2, 3)
+        blocks = exchange(blocks, "narrow").transpose(2, 0, 1, 3)
+        caches.append(blocks.reshape(rows_b, heads_local, pair))
+        if layer == 0:
+            other = jnp.where(lead, stale, swap(fresh))
+        else:
+            other = swap(jnp.where(lead, fresh, stale))
+        attended = attend(queries, fresh, other, own_mask, other_mask, head_dim)
+        terms = jnp.dot(attended, out_weights[layer], preferred_element_type=F32).astype(BF)
+        projected = lax.psum_scatter(terms, both, scatter_dimension=0, tiled=True)
+        after = x_in + pick(table[0], kinds_c, 2) * projected.astype(F32)
+        entry = modulate(row_norm(after), table[1], kinds_c)
+        entry = lax.all_gather(entry, both, axis=0, tiled=True)
+        up = jnp.dot(entry, up_weights[layer], preferred_element_type=F32)
+        inner = jax.nn.gelu(up, approximate=True).astype(BF)
+        terms = jnp.dot(inner, down_weights[layer], preferred_element_type=F32).astype(BF)
+        down = lax.psum_scatter(terms, both, scatter_dimension=0, tiled=True)
+        layer_in = (after + pick(table[1], kinds_c, 2) * down.astype(F32)).astype(BF)
+        results.append(from_rows_c(layer_in))
+    return (by_layer(results, lead), by_layer(caches, lead))
+
+
+def features_split(
+    hidden_in,
+    row_kind,
+    positions,
+    timesteps,
+    stale_cache,
+    w_qkv,
+    qk_norm,
+    w_out,
+    ada_weight,
+    w_up,
+    w_down,
+):
     n_wide = lax.axis_size("wide")
     n_narrow = lax.axis_size("narrow")
     wide_idx = lax.axis_index("wide")
@@ -194,25 +353,21 @@
     pair = stale_cache.shape[4]
     head_dim = pair // 2
     model_width = feat_a * n_narrow
-    by_heads = heads_local % n_narrow == 0
-    heads = heads_local // n_narrow if by_heads else heads_local
+    heads = heads_local
     lead = section == 0
-
-    def swap(value):
-        return lax.ppermute(value, "section", [(0, 1), (1, 0)])
 
     def both_layers(own):
         other = swap(own)
         return (jnp.where(lead, own, other), jnp.where(lead, other, own))
 
-    qkv_weights = both_layers(w_qkv[0])
-    out_weights = both_layers(w_out[0])
-    up_weights = both_layers(w_up[0])
-    down_weights = both_layers(w_down[0])
-    norm_rows = both_layers(qk_norm[0])
-
-    activated = jax.nn.silu(time_features(timesteps, ada_weight.shape[2])).astype(BF)
-    modulation = jnp.einsum("re,kesd->krsd", activated, ada_weight[0], preferred_element_type=F32)
+    qkv_weights = both_layers(w_qkv)
+    out_weights = both_layers(w_out)
+    up_weights = both_layers(w_up)
+    down_weights = both_layers(w_down)
+    norm_rows = both_layers(qk_norm)
+
+    activated = jax.nn.silu(time_features(timesteps, ada_weight.shape[1])).astype(BF)
+    modulation = jnp.einsum("re,kesd->krsd", activated, ada_weight, preferred_element_type=F32)
     tables = both_layers(modulation.reshape(2, 4, 3, feat_a))
 
     kinds = lax.dynamic_slice_in_dim(row_kind, section, 1, 0)[0]
@@ -221,25 +376,11 @@
     other_mask = key_mask(kinds_other, head_dim)
     kinds_a = lax.dynamic_slice_in_dim(kinds, wide_idx * rows_a, rows_a)
     places = lax.dynamic_slice_in_dim(positions, section, 1, 1)[:, 0]
-    kinds_q = kinds
-    if not by_heads:
-        places = lax.dynamic_slice_in_dim(places, narrow_idx * rows_b, rows_b, 1)
-        kinds_q = lax.dynamic_slice_in_dim(kinds, narrow_idx * rows_b, rows_b)
+    places = lax.dynamic_slice_in_dim(places, narrow_idx * rows_b, rows_b, 1)
+    kinds_q = lax.dynamic_slice_in_dim(kinds, narrow_idx * rows_b, rows_b)
     cosine, sine = rotary_tables(places, head_dim)
 
-    def to_heads(rows_part):
-        if by_heads:
-            blocks = rows_part.reshape(rows_b, n_narrow, heads, pair).transpose(1, 2, 0, 3)
-            return exchange(blocks, "narrow").transpose(1, 0, 2, 3).reshape(heads, total_rows, pair)
-        return lax.all_gather(rows_part.transpose(1, 0, 2), "narrow", axis=1, tiled=True)
-
-    def to_rows(pairs):
-        if by_heads:
-            blocks = pairs.reshape(heads, n_narrow, rows_b, pair).transpose(1, 0, 2, 3)
-            return exchange(blocks, "narrow").transpose(2, 0, 1, 3).reshape(rows_b, heads_local, pair)
-        return pairs.transpose(1, 0, 2)
-
-    stale = to_heads(stale_cache[0, 1])
+    stale = lax.all_gather(stale_cache[0, 1].transpose(1, 0, 2), "narrow", axis=1, tiled=True)
 
     def normalize(values):
         moments = lax.psum(
@@ -255,35 +396,30 @@
     for layer in range(2):
         table = tables[layer]
         x_in = layer_in.astype(F32)
-        entry = normalize(x_in) * (1.0 + pick(table[0], kinds_a, 1)) + pick(table[0], kinds_a, 0)
+        entry = modulate(normalize(x_in), table[0], kinds_a)
         qkv_terms = jnp.dot(
-            lax.all_gather(entry.astype(BF), "wide", axis=0, tiled=True),
+            lax.all_gather(entry, "wide", axis=0, tiled=True),
             qkv_weights[layer],
             preferred_element_type=F32,
         ).astype(BF)
-        qkv = lax.psum_scatter(
-            qkv_terms, "narrow", scatter_dimension=1 if by_heads else 0, tiled=True
-        )
-        norms = norm_rows[layer]
-        norm_pair = jnp.stack(
-            [jnp.concatenate([norms[0], norms[2]]), jnp.concatenate([norms[1], norms[3]])]
-        )
-        queries, fresh = prepare(qkv, cosine, sine, kinds_q, norm_pair, heads, head_dim)
-        caches.append(to_rows(fresh))
-        if not by_heads:
-            fresh = lax.all_gather(fresh, "narrow", axis=1, tiled=True)
+        qkv = lax.psum_scatter(qkv_terms, "narrow", scatter_dimension=0, tiled=True)
+        queries, fresh = prepare(
+            qkv, cosine, sine, kinds_q, norm_pairs(norm_rows[layer]), heads, head_dim
+        )
+        caches.append(fresh.transpose(1, 0, 2))
+        fresh = lax.all_gather(fresh, "narrow", axis=1, tiled=True)
         if layer == 0:
             other = jnp.where(lead, stale, swap(fresh))
         else:
             other = swap(jnp.where(lead, fresh, stale))
         attended = attend(queries, fresh, other, own_mask, other_mask, head_dim)
-        attended = lax.all_gather(attended, "narrow", axis=1 if by_heads else 0, tiled=True)
+        attended = lax.all_gather(attended, "narrow", axis=0, tiled=True)
         proj_terms = jnp.dot(attended, out_weights[layer], preferred_element_type=F32).astype(BF)
         projected = lax.psum_scatter(proj_terms, "wide", scatter_dimension=0, tiled=True)
         after = x_in + pick(table[0], kinds_a, 2) * projected.astype(F32)
-        entry = normalize(after) * (1.0 + pick(table[1], kinds_a, 1)) + pick(table[1], kinds_a, 0)
+        entry = modulate(normalize(after), table[1], kinds_a)
         up_terms = jnp.dot(
-            lax.all_gather(entry.astype(BF), "wide", axis=0, tiled=True),
+            lax.all_gather(entry, "wide", axis=0, tiled=True),
             up_weights[layer],
             preferred_element_type=F32,
         ).astype(BF)
@@ -298,12 +434,7 @@
         layer_in = (after + pick(table[1], kinds_a, 2) * down_sum.astype(F32)).astype(BF)
         results.append(layer_in)
 
-    def by_layer(parts):
-        got = swap(jnp.where(lead, parts[1], parts[0]))
-        kept = jnp.where(lead, parts[0], parts[1])
-        return jnp.stack([jnp.where(lead, kept, got), jnp.where(lead, got, kept)])[None]
-
-    return (by_layer(results), by_layer(caches))
+    return (by_layer(results, lead), by_layer(caches, lead))
 
 
 def solution(mesh):

time: 1180 us -> 1510 us (1.28)
  waiting for transfers between devices: 925 us -> 1120 us
  starting transfers between devices: 20.5 us -> 104 us
  local copies, waits for them, and re-layouts: 19.9 us -> 95.5 us
  blocking collectives: 48.5 us -> 25.5 us
    ppermute x9 -> x30, waiting for transfers between devices: 21.1 us -> 367 us  [exchange(): block = lax.ppermute(block, axis, [(i, (i + step) % n) for i in range(n)])]
    reduce_scatter x6 -> x4, waiting for transfers between devices: 311 us -> 559 us  [the longest x2 290 us: features_whole(): projected = lax.psum_scatter(terms, both, scatter_dimension=0, tiled=True)]
    all_gather x8 -> x4, waiting for transfers between devices: 411 us -> 187 us  [features_whole(): entry = lax.all_gather(entry, both, axis=0, tiled=True)]
    unnamed x18 -> x8, waiting for transfers between devices: 169 us -> 0.13 us
    ppermute x9 -> x30, starting transfers between devices: 15.5 us -> 101 us  [exchange(): block = lax.ppermute(block, axis, [(i, (i + step) % n) for i in range(n)])]
    psum x4 -> x0, blocking collectives: 48.5 us -> none  [normalize(): lax.psum(jnp.stack([jnp.sum(values, axis=1), jnp.sum(values * values, axi...]
    dynamic_update_slice x9 -> x30, local copies, waits for them, and re-layouts: 3.04 us -> 44 us  [exchange(): got = lax.dynamic_update_slice_in_dim(got, block, back, 0)]
    all_gather x0 -> x1, blocking collectives: none -> 25.5 us  [features_whole(): lax.all_gather(modulation.reshape(2, 4, 3, feat_a), ('section', 'narrow')...]
  transfers between devices with their start and end apart: 35 -> 47, of which waited for: 23 -> 19; matrix products, arithmetic and copies ran while one was open for 2% -> 8% of each run, Pallas kernels for 1% -> 1%
where the time goes in v2:
time: 1510 us; the launch traced here: 1500 us
  waiting for transfers between devices  1120 us (74%)
  starting transfers between devices  104 us (7%)
  local copies, waits for them, and re-layouts  95.5 us (6%)
  matrix products  74.5 us (5%)
  Pallas kernels  36.8 us (2%)
  other arithmetic  34.5 us (2%)
  blocking collectives  25.5 us (2%)
  between operations  16.3 us (1%)
    ppermute x30, waiting for transfers between devices, exchange(): block = lax.ppermute(block, axis, [(i, (i + step) % n) for i in range(n)])  367 us
    reduce_scatter x2, waiting for transfers between devices, features_whole(): projected = lax.psum_scatter(terms, both, scatter_dimension=0, tiled=True)  290 us
    reduce_scatter x2, waiting for transfers between devices, features_whole(): down = lax.psum_scatter(terms, both, scatter_dimension=0, tiled=True)  269 us
    all_gather x4, waiting for transfers between devices, features_whole(): entry = lax.all_gather(entry, both, axis=0, tiled=True)  187 us
    ppermute x30, starting transfers between devices, exchange(): block = lax.ppermute(block, axis, [(i, (i + step) % n) for i in range(n)])  101 us
    dynamic_update_slice x30, local copies, waits for them, and re-layouts, exchange(): got = lax.dynamic_update_slice_in_dim(got, block, back, 0)  44 us
  transfers between devices with their start and end apart: 47, of which 19 were waited for; matrix products, arithmetic and copies ran while one was open for 8% of the time, Pallas kernels for 1%

profile of v2, /device:TPU:0, one launch (start us, length us, event | category | flops | bytes accessed | tf_op | source)
XLA Modules:
  0.0 1503.3 jit_solution(515054885461481509)
XLA Ops:
  8.4 3.1 collective-permute-start
  11.5 2.6 collective-permute-start.1
  16.2 5.0 fusion.48
  21.3 25.5 %all_gather.15 = f32[8,2,4,3,768]{4,2,3,1,0:T(4,128)S(1)} all-gather(f32[1,2,4,3,768]{4,2,3,1,0:T(4,128)S(1)} %copy.66), channel_id=1, replica_groups=mesh['section'=2,'wide'=4,'narrow'=4] {'section','narrow'}, dimensions={0}, use_global_device_ids=true | all-gather | bytes 663552 | tf_op jit(solution)/shard_map/all_gather | solution.py:274
  49.7 2.8 dynamic_update_slice.120
  52.7 2.8 dynamic_update_slice.121
  55.6 2.8 dynamic_update_slice.122
  58.6 2.8 dynamic_update_slice.123
  65.3 4.5 copy.68
  72.9 2.3 collective-permute-start.4
  82.6 22.9 %collective-permute-done.3 = bf16[1,768,576]{1,2,0:T(8,128)(2,1)} collective-permute-done((bf16[1,768,576]{1,2,0:T(8,128)(2,1)}, bf16[1,768,576]{1,2,0:T(8,128)(2,1)}, u32[]{:S(2)}, u32[]{:S(2)}) %collective-permute-start.3) | collective-permute-done | bytes 884768 | tf_op jit(solution)/shard_map/ppermute | solution.py:167
  107.4 54.8 %collective-permute-done.4 = bf16[1,768,576]{1,2,0:T(8,128)(2,1)} collective-permute-done((bf16[1,768,576]{1,2,0:T(8,128)(2,1)}, bf16[1,768,576]{1,2,0:T(8,128)(2,1)}, u32[]{:S(2)}, u32[]{:S(2)}) %collective-permute-start.4) | collective-permute-done | bytes 884768 | tf_op jit(solution)/shard_map/ppermute | solution.py:167
  165.0 2.0 pad_maximum_fusion.5
  170.2 2.4 sine_multiply_fusion
  173.2 36.4 %collective-permute-start.8 = (bf16[1,3,256,128]{3,2,0,1:T(8,128)(2,1)}, bf16[1,3,256,128]{3,2,0,1:T(8,128)(2,1)S(1)}, u32[]{:S(2)}, u32[]{:S(2)}) collective-permute-start(bf16[1,3,256,128]{3,2,0,1:T(8,128)(2,1)} %get-tuple-element.84), channel_id=1, source_target_pairs={{0,1},{1,2},{2,3},{3,0},{4,5},{5,6},{6,7},{7,4},{8,9},{9,10},{10,1... | collective-permute-start | bytes 589832 | tf_op jit(solution)/shard_map/ppermute | solution.py:167
  211.0 7.0 collective-permute-start.9
  218.1 1.7 constant_dynamic-update-slice_fusion.13
  219.8 12.2 collective-permute-done.13
  231.9 7.4 collective-permute-start.10
  239.3 1.7 constant_dynamic-update-slice_fusion.12
  241.0 1.7 constant_dynamic-update-slice_fusion.11
  247.1 8.4 fusion.38
  257.1 7.9 prepare.2
  270.8 10.6 attend.2
  281.5 4.4 convolution_convert_fusion.3
  287.1 147.4 %reduce-scatter.5.cloned.1.call-done = bf16[64,3072]{1,0:T(8,128)(2,1)} async-done(((bf16[1024,3072]{1,0:T(8,128)(2,1)}), bf16[64,3072]{1,0:T(8,128)(2,1)}) %reduce-scatter.5.cloned.1.call-update) | async-done | bytes 393232 | tf_op jit(solution)/shard_map/reduce_scatter | solution.py:318
  437.8 2.7 slice_bitcast_fusion.11
  443.0 1.8 collective-permute-start.17
  449.7 31.4 %collective-permute-done.16 = bf16[1,768,768]{2,1,0:T(8,128)(2,1)S(1)} collective-permute-done((bf16[1,768,768]{2,1,0:T(8,128)(2,1)S(1)}, bf16[1,768,768]{2,1,0:T(8,128)(2,1)S(1)}, u32[]{:S(2)}, u32[]{:S(2)}) %collective-permute-start.16) | collective-permute-done | bytes 1179680 | tf_op jit(solution)/shard_map/ppermute | solution.py:167
  482.9 106.0 %collective-permute-done.17 = bf16[1,768,768]{2,1,0:T(8,128)(2,1)S(1)} collective-permute-done((bf16[1,768,768]{2,1,0:T(8,128)(2,1)S(1)}, bf16[1,768,768]{2,1,0:T(8,128)(2,1)S(1)}, u32[]{:S(2)}, u32[]{:S(2)}) %collective-permute-start.17) | collective-permute-done | bytes 1179680 | tf_op jit(solution)/shard_map/ppermute | solution.py:167
  590.9 90.2 %collective-permute-done.21 = bf16[1,768,768]{2,1,0:T(8,128)(2,1)S(1)} collective-permute-done((bf16[1,768,768]{2,1,0:T(8,128)(2,1)S(1)}, bf16[1,768,768]{2,1,0:T(8,128)(2,1)S(1)}, u32[]{:S(2)}, u32[]{:S(2)}) %collective-permute-start.21) | collective-permute-done | bytes 1179680 | tf_op jit(solution)/shard_map/ppermute | solution.py:167
  681.7 2.7 pad_maximum_fusion.3
  685.4 10.9 fusion.25
  696.3 7.5 convolution_convert_fusion.2
  705.6 169.3 %reduce-scatter.7.cloned.1.call-done = bf16[64,3072]{1,0:T(8,128)(2,1)} async-done(((bf16[1024,3072]{1,0:T(8,128)(2,1)}), bf16[64,3072]{1,0:T(8,128)(2,1)}) %reduce-scatter.7.cloned.1.call-update) | async-done | bytes 393232 | tf_op jit(solution)/shard_map/reduce_scatter | solution.py:325
  876.6 2.0 fusion.56
  880.2 92.0 %all-gather.9.cloned.1.call-done = bf16[1024,3072]{1,0:T(8,128)(2,1)} async-done(((bf16[64,3072]{1,0:T(8,128)(2,1)}), bf16[1024,3072]{1,0:T(8,128)(2,1)}) %all-gather.9.cloned.1.call-update) | async-done | bytes 6291472 | tf_op jit(solution)/shard_map/all_gather | solution.py:304
  972.2 9.5 fusion.41
  984.4 7.9 prepare.3
  993.7 2.3 collective-permute-done.27.other_ref
  996.0 10.4 attend.3
  1006.4 5.7 convolution_convert_fusion.1
  1013.9 142.3 %reduce-scatter.9.cloned.1.call-done = bf16[64,3072]{1,0:T(8,128)(2,1)} async-done(((bf16[1024,3072]{1,0:T(8,128)(2,1)}), bf16[64,3072]{1,0:T(8,128)(2,1)}) %reduce-scatter.9.cloned.1.call-update) | async-done | bytes 393232 | tf_op jit(solution)/shard_map/reduce_scatter | solution.py:318
  1159.2 93.9 %all-gather.11.cloned.1.call-done = bf16[1024,3072]{1,0:T(8,128)(2,1)} async-done(((bf16[64,3072]{1,0:T(8,128)(2,1)}), bf16[1024,3072]{1,0:T(8,128)(2,1)}) %all-gather.11.cloned.1.call-update) | async-done | bytes 6291472 | tf_op jit(solution)/shard_map/all_gather | solution.py:321
  1253.1 11.6 fusion.33
  1264.7 11.4 convolution_convert_fusion
  1279.5 2.4 collective-permute-start.34
  1282.0 5.4 collective-permute-done.32
  1287.5 8.6 collective-permute-done.33
  1297.2 11.9 collective-permute-start.35
  1310.7 3.8 collective-permute-start.26
  1314.5 2.0 collective-permute-start.36
  1318.2 2.3 collective-permute-start.37
  1320.5 33.6 %collective-permute-done.36 = bf16[1,3,256,128]{3,2,0,1:T(8,128)(2,1)S(1)} collective-permute-done((bf16[1,3,256,128]{3,2,0,1:T(8,128)(2,1)S(1)}, bf16[1,3,256,128]{3,2,0,1:T(8,128)(2,1)S(1)}, u32[]{:S(2)}, u32[]{:S(2)}) %collective-permute-start.36) | collective-permute-done | bytes 196640 | tf_op jit(solution)/shard_map/ppermute | solution.py:167
  1354.5 100.2 %reduce-scatter.11.cloned.1.call-done = bf16[64,3072]{1,0:T(8,128)(2,1)} async-done(((bf16[1024,3072]{1,0:T(8,128)(2,1)}), bf16[64,3072]{1,0:T(8,128)(2,1)}) %reduce-scatter.11.cloned.1.call-update) | async-done | bytes 393232 | tf_op jit(solution)/shard_map/reduce_scatter | solution.py:325
  1458.8 1.8 collective-permute-start.29
  1462.4 2.8 dynamic_update_slice.144
  1465.2 4.0 dynamic_update_slice.145
  1469.2 4.0 dynamic_update_slice.146
  1473.2 4.0 dynamic_update_slice.147
  1477.4 2.8 dynamic_update_slice.148
  1480.2 4.0 dynamic_update_slice.149
  1484.2 4.0 dynamic_update_slice.150
  1488.2 4.0 dynamic_update_slice.151
  (350 shorter events, 90.9 us)
Async XLA Ops:
  7.2 239.9 %all-gather.5.cloned.1.call-start = ((), (), s32[]{:S(2)}) async-start(), calls=%async_computation.4 | async-start | bytes 6684672 | tf_op jit(solution)/shard_map/all_gather | solution.py:304
  8.4 44.1 %collective-permute-start = (bf16[1,64,768]{2,1,0:T(8,128)(2,1)S(1)}, bf16[1,64,768]{2,1,0:T(8,128)(2,1)S(1)}, u32[]{:S(2)}, u32[]{:S(2)}) collective-permute-start(bf16[1,64,768]{2,1,0:T(8,128)(2,1)S(1)} %get-tuple-element.99), channel_id=1, source_target_pairs={{0,1},{1,2},{2,3},{3,0},{4,5},{5,6},{6,7},{7,4},{8,9},{9,10},{10,1... | collective-permute-start | bytes 294920 | tf_op jit(solution)/shard_map/ppermute | solution.py:167
  11.5 44.0 %collective-permute-start.1 = (bf16[1,64,768]{2,1,0:T(8,128)(2,1)S(1)}, bf16[1,64,768]{2,1,0:T(8,128)(2,1)S(1)}, u32[]{:S(2)}, u32[]{:S(2)}) collective-permute-start(bf16[1,64,768]{2,1,0:T(8,128)(2,1)S(1)} %get-tuple-element.98), channel_id=1, source_target_pairs={{0,2},{1,3},{2,0},{3,1},{4,6},{5,7},{6,4},{7,5},{8,10},{9,11},{10,... | collective-permute-start | bytes 294920 | tf_op jit(solution)/shard_map/ppermute | solution.py:167
  14.0 44.4 %collective-permute-start.2 = (bf16[1,64,768]{2,1,0:T(8,128)(2,1)S(1)}, bf16[1,64,768]{2,1,0:T(8,128)(2,1)S(1)}, u32[]{:S(2)}, u32[]{:S(2)}) collective-permute-start(bf16[1,64,768]{2,1,0:T(8,128)(2,1)S(1)} %get-tuple-element.97), channel_id=1, source_target_pairs={{0,3},{1,0},{2,1},{3,2},{4,7},{5,4},{6,5},{7,6},{8,11},{9,8},{10,9... | collective-permute-start | bytes 294920 | tf_op jit(solution)/shard_map/ppermute | solution.py:167
  49.4 386.7 %copy-start.52 = (pred[64]{0:T(512)(128)(4,1)}, pred[64]{0:T(512)(128)(4,1)S(1)}, u32[]{:S(2)}) copy-start(pred[64]{0:T(512)(128)(4,1)S(1)} %get-tuple-element.16) | copy-start | bytes 196
  65.3 369.2 %reduce-scatter.5.cloned.1.call-start = ((), (), s32[]{:S(2)}) async-start(), calls=%async_computation.5 | async-start | bytes 6684672 | tf_op jit(solution)/shard_map/reduce_scatter | solution.py:318
  72.4 33.1 %collective-permute-start.3 = (bf16[1,768,576]{1,2,0:T(8,128)(2,1)}, bf16[1,768,576]{1,2,0:T(8,128)(2,1)}, u32[]{:S(2)}, u32[]{:S(2)}) collective-permute-start(bf16[1,768,576]{1,2,0:T(8,128)(2,1)} %get-tuple-element.48), channel_id=1, source_target_pairs={{0,1},{1,2},{2,3},{3,0},{4,5},{5,6},{6,7},{7,4},{8,9},{9,10},{10,1... | collective-permute-start | bytes 2654216 | tf_op jit(solution)/shard_map/ppermute | solution.py:167
  72.9 89.3 %collective-permute-start.4 = (bf16[1,768,576]{1,2,0:T(8,128)(2,1)}, bf16[1,768,576]{1,2,0:T(8,128)(2,1)}, u32[]{:S(2)}, u32[]{:S(2)}) collective-permute-start(bf16[1,768,576]{1,2,0:T(8,128)(2,1)} %get-tuple-element.47), channel_id=1, source_target_pairs={{0,2},{1,3},{2,0},{3,1},{4,6},{5,7},{6,4},{7,5},{8,10},{9,11},{10,... | collective-permute-start | bytes 2654216 | tf_op jit(solution)/shard_map/ppermute | solution.py:167
  75.2 88.2 %collective-permute-start.5 = (bf16[1,768,576]{1,2,0:T(8,128)(2,1)}, bf16[1,768,576]{1,2,0:T(8,128)(2,1)}, u32[]{:S(2)}, u32[]{:S(2)}) collective-permute-start(bf16[1,768,576]{1,2,0:T(8,128)(2,1)} %get-tuple-element.46), channel_id=1, source_target_pairs={{0,3},{1,0},{2,1},{3,2},{4,7},{5,4},{6,5},{7,6},{8,11},{9,8},{10,9... | collective-permute-start | bytes 2654216 | tf_op jit(solution)/shard_map/ppermute | solution.py:167
  78.6 132.4 %collective-permute-start.12 = (bf16[1,192,768]{2,1,0:T(8,128)(2,1)}, bf16[1,192,768]{2,1,0:T(8,128)(2,1)}, u32[]{:S(2)}, u32[]{:S(2)}) collective-permute-start(bf16[1,192,768]{2,1,0:T(8,128)(2,1)} %get-tuple-element.66), channel_id=1, source_target_pairs={{0,1},{1,2},{2,3},{3,0},{4,5},{5,6},{6,7},{7,4},{8,9},{9,10},{10,1... | collective-permute-start | bytes 884744 | tf_op jit(solution)/shard_map/ppermute | solution.py:167
  79.5 152.4 %collective-permute-start.13 = (bf16[1,192,768]{2,1,0:T(8,128)(2,1)}, bf16[1,192,768]{2,1,0:T(8,128)(2,1)}, u32[]{:S(2)}, u32[]{:S(2)}) collective-permute-start(bf16[1,192,768]{2,1,0:T(8,128)(2,1)} %get-tuple-element.65), channel_id=1, source_target_pairs={{0,2},{1,3},{2,0},{3,1},{4,6},{5,7},{6,4},{7,5},{8,10},{9,11},{10,... | collective-permute-start | bytes 884744 | tf_op jit(solution)/shard_map/ppermute | solution.py:167
  105.5 135.5 %collective-permute-start.14 = (bf16[1,192,768]{2,1,0:T(8,128)(2,1)}, bf16[1,192,768]{2,1,0:T(8,128)(2,1)}, u32[]{:S(2)}, u32[]{:S(2)}) collective-permute-start(bf16[1,192,768]{2,1,0:T(8,128)(2,1)} %get-tuple-element.64), channel_id=1, source_target_pairs={{0,3},{1,0},{2,1},{3,2},{4,7},{5,4},{6,5},{7,6},{8,11},{9,8},{10,9... | collective-permute-start | bytes 884744 | tf_op jit(solution)/shard_map/ppermute | solution.py:167
  162.2 11.0 collective-permute-start.7
  167.8 78.1 %collective-permute-start.6 = (bf16[3072,576]{0,1:T(8,128)(2,1)}, bf16[3072,576]{0,1:T(8,128)(2,1)}, u32[]{:S(2)}, u32[]{:S(2)}) collective-permute-start(bf16[3072,576]{0,1:T(8,128)(2,1)} %pad_maximum_fusion.5), channel_id=1, source_target_pairs={{0,16},{16,0},{1,17},{17,1},{2,18},{18,2},{3,19},{19,3},{4,20},{20... | collective-permute-start | bytes 10616840 | tf_op jit(solution)/shard_map/ppermute | solution.py:204
  173.2 94.6 %collective-permute-start.8 = (bf16[1,3,256,128]{3,2,0,1:T(8,128)(2,1)}, bf16[1,3,256,128]{3,2,0,1:T(8,128)(2,1)S(1)}, u32[]{:S(2)}, u32[]{:S(2)}) collective-permute-start(bf16[1,3,256,128]{3,2,0,1:T(8,128)(2,1)} %get-tuple-element.84), channel_id=1, source_target_pairs={{0,1},{1,2},{2,3},{3,0},{4,5},{5,6},{6,7},{7,4},{8,9},{9,10},{10,1... | collective-permute-start | bytes 589832 | tf_op jit(solution)/shard_map/ppermute | solution.py:167
  211.0 56.8 %collective-permute-start.9 = (bf16[1,3,256,128]{3,2,0,1:T(8,128)(2,1)}, bf16[1,3,256,128]{3,2,0,1:T(8,128)(2,1)}, u32[]{:S(2)}, u32[]{:S(2)}) collective-permute-start(bf16[1,3,256,128]{3,2,0,1:T(8,128)(2,1)} %get-tuple-element.83), channel_id=1, source_target_pairs={{0,2},{1,3},{2,0},{3,1},{4,6},{5,7},{6,4},{7,5},{8,10},{9,11},{10,... | collective-permute-start | bytes 589832 | tf_op jit(solution)/shard_map/ppermute | solution.py:167
  231.9 37.0 %collective-permute-start.10 = (bf16[1,3,256,128]{3,2,0,1:T(8,128)(2,1)}, bf16[1,3,256,128]{3,2,0,1:T(8,128)(2,1)}, u32[]{:S(2)}, u32[]{:S(2)}) collective-permute-start(bf16[1,3,256,128]{3,2,0,1:T(8,128)(2,1)} %get-tuple-element.82), channel_id=1, source_target_pairs={{0,3},{1,0},{2,1},{3,2},{4,7},{5,4},{6,5},{7,6},{8,11},{9,8},{10,9... | collective-permute-start | bytes 589832 | tf_op jit(solution)/shard_map/ppermute | solution.py:167
  246.0 35.5 %collective-permute-start.15 = (bf16[192,3072]{1,0:T(8,128)(2,1)}, bf16[192,3072]{1,0:T(8,128)(2,1)}, u32[]{:S(2)}, u32[]{:S(2)}) collective-permute-start(bf16[192,3072]{1,0:T(8,128)(2,1)} %pad_maximum_fusion.7), channel_id=1, source_target_pairs={{0,16},{16,0},{1,17},{17,1},{2,18},{18,2},{3,19},{19,3},{4,20},{20... | collective-permute-start | bytes 3538952 | tf_op jit(solution)/shard_map/ppermute | solution.py:204
  265.1 4.8 collective-permute-start.11
  285.9 148.5 %copy-start.11 = (f32[8,8,4,768]{3,1,2,0:T(8,128)S(1)}, f32[8,8,4,768]{3,1,2,0:T(8,128)}, u32[]{:S(2)}) copy-start(f32[8,8,4,768]{3,1,2,0:T(8,128)} %copy-done.10) | copy-start | bytes 2359300
  285.9 148.5 %copy-start.49 = (f32[1,1,3072]{2,0,1:T(1,128)S(1)}, f32[1,1,3072]{2,0,1:T(1,128)}, u32[]{:S(2)}) copy-start(f32[1,1,3072]{2,0,1:T(1,128)} %get-tuple-element.146) | copy-start | bytes 36868
  285.9 148.5 %copy-start.50 = (f32[1,1,3072]{2,0,1:T(1,128)S(1)}, f32[1,1,3072]{2,0,1:T(1,128)}, u32[]{:S(2)}) copy-start(f32[1,1,3072]{2,0,1:T(1,128)} %get-tuple-element.147) | copy-start | bytes 36868
  285.9 148.5 %copy-start.51 = (f32[1,1,3072]{2,0,1:T(1,128)S(1)}, f32[1,1,3072]{2,0,1:T(1,128)}, u32[]{:S(2)}) copy-start(f32[1,1,3072]{2,0,1:T(1,128)} %get-tuple-element.148) | copy-start | bytes 36868
  285.9 148.5 %copy-start.56 = (pred[64]{0:T(512)(128)(4,1)S(1)}, pred[64]{0:T(512)(128)(4,1)}, u32[]{:S(2)}) copy-start(pred[64]{0:T(512)(128)(4,1)} %copy-done.55) | copy-start | bytes 196
  286.0 148.5 %copy-start.59 = (pred[64]{0:T(512)(128)(4,1)S(1)}, pred[64]{0:T(512)(128)(4,1)}, u32[]{:S(2)}) copy-start(pred[64]{0:T(512)(128)(4,1)} %copy-done.58) | copy-start | bytes 196
  286.0 399.3 %all-gather.7.cloned.1.call-start = ((), (), s32[]{:S(2)}) async-start(), calls=%async_computation.6 | async-start | bytes 6684672 | tf_op jit(solution)/shard_map/all_gather | solution.py:321
  437.4 437.5 %reduce-scatter.7.cloned.1.call-start = ((), (), s32[]{:S(2)}) async-start(), calls=%async_computation.7 | async-start | bytes 6684672 | tf_op jit(solution)/shard_map/reduce_scatter | solution.py:325
  441.9 39.2 %collective-permute-start.16 = (bf16[1,768,768]{2,1,0:T(8,128)(2,1)S(1)}, bf16[1,768,768]{2,1,0:T(8,128)(2,1)S(1)}, u32[]{:S(2)}, u32[]{:S(2)}) collective-permute-start(bf16[1,768,768]{2,1,0:T(8,128)(2,1)S(1)} %get-tuple-element.36), channel_id=1, source_target_pairs={{0,1},{1,2},{2,3},{3,0},{4,5},{5,6},{6,7},{7,4},{8,9},{9,10},{10,1... | collective-permute-start | bytes 3538952 | tf_op jit(solution)/shard_map/ppermute | solution.py:167
  443.0 145.9 %collective-permute-start.17 = (bf16[1,768,768]{2,1,0:T(8,128)(2,1)S(1)}, bf16[1,768,768]{2,1,0:T(8,128)(2,1)S(1)}, u32[]{:S(2)}, u32[]{:S(2)}) collective-permute-start(bf16[1,768,768]{2,1,0:T(8,128)(2,1)S(1)} %get-tuple-element.35), channel_id=1, source_target_pairs={{0,2},{1,3},{2,0},{3,1},{4,6},{5,7},{6,4},{7,5},{8,10},{9,11},{10,... | collective-permute-start | bytes 3538952 | tf_op jit(solution)/shard_map/ppermute | solution.py:167
  444.8 144.2 %collective-permute-start.18 = (bf16[1,768,768]{2,1,0:T(8,128)(2,1)S(1)}, bf16[1,768,768]{2,1,0:T(8,128)(2,1)S(1)}, u32[]{:S(2)}, u32[]{:S(2)}) collective-permute-start(bf16[1,768,768]{2,1,0:T(8,128)(2,1)S(1)} %get-tuple-element.34), channel_id=1, source_target_pairs={{0,3},{1,0},{2,1},{3,2},{4,7},{5,4},{6,5},{7,6},{8,11},{9,8},{10,9... | collective-permute-start | bytes 3538952 | tf_op jit(solution)/shard_map/ppermute | solution.py:167
  448.1 142.8 %collective-permute-start.20 = (bf16[1,768,768]{2,1,0:T(8,128)(2,1)S(1)}, bf16[1,768,768]{2,1,0:T(8,128)(2,1)S(1)}, u32[]{:S(2)}, u32[]{:S(2)}) collective-permute-start(bf16[1,768,768]{2,1,0:T(8,128)(2,1)S(1)} %get-tuple-element.24), channel_id=1, source_target_pairs={{0,1},{1,2},{2,3},{3,0},{4,5},{5,6},{6,7},{7,4},{8,9},{9,10},{10,1... | collective-permute-start | bytes 3538952 | tf_op jit(solution)/shard_map/ppermute | solution.py:167
  448.5 232.5 %collective-permute-start.21 = (bf16[1,768,768]{2,1,0:T(8,128)(2,1)S(1)}, bf16[1,768,768]{2,1,0:T(8,128)(2,1)S(1)}, u32[]{:S(2)}, u32[]{:S(2)}) collective-permute-start(bf16[1,768,768]{2,1,0:T(8,128)(2,1)S(1)} %get-tuple-element.23), channel_id=1, source_target_pairs={{0,2},{1,3},{2,0},{3,1},{4,6},{5,7},{6,4},{7,5},{8,10},{9,11},{10,... | collective-permute-start | bytes 3538952 | tf_op jit(solution)/shard_map/ppermute | solution.py:167
  481.1 200.1 %collective-permute-start.22 = (bf16[1,768,768]{2,1,0:T(8,128)(2,1)S(1)}, bf16[1,768,768]{2,1,0:T(8,128)(2,1)S(1)}, u32[]{:S(2)}, u32[]{:S(2)}) collective-permute-start(bf16[1,768,768]{2,1,0:T(8,128)(2,1)S(1)} %get-tuple-element.22), channel_id=1, source_target_pairs={{0,3},{1,0},{2,1},{3,2},{4,7},{5,4},{6,5},{7,6},{8,11},{9,8},{10,9... | collective-permute-start | bytes 3538952 | tf_op jit(solution)/shard_map/ppermute | solution.py:167
  589.5 92.2 %copy-start.14 = (bf16[768,768]{1,0:T(8,128)(2,1)}, bf16[768,768]{1,0:T(8,128)(2,1)S(1)}, u32[]{:S(2)}) copy-start(bf16[768,768]{1,0:T(8,128)(2,1)S(1)} %get-tuple-element.31) | copy-start | bytes 3538948
  589.5 95.9 %copy-start.13 = (bf16[768,768]{1,0:T(8,128)(2,1)}, bf16[768,768]{1,0:T(8,128)(2,1)S(1)}, u32[]{:S(2)}) copy-start(bf16[768,768]{1,0:T(8,128)(2,1)S(1)} %get-tuple-element.30) | copy-start | bytes 3538948
  590.8 94.5 %collective-permute-start.19 = (bf16[3072,768]{1,0:T(8,128)(2,1)S(1)}, bf16[3072,768]{1,0:T(8,128)(2,1)}, u32[]{:S(2)}, u32[]{:S(2)}) collective-permute-start(bf16[3072,768]{1,0:T(8,128)(2,1)S(1)} %pad_maximum_fusion.1), channel_id=1, source_target_pairs={{0,16},{16,0},{1,17},{17,1},{2,18},{18,2},{3,19},{19,3},{4,20},{20... | collective-permute-start | bytes 14155784 | tf_op jit(solution)/shard_map/ppermute | solution.py:204
  685.3 11.0 collective-permute-start.23
  703.9 171.0 %copy-start.53 = (pred[64]{0:T(512)(128)(4,1)S(1)}, pred[64]{0:T(512)(128)(4,1)}, u32[]{:S(2)}) copy-start(pred[64]{0:T(512)(128)(4,1)} %copy-done.52) | copy-start | bytes 196
  703.9 175.5 %copy-start.65 = (f32[64]{0:T(128)S(1)}, f32[64]{0:T(128)}, u32[]{:S(2)}) copy-start(f32[64]{0:T(128)} %get-tuple-element.157) | copy-start | bytes 772
  703.9 268.2 %copy-start.27 = (bf16[768,576]{0,1:T(8,128)(2,1)S(1)}, bf16[768,576]{0,1:T(8,128)(2,1)}, u32[]{:S(2)}) copy-start(bf16[768,576]{0,1:T(8,128)(2,1)} %copy-done.25) | copy-start | bytes 2654212
  703.9 268.2 %all-gather.9.cloned.1.call-start = ((), (), s32[]{:S(2)}) async-start(), calls=%async_computation.8 | async-start | bytes 6684672 | tf_op jit(solution)/shard_map/all_gather | solution.py:304
  876.3 95.8 %copy-start.8 = (bf16[64,3072]{1,0:T(8,128)(2,1)}, bf16[64,3072]{1,0:T(8,128)(2,1)S(1)}, u32[]{:S(2)}) copy-start(bf16[64,3072]{1,0:T(8,128)(2,1)S(1)} %get-tuple-element.13) | copy-start | bytes 1179652
  878.6 277.6 %reduce-scatter.9.cloned.1.call-start = ((), (), s32[]{:S(2)}) async-start(), calls=%async_computation.9 | async-start | bytes 6684672 | tf_op jit(solution)/shard_map/reduce_scatter | solution.py:318
  993.6 2.4 collective-permute-start.27
  1012.1 144.1 %copy-start.9 = (bf16[64,3072]{1,0:T(8,128)(2,1)S(1)}, bf16[64,3072]{1,0:T(8,128)(2,1)}, u32[]{:S(2)}) copy-start(bf16[64,3072]{1,0:T(8,128)(2,1)} %copy-done.8) | copy-start | bytes 1179652
  1012.1 144.1 %copy-start.54 = (pred[64]{0:T(512)(128)(4,1)S(1)}, pred[64]{0:T(512)(128)(4,1)}, u32[]{:S(2)}) copy-start(pred[64]{0:T(512)(128)(4,1)} %copy-done.52) | copy-start | bytes 196
  1012.1 144.1 %copy-start.57 = (pred[64]{0:T(512)(128)(4,1)S(1)}, pred[64]{0:T(512)(128)(4,1)}, u32[]{:S(2)}) copy-start(pred[64]{0:T(512)(128)(4,1)} %copy-done.55) | copy-start | bytes 196
  1012.2 144.1 %copy-start.60 = (pred[64]{0:T(512)(128)(4,1)S(1)}, pred[64]{0:T(512)(128)(4,1)}, u32[]{:S(2)}) copy-start(pred[64]{0:T(512)(128)(4,1)} %copy-done.58) | copy-start | bytes 196
  1012.2 240.9 %all-gather.11.cloned.1.call-start = ((), (), s32[]{:S(2)}) async-start(), calls=%async_computation.10 | async-start | bytes 6684672 | tf_op jit(solution)/shard_map/all_gather | solution.py:321
  1159.2 295.5 %reduce-scatter.11.cloned.1.call-start = ((), (), s32[]{:S(2)}) async-start(), calls=%async_computation.11 | async-start | bytes 6684672 | tf_op jit(solution)/shard_map/reduce_scatter | solution.py:325
  1277.3 10.2 collective-permute-start.32
  1278.2 18.0 %collective-permute-start.33 = (bf16[1,3,256,128]{3,2,0,1:T(8,128)(2,1)S(1)}, bf16[1,3,256,128]{3,2,0,1:T(8,128)(2,1)S(1)}, u32[]{:S(2)}, u32[]{:S(2)}) collective-permute-start(bf16[1,3,256,128]{3,2,0,1:T(8,128)(2,1)S(1)} %get-tuple-element.73), channel_id=1, source_target_pairs={{0,2},{1,3},{2,0},{3,1},{4,6},{5,7},{6,4},{7,5},{8,10},{9,11},{10,... | collective-permute-start | bytes 589832 | tf_op jit(solution)/shard_map/ppermute | solution.py:167
  1279.5 17.4 %collective-permute-start.34 = (bf16[1,3,256,128]{3,2,0,1:T(8,128)(2,1)S(1)}, bf16[1,3,256,128]{3,2,0,1:T(8,128)(2,1)S(1)}, u32[]{:S(2)}, u32[]{:S(2)}) collective-permute-start(bf16[1,3,256,128]{3,2,0,1:T(8,128)(2,1)S(1)} %get-tuple-element.72), channel_id=1, source_target_pairs={{0,3},{1,0},{2,1},{3,2},{4,7},{5,4},{6,5},{7,6},{8,11},{9,8},{10,9... | collective-permute-start | bytes 589832 | tf_op jit(solution)/shard_map/ppermute | solution.py:167
  1297.2 21.0 %collective-permute-start.35 = (bf16[1,3,256,128]{3,2,0,1:T(8,128)(2,1)S(1)}, bf16[1,3,256,128]{3,2,0,1:T(8,128)(2,1)S(1)}, u32[]{:S(2)}, u32[]{:S(2)}) collective-permute-start(bf16[1,3,256,128]{3,2,0,1:T(8,128)(2,1)S(1)} %get-tuple-element.77), channel_id=1, source_target_pairs={{0,1},{1,2},{2,3},{3,0},{4,5},{5,6},{6,7},{7,4},{8,9},{9,10},{10,1... | collective-permute-start | bytes 589832 | tf_op jit(solution)/shard_map/ppermute | solution.py:167
  1310.7 148.2 %collective-permute-start.24 = (bf16[1,64,768]{2,0,1:T(2,128)(2,1)}, bf16[1,64,768]{2,0,1:T(2,128)(2,1)}, u32[]{:S(2)}, u32[]{:S(2)}) collective-permute-start(bf16[1,64,768]{2,0,1:T(2,128)(2,1)} %get-tuple-element.91), channel_id=1, source_target_pairs={{0,1},{1,2},{2,3},{3,0},{4,5},{5,6},{6,7},{7,4},{8,9},{9,10},{10,1... | collective-permute-start | bytes 294920 | tf_op jit(solution)/shard_map/ppermute | solution.py:167
  1310.7 150.0 %collective-permute-start.25 = (bf16[1,64,768]{2,0,1:T(2,128)(2,1)}, bf16[1,64,768]{2,0,1:T(2,128)(2,1)}, u32[]{:S(2)}, u32[]{:S(2)}) collective-permute-start(bf16[1,64,768]{2,0,1:T(2,128)(2,1)} %get-tuple-element.90), channel_id=1, source_target_pairs={{0,2},{1,3},{2,0},{3,1},{4,6},{5,7},{6,4},{7,5},{8,10},{9,11},{10,... | collective-permute-start | bytes 294920 | tf_op jit(solution)/shard_map/ppermute | solution.py:167
  1310.7 162.5 %collective-permute-start.26 = (bf16[1,64,768]{2,0,1:T(2,128)(2,1)}, bf16[1,64,768]{2,0,1:T(2,128)(2,1)}, u32[]{:S(2)}, u32[]{:S(2)}) collective-permute-start(bf16[1,64,768]{2,0,1:T(2,128)(2,1)} %get-tuple-element.89), channel_id=1, source_target_pairs={{0,3},{1,0},{2,1},{3,2},{4,7},{5,4},{6,5},{7,6},{8,11},{9,8},{10,9... | collective-permute-start | bytes 294920 | tf_op jit(solution)/shard_map/ppermute | solution.py:167
  1314.5 39.6 %collective-permute-start.36 = (bf16[1,3,256,128]{3,2,0,1:T(8,128)(2,1)S(1)}, bf16[1,3,256,128]{3,2,0,1:T(8,128)(2,1)S(1)}, u32[]{:S(2)}, u32[]{:S(2)}) collective-permute-start(bf16[1,3,256,128]{3,2,0,1:T(8,128)(2,1)S(1)} %get-tuple-element.76), channel_id=1, source_target_pairs={{0,2},{1,3},{2,0},{3,1},{4,6},{5,7},{6,4},{7,5},{8,10},{9,11},{10,... | collective-permute-start | bytes 589832 | tf_op jit(solution)/shard_map/ppermute | solution.py:167
  1318.2 35.9 %collective-permute-start.37 = (bf16[1,3,256,128]{3,2,0,1:T(8,128)(2,1)S(1)}, bf16[1,3,256,128]{3,2,0,1:T(8,128)(2,1)S(1)}, u32[]{:S(2)}, u32[]{:S(2)}) collective-permute-start(bf16[1,3,256,128]{3,2,0,1:T(8,128)(2,1)S(1)} %get-tuple-element.75), channel_id=1, source_target_pairs={{0,3},{1,0},{2,1},{3,2},{4,7},{5,4},{6,5},{7,6},{8,11},{9,8},{10,9... | collective-permute-start | bytes 589832 | tf_op jit(solution)/shard_map/ppermute | solution.py:167
  1354.4 138.0 %collective-permute-start.38 = (bf16[256,12,128]{2,0,1:T(8,128)(2,1)S(1)}, bf16[256,12,128]{2,0,1:T(8,128)(2,1)}, u32[]{:S(2)}, u32[]{:S(2)}) collective-permute-start(bf16[256,12,128]{2,0,1:T(8,128)(2,1)S(1)} %bitcast.278), channel_id=1, source_target_pairs={{0,16},{16,0},{1,17},{17,1},{2,18},{18,2},{3,19},{19,3},{4,20},{20... | collective-permute-start | bytes 2359304 | tf_op jit(solution)/shard_map/ppermute | solution.py:204
  1457.8 22.4 %collective-permute-start.28 = (bf16[1,64,768]{2,0,1:T(2,128)(2,1)}, bf16[1,64,768]{2,0,1:T(2,128)(2,1)}, u32[]{:S(2)}, u32[]{:S(2)}) collective-permute-start(bf16[1,64,768]{2,0,1:T(2,128)(2,1)} %get-tuple-element.95), channel_id=1, source_target_pairs={{0,1},{1,2},{2,3},{3,0},{4,5},{5,6},{6,7},{7,4},{8,9},{9,10},{10,1... | collective-permute-start | bytes 294920 | tf_op jit(solution)/shard_map/ppermute | solution.py:167
  1458.8 25.3 %collective-permute-start.29 = (bf16[1,64,768]{2,0,1:T(2,128)(2,1)}, bf16[1,64,768]{2,0,1:T(2,128)(2,1)}, u32[]{:S(2)}, u32[]{:S(2)}) collective-permute-start(bf16[1,64,768]{2,0,1:T(2,128)(2,1)} %get-tuple-element.94), channel_id=1, source_target_pairs={{0,2},{1,3},{2,0},{3,1},{4,6},{5,7},{6,4},{7,5},{8,10},{9,11},{10,... | collective-permute-start | bytes 294920 | tf_op jit(solution)/shard_map/ppermute | solution.py:167
  1460.7 27.5 %collective-permute-start.30 = (bf16[1,64,768]{2,0,1:T(2,128)(2,1)}, bf16[1,64,768]{2,0,1:T(2,128)(2,1)}, u32[]{:S(2)}, u32[]{:S(2)}) collective-permute-start(bf16[1,64,768]{2,0,1:T(2,128)(2,1)} %get-tuple-element.93), channel_id=1, source_target_pairs={{0,3},{1,0},{2,1},{3,2},{4,7},{5,4},{6,5},{7,6},{8,11},{9,8},{10,9... | collective-permute-start | bytes 294920 | tf_op jit(solution)/shard_map/ppermute | solution.py:167
  1492.3 2.7 collective-permute-start.31
  (51 other events, 506.0 us)
Sparse Core Ops, SparseCore 0:
  65.4 181.6 all-gather.4
  286.1 148.2 reduce-scatter.4
  437.9 211.3 all-gather.6
  704.0 170.8 reduce-scatter.6
  878.7 93.3 all-gather.8
  1012.3 143.8 reduce-scatter.8
  1159.6 93.3 all-gather.10
  1276.2 178.3 reduce-scatter.10

commit v3 on v2

--- a/solution.py
+++ b/solution.py
@@ -195,8 +195,9 @@
         w_up[0],
         w_down[0],
     )
-    if stale_cache.shape[3] % lax.axis_size("narrow") == 0:
-        return features_whole(*operands)
+    n_narrow = lax.axis_size("narrow")
+    if n_narrow == lax.axis_size("wide") and stale_cache.shape[3] % n_narrow == 0:
+        return in_halves(*operands)
     return features_split(*operands)
 
 
@@ -218,13 +219,53 @@
     return (values * (1.0 + pick(table, kinds, 1)) + pick(table, kinds, 0)).astype(BF)
 
 
-def row_norm(values):
-    center = values - jnp.mean(values, axis=1, keepdims=True)
-    variance = jnp.mean(center * center, axis=1, keepdims=True)
-    return center * lax.rsqrt(variance + EPS_ROW)
-
-
-def features_whole(
+def wide_pairs(step):
+    return [(i, i ^ step) for i in range(lax.axis_size("wide"))]
+
+
+def gather_wide(block):
+    got = [lax.ppermute(block, "wide", wide_pairs(step)) for step in range(1, lax.axis_size("wide"))]
+    return jnp.concatenate([block] + got, axis=0)
+
+
+def scatter_wide(terms):
+    total = terms[0].astype(F32)
+    for step in range(1, len(terms)):
+        total += lax.ppermute(terms[step], "wide", wide_pairs(step)).astype(F32)
+    return total
+
+
+def gather_line(block):
+    n = lax.axis_size("narrow")
+    me = lax.axis_index("narrow")
+    from_left = [block]
+    from_right = [block]
+    for step in range(1, n):
+        right = [(i, i + 1) for i in range(step - 1, n - 1)]
+        left = [(i + 1, i) for i in range(0, n - step)]
+        from_left.append(lax.ppermute(from_left[-1], "narrow", right))
+        from_right.append(lax.ppermute(from_right[-1], "narrow", left))
+    return [block] + [
+        jnp.where(me >= step, from_left[step], from_right[n - step]) for step in range(1, n)
+    ]
+
+
+def line_norm(values, model_width):
+    n = lax.axis_size("narrow")
+    width = values.shape[1]
+    mean = jnp.mean(values, axis=1)
+    center = values - mean[:, None]
+    own = jnp.stack([mean, jnp.sum(center * center, axis=1)])
+    parts = [own]
+    for step in range(1, n):
+        parts.append(lax.ppermute(own, "narrow", [(i, (i + step) % n) for i in range(n)]))
+    whole_mean = sum(part[0] for part in parts) / n
+    spread = sum(part[1] + width * (part[0] - whole_mean) ** 2 for part in parts)
+    scale = lax.rsqrt(spread / model_width + EPS_ROW)
+    return (values - whole_mean[:, None]) * scale[:, None]
+
+
+def in_halves(
     hidden_in,
     row_kind,
     positions,
@@ -244,87 +285,109 @@
     section = lax.axis_index("section")
     lead = section == 0
     _, rows_a, feat_a = hidden_in.shape
+    halves = 2
+    part = rows_a // halves
     total_rows = rows_a * n_wide
     rows_b = total_rows // n_narrow
-    rows_c = rows_a // n_narrow
     heads_local = stale_cache.shape[3]
     heads = heads_local // n_narrow
     pair = stale_cache.shape[4]
     head_dim = pair // 2
     model_width = feat_a * n_narrow
-    both = ("wide", "narrow")
-
-    def weights_for(own, axis):
-        parts = jnp.stack(jnp.split(own, n_narrow, axis))
-        got = exchange(parts, "narrow")
-        joined = jnp.concatenate([got[i] for i in range(n_narrow)], axis=1 - axis)
-        other = swap(joined)
-        return (jnp.where(lead, joined, other), jnp.where(lead, other, joined))
-
-    def to_rows_c(block):
-        got = exchange(block.reshape(n_narrow, rows_c, feat_a), "narrow")
-        return got.transpose(1, 0, 2).reshape(rows_c, model_width)
-
-    def from_rows_c(block):
-        got = exchange(block.reshape(rows_c, n_narrow, feat_a).transpose(1, 0, 2), "narrow")
-        return got.reshape(rows_a, feat_a)
+
+    def both_layers(own):
+        other = swap(own)
+        return (jnp.where(lead, own, other), jnp.where(lead, other, own))
+
+    def relative(values):
+        blocks = values.reshape(n_wide, halves, part)
+        order = [lax.dynamic_index_in_dim(blocks, wide_idx ^ step, 0, False) for step in range(n_wide)]
+        return jnp.stack(order, axis=1).reshape(total_rows)
 
     activated = jax.nn.silu(time_features(timesteps, ada_weight.shape[1])).astype(BF)
     modulation = jnp.einsum("re,kesd->krsd", activated, ada_weight, preferred_element_type=F32)
-    modulation = lax.all_gather(modulation.reshape(2, 4, 3, feat_a), ("section", "narrow"), axis=0)
-    tables = modulation.reshape(2, n_narrow, 2, 4, 3, feat_a).transpose(0, 2, 3, 4, 1, 5)
-    tables = tables.reshape(2, 2, 4, 3, model_width)
-
-    qkv_weights = weights_for(w_qkv, 1)
-    out_weights = weights_for(w_out, 0)
-    up_weights = weights_for(w_up, 1)
-    down_weights = weights_for(w_down, 0)
-    own_norms = qk_norm
-    other_norms = swap(qk_norm)
-    norm_rows = (jnp.where(lead, own_norms, other_norms), jnp.where(lead, other_norms, own_norms))
-
-    kinds = lax.dynamic_slice_in_dim(row_kind, section, 1, 0)[0]
-    kinds_other = lax.dynamic_slice_in_dim(row_kind, 1 - section, 1, 0)[0]
-    own_mask = key_mask(kinds, head_dim)
-    other_mask = key_mask(kinds_other, head_dim)
-    kinds_c = lax.dynamic_slice_in_dim(kinds, wide_idx * rows_a + narrow_idx * rows_c, rows_c)
-    places = lax.dynamic_slice_in_dim(positions, section, 1, 1)[:, 0]
+    tables = both_layers(modulation.reshape(2, 4, 3, feat_a))
+    qkv_weights = both_layers(w_qkv)
+    norm_rows = both_layers(qk_norm)
+    out_weights = both_layers(w_out)
+    up_weights = both_layers(w_up)
+    down_weights = both_layers(w_down)
+
+    kinds = lax.dynamic_index_in_dim(row_kind, section, 0, False)
+    kinds_other = lax.dynamic_index_in_dim(row_kind, 1 - section, 0, False)
+    kinds_r = relative(kinds)
+    own_mask = key_mask(kinds_r, head_dim)
+    other_mask = key_mask(jnp.where(lead, kinds_other, relative(kinds_other)), head_dim)
+    kinds_a = lax.dynamic_slice_in_dim(kinds, wide_idx * rows_a, rows_a)
+    kinds_h = [kinds_a[h * part : (h + 1) * part] for h in range(halves)]
+    places = lax.dynamic_index_in_dim(positions, section, 1, False)
+    places = jnp.stack([relative(places[i]) for i in range(3)])
     cosine, sine = rotary_tables(places, head_dim)
+    chunk = total_rows // halves
 
     blocks = stale_cache[0, 1].reshape(rows_b, n_narrow, heads, pair).transpose(1, 2, 0, 3)
     stale = exchange(blocks, "narrow").transpose(1, 0, 2, 3).reshape(heads, total_rows, pair)
 
-    layer_in = to_rows_c(lax.dynamic_slice_in_dim(hidden_in, section, 1, 0)[0])
+    def to_rows(fresh):
+        blocks = [f.reshape(heads, n_wide, part, pair) for f in fresh]
+        per_narrow = []
+        for there in range(n_narrow):
+            picked = [lax.dynamic_index_in_dim(b, wide_idx ^ there, 1, False) for b in blocks]
+            per_narrow.append(jnp.concatenate(picked, axis=1))
+        got = exchange(jnp.stack(per_narrow), "narrow")
+        return got.transpose(2, 0, 1, 3).reshape(rows_b, heads_local, pair)
+
+    layer_in = lax.dynamic_index_in_dim(hidden_in, section, 0, False)
+    layer_in = [layer_in[h * part : (h + 1) * part] for h in range(halves)]
     results = []
     caches = []
     for layer in range(2):
         table = tables[layer]
-        x_in = layer_in.astype(F32)
-        entry = modulate(row_norm(x_in), table[0], kinds_c)
-        entry = lax.all_gather(entry, both, axis=0, tiled=True)
-        qkv = jnp.dot(entry, qkv_weights[layer], preferred_element_type=F32).astype(BF)
-        queries, fresh = prepare(
-            qkv, cosine, sine, kinds, norm_pairs(norm_rows[layer]), heads, head_dim
-        )
-        blocks = fresh.reshape(heads, n_narrow, rows_b, pair).transpose(1, 0, 2, 3)
-        blocks = exchange(blocks, "narrow").transpose(2, 0, 1, 3)
-        caches.append(blocks.reshape(rows_b, heads_local, pair))
+        norm_pair = norm_pairs(norm_rows[layer])
+        x_in = [block.astype(F32) for block in layer_in]
+        queries = []
+        fresh = []
+        for h in range(halves):
+            entry = modulate(line_norm(x_in[h], model_width), table[0], kinds_h[h])
+            terms = jnp.dot(gather_wide(entry), qkv_weights[layer], preferred_element_type=F32)
+            qkv = lax.psum_scatter(terms.astype(BF), "narrow", scatter_dimension=1, tiled=True)
+            rows = slice(h * chunk, (h + 1) * chunk)
+            q, pairs = prepare(
+                qkv, cosine[rows], sine[rows], kinds_r[rows], norm_pair, heads, head_dim
+            )
+            queries.append(q)
+            fresh.append(pairs)
+        caches.append(to_rows(fresh))
+        own = jnp.concatenate(fresh, axis=1)
         if layer == 0:
-            other = jnp.where(lead, stale, swap(fresh))
+            other = jnp.where(lead, stale, lax.ppermute(own, "section", [(0, 1)]))
         else:
-            other = swap(jnp.where(lead, fresh, stale))
-        attended = attend(queries, fresh, other, own_mask, other_mask, head_dim)
-        terms = jnp.dot(attended, out_weights[layer], preferred_element_type=F32).astype(BF)
-        projected = lax.psum_scatter(terms, both, scatter_dimension=0, tiled=True)
-        after = x_in + pick(table[0], kinds_c, 2) * projected.astype(F32)
-        entry = modulate(row_norm(after), table[1], kinds_c)
-        entry = lax.all_gather(entry, both, axis=0, tiled=True)
-        up = jnp.dot(entry, up_weights[layer], preferred_element_type=F32)
-        inner = jax.nn.gelu(up, approximate=True).astype(BF)
-        terms = jnp.dot(inner, down_weights[layer], preferred_element_type=F32).astype(BF)
-        down = lax.psum_scatter(terms, both, scatter_dimension=0, tiled=True)
-        layer_in = (after + pick(table[1], kinds_c, 2) * down.astype(F32)).astype(BF)
-        results.append(from_rows_c(layer_in))
+            other = swap(jnp.where(lead, own, stale))
+        after = []
+        for h in range(halves):
+            attended = attend(queries[h], own, other, own_mask, other_mask, head_dim)
+            attended = lax.all_gather(attended, "narrow", axis=1, tiled=True)
+            terms = jnp.dot(attended, out_weights[layer], preferred_element_type=F32).astype(BF)
+            projected = scatter_wide([terms[r * part : (r + 1) * part] for r in range(n_wide)])
+            after.append(x_in[h] + pick(table[0], kinds_h[h], 2) * projected)
+        inner = []
+        for h in range(halves):
+            entry = modulate(line_norm(after[h], model_width), table[1], kinds_h[h])
+            terms = jnp.dot(gather_wide(entry), up_weights[layer], preferred_element_type=F32)
+            up = lax.psum_scatter(terms.astype(BF), "narrow", scatter_dimension=0, tiled=True)
+            inner.append(jax.nn.gelu(up.astype(F32), approximate=True).astype(BF))
+        layer_in = []
+        for h in range(halves):
+            gathered = jnp.concatenate(gather_line(inner[h]), axis=0)
+            terms = jnp.dot(gathered, down_weights[layer], preferred_element_type=F32).astype(BF)
+            size = chunk // n_narrow
+            ordered = [
+                lax.dynamic_slice_in_dim(terms, (narrow_idx + n_narrow - r) % n_narrow * size, size, 0)
+                for r in range(n_narrow)
+            ]
+            down = scatter_wide(ordered)
+            layer_in.append((after[h] + pick(table[1], kinds_h[h], 2) * down).astype(BF))
+        results.append(jnp.concatenate(layer_in, axis=0))
     return (by_layer(results, lead), by_layer(caches, lead))
 
 

time: 1510 us -> 972 us (0.64)
  waiting for transfers between devices: 1120 us -> 468 us
  starting transfers between devices: 104 us -> 198 us
  blocking collectives: 25.5 us -> 90.9 us
  local copies, waits for them, and re-layouts: 95.5 us -> 31.2 us
    reduce_scatter x4, waiting for transfers between devices: 559 us -> 67.2 us  [in_halves(): lax.psum_scatter(terms.astype(BF), 'narrow', scatter_dimension=0, tiled=T...]
    ppermute x30 -> x9, waiting for transfers between devices: 367 us -> 40.8 us  [exchange(): block = lax.ppermute(block, axis, [(i, (i + step) % n) for i in range(n)])]
    ppermute x0 -> x97, waiting for transfers between devices: none -> 243 us  [the longest x12 133 us: gather_line(): from_right.append(lax.ppermute(from_right[-1], 'narrow', left))]
    all_gather x4 -> x0, waiting for transfers between devices: 187 us -> none  [features_whole(): entry = lax.all_gather(entry, both, axis=0, tiled=True)]
    ppermute x0 -> x97, starting transfers between devices: none -> 181 us  [the longest x24 72 us: line_norm(): lax.ppermute(own, 'narrow', [(i, (i + step) % n) for i in range(n)])]
    unnamed x8 -> x12, waiting for transfers between devices: 0.13 us -> 113 us
    ppermute x30 -> x9, starting transfers between devices: 101 us -> 14.8 us  [exchange(): block = lax.ppermute(block, axis, [(i, (i + step) % n) for i in range(n)])]
    all_gather x1 -> x4, blocking collectives: 25.5 us -> 90.9 us  [in_halves(): attended = lax.all_gather(attended, 'narrow', axis=1, tiled=True)]
  transfers between devices with their start and end apart: 47 -> 123, of which waited for: 19 -> 69; matrix products, arithmetic and copies ran while one was open for 8% -> 12% of each run, Pallas kernels for 1% -> 2%
where the time goes in v3:
time: 972 us; the launch traced here: 964 us
  waiting for transfers between devices  468 us (48%)
  starting transfers between devices  198 us (20%)
  blocking collectives  90.9 us (9%)
  matrix products  83.8 us (9%)
  other arithmetic  38.3 us (4%)
  Pallas kernels  36.7 us (4%)
  local copies, waits for them, and re-layouts  31.2 us (3%)
  between operations  16.7 us (2%)
    ppermute x12, waiting for transfers between devices, gather_line(): from_right.append(lax.ppermute(from_right[-1], 'narrow', left))  133 us
    unnamed x12, waiting for transfers between devices  113 us
    all_gather x4, blocking collectives, in_halves(): attended = lax.all_gather(attended, 'narrow', axis=1, tiled=True)  90.9 us
    ppermute x24, starting transfers between devices, line_norm(): lax.ppermute(own, 'narrow', [(i, (i + step) % n) for i in range(n)])  72 us
    reduce_scatter x4, waiting for transfers between devices, in_halves(): lax.psum_scatter(terms.astype(BF), 'narrow', scatter_dimension=0, tiled=T...  67.2 us
    ppermute x24, waiting for transfers between devices, gather_wide(): lax.ppermute(block, 'wide', wide_pairs(step))  45.4 us
    ppermute x9, waiting for transfers between devices, exchange(): block = lax.ppermute(block, axis, [(i, (i + step) % n) for i in range(n)])  40.8 us
    ppermute x24, waiting for transfers between devices, scatter_wide(): total += lax.ppermute(terms[step], 'wide', wide_pairs(step)).astype(F32)  38.1 us
  transfers between devices with their start and end apart: 123, of which 69 were waited for; matrix products, arithmetic and copies ran while one was open for 12% of the time, Pallas kernels for 2%

profile of v3, /device:TPU:0, one launch (start us, length us, event | category | flops | bytes accessed | tf_op | source)
XLA Modules:
  0.0 964.1 jit_solution(15450863416535251146)
XLA Ops:
  17.6 5.1 fusion.74
  29.5 4.3 collective-permute-done.4
  33.8 4.6 collective-permute-done.5
  38.4 5.5 fusion.2
  48.6 4.0 collective-permute-done.9
  56.6 4.1 collective-permute-done.12
  60.6 3.0 collective-permute-done.13
  63.7 5.6 fusion.3
  79.9 17.9 %reduce-scatter.25.cloned.1.call-done = bf16[576,512]{1,0:T(8,128)(2,1)} async-done(((bf16[2304,512]{1,0:T(8,128)(2,1)}), bf16[576,512]{1,0:T(8,128)(2,1)}) %reduce-scatter.25.cloned.1.call-update) | async-done | bytes 589840
  99.2 51.4 %reduce-scatter.27.cloned.1.call-done = bf16[576,512]{1,0:T(8,128)(2,1)} async-done(((bf16[2304,512]{1,0:T(8,128)(2,1)}), bf16[576,512]{1,0:T(8,128)(2,1)}) %reduce-scatter.27.cloned.1.call-update) | async-done | bytes 589840
  152.0 4.0 prepare.4
  156.7 3.9 prepare.5
  171.5 5.2 attend.4
  179.2 19.5 %all_gather.12 = bf16[512,768]{0,1:T(8,128)(2,1)S(1)} all-gather(bf16[512,192]{0,1:T(8,128)(2,1)} %copy.67), channel_id=1, replica_groups=mesh['section'=2,'wide'=4,'narrow'=4] {'narrow'}, dimensions={1}, use_global_device_ids=true | all-gather | bytes 983040 | tf_op jit(solution)/shard_map/all_gather | solution.py:369
  227.2 5.4 convolution_convert_fusion.5
  233.7 5.2 attend.5
  240.7 28.1 %all_gather.13 = bf16[512,768]{0,1:T(8,128)(2,1)S(1)} all-gather(bf16[512,192]{0,1:T(8,128)(2,1)S(1)} %copy.69), channel_id=1, replica_groups=mesh['section'=2,'wide'=4,'narrow'=4] {'narrow'}, dimensions={1}, use_global_device_ids=true | all-gather | bytes 983040 | tf_op jit(solution)/shard_map/all_gather | solution.py:369
  282.4 3.2 collective-permute-start.44
  300.0 5.3 convolution_convert_fusion.4
  308.5 5.5 collective-permute-start.30
  313.9 44.2 %collective-permute-done.31 = bf16[128,3072]{1,0:T(8,128)(2,1)S(1)} collective-permute-done((bf16[128,3072]{1,0:T(8,128)(2,1)S(1)}, bf16[128,3072]{1,0:T(8,128)(2,1)S(1)}, u32[]{:S(2)}, u32[]{:S(2)}) %collective-permute-start.31) | collective-permute-done | bytes 786464 | tf_op jit(solution)/shard_map/ppermute | solution.py:247
  361.0 35.5 %collective-permute-done.32 = bf16[128,3072]{1,0:T(8,128)(2,1)} collective-permute-done((bf16[128,3072]{1,0:T(8,128)(2,1)S(1)}, bf16[128,3072]{1,0:T(8,128)(2,1)}, u32[]{:S(2)}, u32[]{:S(2)}) %collective-permute-start.32) | collective-permute-done | bytes 786464 | tf_op jit(solution)/shard_map/ppermute | solution.py:247
  401.8 7.0 collective-permute-start.49
  411.1 8.0 collective-permute-done.33
  420.5 5.1 fusion.71
  430.8 3.9 collective-permute-done.50
  439.7 21.4 %collective-permute-start.58 = (f32[2,128]{1,0:T(2,128)S(1)}, f32[2,128]{1,0:T(2,128)S(1)}, u32[]{:S(2)}, u32[]{:S(2)}) collective-permute-start(f32[2,128]{1,0:T(2,128)S(1)} %pad_maximum_fusion.13), channel_id=1, source_target_pairs={{0,1},{1,2},{2,3},{3,0},{4,5},{5,6},{6,7},{7,4},{8,9},{9,10},{10,1... | collective-permute-start | bytes 3080 | tf_op jit(solution)/shard_map/ppermute | solution.py:261
  461.0 4.5 collective-permute-start.59
  468.1 3.8 collective-permute-done.59
  481.7 5.5 fusion.4
  487.3 3.0 collective-permute-done.52
  491.7 5.4 fusion.68
  500.7 4.3 collective-permute-done.55
  508.1 19.3 %collective-permute-start.65 = (f32[2,128]{1,0:T(2,128)S(1)}, f32[2,128]{1,0:T(2,128)S(1)}, u32[]{:S(2)}, u32[]{:S(2)}) collective-permute-start(f32[2,128]{1,0:T(2,128)S(1)} %pad_maximum_fusion.15), channel_id=1, source_target_pairs={{0,2},{1,3},{2,0},{3,1},{4,6},{5,7},{6,4},{7,5},{8,10},{9,11},{10,... | collective-permute-start | bytes 3080 | tf_op jit(solution)/shard_map/ppermute | solution.py:261
  531.7 4.7 collective-permute-start.67
  540.1 4.1 collective-permute-done.68
  544.2 5.5 fusion.5
  551.9 43.8 %reduce-scatter.31.cloned.1.call-done = bf16[576,512]{1,0:T(8,128)(2,1)} async-done(((bf16[2304,512]{1,0:T(8,128)(2,1)}), bf16[576,512]{1,0:T(8,128)(2,1)}) %reduce-scatter.31.cloned.1.call-update) | async-done | bytes 589840
  598.0 4.0 prepare.6
  602.0 4.0 prepare.7
  608.6 5.2 attend.6
  614.0 18.1 %all_gather.14 = bf16[512,768]{0,1:T(8,128)(2,1)S(1)} all-gather(bf16[512,192]{0,1:T(8,128)(2,1)S(1)} %copy.75), channel_id=1, replica_groups=mesh['section'=2,'wide'=4,'narrow'=4] {'narrow'}, dimensions={1}, use_global_device_ids=true | all-gather | bytes 983040 | tf_op jit(solution)/shard_map/all_gather | solution.py:369
  638.3 3.7 collective-permute-done.71
  642.0 3.3 collective-permute-done.72
  658.5 3.0 collective-permute-done.78
  661.5 7.8 convolution_convert_fusion.1
  670.3 5.2 attend.7
  675.6 25.2 %all_gather.15 = bf16[512,768]{0,1:T(8,128)(2,1)S(1)} all-gather(bf16[512,192]{0,1:T(8,128)(2,1)S(1)} %copy.77), channel_id=1, replica_groups=mesh['section'=2,'wide'=4,'narrow'=4] {'narrow'}, dimensions={1}, use_global_device_ids=true | all-gather | bytes 983040 | tf_op jit(solution)/shard_map/all_gather | solution.py:369
  707.0 4.3 collective-permute-done.89
  711.3 3.1 collective-permute-done.90
  720.6 2.9 collective-permute-done.94
  732.3 7.7 convolution_convert_fusion
  750.2 5.4 collective-permute-start.80
  755.6 67.2 %reduce-scatter.23.cloned.1.call-done = bf16[128,3072]{1,0:T(8,128)(2,1)} async-done(((bf16[512,3072]{1,0:T(8,128)(2,1)}), bf16[128,3072]{1,0:T(8,128)(2,1)}) %reduce-scatter.23.cloned.1.call-update) | async-done | bytes 786448 | tf_op jit(solution)/shard_map/reduce_scatter | solution.py:377
  825.8 5.2 collective-permute-start.98
  834.3 18.0 %collective-permute-done.111 = bf16[1,3,256,128]{3,2,0,1:T(8,128)(2,1)S(1)} collective-permute-done((bf16[1,3,256,128]{3,2,0,1:T(8,128)(2,1)S(1)}, bf16[1,3,256,128]{3,2,0,1:T(8,128)(2,1)S(1)}, u32[]{:S(2)}, u32[]{:S(2)}) %collective-permute-start.111) | collective-permute-done | bytes 196640 | tf_op jit(solution)/shard_map/ppermute | solution.py:167
  852.3 3.7 collective-permute-start.112
  859.9 5.7 collective-permute-done.112
  868.0 15.3 %collective-permute-done.113 = bf16[1,3,256,128]{3,2,0,1:T(8,128)(2,1)S(1)} collective-permute-done((bf16[1,3,256,128]{3,2,0,1:T(8,128)(2,1)S(1)}, bf16[1,3,256,128]{3,2,0,1:T(8,128)(2,1)S(1)}, u32[]{:S(2)}, u32[]{:S(2)}) %collective-permute-start.113) | collective-permute-done | bytes 196640 | tf_op jit(solution)/shard_map/ppermute | solution.py:167
  888.1 18.2 %collective-permute-done.100 = bf16[128,3072]{1,0:T(8,128)(2,1)S(1)} collective-permute-done((bf16[128,3072]{1,0:T(8,128)(2,1)S(1)}, bf16[128,3072]{1,0:T(8,128)(2,1)S(1)}, u32[]{:S(2)}, u32[]{:S(2)}) %collective-permute-start.100) | collective-permute-done | bytes 786464 | tf_op jit(solution)/shard_map/ppermute | solution.py:247
  908.6 14.5 %collective-permute-done.83 = bf16[128,3072]{1,0:T(8,128)(2,1)S(1)} collective-permute-done((bf16[128,3072]{1,0:T(8,128)(2,1)S(1)}, bf16[128,3072]{1,0:T(8,128)(2,1)S(1)}, u32[]{:S(2)}, u32[]{:S(2)}) %collective-permute-start.83) | collective-permute-done | bytes 786464 | tf_op jit(solution)/shard_map/ppermute | solution.py:247
  924.5 5.3 fusion.65
  931.8 6.2 collective-permute-done.101
  939.4 5.1 fusion.62
  (557 shorter events, 260.0 us)
Async XLA Ops:
  7.2 90.7 %reduce-scatter.25.cloned.1.call-start = ((), (), s32[]{:S(2)}) async-start(), calls=%async_computation.12 | async-start | bytes 2949120
  7.2 31.2 %collective-permute-start.7 = (bf16[768,2304]{1,0:T(8,128)(2,1)}, bf16[768,2304]{1,0:T(8,128)(2,1)}, u32[]{:S(2)}, u32[]{:S(2)}) collective-permute-start(bf16[768,2304]{1,0:T(8,128)(2,1)} %bitcast.940), channel_id=1, source_target_pairs={{0,16},{16,0},{1,17},{17,1},{2,18},{18,2},{3,19},{19,3},{4,20},{20... | collective-permute-start | bytes 10616840 | tf_op jit(solution)/shard_map/ppermute | solution.py:205
  10.2 12.8 %collective-permute-start.1 = (f32[2,128]{1,0:T(2,128)S(1)}, f32[2,128]{1,0:T(2,128)S(1)}, u32[]{:S(2)}, u32[]{:S(2)}) collective-permute-start(f32[2,128]{1,0:T(2,128)S(1)} %pad_maximum_fusion.8), channel_id=1, source_target_pairs={{0,1},{1,2},{2,3},{3,0},{4,5},{5,6},{6,7},{7,4},{8,9},{9,10},{10,1... | collective-permute-start | bytes 3080 | tf_op jit(solution)/shard_map/ppermute | solution.py:261
  12.8 10.1 %collective-permute-start.2 = (f32[2,128]{1,0:T(2,128)S(1)}, f32[2,128]{1,0:T(2,128)S(1)}, u32[]{:S(2)}, u32[]{:S(2)}) collective-permute-start(f32[2,128]{1,0:T(2,128)S(1)} %pad_maximum_fusion.8), channel_id=1, source_target_pairs={{0,2},{1,3},{2,0},{3,1},{4,6},{5,7},{6,4},{7,5},{8,10},{9,11},{10,... | collective-permute-start | bytes 3080 | tf_op jit(solution)/shard_map/ppermute | solution.py:261
  27.5 10.9 %collective-permute-start.5 = (bf16[128,768]{1,0:T(8,128)(2,1)S(1)}, bf16[128,768]{1,0:T(8,128)(2,1)S(1)}, u32[]{:S(2)}, u32[]{:S(2)}) collective-permute-start(bf16[128,768]{1,0:T(8,128)(2,1)S(1)} %fusion.144), channel_id=1, source_target_pairs={{0,8},{4,12},{8,0},{12,4},{1,9},{5,13},{9,1},{13,5},{2,10},{6,14},... | collective-permute-start | bytes 589832 | tf_op jit(solution)/shard_map/ppermute | solution.py:227
  29.1 9.4 collective-permute-start.6
  44.0 106.7 %reduce-scatter.27.cloned.1.call-start = ((), (), s32[]{:S(2)}) async-start(), calls=%async_computation.13 | async-start | bytes 2949120
  54.3 9.4 collective-permute-start.13
  69.3 236.2 %reduce-scatter.17.cloned.1.call-start = ((), (), s32[]{:S(2)}) async-start(), calls=%async_computation.8 | async-start | bytes 3932160 | tf_op jit(solution)/shard_map/reduce_scatter | solution.py:377
  70.0 9.2 collective-permute-start.8
  71.6 93.2 %collective-permute-start.15 = (bf16[1,3,256,128]{3,2,0,1:T(8,128)(2,1)}, bf16[1,3,256,128]{3,2,0,1:T(8,128)(2,1)}, u32[]{:S(2)}, u32[]{:S(2)}) collective-permute-start(bf16[1,3,256,128]{3,2,0,1:T(8,128)(2,1)} %get-tuple-element.144), channel_id=1, source_target_pairs={{0,1},{1,2},{2,3},{3,0},{4,5},{5,6},{6,7},{7,4},{8,9},{9,10},{10,1... | collective-permute-start | bytes 589832 | tf_op jit(solution)/shard_map/ppermute | solution.py:167
  71.8 96.0 %collective-permute-start.16 = (bf16[1,3,256,128]{3,2,0,1:T(8,128)(2,1)S(1)}, bf16[1,3,256,128]{3,2,0,1:T(8,128)(2,1)}, u32[]{:S(2)}, u32[]{:S(2)}) collective-permute-start(bf16[1,3,256,128]{3,2,0,1:T(8,128)(2,1)S(1)} %get-tuple-element.143), channel_id=1, source_target_pairs={{0,2},{1,3},{2,0},{3,1},{4,6},{5,7},{6,4},{7,5},{8,10},{9,11},{10,... | collective-permute-start | bytes 589832 | tf_op jit(solution)/shard_map/ppermute | solution.py:167
  72.6 126.2 %collective-permute-start.19 = (bf16[768,768]{1,0:T(8,128)(2,1)}, bf16[768,768]{1,0:T(8,128)(2,1)}, u32[]{:S(2)}, u32[]{:S(2)}) collective-permute-start(bf16[768,768]{1,0:T(8,128)(2,1)} %bitcast.941), channel_id=1, source_target_pairs={{0,16},{16,0},{1,17},{17,1},{2,18},{18,2},{3,19},{19,3},{4,20},{20... | collective-permute-start | bytes 3538952 | tf_op jit(solution)/shard_map/ppermute | solution.py:205
  72.6 149.7 %collective-permute-start.29 = (bf16[768,3072]{1,0:T(8,128)(2,1)}, bf16[768,3072]{1,0:T(8,128)(2,1)}, u32[]{:S(2)}, u32[]{:S(2)}) collective-permute-start(bf16[768,3072]{1,0:T(8,128)(2,1)} %bitcast.928), channel_id=1, source_target_pairs={{0,16},{16,0},{1,17},{17,1},{2,18},{18,2},{3,19},{19,3},{4,20},{20... | collective-permute-start | bytes 14155784 | tf_op jit(solution)/shard_map/ppermute | solution.py:205
  160.8 9.8 %collective-permute-start.18 = (bf16[3,1024,128]{2,1,0:T(8,128)(2,1)S(1)}, bf16[3,1024,128]{2,1,0:T(8,128)(2,1)}, u32[]{:S(2)}, u32[]{:S(2)}) collective-permute-start(bf16[3,1024,128]{2,1,0:T(8,128)(2,1)S(1)} %constant_dynamic-update-slice_fusion.9.own_ref), channel_id=1, source_target_pairs={{0,16},{1,17},{2,18},{3,19},{4,20},{5,21},{6,22},{7,23},{8,24},{9,... | collective-permute-start | bytes 2359304 | tf_op jit(solution)/shard_map/ppermute | solution.py:363
  232.6 165.2 %reduce-scatter.19.cloned.1.call-start = ((), (), s32[]{:S(2)}) async-start(), calls=%async_computation.9 | async-start | bytes 3932160 | tf_op jit(solution)/shard_map/reduce_scatter | solution.py:377
  305.4 245.2 %reduce-scatter.29.cloned.1.call-start = ((), (), s32[]{:S(2)}) async-start(), calls=%async_computation.14 | async-start | bytes 2949120
  305.4 115.1 %collective-permute-start.36 = (bf16[3072,768]{1,0:T(8,128)(2,1)}, bf16[3072,768]{1,0:T(8,128)(2,1)}, u32[]{:S(2)}, u32[]{:S(2)}) collective-permute-start(bf16[3072,768]{1,0:T(8,128)(2,1)} %bitcast.937), channel_id=1, source_target_pairs={{0,16},{16,0},{1,17},{17,1},{2,18},{18,2},{3,19},{19,3},{4,20},{20... | collective-permute-start | bytes 14155784 | tf_op jit(solution)/shard_map/ppermute | solution.py:205
  307.2 51.0 %collective-permute-start.31 = (bf16[128,3072]{1,0:T(8,128)(2,1)S(1)}, bf16[128,3072]{1,0:T(8,128)(2,1)S(1)}, u32[]{:S(2)}, u32[]{:S(2)}) collective-permute-start(bf16[128,3072]{1,0:T(8,128)(2,1)S(1)} %fusion.43), channel_id=1, source_target_pairs={{1,0},{2,1},{3,2},{5,4},{6,5},{7,6},{9,8},{10,9},{11,10},{13,12},{... | collective-permute-start | bytes 2359304 | tf_op jit(solution)/shard_map/ppermute | solution.py:247
  308.5 51.0 %collective-permute-start.30 = (bf16[128,3072]{1,0:T(8,128)(2,1)S(1)}, bf16[128,3072]{1,0:T(8,128)(2,1)}, u32[]{:S(2)}, u32[]{:S(2)}) collective-permute-start(bf16[128,3072]{1,0:T(8,128)(2,1)S(1)} %fusion.43), channel_id=1, source_target_pairs={{0,1},{1,2},{2,3},{4,5},{5,6},{6,7},{8,9},{9,10},{10,11},{12,13},{... | collective-permute-start | bytes 2359304 | tf_op jit(solution)/shard_map/ppermute | solution.py:246
  358.2 38.3 %collective-permute-start.32 = (bf16[128,3072]{1,0:T(8,128)(2,1)S(1)}, bf16[128,3072]{1,0:T(8,128)(2,1)}, u32[]{:S(2)}, u32[]{:S(2)}) collective-permute-start(bf16[128,3072]{1,0:T(8,128)(2,1)S(1)} %collective-permute-done.31), channel_id=1, source_target_pairs={{1,0},{2,1},{5,4},{6,5},{9,8},{10,9},{13,12},{14,13},{17,16},{18,1... | collective-permute-start | bytes 2359304 | tf_op jit(solution)/shard_map/ppermute | solution.py:247
  359.5 49.3 %collective-permute-start.34 = (bf16[128,3072]{1,0:T(8,128)(2,1)}, bf16[128,3072]{1,0:T(8,128)(2,1)}, u32[]{:S(2)}, u32[]{:S(2)}) collective-permute-start(bf16[128,3072]{1,0:T(8,128)(2,1)} %collective-permute-done.30), channel_id=1, source_target_pairs={{1,2},{2,3},{5,6},{6,7},{9,10},{10,11},{13,14},{14,15},{17,18},{18... | collective-permute-start | bytes 2359304 | tf_op jit(solution)/shard_map/ppermute | solution.py:246
  396.5 22.6 %collective-permute-start.33 = (bf16[128,3072]{1,0:T(8,128)(2,1)}, bf16[128,3072]{1,0:T(8,128)(2,1)}, u32[]{:S(2)}, u32[]{:S(2)}) collective-permute-start(bf16[128,3072]{1,0:T(8,128)(2,1)} %collective-permute-done.32), channel_id=1, source_target_pairs={{1,0},{5,4},{9,8},{13,12},{17,16},{21,20},{25,24},{29,28}} | collective-permute-start | bytes 2359304 | tf_op jit(solution)/shard_map/ppermute | solution.py:247
  400.4 34.3 %collective-permute-start.50 = (bf16[128,3072]{1,0:T(8,128)(2,1)}, bf16[128,3072]{1,0:T(8,128)(2,1)S(1)}, u32[]{:S(2)}, u32[]{:S(2)}) collective-permute-start(bf16[128,3072]{1,0:T(8,128)(2,1)} %fusion.49), channel_id=1, source_target_pairs={{1,0},{2,1},{3,2},{5,4},{6,5},{7,6},{9,8},{10,9},{11,10},{13,12},{... | collective-permute-start | bytes 2359304 | tf_op jit(solution)/shard_map/ppermute | solution.py:247
  401.8 34.2 %collective-permute-start.49 = (bf16[128,3072]{1,0:T(8,128)(2,1)}, bf16[128,3072]{1,0:T(8,128)(2,1)}, u32[]{:S(2)}, u32[]{:S(2)}) collective-permute-start(bf16[128,3072]{1,0:T(8,128)(2,1)} %fusion.49), channel_id=1, source_target_pairs={{0,1},{1,2},{2,3},{4,5},{5,6},{6,7},{8,9},{9,10},{10,11},{12,13},{... | collective-permute-start | bytes 2359304 | tf_op jit(solution)/shard_map/ppermute | solution.py:246
  408.8 11.6 %collective-permute-start.35 = (bf16[128,3072]{1,0:T(8,128)(2,1)}, bf16[128,3072]{1,0:T(8,128)(2,1)S(1)}, u32[]{:S(2)}, u32[]{:S(2)}) collective-permute-start(bf16[128,3072]{1,0:T(8,128)(2,1)} %collective-permute-done.34), channel_id=1, source_target_pairs={{2,3},{6,7},{10,11},{14,15},{18,19},{22,23},{26,27},{30,31}} | collective-permute-start | bytes 2359304 | tf_op jit(solution)/shard_map/ppermute | solution.py:246
  427.3 10.2 %collective-permute-start.37 = (bf16[128,768]{1,0:T(8,128)(2,1)}, bf16[128,768]{1,0:T(8,128)(2,1)}, u32[]{:S(2)}, u32[]{:S(2)}) collective-permute-start(bf16[128,768]{1,0:T(8,128)(2,1)} %get-tuple-element.130), channel_id=1, source_target_pairs={{0,4},{4,0},{8,12},{12,8},{1,5},{5,1},{9,13},{13,9},{2,6},{6,2},{1... | collective-permute-start | bytes 589832 | tf_op jit(solution)/shard_map/ppermute | solution.py:234
  428.0 9.6 collective-permute-start.38
  434.7 32.1 %collective-permute-start.51 = (bf16[128,3072]{1,0:T(8,128)(2,1)S(1)}, bf16[128,3072]{1,0:T(8,128)(2,1)}, u32[]{:S(2)}, u32[]{:S(2)}) collective-permute-start(bf16[128,3072]{1,0:T(8,128)(2,1)S(1)} %collective-permute-done.50), channel_id=1, source_target_pairs={{1,0},{2,1},{5,4},{6,5},{9,8},{10,9},{13,12},{14,13},{17,16},{18,1... | collective-permute-start | bytes 2359304 | tf_op jit(solution)/shard_map/ppermute | solution.py:247
  436.0 39.9 %collective-permute-start.53 = (bf16[128,3072]{1,0:T(8,128)(2,1)}, bf16[128,3072]{1,0:T(8,128)(2,1)}, u32[]{:S(2)}, u32[]{:S(2)}) collective-permute-start(bf16[128,3072]{1,0:T(8,128)(2,1)} %collective-permute-done.49), channel_id=1, source_target_pairs={{1,2},{2,3},{5,6},{6,7},{9,10},{10,11},{13,14},{14,15},{17,18},{18... | collective-permute-start | bytes 2359304 | tf_op jit(solution)/shard_map/ppermute | solution.py:246
  439.7 28.4 %collective-permute-start.58 = (f32[2,128]{1,0:T(2,128)S(1)}, f32[2,128]{1,0:T(2,128)S(1)}, u32[]{:S(2)}, u32[]{:S(2)}) collective-permute-start(f32[2,128]{1,0:T(2,128)S(1)} %pad_maximum_fusion.13), channel_id=1, source_target_pairs={{0,1},{1,2},{2,3},{3,0},{4,5},{5,6},{6,7},{7,4},{8,9},{9,10},{10,1... | collective-permute-start | bytes 3080 | tf_op jit(solution)/shard_map/ppermute | solution.py:261
  461.0 10.8 %collective-permute-start.59 = (f32[2,128]{1,0:T(2,128)S(1)}, f32[2,128]{1,0:T(2,128)S(1)}, u32[]{:S(2)}, u32[]{:S(2)}) collective-permute-start(f32[2,128]{1,0:T(2,128)S(1)} %pad_maximum_fusion.13), channel_id=1, source_target_pairs={{0,2},{1,3},{2,0},{3,1},{4,6},{5,7},{6,4},{7,5},{8,10},{9,11},{10,... | collective-permute-start | bytes 3080 | tf_op jit(solution)/shard_map/ppermute | solution.py:261
  466.8 23.5 %collective-permute-start.52 = (bf16[128,3072]{1,0:T(8,128)(2,1)}, bf16[128,3072]{1,0:T(8,128)(2,1)}, u32[]{:S(2)}, u32[]{:S(2)}) collective-permute-start(bf16[128,3072]{1,0:T(8,128)(2,1)} %collective-permute-done.51), channel_id=1, source_target_pairs={{1,0},{5,4},{9,8},{13,12},{17,16},{21,20},{25,24},{29,28}} | collective-permute-start | bytes 2359304 | tf_op jit(solution)/shard_map/ppermute | solution.py:247
  478.0 13.6 %collective-permute-start.54 = (bf16[128,3072]{1,0:T(8,128)(2,1)}, bf16[128,3072]{1,0:T(8,128)(2,1)}, u32[]{:S(2)}, u32[]{:S(2)}) collective-permute-start(bf16[128,3072]{1,0:T(8,128)(2,1)} %collective-permute-done.53), channel_id=1, source_target_pairs={{2,3},{6,7},{10,11},{14,15},{18,19},{22,23},{26,27},{30,31}} | collective-permute-start | bytes 2359304 | tf_op jit(solution)/shard_map/ppermute | solution.py:246
  487.2 108.5 %reduce-scatter.31.cloned.1.call-start = ((), (), s32[]{:S(2)}) async-start(), calls=%async_computation.15 | async-start | bytes 2949120
  497.4 10.1 %collective-permute-start.56 = (bf16[128,768]{1,0:T(8,128)(2,1)S(1)}, bf16[128,768]{1,0:T(8,128)(2,1)S(1)}, u32[]{:S(2)}, u32[]{:S(2)}) collective-permute-start(bf16[128,768]{1,0:T(8,128)(2,1)S(1)} %get-tuple-element.138), channel_id=1, source_target_pairs={{0,8},{4,12},{8,0},{12,4},{1,9},{5,13},{9,1},{13,5},{2,10},{6,14},... | collective-permute-start | bytes 589832 | tf_op jit(solution)/shard_map/ppermute | solution.py:234
  508.0 20.6 %collective-permute-start.64 = (f32[2,128]{1,0:T(2,128)S(1)}, f32[2,128]{1,0:T(2,128)S(1)}, u32[]{:S(2)}, u32[]{:S(2)}) collective-permute-start(f32[2,128]{1,0:T(2,128)S(1)} %pad_maximum_fusion.15), channel_id=1, source_target_pairs={{0,1},{1,2},{2,3},{3,0},{4,5},{5,6},{6,7},{7,4},{8,9},{9,10},{10,1... | collective-permute-start | bytes 3080 | tf_op jit(solution)/shard_map/ppermute | solution.py:261
  508.1 21.1 %collective-permute-start.65 = (f32[2,128]{1,0:T(2,128)S(1)}, f32[2,128]{1,0:T(2,128)S(1)}, u32[]{:S(2)}, u32[]{:S(2)}) collective-permute-start(f32[2,128]{1,0:T(2,128)S(1)} %pad_maximum_fusion.15), channel_id=1, source_target_pairs={{0,2},{1,3},{2,0},{3,1},{4,6},{5,7},{6,4},{7,5},{8,10},{9,11},{10,... | collective-permute-start | bytes 3080 | tf_op jit(solution)/shard_map/ppermute | solution.py:261
  549.8 196.6 %reduce-scatter.21.cloned.1.call-start = ((), (), s32[]{:S(2)}) async-start(), calls=%async_computation.10 | async-start | bytes 3932160 | tf_op jit(solution)/shard_map/reduce_scatter | solution.py:377
  636.3 9.0 collective-permute-start.72
  669.3 153.5 %reduce-scatter.23.cloned.1.call-start = ((), (), s32[]{:S(2)}) async-start(), calls=%async_computation.11 | async-start | bytes 3932160 | tf_op jit(solution)/shard_map/reduce_scatter | solution.py:377
  704.6 9.8 %collective-permute-start.90 = (bf16[128,768]{1,0:T(8,128)(2,1)S(1)}, bf16[128,768]{1,0:T(8,128)(2,1)S(1)}, u32[]{:S(2)}, u32[]{:S(2)}) collective-permute-start(bf16[128,768]{1,0:T(8,128)(2,1)S(1)} %get-tuple-element.129), channel_id=1, source_target_pairs={{0,8},{4,12},{8,0},{12,4},{1,9},{5,13},{9,1},{13,5},{2,10},{6,14},... | collective-permute-start | bytes 589832 | tf_op jit(solution)/shard_map/ppermute | solution.py:234
  742.2 82.3 %collective-permute-start.108 = (bf16[1,3,256,128]{3,2,0,1:T(8,128)(2,1)}, bf16[1,3,256,128]{3,2,0,1:T(8,128)(2,1)}, u32[]{:S(2)}, u32[]{:S(2)}) collective-permute-start(bf16[1,3,256,128]{3,2,0,1:T(8,128)(2,1)} %get-tuple-element.112), channel_id=1, source_target_pairs={{0,1},{1,2},{2,3},{3,0},{4,5},{5,6},{6,7},{7,4},{8,9},{9,10},{10,1... | collective-permute-start | bytes 589832 | tf_op jit(solution)/shard_map/ppermute | solution.py:167
  743.5 82.3 %collective-permute-start.109 = (bf16[1,3,256,128]{3,2,0,1:T(8,128)(2,1)S(1)}, bf16[1,3,256,128]{3,2,0,1:T(8,128)(2,1)}, u32[]{:S(2)}, u32[]{:S(2)}) collective-permute-start(bf16[1,3,256,128]{3,2,0,1:T(8,128)(2,1)S(1)} %get-tuple-element.111), channel_id=1, source_target_pairs={{0,2},{1,3},{2,0},{3,1},{4,6},{5,7},{6,4},{7,5},{8,10},{9,11},{10,... | collective-permute-start | bytes 589832 | tf_op jit(solution)/shard_map/ppermute | solution.py:167
  744.1 87.2 %collective-permute-start.110 = (bf16[1,3,256,128]{3,2,0,1:T(8,128)(2,1)S(1)}, bf16[1,3,256,128]{3,2,0,1:T(8,128)(2,1)}, u32[]{:S(2)}, u32[]{:S(2)}) collective-permute-start(bf16[1,3,256,128]{3,2,0,1:T(8,128)(2,1)S(1)} %get-tuple-element.110), channel_id=1, source_target_pairs={{0,3},{1,0},{2,1},{3,2},{4,7},{5,4},{6,5},{7,6},{8,11},{9,8},{10,9... | collective-permute-start | bytes 589832 | tf_op jit(solution)/shard_map/ppermute | solution.py:167
  748.9 107.0 %collective-permute-start.81 = (bf16[128,3072]{1,0:T(8,128)(2,1)}, bf16[128,3072]{1,0:T(8,128)(2,1)}, u32[]{:S(2)}, u32[]{:S(2)}) collective-permute-start(bf16[128,3072]{1,0:T(8,128)(2,1)} %fusion.55), channel_id=1, source_target_pairs={{1,0},{2,1},{3,2},{5,4},{6,5},{7,6},{9,8},{10,9},{11,10},{13,12},{... | collective-permute-start | bytes 2359304 | tf_op jit(solution)/shard_map/ppermute | solution.py:247
  750.2 107.0 %collective-permute-start.80 = (bf16[128,3072]{1,0:T(8,128)(2,1)}, bf16[128,3072]{1,0:T(8,128)(2,1)}, u32[]{:S(2)}, u32[]{:S(2)}) collective-permute-start(bf16[128,3072]{1,0:T(8,128)(2,1)} %fusion.55), channel_id=1, source_target_pairs={{0,1},{1,2},{2,3},{4,5},{5,6},{6,7},{8,9},{9,10},{10,11},{12,13},{... | collective-permute-start | bytes 2359304 | tf_op jit(solution)/shard_map/ppermute | solution.py:246
  824.5 58.8 %collective-permute-start.99 = (bf16[128,3072]{1,0:T(8,128)(2,1)S(1)}, bf16[128,3072]{1,0:T(8,128)(2,1)S(1)}, u32[]{:S(2)}, u32[]{:S(2)}) collective-permute-start(bf16[128,3072]{1,0:T(8,128)(2,1)S(1)} %fusion.61), channel_id=1, source_target_pairs={{1,0},{2,1},{3,2},{5,4},{6,5},{7,6},{9,8},{10,9},{11,10},{13,12},{... | collective-permute-start | bytes 2359304 | tf_op jit(solution)/shard_map/ppermute | solution.py:247
  825.8 58.8 %collective-permute-start.98 = (bf16[128,3072]{1,0:T(8,128)(2,1)S(1)}, bf16[128,3072]{1,0:T(8,128)(2,1)S(1)}, u32[]{:S(2)}, u32[]{:S(2)}) collective-permute-start(bf16[128,3072]{1,0:T(8,128)(2,1)S(1)} %fusion.61), channel_id=1, source_target_pairs={{0,1},{1,2},{2,3},{4,5},{5,6},{6,7},{8,9},{9,10},{10,11},{12,13},{... | collective-permute-start | bytes 2359304 | tf_op jit(solution)/shard_map/ppermute | solution.py:246
  831.3 21.0 %collective-permute-start.111 = (bf16[1,3,256,128]{3,2,0,1:T(8,128)(2,1)S(1)}, bf16[1,3,256,128]{3,2,0,1:T(8,128)(2,1)S(1)}, u32[]{:S(2)}, u32[]{:S(2)}) collective-permute-start(bf16[1,3,256,128]{3,2,0,1:T(8,128)(2,1)S(1)} %get-tuple-element.116), channel_id=1, source_target_pairs={{0,1},{1,2},{2,3},{3,0},{4,5},{5,6},{6,7},{7,4},{8,9},{9,10},{10,1... | collective-permute-start | bytes 589832 | tf_op jit(solution)/shard_map/ppermute | solution.py:167
  852.3 13.3 %collective-permute-start.112 = (bf16[1,3,256,128]{3,2,0,1:T(8,128)(2,1)S(1)}, bf16[1,3,256,128]{3,2,0,1:T(8,128)(2,1)S(1)}, u32[]{:S(2)}, u32[]{:S(2)}) collective-permute-start(bf16[1,3,256,128]{3,2,0,1:T(8,128)(2,1)S(1)} %get-tuple-element.115), channel_id=1, source_target_pairs={{0,2},{1,3},{2,0},{3,1},{4,6},{5,7},{6,4},{7,5},{8,10},{9,11},{10,... | collective-permute-start | bytes 589832 | tf_op jit(solution)/shard_map/ppermute | solution.py:167
  855.9 29.7 %collective-permute-start.82 = (bf16[128,3072]{1,0:T(8,128)(2,1)}, bf16[128,3072]{1,0:T(8,128)(2,1)S(1)}, u32[]{:S(2)}, u32[]{:S(2)}) collective-permute-start(bf16[128,3072]{1,0:T(8,128)(2,1)} %collective-permute-done.81), channel_id=1, source_target_pairs={{1,0},{2,1},{5,4},{6,5},{9,8},{10,9},{13,12},{14,13},{17,16},{18,1... | collective-permute-start | bytes 2359304 | tf_op jit(solution)/shard_map/ppermute | solution.py:247
  857.2 30.0 %collective-permute-start.84 = (bf16[128,3072]{1,0:T(8,128)(2,1)}, bf16[128,3072]{1,0:T(8,128)(2,1)S(1)}, u32[]{:S(2)}, u32[]{:S(2)}) collective-permute-start(bf16[128,3072]{1,0:T(8,128)(2,1)} %collective-permute-done.80), channel_id=1, source_target_pairs={{1,2},{2,3},{5,6},{6,7},{9,10},{10,11},{13,14},{14,15},{17,18},{18... | collective-permute-start | bytes 2359304 | tf_op jit(solution)/shard_map/ppermute | solution.py:246
  865.6 17.6 %collective-permute-start.113 = (bf16[1,3,256,128]{3,2,0,1:T(8,128)(2,1)S(1)}, bf16[1,3,256,128]{3,2,0,1:T(8,128)(2,1)S(1)}, u32[]{:S(2)}, u32[]{:S(2)}) collective-permute-start(bf16[1,3,256,128]{3,2,0,1:T(8,128)(2,1)S(1)} %get-tuple-element.114), channel_id=1, source_target_pairs={{0,3},{1,0},{2,1},{3,2},{4,7},{5,4},{6,5},{7,6},{8,11},{9,8},{10,9... | collective-permute-start | bytes 589832 | tf_op jit(solution)/shard_map/ppermute | solution.py:167
  883.3 23.0 %collective-permute-start.100 = (bf16[128,3072]{1,0:T(8,128)(2,1)S(1)}, bf16[128,3072]{1,0:T(8,128)(2,1)S(1)}, u32[]{:S(2)}, u32[]{:S(2)}) collective-permute-start(bf16[128,3072]{1,0:T(8,128)(2,1)S(1)} %collective-permute-done.99), channel_id=1, source_target_pairs={{1,0},{2,1},{5,4},{6,5},{9,8},{10,9},{13,12},{14,13},{17,16},{18,1... | collective-permute-start | bytes 2359304 | tf_op jit(solution)/shard_map/ppermute | solution.py:247
  884.6 22.9 %collective-permute-start.102 = (bf16[128,3072]{1,0:T(8,128)(2,1)S(1)}, bf16[128,3072]{1,0:T(8,128)(2,1)S(1)}, u32[]{:S(2)}, u32[]{:S(2)}) collective-permute-start(bf16[128,3072]{1,0:T(8,128)(2,1)S(1)} %collective-permute-done.98), channel_id=1, source_target_pairs={{1,2},{2,3},{5,6},{6,7},{9,10},{10,11},{13,14},{14,15},{17,18},{18... | collective-permute-start | bytes 2359304 | tf_op jit(solution)/shard_map/ppermute | solution.py:246
  885.5 68.4 %collective-permute-start.114 = (bf16[256,12,128]{2,0,1:T(8,128)(2,1)S(1)}, bf16[256,12,128]{2,0,1:T(8,128)(2,1)S(1)}, u32[]{:S(2)}, u32[]{:S(2)}) collective-permute-start(bf16[256,12,128]{2,0,1:T(8,128)(2,1)S(1)} %bitcast.875), channel_id=1, source_target_pairs={{0,16},{16,0},{1,17},{17,1},{2,18},{18,2},{3,19},{19,3},{4,20},{20... | collective-permute-start | bytes 2359304 | tf_op jit(solution)/shard_map/ppermute | solution.py:205
  885.7 37.4 %collective-permute-start.83 = (bf16[128,3072]{1,0:T(8,128)(2,1)S(1)}, bf16[128,3072]{1,0:T(8,128)(2,1)S(1)}, u32[]{:S(2)}, u32[]{:S(2)}) collective-permute-start(bf16[128,3072]{1,0:T(8,128)(2,1)S(1)} %collective-permute-done.82), channel_id=1, source_target_pairs={{1,0},{5,4},{9,8},{13,12},{17,16},{21,20},{25,24},{29,28}} | collective-permute-start | bytes 2359304 | tf_op jit(solution)/shard_map/ppermute | solution.py:247
  887.4 35.8 %collective-permute-start.85 = (bf16[128,3072]{1,0:T(8,128)(2,1)S(1)}, bf16[128,3072]{1,0:T(8,128)(2,1)S(1)}, u32[]{:S(2)}, u32[]{:S(2)}) collective-permute-start(bf16[128,3072]{1,0:T(8,128)(2,1)S(1)} %collective-permute-done.84), channel_id=1, source_target_pairs={{2,3},{6,7},{10,11},{14,15},{18,19},{22,23},{26,27},{30,31}} | collective-permute-start | bytes 2359304 | tf_op jit(solution)/shard_map/ppermute | solution.py:246
  906.3 31.7 %collective-permute-start.101 = (bf16[128,3072]{1,0:T(8,128)(2,1)S(1)}, bf16[128,3072]{1,0:T(8,128)(2,1)S(1)}, u32[]{:S(2)}, u32[]{:S(2)}) collective-permute-start(bf16[128,3072]{1,0:T(8,128)(2,1)S(1)} %collective-permute-done.100), channel_id=1, source_target_pairs={{1,0},{5,4},{9,8},{13,12},{17,16},{21,20},{25,24},{29,28}} | collective-permute-start | bytes 2359304 | tf_op jit(solution)/shard_map/ppermute | solution.py:247
  907.7 31.6 %collective-permute-start.103 = (bf16[128,3072]{1,0:T(8,128)(2,1)S(1)}, bf16[128,3072]{1,0:T(8,128)(2,1)S(1)}, u32[]{:S(2)}, u32[]{:S(2)}) collective-permute-start(bf16[128,3072]{1,0:T(8,128)(2,1)S(1)} %collective-permute-done.102), channel_id=1, source_target_pairs={{2,3},{6,7},{10,11},{14,15},{18,19},{22,23},{26,27},{30,31}} | collective-permute-start | bytes 2359304 | tf_op jit(solution)/shard_map/ppermute | solution.py:246
  929.9 15.9 %collective-permute-start.86 = (bf16[128,768]{1,0:T(8,128)(2,1)S(1)}, bf16[128,768]{1,0:T(8,128)(2,1)S(1)}, u32[]{:S(2)}, u32[]{:S(2)}) collective-permute-start(bf16[128,768]{1,0:T(8,128)(2,1)S(1)} %get-tuple-element.118), channel_id=1, source_target_pairs={{0,4},{4,0},{8,12},{12,8},{1,5},{5,1},{9,13},{13,9},{2,6},{6,2},{1... | collective-permute-start | bytes 589832 | tf_op jit(solution)/shard_map/ppermute | solution.py:234
  930.8 16.1 %collective-permute-start.87 = (bf16[128,768]{1,0:T(8,128)(2,1)S(1)}, bf16[128,768]{1,0:T(8,128)(2,1)S(1)}, u32[]{:S(2)}, u32[]{:S(2)}) collective-permute-start(bf16[128,768]{1,0:T(8,128)(2,1)S(1)} %get-tuple-element.120), channel_id=1, source_target_pairs={{0,8},{4,12},{8,0},{12,4},{1,9},{5,13},{9,1},{13,5},{2,10},{6,14},... | collective-permute-start | bytes 589832 | tf_op jit(solution)/shard_map/ppermute | solution.py:234
  937.9 10.2 %collective-permute-start.88 = (bf16[128,768]{1,0:T(8,128)(2,1)S(1)}, bf16[128,768]{1,0:T(8,128)(2,1)S(1)}, u32[]{:S(2)}, u32[]{:S(2)}) collective-permute-start(bf16[128,768]{1,0:T(8,128)(2,1)S(1)} %get-tuple-element.119), channel_id=1, source_target_pairs={{0,12},{4,8},{8,4},{12,0},{1,13},{5,9},{9,5},{13,1},{2,14},{6,10},... | collective-permute-start | bytes 589832 | tf_op jit(solution)/shard_map/ppermute | solution.py:234
  (136 other events, 1588.9 us)
Sparse Core Ops, SparseCore 0:
  44.1 53.6 reduce-scatter.24
  100.1 50.4 reduce-scatter.26
  232.7 71.6 reduce-scatter.16
  306.6 83.2 reduce-scatter.18
  487.4 51.3 reduce-scatter.28
  549.9 45.7 reduce-scatter.30
  669.4 74.8 reduce-scatter.20
  746.6 76.2 reduce-scatter.22

commit v4 on v3

--- a/solution.py
+++ b/solution.py
@@ -250,6 +250,13 @@
     ]
 
 
+def gather_direct(block):
+    n = lax.axis_size("narrow")
+    return [block] + [
+        lax.ppermute(block, "narrow", [(i, (i + step) % n) for i in range(n)]) for step in range(1, n)
+    ]
+
+
 def line_norm(values, model_width):
     n = lax.axis_size("narrow")
     width = values.shape[1]
@@ -328,6 +335,13 @@
     blocks = stale_cache[0, 1].reshape(rows_b, n_narrow, heads, pair).transpose(1, 2, 0, 3)
     stale = exchange(blocks, "narrow").transpose(1, 0, 2, 3).reshape(heads, total_rows, pair)
 
+    def turned(block, axis):
+        size = block.shape[axis] // n_narrow
+        starts = [(narrow_idx + n_narrow - step) % n_narrow * size for step in range(n_narrow)]
+        return [lax.dynamic_slice_in_dim(block, start, size, axis) for start in starts]
+
+    out_weights = [jnp.concatenate(turned(weight, 0), axis=0) for weight in out_weights]
+
     def to_rows(fresh):
         blocks = [f.reshape(heads, n_wide, part, pair) for f in fresh]
         per_narrow = []
@@ -366,26 +380,29 @@
         after = []
         for h in range(halves):
             attended = attend(queries[h], own, other, own_mask, other_mask, head_dim)
-            attended = lax.all_gather(attended, "narrow", axis=1, tiled=True)
+            attended = jnp.concatenate(gather_direct(attended), axis=1)
             terms = jnp.dot(attended, out_weights[layer], preferred_element_type=F32).astype(BF)
             projected = scatter_wide([terms[r * part : (r + 1) * part] for r in range(n_wide)])
             after.append(x_in[h] + pick(table[0], kinds_h[h], 2) * projected)
-        inner = []
+        up = []
         for h in range(halves):
             entry = modulate(line_norm(after[h], model_width), table[1], kinds_h[h])
             terms = jnp.dot(gather_wide(entry), up_weights[layer], preferred_element_type=F32)
-            up = lax.psum_scatter(terms.astype(BF), "narrow", scatter_dimension=0, tiled=True)
-            inner.append(jax.nn.gelu(up.astype(F32), approximate=True).astype(BF))
+            up.append(lax.psum_scatter(terms.astype(BF), "narrow", scatter_dimension=0, tiled=True))
+        first = gather_line(jax.nn.gelu(up[0].astype(F32), approximate=True).astype(BF))
+        first, last = lax.optimization_barrier((first, up[1]))
+        last = jax.nn.gelu(last.astype(F32), approximate=True).astype(BF)
+        gathered = [
+            jnp.concatenate(first, axis=0),
+            lax.all_gather(last, "narrow", axis=0, tiled=True),
+        ]
         layer_in = []
         for h in range(halves):
-            gathered = jnp.concatenate(gather_line(inner[h]), axis=0)
-            terms = jnp.dot(gathered, down_weights[layer], preferred_element_type=F32).astype(BF)
-            size = chunk // n_narrow
-            ordered = [
-                lax.dynamic_slice_in_dim(terms, (narrow_idx + n_narrow - r) % n_narrow * size, size, 0)
-                for r in range(n_narrow)
-            ]
-            down = scatter_wide(ordered)
+            terms = jnp.dot(gathered[h], down_weights[layer], preferred_element_type=F32).astype(BF)
+            if h == 0:
+                down = scatter_wide(turned(terms, 0))
+            else:
+                down = scatter_wide([terms[r * part : (r + 1) * part] for r in range(n_wide)])
             layer_in.append((after[h] + pick(table[1], kinds_h[h], 2) * down).astype(BF))
         results.append(jnp.concatenate(layer_in, axis=0))
     return (by_layer(results, lead), by_layer(caches, lead))

time: 972 us -> 1000 us (1.029)
  waiting for transfers between devices: 468 us -> 600 us
  blocking collectives: 90.9 us -> 0 us
    all_gather x4 -> x0, blocking collectives: 90.9 us -> none  [in_halves(): attended = lax.all_gather(attended, 'narrow', axis=1, tiled=True)]
    ppermute x0 -> x12, waiting for transfers between devices: none -> 84.3 us  [gather_direct(): lax.ppermute(block, 'narrow', [(i, (i + step) % n) for i in range(n)])]
    reduce_scatter x4, waiting for transfers between devices: 67.2 us -> 0.04 us  [in_halves(): lax.psum_scatter(terms.astype(BF), 'narrow', scatter_dimension=0, tiled=T...]
    ppermute x12 -> x6, waiting for transfers between devices: 0.03 us -> 56.2 us  [gather_line(): from_left.append(lax.ppermute(from_left[-1], 'narrow', right))]
    all_gather x0 -> x2, waiting for transfers between devices: none -> 32.7 us  [in_halves(): lax.all_gather(last, 'narrow', axis=0, tiled=True)]
    ppermute x12 -> x6, starting transfers between devices: 32 us -> 10 us  [gather_line(): from_left.append(lax.ppermute(from_left[-1], 'narrow', right))]
    ppermute x0 -> x12, starting transfers between devices: none -> 19.2 us  [gather_direct(): lax.ppermute(block, 'narrow', [(i, (i + step) % n) for i in range(n)])]
    ppermute x24, waiting for transfers between devices: 38.1 us -> 51 us  [scatter_wide(): total += lax.ppermute(terms[step], 'wide', wide_pairs(step)).astype(F32)]
  transfers between devices with their start and end apart: 123 -> 125, of which waited for: 69 -> 76; matrix products, arithmetic and copies ran while one was open for 12% -> 11% of each run, Pallas kernels for 2% -> 3%
where the time goes in v4:
time: 1000 us; the launch traced here: 995 us
  waiting for transfers between devices  600 us (60%)
  starting transfers between devices  193 us (19%)
  matrix products  82.1 us (8%)
  other arithmetic  41.4 us (4%)
  Pallas kernels  36.8 us (4%)
  local copies, waits for them, and re-layouts  24.7 us (2%)
  between operations  16.7 us (2%)
    ppermute x6, waiting for transfers between devices, gather_line(): from_right.append(lax.ppermute(from_right[-1], 'narrow', left))  144 us
    unnamed x14, waiting for transfers between devices  117 us
    ppermute x12, waiting for transfers between devices, gather_direct(): lax.ppermute(block, 'narrow', [(i, (i + step) % n) for i in range(n)])  84.3 us
    ppermute x24, starting transfers between devices, line_norm(): lax.ppermute(own, 'narrow', [(i, (i + step) % n) for i in range(n)])  78.9 us
    ppermute x6, waiting for transfers between devices, gather_line(): from_left.append(lax.ppermute(from_left[-1], 'narrow', right))  56.2 us
    ppermute x24, waiting for transfers between devices, gather_wide(): lax.ppermute(block, 'wide', wide_pairs(step))  54.5 us
    ppermute x24, waiting for transfers between devices, scatter_wide(): total += lax.ppermute(terms[step], 'wide', wide_pairs(step)).astype(F32)  51 us
    ppermute x9, waiting for transfers between devices, exchange(): block = lax.ppermute(block, axis, [(i, (i + step) % n) for i in range(n)])  37.2 us
  transfers between devices with their start and end apart: 125, of which 76 were waited for; matrix products, arithmetic and copies ran while one was open for 11% of the time, Pallas kernels for 3%

profile of v4, /device:TPU:0, one launch (start us, length us, event | category | flops | bytes accessed | tf_op | source)
XLA Modules:
  0.0 994.9 jit_solution(17505105626500867335)
XLA Ops:
  17.6 5.1 fusion.56
  29.5 4.3 collective-permute-done.4
  33.8 4.6 collective-permute-done.5
  38.4 5.5 fusion.2
  48.6 4.0 collective-permute-done.9
  56.6 4.1 collective-permute-done.12
  63.7 5.6 fusion.3
  80.0 17.8 %reduce-scatter.25.cloned.1.call-done = bf16[576,512]{1,0:T(8,128)(2,1)} async-done(((bf16[2304,512]{1,0:T(8,128)(2,1)}), bf16[576,512]{1,0:T(8,128)(2,1)}) %reduce-scatter.25.cloned.1.call-update) | async-done | bytes 589840
  99.2 51.4 %reduce-scatter.27.cloned.1.call-done = bf16[576,512]{1,0:T(8,128)(2,1)} async-done(((bf16[2304,512]{1,0:T(8,128)(2,1)}), bf16[576,512]{1,0:T(8,128)(2,1)}) %reduce-scatter.27.cloned.1.call-update) | async-done | bytes 589840
  152.0 4.0 prepare.4
  156.0 4.0 prepare.5
  170.9 5.2 attend.4
  187.3 9.1 collective-permute-done.20
  201.0 4.3 collective-permute-done.23
  205.3 4.4 collective-permute-done.24
  211.2 6.2 collective-permute-start.26
  232.0 5.4 convolution_convert_fusion.5
  238.6 5.2 attend.5
  249.0 11.2 %collective-permute-done.39 = bf16[512,192]{1,0:T(8,128)(2,1)S(1)} collective-permute-done((bf16[512,192]{1,0:T(8,128)(2,1)S(1)}, bf16[512,192]{1,0:T(8,128)(2,1)S(1)}, u32[]{:S(2)}, u32[]{:S(2)}) %collective-permute-start.39) | collective-permute-done | bytes 196640 | tf_op jit(solution)/shard_map/ppermute | solution.py:256
  260.2 17.7 %collective-permute-done.40 = bf16[512,192]{1,0:T(8,128)(2,1)S(1)} collective-permute-done((bf16[512,192]{1,0:T(8,128)(2,1)S(1)}, bf16[512,192]{1,0:T(8,128)(2,1)S(1)}, u32[]{:S(2)}, u32[]{:S(2)}) %collective-permute-start.40) | collective-permute-done | bytes 196640 | tf_op jit(solution)/shard_map/ppermute | solution.py:256
  283.1 4.3 collective-permute-done.42
  291.9 20.0 %collective-permute-start.45 = (f32[2,128]{1,0:T(2,128)S(1)}, f32[2,128]{1,0:T(2,128)S(1)}, u32[]{:S(2)}, u32[]{:S(2)}) collective-permute-start(f32[2,128]{1,0:T(2,128)S(1)} %pad_maximum_fusion.18), channel_id=1, source_target_pairs={{0,1},{1,2},{2,3},{3,0},{4,5},{5,6},{6,7},{7,4},{8,9},{9,10},{10,1... | collective-permute-start | bytes 3080 | tf_op jit(solution)/shard_map/ppermute | solution.py:268
  327.3 4.7 convolution_convert_fusion.4
  338.1 31.5 %collective-permute-done.33 = bf16[128,3072]{1,0:T(8,128)(2,1)S(1)} collective-permute-done((bf16[128,3072]{1,0:T(8,128)(2,1)S(1)}, bf16[128,3072]{1,0:T(8,128)(2,1)S(1)}, u32[]{:S(2)}, u32[]{:S(2)}) %collective-permute-start.33) | collective-permute-done | bytes 786464 | tf_op jit(solution)/shard_map/ppermute | solution.py:246
  372.1 19.7 %collective-permute-done.34 = bf16[128,3072]{1,0:T(8,128)(2,1)S(1)} collective-permute-done((bf16[128,3072]{1,0:T(8,128)(2,1)S(1)}, bf16[128,3072]{1,0:T(8,128)(2,1)S(1)}, u32[]{:S(2)}, u32[]{:S(2)}) %collective-permute-start.34) | collective-permute-done | bytes 786464 | tf_op jit(solution)/shard_map/ppermute | solution.py:247
  394.7 29.5 %collective-permute-done.35 = bf16[128,3072]{1,0:T(8,128)(2,1)} collective-permute-done((bf16[128,3072]{1,0:T(8,128)(2,1)S(1)}, bf16[128,3072]{1,0:T(8,128)(2,1)}, u32[]{:S(2)}, u32[]{:S(2)}) %collective-permute-start.35) | collective-permute-done | bytes 786464 | tf_op jit(solution)/shard_map/ppermute | solution.py:247
  427.9 17.3 %collective-permute-done.36 = bf16[128,3072]{1,0:T(8,128)(2,1)S(1)} collective-permute-done((bf16[128,3072]{1,0:T(8,128)(2,1)}, bf16[128,3072]{1,0:T(8,128)(2,1)S(1)}, u32[]{:S(2)}, u32[]{:S(2)}) %collective-permute-start.36) | collective-permute-done | bytes 786464 | tf_op jit(solution)/shard_map/ppermute | solution.py:247
  449.3 5.7 fusion.53
  460.2 4.5 collective-permute-done.52
  480.0 3.8 collective-permute-done.61
  486.8 6.5 fusion.4
  493.4 16.7 %all-gather.3.cloned.1.call-done = bf16[512,3072]{1,0:T(8,128)(2,1)} async-done(((bf16[128,3072]{1,0:T(8,128)(2,1)}), bf16[512,3072]{1,0:T(8,128)(2,1)}) %all-gather.3.cloned.1.call-update) | async-done | bytes 3145744 | tf_op jit(solution)/shard_map/all_gather | solution.py:397
  510.0 6.0 fusion.49
  519.7 4.1 collective-permute-done.55
  523.8 5.7 collective-permute-done.56
  540.2 4.3 collective-permute-done.67
  544.5 3.8 collective-permute-done.68
  548.3 5.5 fusion.5
  554.7 4.3 reduce-scatter.29.cloned.1.call-done
  560.3 4.0 prepare.6
  565.1 43.7 %reduce-scatter.31.cloned.1.call-done = bf16[576,512]{1,0:T(8,128)(2,1)} async-done(((bf16[2304,512]{1,0:T(8,128)(2,1)}), bf16[576,512]{1,0:T(8,128)(2,1)}) %reduce-scatter.31.cloned.1.call-update) | async-done | bytes 589840
  610.2 4.0 prepare.7
  617.2 5.2 attend.6
  627.4 6.1 collective-permute-done.71
  633.6 10.4 %collective-permute-done.72 = bf16[512,192]{1,0:T(8,128)(2,1)S(1)} collective-permute-done((bf16[512,192]{1,0:T(8,128)(2,1)S(1)}, bf16[512,192]{1,0:T(8,128)(2,1)S(1)}, u32[]{:S(2)}, u32[]{:S(2)}) %collective-permute-start.72) | collective-permute-done | bytes 196640 | tf_op jit(solution)/shard_map/ppermute | solution.py:256
  648.5 4.0 collective-permute-done.74
  656.3 6.0 collective-permute-start.77
  677.2 7.7 convolution_convert_fusion.1
  686.0 5.2 attend.7
  695.2 12.5 %collective-permute-done.89 = bf16[512,192]{1,0:T(8,128)(2,1)S(1)} collective-permute-done((bf16[512,192]{1,0:T(8,128)(2,1)S(1)}, bf16[512,192]{1,0:T(8,128)(2,1)S(1)}, u32[]{:S(2)}, u32[]{:S(2)}) %collective-permute-start.89) | collective-permute-done | bytes 196640 | tf_op jit(solution)/shard_map/ppermute | solution.py:256
  707.6 12.6 %collective-permute-done.90 = bf16[512,192]{1,0:T(8,128)(2,1)S(1)} collective-permute-done((bf16[512,192]{1,0:T(8,128)(2,1)S(1)}, bf16[512,192]{1,0:T(8,128)(2,1)S(1)}, u32[]{:S(2)}, u32[]{:S(2)}) %collective-permute-start.90) | collective-permute-done | bytes 196640 | tf_op jit(solution)/shard_map/ppermute | solution.py:256
  730.7 19.0 %collective-permute-start.95 = (f32[2,128]{1,0:T(2,128)S(1)}, f32[2,128]{1,0:T(2,128)S(1)}, u32[]{:S(2)}, u32[]{:S(2)}) collective-permute-start(f32[2,128]{1,0:T(2,128)S(1)} %pad_maximum_fusion.23), channel_id=1, source_target_pairs={{0,1},{1,2},{2,3},{3,0},{4,5},{5,6},{6,7},{7,4},{8,9},{9,10},{10,1... | collective-permute-start | bytes 3080 | tf_op jit(solution)/shard_map/ppermute | solution.py:268
  764.3 7.1 convolution_convert_fusion
  777.0 24.6 %collective-permute-done.83 = bf16[128,3072]{1,0:T(8,128)(2,1)S(1)} collective-permute-done((bf16[128,3072]{1,0:T(8,128)(2,1)S(1)}, bf16[128,3072]{1,0:T(8,128)(2,1)S(1)}, u32[]{:S(2)}, u32[]{:S(2)}) %collective-permute-start.83) | collective-permute-done | bytes 786464 | tf_op jit(solution)/shard_map/ppermute | solution.py:246
  802.3 34.1 %collective-permute-done.84 = bf16[128,3072]{1,0:T(8,128)(2,1)S(1)} collective-permute-done((bf16[128,3072]{1,0:T(8,128)(2,1)S(1)}, bf16[128,3072]{1,0:T(8,128)(2,1)S(1)}, u32[]{:S(2)}, u32[]{:S(2)}) %collective-permute-start.84) | collective-permute-done | bytes 786464 | tf_op jit(solution)/shard_map/ppermute | solution.py:247
  838.4 23.7 %collective-permute-done.85 = bf16[128,3072]{1,0:T(8,128)(2,1)S(1)} collective-permute-done((bf16[128,3072]{1,0:T(8,128)(2,1)S(1)}, bf16[128,3072]{1,0:T(8,128)(2,1)S(1)}, u32[]{:S(2)}, u32[]{:S(2)}) %collective-permute-start.85) | collective-permute-done | bytes 786464 | tf_op jit(solution)/shard_map/ppermute | solution.py:247
  865.3 19.2 %collective-permute-done.86 = bf16[128,3072]{1,0:T(8,128)(2,1)S(1)} collective-permute-done((bf16[128,3072]{1,0:T(8,128)(2,1)S(1)}, bf16[128,3072]{1,0:T(8,128)(2,1)S(1)}, u32[]{:S(2)}, u32[]{:S(2)}) %collective-permute-start.86) | collective-permute-done | bytes 786464 | tf_op jit(solution)/shard_map/ppermute | solution.py:247
  888.8 8.6 collective-permute-start.109
  901.2 6.5 collective-permute-done.109
  907.9 4.1 collective-permute-start.113
  912.8 21.9 %collective-permute-done.112 = bf16[1,3,256,128]{3,2,0,1:T(8,128)(2,1)S(1)} collective-permute-done((bf16[1,3,256,128]{3,2,0,1:T(8,128)(2,1)S(1)}, bf16[1,3,256,128]{3,2,0,1:T(8,128)(2,1)S(1)}, u32[]{:S(2)}, u32[]{:S(2)}) %collective-permute-start.112) | collective-permute-done | bytes 196640 | tf_op jit(solution)/shard_map/ppermute | solution.py:167
  940.2 6.4 fusion.50
  950.3 16.0 %all-gather.5.cloned.1.call-done = bf16[512,3072]{1,0:T(8,128)(2,1)} async-done(((bf16[128,3072]{1,0:T(8,128)(2,1)}), bf16[512,3072]{1,0:T(8,128)(2,1)}) %all-gather.5.cloned.1.call-update) | async-done | bytes 3145744 | tf_op jit(solution)/shard_map/all_gather | solution.py:397
  966.3 7.3 fusion.48
  (569 shorter events, 280.7 us)
Async XLA Ops:
  7.2 90.7 %reduce-scatter.25.cloned.1.call-start = ((), (), s32[]{:S(2)}) async-start(), calls=%async_computation.14 | async-start | bytes 2949120
  7.2 31.2 %collective-permute-start.7 = (bf16[768,2304]{1,0:T(8,128)(2,1)}, bf16[768,2304]{1,0:T(8,128)(2,1)}, u32[]{:S(2)}, u32[]{:S(2)}) collective-permute-start(bf16[768,2304]{1,0:T(8,128)(2,1)} %bitcast.921), channel_id=1, source_target_pairs={{0,16},{16,0},{1,17},{17,1},{2,18},{18,2},{3,19},{19,3},{4,20},{20... | collective-permute-start | bytes 10616840 | tf_op jit(solution)/shard_map/ppermute | solution.py:205
  10.2 12.8 %collective-permute-start.1 = (f32[2,128]{1,0:T(2,128)S(1)}, f32[2,128]{1,0:T(2,128)S(1)}, u32[]{:S(2)}, u32[]{:S(2)}) collective-permute-start(f32[2,128]{1,0:T(2,128)S(1)} %pad_maximum_fusion.14), channel_id=1, source_target_pairs={{0,1},{1,2},{2,3},{3,0},{4,5},{5,6},{6,7},{7,4},{8,9},{9,10},{10,1... | collective-permute-start | bytes 3080 | tf_op jit(solution)/shard_map/ppermute | solution.py:268
  12.8 10.1 %collective-permute-start.2 = (f32[2,128]{1,0:T(2,128)S(1)}, f32[2,128]{1,0:T(2,128)S(1)}, u32[]{:S(2)}, u32[]{:S(2)}) collective-permute-start(f32[2,128]{1,0:T(2,128)S(1)} %pad_maximum_fusion.14), channel_id=1, source_target_pairs={{0,2},{1,3},{2,0},{3,1},{4,6},{5,7},{6,4},{7,5},{8,10},{9,11},{10,... | collective-permute-start | bytes 3080 | tf_op jit(solution)/shard_map/ppermute | solution.py:268
  27.5 10.9 %collective-permute-start.5 = (bf16[128,768]{1,0:T(8,128)(2,1)S(1)}, bf16[128,768]{1,0:T(8,128)(2,1)S(1)}, u32[]{:S(2)}, u32[]{:S(2)}) collective-permute-start(bf16[128,768]{1,0:T(8,128)(2,1)S(1)} %fusion.154), channel_id=1, source_target_pairs={{0,8},{4,12},{8,0},{12,4},{1,9},{5,13},{9,1},{13,5},{2,10},{6,14},... | collective-permute-start | bytes 589832 | tf_op jit(solution)/shard_map/ppermute | solution.py:227
  44.0 106.7 %reduce-scatter.27.cloned.1.call-start = ((), (), s32[]{:S(2)}) async-start(), calls=%async_computation.15 | async-start | bytes 2949120
  69.3 262.8 %reduce-scatter.17.cloned.1.call-start = ((), (), s32[]{:S(2)}) async-start(), calls=%async_computation.8 | async-start | bytes 3932160 | tf_op jit(solution)/shard_map/reduce_scatter | solution.py:391
  71.7 93.3 %collective-permute-start.15 = (bf16[1,3,256,128]{3,2,0,1:T(8,128)(2,1)}, bf16[1,3,256,128]{3,2,0,1:T(8,128)(2,1)}, u32[]{:S(2)}, u32[]{:S(2)}) collective-permute-start(bf16[1,3,256,128]{3,2,0,1:T(8,128)(2,1)} %get-tuple-element.174), channel_id=1, source_target_pairs={{0,1},{1,2},{2,3},{3,0},{4,5},{5,6},{6,7},{7,4},{8,9},{9,10},{10,1... | collective-permute-start | bytes 589832 | tf_op jit(solution)/shard_map/ppermute | solution.py:167
  71.8 96.1 %collective-permute-start.16 = (bf16[1,3,256,128]{3,2,0,1:T(8,128)(2,1)S(1)}, bf16[1,3,256,128]{3,2,0,1:T(8,128)(2,1)}, u32[]{:S(2)}, u32[]{:S(2)}) collective-permute-start(bf16[1,3,256,128]{3,2,0,1:T(8,128)(2,1)S(1)} %get-tuple-element.173), channel_id=1, source_target_pairs={{0,2},{1,3},{2,0},{3,1},{4,6},{5,7},{6,4},{7,5},{8,10},{9,11},{10,... | collective-permute-start | bytes 589832 | tf_op jit(solution)/shard_map/ppermute | solution.py:167
  72.6 108.6 %collective-permute-start.22 = (bf16[768,768]{1,0:T(8,128)(2,1)}, bf16[768,768]{1,0:T(8,128)(2,1)}, u32[]{:S(2)}, u32[]{:S(2)}) collective-permute-start(bf16[768,768]{1,0:T(8,128)(2,1)} %bitcast.78), channel_id=1, source_target_pairs={{0,16},{16,0},{1,17},{17,1},{2,18},{18,2},{3,19},{19,3},{4,20},{20... | collective-permute-start | bytes 3538952 | tf_op jit(solution)/shard_map/ppermute | solution.py:205
  72.6 153.2 %collective-permute-start.32 = (bf16[768,3072]{1,0:T(8,128)(2,1)}, bf16[768,3072]{1,0:T(8,128)(2,1)}, u32[]{:S(2)}, u32[]{:S(2)}) collective-permute-start(bf16[768,3072]{1,0:T(8,128)(2,1)} %bitcast.911), channel_id=1, source_target_pairs={{0,16},{16,0},{1,17},{17,1},{2,18},{18,2},{3,19},{19,3},{4,20},{20... | collective-permute-start | bytes 14155784 | tf_op jit(solution)/shard_map/ppermute | solution.py:205
  160.9 9.8 collective-permute-start.18
  176.1 11.2 %collective-permute-start.19 = (bf16[512,192]{1,0:T(8,128)(2,1)S(1)}, bf16[512,192]{1,0:T(8,128)(2,1)S(1)}, u32[]{:S(2)}, u32[]{:S(2)}) collective-permute-start(bf16[512,192]{1,0:T(8,128)(2,1)S(1)} %attend.4), channel_id=1, source_target_pairs={{0,1},{1,2},{2,3},{3,0},{4,5},{5,6},{6,7},{7,4},{8,9},{9,10},{10,1... | collective-permute-start | bytes 589832 | tf_op jit(solution)/shard_map/ppermute | solution.py:256
  176.9 19.6 %collective-permute-start.20 = (bf16[512,192]{1,0:T(8,128)(2,1)S(1)}, bf16[512,192]{1,0:T(8,128)(2,1)S(1)}, u32[]{:S(2)}, u32[]{:S(2)}) collective-permute-start(bf16[512,192]{1,0:T(8,128)(2,1)S(1)} %attend.4), channel_id=1, source_target_pairs={{0,2},{1,3},{2,0},{3,1},{4,6},{5,7},{6,4},{7,5},{8,10},{9,11},{10,... | collective-permute-start | bytes 589832 | tf_op jit(solution)/shard_map/ppermute | solution.py:256
  180.5 16.0 %collective-permute-start.21 = (bf16[512,192]{1,0:T(8,128)(2,1)S(1)}, bf16[512,192]{1,0:T(8,128)(2,1)S(1)}, u32[]{:S(2)}, u32[]{:S(2)}) collective-permute-start(bf16[512,192]{1,0:T(8,128)(2,1)S(1)} %attend.4), channel_id=1, source_target_pairs={{0,3},{1,0},{2,1},{3,2},{4,7},{5,4},{6,5},{7,6},{8,11},{9,8},{10,9... | collective-permute-start | bytes 589832 | tf_op jit(solution)/shard_map/ppermute | solution.py:256
  199.0 10.7 %collective-permute-start.24 = (bf16[128,768]{1,0:T(8,128)(2,1)S(1)}, bf16[128,768]{1,0:T(8,128)(2,1)S(1)}, u32[]{:S(2)}, u32[]{:S(2)}) collective-permute-start(bf16[128,768]{1,0:T(8,128)(2,1)S(1)} %get-tuple-element.168), channel_id=1, source_target_pairs={{0,8},{4,12},{8,0},{12,4},{1,9},{5,13},{9,1},{13,5},{2,10},{6,14},... | collective-permute-start | bytes 589832 | tf_op jit(solution)/shard_map/ppermute | solution.py:234
  237.5 208.7 %reduce-scatter.19.cloned.1.call-start = ((), (), s32[]{:S(2)}) async-start(), calls=%async_computation.9 | async-start | bytes 3932160 | tf_op jit(solution)/shard_map/reduce_scatter | solution.py:391
  243.8 16.4 %collective-permute-start.39 = (bf16[512,192]{1,0:T(8,128)(2,1)S(1)}, bf16[512,192]{1,0:T(8,128)(2,1)S(1)}, u32[]{:S(2)}, u32[]{:S(2)}) collective-permute-start(bf16[512,192]{1,0:T(8,128)(2,1)S(1)} %attend.5), channel_id=1, source_target_pairs={{0,1},{1,2},{2,3},{3,0},{4,5},{5,6},{6,7},{7,4},{8,9},{9,10},{10,1... | collective-permute-start | bytes 589832 | tf_op jit(solution)/shard_map/ppermute | solution.py:256
  244.6 33.3 %collective-permute-start.40 = (bf16[512,192]{1,0:T(8,128)(2,1)S(1)}, bf16[512,192]{1,0:T(8,128)(2,1)S(1)}, u32[]{:S(2)}, u32[]{:S(2)}) collective-permute-start(bf16[512,192]{1,0:T(8,128)(2,1)S(1)} %attend.5), channel_id=1, source_target_pairs={{0,2},{1,3},{2,0},{3,1},{4,6},{5,7},{6,4},{7,5},{8,10},{9,11},{10,... | collective-permute-start | bytes 589832 | tf_op jit(solution)/shard_map/ppermute | solution.py:256
  248.0 30.6 %collective-permute-start.41 = (bf16[512,192]{1,0:T(8,128)(2,1)S(1)}, bf16[512,192]{1,0:T(8,128)(2,1)S(1)}, u32[]{:S(2)}, u32[]{:S(2)}) collective-permute-start(bf16[512,192]{1,0:T(8,128)(2,1)S(1)} %attend.5), channel_id=1, source_target_pairs={{0,3},{1,0},{2,1},{3,2},{4,7},{5,4},{6,5},{7,6},{8,11},{9,8},{10,9... | collective-permute-start | bytes 589832 | tf_op jit(solution)/shard_map/ppermute | solution.py:256
  279.6 10.9 %collective-permute-start.43 = (bf16[128,768]{1,0:T(8,128)(2,1)S(1)}, bf16[128,768]{1,0:T(8,128)(2,1)S(1)}, u32[]{:S(2)}, u32[]{:S(2)}) collective-permute-start(bf16[128,768]{1,0:T(8,128)(2,1)S(1)} %get-tuple-element.171), channel_id=1, source_target_pairs={{0,8},{4,12},{8,0},{12,4},{1,9},{5,13},{9,1},{13,5},{2,10},{6,14},... | collective-permute-start | bytes 589832 | tf_op jit(solution)/shard_map/ppermute | solution.py:234
  291.9 22.5 %collective-permute-start.45 = (f32[2,128]{1,0:T(2,128)S(1)}, f32[2,128]{1,0:T(2,128)S(1)}, u32[]{:S(2)}, u32[]{:S(2)}) collective-permute-start(f32[2,128]{1,0:T(2,128)S(1)} %pad_maximum_fusion.18), channel_id=1, source_target_pairs={{0,1},{1,2},{2,3},{3,0},{4,5},{5,6},{6,7},{7,4},{8,9},{9,10},{10,1... | collective-permute-start | bytes 3080 | tf_op jit(solution)/shard_map/ppermute | solution.py:268
  332.1 178.0 %all-gather.3.cloned.1.call-start = ((), (), s32[]{:S(2)}) async-start(), calls=%async_computation.10 | async-start | bytes 3932160 | tf_op jit(solution)/shard_map/all_gather | solution.py:397
  333.8 35.8 %collective-permute-start.33 = (bf16[128,3072]{1,0:T(8,128)(2,1)S(1)}, bf16[128,3072]{1,0:T(8,128)(2,1)S(1)}, u32[]{:S(2)}, u32[]{:S(2)}) collective-permute-start(bf16[128,3072]{1,0:T(8,128)(2,1)S(1)} %fusion.29), channel_id=1, source_target_pairs={{0,1},{1,2},{2,3},{4,5},{5,6},{6,7},{8,9},{9,10},{10,11},{12,13},{... | collective-permute-start | bytes 2359304 | tf_op jit(solution)/shard_map/ppermute | solution.py:246
  336.8 55.0 %collective-permute-start.34 = (bf16[128,3072]{1,0:T(8,128)(2,1)S(1)}, bf16[128,3072]{1,0:T(8,128)(2,1)S(1)}, u32[]{:S(2)}, u32[]{:S(2)}) collective-permute-start(bf16[128,3072]{1,0:T(8,128)(2,1)S(1)} %fusion.29), channel_id=1, source_target_pairs={{1,0},{2,1},{3,2},{5,4},{6,5},{7,6},{9,8},{10,9},{11,10},{13,12},{... | collective-permute-start | bytes 2359304 | tf_op jit(solution)/shard_map/ppermute | solution.py:247
  370.5 22.7 %collective-permute-start.37 = (bf16[128,3072]{1,0:T(8,128)(2,1)S(1)}, bf16[128,3072]{1,0:T(8,128)(2,1)}, u32[]{:S(2)}, u32[]{:S(2)}) collective-permute-start(bf16[128,3072]{1,0:T(8,128)(2,1)S(1)} %collective-permute-done.33), channel_id=1, source_target_pairs={{1,2},{2,3},{5,6},{6,7},{9,10},{10,11},{13,14},{14,15},{17,18},{18... | collective-permute-start | bytes 2359304 | tf_op jit(solution)/shard_map/ppermute | solution.py:246
  391.8 32.5 %collective-permute-start.35 = (bf16[128,3072]{1,0:T(8,128)(2,1)S(1)}, bf16[128,3072]{1,0:T(8,128)(2,1)}, u32[]{:S(2)}, u32[]{:S(2)}) collective-permute-start(bf16[128,3072]{1,0:T(8,128)(2,1)S(1)} %collective-permute-done.34), channel_id=1, source_target_pairs={{1,0},{2,1},{5,4},{6,5},{9,8},{10,9},{13,12},{14,13},{17,16},{18,1... | collective-permute-start | bytes 2359304 | tf_op jit(solution)/shard_map/ppermute | solution.py:247
  393.1 56.2 %collective-permute-start.51 = (bf16[3072,768]{1,0:T(8,128)(2,1)}, bf16[3072,768]{1,0:T(8,128)(2,1)}, u32[]{:S(2)}, u32[]{:S(2)}) collective-permute-start(bf16[3072,768]{1,0:T(8,128)(2,1)} %bitcast.920), channel_id=1, source_target_pairs={{0,16},{16,0},{1,17},{17,1},{2,18},{18,2},{3,19},{19,3},{4,20},{20... | collective-permute-start | bytes 14155784 | tf_op jit(solution)/shard_map/ppermute | solution.py:205
  393.2 33.7 %collective-permute-start.38 = (bf16[128,3072]{1,0:T(8,128)(2,1)}, bf16[128,3072]{1,0:T(8,128)(2,1)}, u32[]{:S(2)}, u32[]{:S(2)}) collective-permute-start(bf16[128,3072]{1,0:T(8,128)(2,1)} %collective-permute-done.37), channel_id=1, source_target_pairs={{2,3},{6,7},{10,11},{14,15},{18,19},{22,23},{26,27},{30,31}} | collective-permute-start | bytes 2359304 | tf_op jit(solution)/shard_map/ppermute | solution.py:246
  424.3 20.9 %collective-permute-start.36 = (bf16[128,3072]{1,0:T(8,128)(2,1)}, bf16[128,3072]{1,0:T(8,128)(2,1)S(1)}, u32[]{:S(2)}, u32[]{:S(2)}) collective-permute-start(bf16[128,3072]{1,0:T(8,128)(2,1)} %collective-permute-done.35), channel_id=1, source_target_pairs={{1,0},{5,4},{9,8},{13,12},{17,16},{21,20},{25,24},{29,28}} | collective-permute-start | bytes 2359304 | tf_op jit(solution)/shard_map/ppermute | solution.py:247
  448.8 110.2 %reduce-scatter.29.cloned.1.call-start = ((), (), s32[]{:S(2)}) async-start(), calls=%async_computation.16 | async-start | bytes 2949120
  457.6 10.5 %collective-permute-start.53 = (bf16[128,768]{1,0:T(8,128)(2,1)}, bf16[128,768]{1,0:T(8,128)(2,1)S(1)}, u32[]{:S(2)}, u32[]{:S(2)}) collective-permute-start(bf16[128,768]{1,0:T(8,128)(2,1)} %get-tuple-element.162), channel_id=1, source_target_pairs={{0,8},{4,12},{8,0},{12,4},{1,9},{5,13},{9,1},{13,5},{2,10},{6,14},... | collective-permute-start | bytes 589832 | tf_op jit(solution)/shard_map/ppermute | solution.py:234
  457.8 10.3 %collective-permute-start.54 = (bf16[128,768]{1,0:T(8,128)(2,1)S(1)}, bf16[128,768]{1,0:T(8,128)(2,1)S(1)}, u32[]{:S(2)}, u32[]{:S(2)}) collective-permute-start(bf16[128,768]{1,0:T(8,128)(2,1)S(1)} %get-tuple-element.161), channel_id=1, source_target_pairs={{0,12},{4,8},{8,4},{12,0},{1,13},{5,9},{9,5},{13,1},{2,14},{6,10},... | collective-permute-start | bytes 589832 | tf_op jit(solution)/shard_map/ppermute | solution.py:234
  493.3 115.5 %reduce-scatter.31.cloned.1.call-start = ((), (), s32[]{:S(2)}) async-start(), calls=%async_computation.17 | async-start | bytes 2949120
  517.7 11.9 %collective-permute-start.56 = (bf16[128,768]{1,0:T(8,128)(2,1)S(1)}, bf16[128,768]{1,0:T(8,128)(2,1)S(1)}, u32[]{:S(2)}, u32[]{:S(2)}) collective-permute-start(bf16[128,768]{1,0:T(8,128)(2,1)S(1)} %get-tuple-element.165), channel_id=1, source_target_pairs={{0,8},{4,12},{8,0},{12,4},{1,9},{5,13},{9,1},{13,5},{2,10},{6,14},... | collective-permute-start | bytes 589832 | tf_op jit(solution)/shard_map/ppermute | solution.py:234
  519.1 10.4 %collective-permute-start.57 = (bf16[128,768]{1,0:T(8,128)(2,1)S(1)}, bf16[128,768]{1,0:T(8,128)(2,1)S(1)}, u32[]{:S(2)}, u32[]{:S(2)}) collective-permute-start(bf16[128,768]{1,0:T(8,128)(2,1)S(1)} %get-tuple-element.164), channel_id=1, source_target_pairs={{0,12},{4,8},{8,4},{12,0},{1,13},{5,9},{9,5},{13,1},{2,14},{6,10},... | collective-permute-start | bytes 589832 | tf_op jit(solution)/shard_map/ppermute | solution.py:234
  537.3 11.0 %collective-permute-start.68 = (bf16[128,768]{1,0:T(8,128)(2,1)S(1)}, bf16[128,768]{1,0:T(8,128)(2,1)S(1)}, u32[]{:S(2)}, u32[]{:S(2)}) collective-permute-start(bf16[128,768]{1,0:T(8,128)(2,1)S(1)} %fusion.172), channel_id=1, source_target_pairs={{0,8},{4,12},{8,0},{12,4},{1,9},{5,13},{9,1},{13,5},{2,10},{6,14},... | collective-permute-start | bytes 589832 | tf_op jit(solution)/shard_map/ppermute | solution.py:227
  553.9 217.5 %reduce-scatter.21.cloned.1.call-start = ((), (), s32[]{:S(2)}) async-start(), calls=%async_computation.11 | async-start | bytes 3932160 | tf_op jit(solution)/shard_map/reduce_scatter | solution.py:391
  622.4 11.1 %collective-permute-start.71 = (bf16[512,192]{1,0:T(8,128)(2,1)S(1)}, bf16[512,192]{1,0:T(8,128)(2,1)S(1)}, u32[]{:S(2)}, u32[]{:S(2)}) collective-permute-start(bf16[512,192]{1,0:T(8,128)(2,1)S(1)} %attend.6), channel_id=1, source_target_pairs={{0,1},{1,2},{2,3},{3,0},{4,5},{5,6},{6,7},{7,4},{8,9},{9,10},{10,1... | collective-permute-start | bytes 589832 | tf_op jit(solution)/shard_map/ppermute | solution.py:256
  622.9 21.1 %collective-permute-start.72 = (bf16[512,192]{1,0:T(8,128)(2,1)S(1)}, bf16[512,192]{1,0:T(8,128)(2,1)S(1)}, u32[]{:S(2)}, u32[]{:S(2)}) collective-permute-start(bf16[512,192]{1,0:T(8,128)(2,1)S(1)} %attend.6), channel_id=1, source_target_pairs={{0,2},{1,3},{2,0},{3,1},{4,6},{5,7},{6,4},{7,5},{8,10},{9,11},{10,... | collective-permute-start | bytes 589832 | tf_op jit(solution)/shard_map/ppermute | solution.py:256
  624.6 19.4 %collective-permute-start.73 = (bf16[512,192]{1,0:T(8,128)(2,1)S(1)}, bf16[512,192]{1,0:T(8,128)(2,1)S(1)}, u32[]{:S(2)}, u32[]{:S(2)}) collective-permute-start(bf16[512,192]{1,0:T(8,128)(2,1)S(1)} %attend.6), channel_id=1, source_target_pairs={{0,3},{1,0},{2,1},{3,2},{4,7},{5,4},{6,5},{7,6},{8,11},{9,8},{10,9... | collective-permute-start | bytes 589832 | tf_op jit(solution)/shard_map/ppermute | solution.py:256
  685.0 200.6 %reduce-scatter.23.cloned.1.call-start = ((), (), s32[]{:S(2)}) async-start(), calls=%async_computation.12 | async-start | bytes 3932160 | tf_op jit(solution)/shard_map/reduce_scatter | solution.py:391
  691.2 16.4 %collective-permute-start.89 = (bf16[512,192]{1,0:T(8,128)(2,1)S(1)}, bf16[512,192]{1,0:T(8,128)(2,1)S(1)}, u32[]{:S(2)}, u32[]{:S(2)}) collective-permute-start(bf16[512,192]{1,0:T(8,128)(2,1)S(1)} %attend.7), channel_id=1, source_target_pairs={{0,1},{1,2},{2,3},{3,0},{4,5},{5,6},{6,7},{7,4},{8,9},{9,10},{10,1... | collective-permute-start | bytes 589832 | tf_op jit(solution)/shard_map/ppermute | solution.py:256
  691.3 28.9 %collective-permute-start.90 = (bf16[512,192]{1,0:T(8,128)(2,1)S(1)}, bf16[512,192]{1,0:T(8,128)(2,1)S(1)}, u32[]{:S(2)}, u32[]{:S(2)}) collective-permute-start(bf16[512,192]{1,0:T(8,128)(2,1)S(1)} %attend.7), channel_id=1, source_target_pairs={{0,2},{1,3},{2,0},{3,1},{4,6},{5,7},{6,4},{7,5},{8,10},{9,11},{10,... | collective-permute-start | bytes 589832 | tf_op jit(solution)/shard_map/ppermute | solution.py:256
  694.1 26.9 %collective-permute-start.91 = (bf16[512,192]{1,0:T(8,128)(2,1)S(1)}, bf16[512,192]{1,0:T(8,128)(2,1)S(1)}, u32[]{:S(2)}, u32[]{:S(2)}) collective-permute-start(bf16[512,192]{1,0:T(8,128)(2,1)S(1)} %attend.7), channel_id=1, source_target_pairs={{0,3},{1,0},{2,1},{3,2},{4,7},{5,4},{6,5},{7,6},{8,11},{9,8},{10,9... | collective-permute-start | bytes 589832 | tf_op jit(solution)/shard_map/ppermute | solution.py:256
  730.7 21.5 %collective-permute-start.95 = (f32[2,128]{1,0:T(2,128)S(1)}, f32[2,128]{1,0:T(2,128)S(1)}, u32[]{:S(2)}, u32[]{:S(2)}) collective-permute-start(f32[2,128]{1,0:T(2,128)S(1)} %pad_maximum_fusion.23), channel_id=1, source_target_pairs={{0,1},{1,2},{2,3},{3,0},{4,5},{5,6},{6,7},{7,4},{8,9},{9,10},{10,1... | collective-permute-start | bytes 3080 | tf_op jit(solution)/shard_map/ppermute | solution.py:268
  771.4 195.0 %all-gather.5.cloned.1.call-start = ((), (), s32[]{:S(2)}) async-start(), calls=%async_computation.13 | async-start | bytes 3932160 | tf_op jit(solution)/shard_map/all_gather | solution.py:397
  773.1 28.5 %collective-permute-start.83 = (bf16[128,3072]{1,0:T(8,128)(2,1)S(1)}, bf16[128,3072]{1,0:T(8,128)(2,1)S(1)}, u32[]{:S(2)}, u32[]{:S(2)}) collective-permute-start(bf16[128,3072]{1,0:T(8,128)(2,1)S(1)} %fusion.41), channel_id=1, source_target_pairs={{0,1},{1,2},{2,3},{4,5},{5,6},{6,7},{8,9},{9,10},{10,11},{12,13},{... | collective-permute-start | bytes 2359304 | tf_op jit(solution)/shard_map/ppermute | solution.py:246
  775.7 60.7 %collective-permute-start.84 = (bf16[128,3072]{1,0:T(8,128)(2,1)S(1)}, bf16[128,3072]{1,0:T(8,128)(2,1)S(1)}, u32[]{:S(2)}, u32[]{:S(2)}) collective-permute-start(bf16[128,3072]{1,0:T(8,128)(2,1)S(1)} %fusion.41), channel_id=1, source_target_pairs={{1,0},{2,1},{3,2},{5,4},{6,5},{7,6},{9,8},{10,9},{11,10},{13,12},{... | collective-permute-start | bytes 2359304 | tf_op jit(solution)/shard_map/ppermute | solution.py:247
  801.6 36.1 %collective-permute-start.87 = (bf16[128,3072]{1,0:T(8,128)(2,1)S(1)}, bf16[128,3072]{1,0:T(8,128)(2,1)S(1)}, u32[]{:S(2)}, u32[]{:S(2)}) collective-permute-start(bf16[128,3072]{1,0:T(8,128)(2,1)S(1)} %collective-permute-done.83), channel_id=1, source_target_pairs={{1,2},{2,3},{5,6},{6,7},{9,10},{10,11},{13,14},{14,15},{17,18},{18... | collective-permute-start | bytes 2359304 | tf_op jit(solution)/shard_map/ppermute | solution.py:246
  836.4 25.7 %collective-permute-start.85 = (bf16[128,3072]{1,0:T(8,128)(2,1)S(1)}, bf16[128,3072]{1,0:T(8,128)(2,1)S(1)}, u32[]{:S(2)}, u32[]{:S(2)}) collective-permute-start(bf16[128,3072]{1,0:T(8,128)(2,1)S(1)} %collective-permute-done.84), channel_id=1, source_target_pairs={{1,0},{2,1},{5,4},{6,5},{9,8},{10,9},{13,12},{14,13},{17,16},{18,1... | collective-permute-start | bytes 2359304 | tf_op jit(solution)/shard_map/ppermute | solution.py:247
  837.7 26.6 %collective-permute-start.88 = (bf16[128,3072]{1,0:T(8,128)(2,1)S(1)}, bf16[128,3072]{1,0:T(8,128)(2,1)S(1)}, u32[]{:S(2)}, u32[]{:S(2)}) collective-permute-start(bf16[128,3072]{1,0:T(8,128)(2,1)S(1)} %collective-permute-done.87), channel_id=1, source_target_pairs={{2,3},{6,7},{10,11},{14,15},{18,19},{22,23},{26,27},{30,31}} | collective-permute-start | bytes 2359304 | tf_op jit(solution)/shard_map/ppermute | solution.py:246
  862.1 22.4 %collective-permute-start.86 = (bf16[128,3072]{1,0:T(8,128)(2,1)S(1)}, bf16[128,3072]{1,0:T(8,128)(2,1)S(1)}, u32[]{:S(2)}, u32[]{:S(2)}) collective-permute-start(bf16[128,3072]{1,0:T(8,128)(2,1)S(1)} %collective-permute-done.85), channel_id=1, source_target_pairs={{1,0},{5,4},{9,8},{13,12},{17,16},{21,20},{25,24},{29,28}} | collective-permute-start | bytes 2359304 | tf_op jit(solution)/shard_map/ppermute | solution.py:247
  888.8 11.8 %collective-permute-start.108 = (bf16[1,3,256,128]{3,2,0,1:T(8,128)(2,1)S(1)}, bf16[1,3,256,128]{3,2,0,1:T(8,128)(2,1)S(1)}, u32[]{:S(2)}, u32[]{:S(2)}) collective-permute-start(bf16[1,3,256,128]{3,2,0,1:T(8,128)(2,1)S(1)} %get-tuple-element.142), channel_id=1, source_target_pairs={{0,1},{1,2},{2,3},{3,0},{4,5},{5,6},{6,7},{7,4},{8,9},{9,10},{10,1... | collective-permute-start | bytes 589832 | tf_op jit(solution)/shard_map/ppermute | solution.py:167
  888.8 18.9 %collective-permute-start.109 = (bf16[1,3,256,128]{3,2,0,1:T(8,128)(2,1)S(1)}, bf16[1,3,256,128]{3,2,0,1:T(8,128)(2,1)S(1)}, u32[]{:S(2)}, u32[]{:S(2)}) collective-permute-start(bf16[1,3,256,128]{3,2,0,1:T(8,128)(2,1)S(1)} %get-tuple-element.141), channel_id=1, source_target_pairs={{0,2},{1,3},{2,0},{3,1},{4,6},{5,7},{6,4},{7,5},{8,10},{9,11},{10,... | collective-permute-start | bytes 589832 | tf_op jit(solution)/shard_map/ppermute | solution.py:167
  897.4 10.4 %collective-permute-start.110 = (bf16[1,3,256,128]{3,2,0,1:T(8,128)(2,1)S(1)}, bf16[1,3,256,128]{3,2,0,1:T(8,128)(2,1)S(1)}, u32[]{:S(2)}, u32[]{:S(2)}) collective-permute-start(bf16[1,3,256,128]{3,2,0,1:T(8,128)(2,1)S(1)} %get-tuple-element.140), channel_id=1, source_target_pairs={{0,3},{1,0},{2,1},{3,2},{4,7},{5,4},{6,5},{7,6},{8,11},{9,8},{10,9... | collective-permute-start | bytes 589832 | tf_op jit(solution)/shard_map/ppermute | solution.py:167
  901.1 11.6 %collective-permute-start.111 = (bf16[1,3,256,128]{3,2,0,1:T(8,128)(2,1)S(1)}, bf16[1,3,256,128]{3,2,0,1:T(8,128)(2,1)S(1)}, u32[]{:S(2)}, u32[]{:S(2)}) collective-permute-start(bf16[1,3,256,128]{3,2,0,1:T(8,128)(2,1)S(1)} %get-tuple-element.146), channel_id=1, source_target_pairs={{0,1},{1,2},{2,3},{3,0},{4,5},{5,6},{6,7},{7,4},{8,9},{9,10},{10,1... | collective-permute-start | bytes 589832 | tf_op jit(solution)/shard_map/ppermute | solution.py:167
  907.8 26.9 %collective-permute-start.112 = (bf16[1,3,256,128]{3,2,0,1:T(8,128)(2,1)S(1)}, bf16[1,3,256,128]{3,2,0,1:T(8,128)(2,1)S(1)}, u32[]{:S(2)}, u32[]{:S(2)}) collective-permute-start(bf16[1,3,256,128]{3,2,0,1:T(8,128)(2,1)S(1)} %get-tuple-element.145), channel_id=1, source_target_pairs={{0,2},{1,3},{2,0},{3,1},{4,6},{5,7},{6,4},{7,5},{8,10},{9,11},{10,... | collective-permute-start | bytes 589832 | tf_op jit(solution)/shard_map/ppermute | solution.py:167
  907.9 30.3 %collective-permute-start.113 = (bf16[1,3,256,128]{3,2,0,1:T(8,128)(2,1)S(1)}, bf16[1,3,256,128]{3,2,0,1:T(8,128)(2,1)S(1)}, u32[]{:S(2)}, u32[]{:S(2)}) collective-permute-start(bf16[1,3,256,128]{3,2,0,1:T(8,128)(2,1)S(1)} %get-tuple-element.144), channel_id=1, source_target_pairs={{0,3},{1,0},{2,1},{3,2},{4,7},{5,4},{6,5},{7,6},{8,11},{9,8},{10,9... | collective-permute-start | bytes 589832 | tf_op jit(solution)/shard_map/ppermute | solution.py:167
  939.3 44.6 %collective-permute-start.114 = (bf16[256,12,128]{2,0,1:T(8,128)(2,1)}, bf16[256,12,128]{2,0,1:T(8,128)(2,1)}, u32[]{:S(2)}, u32[]{:S(2)}) collective-permute-start(bf16[256,12,128]{2,0,1:T(8,128)(2,1)} %bitcast.173), channel_id=1, source_target_pairs={{0,16},{16,0},{1,17},{17,1},{2,18},{18,2},{3,19},{19,3},{4,20},{20... | collective-permute-start | bytes 2359304 | tf_op jit(solution)/shard_map/ppermute | solution.py:205
  946.8 27.0 %collective-permute-start.101 = (bf16[128,768]{1,0:T(8,128)(2,1)S(1)}, bf16[128,768]{1,0:T(8,128)(2,1)S(1)}, u32[]{:S(2)}, u32[]{:S(2)}) collective-permute-start(bf16[128,768]{1,0:T(8,128)(2,1)S(1)} %get-tuple-element.148), channel_id=1, source_target_pairs={{0,4},{4,0},{8,12},{12,8},{1,5},{5,1},{9,13},{13,9},{2,6},{6,2},{1... | collective-permute-start | bytes 589832 | tf_op jit(solution)/shard_map/ppermute | solution.py:234
  946.8 28.8 %collective-permute-start.102 = (bf16[128,768]{1,0:T(8,128)(2,1)S(1)}, bf16[128,768]{1,0:T(8,128)(2,1)S(1)}, u32[]{:S(2)}, u32[]{:S(2)}) collective-permute-start(bf16[128,768]{1,0:T(8,128)(2,1)S(1)} %get-tuple-element.150), channel_id=1, source_target_pairs={{0,8},{4,12},{8,0},{12,4},{1,9},{5,13},{9,1},{13,5},{2,10},{6,14},... | collective-permute-start | bytes 589832 | tf_op jit(solution)/shard_map/ppermute | solution.py:234
  947.6 29.7 %collective-permute-start.103 = (bf16[128,768]{1,0:T(8,128)(2,1)S(1)}, bf16[128,768]{1,0:T(8,128)(2,1)S(1)}, u32[]{:S(2)}, u32[]{:S(2)}) collective-permute-start(bf16[128,768]{1,0:T(8,128)(2,1)S(1)} %get-tuple-element.149), channel_id=1, source_target_pairs={{0,12},{4,8},{8,4},{12,0},{1,13},{5,9},{9,5},{13,1},{2,14},{6,10},... | collective-permute-start | bytes 589832 | tf_op jit(solution)/shard_map/ppermute | solution.py:234
  973.8 9.8 collective-permute-start.105
  (147 other events, 2038.0 us)
Sparse Core Ops, SparseCore 0:
  44.1 53.7 reduce-scatter.24
  100.1 50.4 reduce-scatter.26
  237.6 78.5 reduce-scatter.16
  332.2 81.7 reduce-scatter.18
  448.9 61.1 all-gather.2
  512.2 46.7 reduce-scatter.28
  561.2 47.4 reduce-scatter.30
  685.1 73.0 reduce-scatter.20
  771.5 79.7 reduce-scatter.22
  888.3 77.9 all-gather.4

commit v5 on v3

--- a/solution.py
+++ b/solution.py
@@ -235,34 +235,68 @@
     return total
 
 
-def gather_line(block):
+def gather_direct(block):
+    n = lax.axis_size("narrow")
+    return [block] + [
+        lax.ppermute(block, "narrow", [(i, (i + step) % n) for i in range(n)]) for step in range(1, n)
+    ]
+
+
+def scatter_direct(terms):
+    n = lax.axis_size("narrow")
+    total = terms[0].astype(F32)
+    for step in range(1, n):
+        pairs = [(i, (i + n - step) % n) for i in range(n)]
+        total += lax.ppermute(terms[step], "narrow", pairs).astype(F32)
+    return total
+
+
+def exchange_of(layer, own, axis):
     n = lax.axis_size("narrow")
     me = lax.axis_index("narrow")
-    from_left = [block]
-    from_right = [block]
-    for step in range(1, n):
-        right = [(i, i + 1) for i in range(step - 1, n - 1)]
-        left = [(i + 1, i) for i in range(0, n - step)]
-        from_left.append(lax.ppermute(from_left[-1], "narrow", right))
-        from_right.append(lax.ppermute(from_right[-1], "narrow", left))
-    return [block] + [
-        jnp.where(me >= step, from_left[step], from_right[n - step]) for step in range(1, n)
-    ]
-
-
-def line_norm(values, model_width):
+    size = own.shape[axis] // n
+    got = []
+    for step in range(n):
+        block = lax.dynamic_slice_in_dim(own, (me + step) % n * size, size, axis)
+        if step:
+            pairs = [(layer * n + i, layer * n + (i + step) % n) for i in range(n)]
+            block = lax.ppermute(block, ("section", "narrow"), pairs)
+        got.append(block)
+    joined = jnp.concatenate(got, axis=1 - axis)
+    passed = lax.ppermute(joined, "section", [(layer, 1 - layer)])
+    return jnp.where(lax.axis_index("section") == layer, joined, passed)
+
+
+def gather_centered(values):
+    mean = jnp.mean(values, axis=1, keepdims=True)
+    center = (values - mean).astype(BF)
+    high = lax.reduce_precision(mean, 8, 7)
+    middle = lax.reduce_precision(mean - high, 8, 7)
+    low = mean - high - middle
+    lane = jnp.arange(128)[None, :]
+    pieces = jnp.where(lane == 0, high, jnp.where(lane == 1, middle, jnp.where(lane == 2, low, 0.0)))
+    blocks = gather_direct(jnp.concatenate([center, pieces.astype(BF)], axis=1))
+    width = values.shape[1]
+    centers = [block[:, :width].astype(F32) for block in blocks]
+    means = [jnp.sum(block[:, width : width + 3].astype(F32), axis=1, keepdims=True) for block in blocks]
+    return centers, means
+
+
+def whole_norm(values, table, kinds):
     n = lax.axis_size("narrow")
     width = values.shape[1]
-    mean = jnp.mean(values, axis=1)
-    center = values - mean[:, None]
-    own = jnp.stack([mean, jnp.sum(center * center, axis=1)])
-    parts = [own]
-    for step in range(1, n):
-        parts.append(lax.ppermute(own, "narrow", [(i, (i + step) % n) for i in range(n)]))
-    whole_mean = sum(part[0] for part in parts) / n
-    spread = sum(part[1] + width * (part[0] - whole_mean) ** 2 for part in parts)
-    scale = lax.rsqrt(spread / model_width + EPS_ROW)
-    return (values - whole_mean[:, None]) * scale[:, None]
+    centers, means = gather_centered(values)
+    mean = sum(means) / n
+    spread = sum(
+        jnp.sum(c * c, axis=1, keepdims=True) + width * (m - mean) ** 2 for c, m in zip(centers, means)
+    )
+    scale = lax.rsqrt(spread / (n * width) + EPS_ROW)
+    normed = jnp.concatenate([(c + (m - mean)) * scale for c, m in zip(centers, means)], axis=1)
+    return modulate(normed, table, kinds)
+
+
+def ordered(*values):
+    return lax.optimization_barrier(values)
 
 
 def in_halves(
@@ -293,7 +327,6 @@
     heads = heads_local // n_narrow
     pair = stale_cache.shape[4]
     head_dim = pair // 2
-    model_width = feat_a * n_narrow
 
     def both_layers(own):
         other = swap(own)
@@ -306,12 +339,14 @@
 
     activated = jax.nn.silu(time_features(timesteps, ada_weight.shape[1])).astype(BF)
     modulation = jnp.einsum("re,kesd->krsd", activated, ada_weight, preferred_element_type=F32)
-    tables = both_layers(modulation.reshape(2, 4, 3, feat_a))
-    qkv_weights = both_layers(w_qkv)
+    modulation = gather_direct(modulation.reshape(2, 4, 3, feat_a))
+    tables = both_layers(jnp.concatenate(modulation, axis=-1))
     norm_rows = both_layers(qk_norm)
-    out_weights = both_layers(w_out)
-    up_weights = both_layers(w_up)
-    down_weights = both_layers(w_down)
+    size = w_out.shape[0] // n_narrow
+    starts = [(narrow_idx + n_narrow - step) % n_narrow * size for step in range(n_narrow)]
+    out_weights = both_layers(
+        jnp.concatenate([lax.dynamic_slice_in_dim(w_out, start, size, 0) for start in starts], axis=0)
+    )
 
     kinds = lax.dynamic_index_in_dim(row_kind, section, 0, False)
     kinds_other = lax.dynamic_index_in_dim(row_kind, 1 - section, 0, False)
@@ -337,10 +372,14 @@
         got = exchange(jnp.stack(per_narrow), "narrow")
         return got.transpose(2, 0, 1, 3).reshape(rows_b, heads_local, pair)
 
+    def by_wide(terms):
+        return [terms[r * part : (r + 1) * part] for r in range(n_wide)]
+
     layer_in = lax.dynamic_index_in_dim(hidden_in, section, 0, False)
     layer_in = [layer_in[h * part : (h + 1) * part] for h in range(halves)]
     results = []
     caches = []
+    qkv_weight = exchange_of(0, w_qkv, 1)
     for layer in range(2):
         table = tables[layer]
         norm_pair = norm_pairs(norm_rows[layer])
@@ -348,46 +387,56 @@
         queries = []
         fresh = []
         for h in range(halves):
-            entry = modulate(line_norm(x_in[h], model_width), table[0], kinds_h[h])
-            terms = jnp.dot(gather_wide(entry), qkv_weights[layer], preferred_element_type=F32)
-            qkv = lax.psum_scatter(terms.astype(BF), "narrow", scatter_dimension=1, tiled=True)
+            entry = whole_norm(x_in[h], table[0], kinds_h[h])
+            if h == 0 and layer == 0:
+                entry, w_up_now = ordered(entry, w_up)
+                up_weight = exchange_of(0, w_up_now, 1)
+            entry = gather_wide(entry)
+            qkv = jnp.dot(entry, qkv_weight, preferred_element_type=F32).astype(BF)
+            if h == 0:
+                qkv, w_down_now = ordered(qkv, w_down)
+                down_weight = exchange_of(layer, w_down_now, 0)
             rows = slice(h * chunk, (h + 1) * chunk)
             q, pairs = prepare(
                 qkv, cosine[rows], sine[rows], kinds_r[rows], norm_pair, heads, head_dim
             )
             queries.append(q)
             fresh.append(pairs)
-        caches.append(to_rows(fresh))
-        own = jnp.concatenate(fresh, axis=1)
+        own, up_weight = ordered(jnp.concatenate(fresh, axis=1), up_weight)
         if layer == 0:
             other = jnp.where(lead, stale, lax.ppermute(own, "section", [(0, 1)]))
         else:
             other = swap(jnp.where(lead, own, stale))
+        cache = to_rows(fresh)
         after = []
         for h in range(halves):
             attended = attend(queries[h], own, other, own_mask, other_mask, head_dim)
-            attended = lax.all_gather(attended, "narrow", axis=1, tiled=True)
+            attended = jnp.concatenate(gather_direct(attended), axis=1)
             terms = jnp.dot(attended, out_weights[layer], preferred_element_type=F32).astype(BF)
-            projected = scatter_wide([terms[r * part : (r + 1) * part] for r in range(n_wide)])
-            after.append(x_in[h] + pick(table[0], kinds_h[h], 2) * projected)
-        inner = []
-        for h in range(halves):
-            entry = modulate(line_norm(after[h], model_width), table[1], kinds_h[h])
-            terms = jnp.dot(gather_wide(entry), up_weights[layer], preferred_element_type=F32)
-            up = lax.psum_scatter(terms.astype(BF), "narrow", scatter_dimension=0, tiled=True)
-            inner.append(jax.nn.gelu(up.astype(F32), approximate=True).astype(BF))
+            projected = scatter_wide(by_wide(terms))
+            after.append(x_in[h] + pick(table[0][..., :feat_a], kinds_h[h], 2) * projected)
+        after[0], down_weight, cache = ordered(after[0], down_weight, cache)
+        caches.append(cache)
         layer_in = []
         for h in range(halves):
-            gathered = jnp.concatenate(gather_line(inner[h]), axis=0)
-            terms = jnp.dot(gathered, down_weights[layer], preferred_element_type=F32).astype(BF)
-            size = chunk // n_narrow
-            ordered = [
-                lax.dynamic_slice_in_dim(terms, (narrow_idx + n_narrow - r) % n_narrow * size, size, 0)
-                for r in range(n_narrow)
-            ]
-            down = scatter_wide(ordered)
-            layer_in.append((after[h] + pick(table[1], kinds_h[h], 2) * down).astype(BF))
+            entry = whole_norm(after[h], table[1], kinds_h[h])
+            if layer == 0 and h == 0:
+                entry, w_qkv_now = ordered(entry, w_qkv)
+                qkv_weight = exchange_of(1, w_qkv_now, 1)
+            entry = gather_wide(entry)
+            up = jnp.dot(entry, up_weight, preferred_element_type=F32)
+            inner = jax.nn.gelu(up, approximate=True).astype(BF)
+            if layer == 0 and h == 1:
+                inner, w_up_now, qkv_weight = ordered(inner, w_up, qkv_weight)
+                next_up_weight = exchange_of(1, w_up_now, 1)
+            terms = jnp.dot(inner, down_weight, preferred_element_type=F32).astype(BF)
+            down = scatter_wide(by_wide(terms)).astype(BF)
+            down = scatter_direct([down[:, d * feat_a : (d + 1) * feat_a] for d in range(n_narrow)])
+            gate = pick(table[1][..., :feat_a], kinds_h[h], 2)
+            layer_in.append((after[h] + gate * down).astype(BF))
         results.append(jnp.concatenate(layer_in, axis=0))
+        if layer == 0:
+            up_weight = next_up_weight
     return (by_layer(results, lead), by_layer(caches, lead))
 
 

time: 972 us -> 1140 us (1.17)
  waiting for transfers between devices: 468 us -> 579 us
  starting transfers between devices: 198 us -> 294 us
  blocking collectives: 90.9 us -> 0 us
  other arithmetic: 38.3 us -> 88.1 us
  local copies, waits for them, and re-layouts: 31.2 us -> 54.5 us
  matrix products: 83.8 us -> 70.2 us
  between operations: 16.7 us -> 4.58 us
    ppermute x48 -> x75, waiting for transfers between devices: 160 us -> 290 us  [the longest x39 121 us: gather_direct(): lax.ppermute(block, 'narrow', [(i, (i + step) % n) for i in range(n)])]
    unnamed x12 -> x0, waiting for transfers between devices: 113 us -> none
    ppermute x24, waiting for transfers between devices: 45.4 us -> 150 us  [gather_wide(): lax.ppermute(block, 'wide', wide_pairs(step))]
    all_gather x4 -> x0, blocking collectives: 90.9 us -> none  [in_halves(): attended = lax.all_gather(attended, 'narrow', axis=1, tiled=True)]
    ppermute x24, waiting for transfers between devices: 38.1 us -> 113 us  [scatter_wide(): total += lax.ppermute(terms[step], 'wide', wide_pairs(step)).astype(F32)]
    reduce_scatter x4 -> x0, waiting for transfers between devices: 67.2 us -> none  [in_halves(): lax.psum_scatter(terms.astype(BF), 'narrow', scatter_dimension=0, tiled=T...]
    ppermute x9 -> x6, starting transfers between devices: 1.39 us -> 56.7 us  [swap(): return lax.ppermute(value, 'section', [(0, 1), (1, 0)])]
    ppermute x48 -> x75, starting transfers between devices: 120 us -> 161 us  [the longest x39 83.1 us: gather_direct(): lax.ppermute(block, 'narrow', [(i, (i + step) % n) for i in range(n)])]
  transfers between devices with their start and end apart: 123 -> 139, of which waited for: 69 -> 54; matrix products, arithmetic and copies ran while one was open for 12% -> 15% of each run, Pallas kernels for 2% -> 3%
where the time goes in v5:
time: 1140 us; the launch traced here: 1130 us
  waiting for transfers between devices  579 us (51%)
  starting transfers between devices  294 us (26%)
  other arithmetic  88.1 us (8%)
  matrix products  70.2 us (6%)
  local copies, waits for them, and re-layouts  54.5 us (5%)
  Pallas kernels  36.8 us (3%)
    ppermute x24, waiting for transfers between devices, gather_wide(): lax.ppermute(block, 'wide', wide_pairs(step))  150 us
    ppermute x39, waiting for transfers between devices, gather_direct(): lax.ppermute(block, 'narrow', [(i, (i + step) % n) for i in range(n)])  121 us
    ppermute x24, waiting for transfers between devices, scatter_wide(): total += lax.ppermute(terms[step], 'wide', wide_pairs(step)).astype(F32)  113 us
    ppermute x18, waiting for transfers between devices, exchange_of(): block = lax.ppermute(block, ('section', 'narrow'), pairs)  111 us
    ppermute x39, starting transfers between devices, gather_direct(): lax.ppermute(block, 'narrow', [(i, (i + step) % n) for i in range(n)])  83.1 us
    ppermute x12, waiting for transfers between devices, scatter_direct(): total += lax.ppermute(terms[step], 'narrow', pairs).astype(F32)  58.5 us
    ppermute x6, starting transfers between devices, swap(): return lax.ppermute(value, 'section', [(0, 1), (1, 0)])  56.7 us
    dot_general x4, matrix products, in_halves(): terms = jnp.dot(inner, down_weight, preferred_element_type=F32).astype(BF)  41.9 us
  transfers between devices with their start and end apart: 139, of which 54 were waited for; matrix products, arithmetic and copies ran while one was open for 15% of the time, Pallas kernels for 3%

profile of v5, /device:TPU:0, one launch (start us, length us, event | category | flops | bytes accessed | tf_op | source)
XLA Modules:
  0.0 1127.1 jit_solution(12970259756259457806)
XLA Ops:
  4.6 5.0 collective-permute-start.17
  9.9 5.0 fusion.126
  36.1 5.7 copy.97
  59.3 8.1 collective-permute-done.25
  68.4 7.1 collective-permute-done.26
  77.9 9.2 collective-permute-start.4
  87.2 10.8 collective-permute-start.12
  110.5 31.0 %collective-permute-done.11 = bf16[768,576]{0,1:T(8,128)(2,1)S(1)} collective-permute-done((bf16[768,576]{0,1:T(8,128)(2,1)S(1)}, bf16[768,576]{0,1:T(8,128)(2,1)S(1)}, u32[]{:S(2)}, u32[]{:S(2)}) %collective-permute-start.11) | collective-permute-done | bytes 884768 | tf_op jit(solution)/shard_map/ppermute | solution.py:263
  166.9 34.4 %collective-permute-done.22 = bf16[768,768]{1,0:T(8,128)(2,1)S(1)} collective-permute-done((bf16[768,768]{1,0:T(8,128)(2,1)S(1)}, bf16[768,768]{1,0:T(8,128)(2,1)S(1)}, u32[]{:S(2)}, u32[]{:S(2)}) %collective-permute-start.22) | collective-permute-done | bytes 1179680 | tf_op jit(solution)/shard_map/ppermute | solution.py:263
  221.7 10.2 collective-permute-done.20
  233.8 14.4 %collective-permute-done.19 = bf16[128,3072]{1,0:T(8,128)(2,1)S(1)} collective-permute-done((bf16[128,3072]{1,0:T(8,128)(2,1)S(1)}, bf16[128,3072]{1,0:T(8,128)(2,1)S(1)}, u32[]{:S(2)}, u32[]{:S(2)}) %collective-permute-start.19) | collective-permute-done | bytes 786464 | tf_op jit(solution)/shard_map/ppermute | solution.py:227
  260.9 37.9 %collective-permute-done.37 = bf16[768,768]{1,0:T(8,128)(2,1)} collective-permute-done((bf16[768,768]{1,0:T(8,128)(2,1)}, bf16[768,768]{1,0:T(8,128)(2,1)}, u32[]{:S(2)}, u32[]{:S(2)}) %collective-permute-start.37) | collective-permute-done | bytes 1179680 | tf_op jit(solution)/shard_map/ppermute | solution.py:263
  298.8 4.9 pad_maximum_fusion.1
  321.8 5.2 attend.4
  329.4 4.9 collective-permute-start.29
  335.4 5.2 attend.5
  340.8 8.8 collective-permute-start.56
  349.6 13.8 %collective-permute-done.30 = bf16[512,192]{1,0:T(8,128)(2,1)S(1)} collective-permute-done((bf16[512,192]{1,0:T(8,128)(2,1)S(1)}, bf16[512,192]{1,0:T(8,128)(2,1)S(1)}, u32[]{:S(2)}, u32[]{:S(2)}) %collective-permute-start.30) | collective-permute-done | bytes 196640 | tf_op jit(solution)/shard_map/ppermute | solution.py:241
  367.4 7.0 collective-permute-done.56
  381.3 5.5 broadcast_select_fusion.2
  392.4 6.0 collective-permute-done.44
  398.3 5.2 collective-permute-start.43
  403.7 6.6 collective-permute-done.43
  418.2 15.4 %collective-permute-done.48 = bf16[128,3072]{1,0:T(8,128)(2,1)S(1)} collective-permute-done((bf16[128,3072]{1,0:T(8,128)(2,1)S(1)}, bf16[128,3072]{1,0:T(8,128)(2,1)S(1)}, u32[]{:S(2)}, u32[]{:S(2)}) %collective-permute-start.48) | collective-permute-done | bytes 786464 | tf_op jit(solution)/shard_map/ppermute | solution.py:227
  433.6 12.2 %collective-permute-done.47 = bf16[128,3072]{1,0:T(8,128)(2,1)S(1)} collective-permute-done((bf16[128,3072]{1,0:T(8,128)(2,1)S(1)}, bf16[128,3072]{1,0:T(8,128)(2,1)S(1)}, u32[]{:S(2)}, u32[]{:S(2)}) %collective-permute-start.47) | collective-permute-done | bytes 786464 | tf_op jit(solution)/shard_map/ppermute | solution.py:227
  446.7 12.9 %convolution_convert_fusion.3 = bf16[512,3072]{1,0:T(8,128)(2,1)} fusion(bf16[768,3072]{1,0:T(8,128)(2,1)} %broadcast_select_fusion.2, bf16[3072,768]{1,0:T(8,128)(2,1)} %broadcast_select_fusion.3, bf16[128,3072]{1,0:T(8,128)(2,1)} %copy-done.127, bf16[128,3072]{1,0:T(8,128)(2,1)} %copy-done.128, bf16[128,3072]{1,0:T(8,128)(2,1)} %collective-permute-done.46, ...), kind=kOutput, calls=%fused_computation.13 | convolution fusion | flops 4849532928 | bytes 15728640 | tf_op jit(solution)/shard_map/dot_general | solution.py:432
  467.1 15.9 %collective-permute-done.51 = bf16[128,3072]{1,0:T(8,128)(2,1)S(1)} collective-permute-done((bf16[128,3072]{1,0:T(8,128)(2,1)S(1)}, bf16[128,3072]{1,0:T(8,128)(2,1)S(1)}, u32[]{:S(2)}, u32[]{:S(2)}) %collective-permute-start.51) | collective-permute-done | bytes 786464 | tf_op jit(solution)/shard_map/ppermute | solution.py:234
  483.7 15.3 %collective-permute-done.50 = bf16[128,3072]{1,0:T(8,128)(2,1)S(1)} collective-permute-done((bf16[128,3072]{1,0:T(8,128)(2,1)S(1)}, bf16[128,3072]{1,0:T(8,128)(2,1)S(1)}, u32[]{:S(2)}, u32[]{:S(2)}) %collective-permute-start.50) | collective-permute-done | bytes 786464 | tf_op jit(solution)/shard_map/ppermute | solution.py:234
  510.6 7.3 collective-permute-done.53
  532.5 14.6 %collective-permute-done.62 = bf16[128,896]{1,0:T(8,128)(2,1)S(1)} collective-permute-done((bf16[128,896]{1,0:T(8,128)(2,1)S(1)}, bf16[128,896]{1,0:T(8,128)(2,1)S(1)}, u32[]{:S(2)}, u32[]{:S(2)}) %collective-permute-start.62) | collective-permute-done | bytes 229408 | tf_op jit(solution)/shard_map/ppermute | solution.py:241
  558.0 6.3 collective-permute-done.78
  566.6 20.8 %collective-permute-done.65 = bf16[128,3072]{1,0:T(8,128)(2,1)S(1)} collective-permute-done((bf16[128,3072]{1,0:T(8,128)(2,1)S(1)}, bf16[128,3072]{1,0:T(8,128)(2,1)S(1)}, u32[]{:S(2)}, u32[]{:S(2)}) %collective-permute-start.65) | collective-permute-done | bytes 786464 | tf_op jit(solution)/shard_map/ppermute | solution.py:227
  587.4 4.7 fusion.81
  604.5 13.2 %collective-permute-done.73 = bf16[128,3072]{1,0:T(8,128)(2,1)S(1)} collective-permute-done((bf16[128,3072]{1,0:T(8,128)(2,1)S(1)}, bf16[128,3072]{1,0:T(8,128)(2,1)S(1)}, u32[]{:S(2)}, u32[]{:S(2)}) %collective-permute-start.73) | collective-permute-done | bytes 786464 | tf_op jit(solution)/shard_map/ppermute | solution.py:234
  619.3 15.4 %collective-permute-done.72 = bf16[128,3072]{1,0:T(8,128)(2,1)S(1)} collective-permute-done((bf16[128,3072]{1,0:T(8,128)(2,1)S(1)}, bf16[128,3072]{1,0:T(8,128)(2,1)S(1)}, u32[]{:S(2)}, u32[]{:S(2)}) %collective-permute-start.72) | collective-permute-done | bytes 786464 | tf_op jit(solution)/shard_map/ppermute | solution.py:234
  636.0 6.6 collective-permute-start.76
  642.6 9.0 collective-permute-done.82
  651.5 15.9 %collective-permute-done.81 = bf16[128,3072]{1,0:T(8,128)(2,1)S(1)} collective-permute-done((bf16[128,3072]{1,0:T(8,128)(2,1)S(1)}, bf16[128,3072]{1,0:T(8,128)(2,1)S(1)}, u32[]{:S(2)}, u32[]{:S(2)}) %collective-permute-start.81) | collective-permute-done | bytes 786464 | tf_op jit(solution)/shard_map/ppermute | solution.py:227
  671.6 8.2 collective-permute-start.75
  680.8 34.3 %collective-permute-done.75 = bf16[128,768]{1,0:T(8,128)(2,1)S(1)} collective-permute-done((bf16[128,768]{1,0:T(8,128)(2,1)S(1)}, bf16[128,768]{1,0:T(8,128)(2,1)S(1)}, u32[]{:S(2)}, u32[]{:S(2)}) %collective-permute-start.75) | collective-permute-done | bytes 196640 | tf_op jit(solution)/shard_map/ppermute | solution.py:250
  722.6 5.4 collective-permute-start.84
  736.0 5.6 collective-permute-done.84
  756.4 8.3 collective-permute-done.87
  776.2 6.0 broadcast_select_fusion.1
  782.4 56.5 %collective-permute-start.93 = (bf16[3,1024,128]{2,1,0:T(8,128)(2,1)S(1)}, bf16[3,1024,128]{2,1,0:T(8,128)(2,1)S(1)}, u32[]{:S(2)}, u32[]{:S(2)}) collective-permute-start(bf16[3,1024,128]{2,1,0:T(8,128)(2,1)S(1)} %bitcast_select_fusion), channel_id=1, source_target_pairs={{0,16},{16,0},{1,17},{17,1},{2,18},{18,2},{3,19},{19,3},{4,20},{20... | collective-permute-start | bytes 2359304 | tf_op jit(solution)/shard_map/ppermute | solution.py:205
  849.6 7.2 collective-permute-done.105
  857.0 5.2 attend.7
  862.2 8.1 collective-permute-start.121
  871.0 6.1 broadcast_select_fusion
  877.1 5.2 attend.6
  886.7 7.6 collective-permute-done.120
  900.2 13.5 %collective-permute-done.95 = bf16[512,192]{1,0:T(8,128)(2,1)S(1)} collective-permute-done((bf16[512,192]{1,0:T(8,128)(2,1)S(1)}, bf16[512,192]{1,0:T(8,128)(2,1)S(1)}, u32[]{:S(2)}, u32[]{:S(2)}) %collective-permute-start.95) | collective-permute-done | bytes 196640 | tf_op jit(solution)/shard_map/ppermute | solution.py:241
  935.7 23.2 %collective-permute-done.126 = bf16[128,896]{1,0:T(8,128)(2,1)S(1)} collective-permute-done((bf16[128,896]{1,0:T(8,128)(2,1)S(1)}, bf16[128,896]{1,0:T(8,128)(2,1)S(1)}, u32[]{:S(2)}, u32[]{:S(2)}) %collective-permute-start.126) | collective-permute-done | bytes 229408 | tf_op jit(solution)/shard_map/ppermute | solution.py:241
  962.7 6.5 collective-permute-done.108
  975.7 7.1 collective-permute-done.130
  984.0 15.6 %collective-permute-done.129 = bf16[128,3072]{1,0:T(8,128)(2,1)S(1)} collective-permute-done((bf16[128,3072]{1,0:T(8,128)(2,1)S(1)}, bf16[128,3072]{1,0:T(8,128)(2,1)S(1)}, u32[]{:S(2)}, u32[]{:S(2)}) %collective-permute-start.129) | collective-permute-done | bytes 786464 | tf_op jit(solution)/shard_map/ppermute | solution.py:227
  1000.7 13.0 %convolution_convert_fusion = bf16[512,3072]{1,0:T(8,128)(2,1)} fusion(bf16[768,3072]{1,0:T(8,128)(2,1)} %broadcast_select_fusion, bf16[3072,768]{1,0:T(8,128)(2,1)} %broadcast_select_fusion.1, bf16[128,3072]{1,0:T(8,128)(2,1)} %copy-done.125, bf16[128,3072]{1,0:T(8,128)(2,1)} %copy-done.126, bf16[128,3072]{1,0:T(8,128)(2,1)} %collective-permute-done.128, ...), kind=kOutput, calls=%fused_computation.10 | convolution fusion | flops 4849532928 | bytes 15728640 | tf_op jit(solution)/shard_map/dot_general | solution.py:432
  1019.2 14.2 %collective-permute-done.111 = bf16[128,3072]{1,0:T(8,128)(2,1)} collective-permute-done((bf16[128,3072]{1,0:T(8,128)(2,1)}, bf16[128,3072]{1,0:T(8,128)(2,1)}, u32[]{:S(2)}, u32[]{:S(2)}) %collective-permute-start.111) | collective-permute-done | bytes 786464 | tf_op jit(solution)/shard_map/ppermute | solution.py:227
  1034.5 13.1 %convolution_convert_fusion.1 = bf16[512,3072]{1,0:T(8,128)(2,1)} fusion(bf16[768,3072]{1,0:T(8,128)(2,1)} %broadcast_select_fusion, bf16[3072,768]{1,0:T(8,128)(2,1)} %broadcast_select_fusion.1, bf16[128,3072]{1,0:T(8,128)(2,1)} %collective-permute-done.112, bf16[128,3072]{1,0:T(8,128)(2,1)} %collective-permute-done.111, ...), kind=kOutput, calls=%fused_computation.11 | convolution fusion | flops 4849532928 | bytes 15728640 | tf_op jit(solution)/shard_map/dot_general | solution.py:432
  1051.9 15.2 %collective-permute-done.132 = bf16[128,3072]{1,0:T(8,128)(2,1)} collective-permute-done((bf16[128,3072]{1,0:T(8,128)(2,1)}, bf16[128,3072]{1,0:T(8,128)(2,1)}, u32[]{:S(2)}, u32[]{:S(2)}) %collective-permute-start.132) | collective-permute-done | bytes 786464 | tf_op jit(solution)/shard_map/ppermute | solution.py:234
  1070.7 13.3 %collective-permute-done.115 = bf16[128,3072]{1,0:T(8,128)(2,1)S(1)} collective-permute-done((bf16[128,3072]{1,0:T(8,128)(2,1)S(1)}, bf16[128,3072]{1,0:T(8,128)(2,1)S(1)}, u32[]{:S(2)}, u32[]{:S(2)}) %collective-permute-start.115) | collective-permute-done | bytes 786464 | tf_op jit(solution)/shard_map/ppermute | solution.py:234
  1084.0 16.3 %collective-permute-done.114 = bf16[128,3072]{1,0:T(8,128)(2,1)S(1)} collective-permute-done((bf16[128,3072]{1,0:T(8,128)(2,1)S(1)}, bf16[128,3072]{1,0:T(8,128)(2,1)S(1)}, u32[]{:S(2)}, u32[]{:S(2)}) %collective-permute-start.114) | collective-permute-done | bytes 786464 | tf_op jit(solution)/shard_map/ppermute | solution.py:234
  1109.9 5.6 collective-permute-done.118
  1115.5 7.3 collective-permute-done.117
  (798 shorter events, 357.3 us)
Async XLA Ops:
  4.6 151.3 %collective-permute-start.17 = (bf16[128,896]{1,0:T(8,128)(2,1)}, bf16[128,896]{1,0:T(8,128)(2,1)S(1)}, u32[]{:S(2)}, u32[]{:S(2)}) collective-permute-start(bf16[128,896]{1,0:T(8,128)(2,1)} %pad_maximum_fusion.18), channel_id=1, source_target_pairs={{0,3},{1,0},{2,1},{3,2},{4,7},{5,4},{6,5},{7,6},{8,11},{9,8},{10,9... | collective-permute-start | bytes 688136 | tf_op jit(solution)/shard_map/ppermute | solution.py:241
  9.7 138.0 %collective-permute-start.16 = (bf16[128,896]{1,0:T(8,128)(2,1)}, bf16[128,896]{1,0:T(8,128)(2,1)}, u32[]{:S(2)}, u32[]{:S(2)}) collective-permute-start(bf16[128,896]{1,0:T(8,128)(2,1)} %pad_maximum_fusion.18), channel_id=1, source_target_pairs={{0,2},{1,3},{2,0},{3,1},{4,6},{5,7},{6,4},{7,5},{8,10},{9,11},{10,... | collective-permute-start | bytes 688136 | tf_op jit(solution)/shard_map/ppermute | solution.py:241
  15.6 38.6 %collective-permute-start.2 = (f32[2,4,3,768]{3,0,2,1:T(2,128)}, f32[2,4,3,768]{3,0,2,1:T(2,128)}, u32[]{:S(2)}, u32[]{:S(2)}) collective-permute-start(f32[2,4,3,768]{3,0,2,1:T(2,128)} %bitcast.7), channel_id=1, source_target_pairs={{0,3},{1,0},{2,1},{3,2},{4,7},{5,4},{6,5},{7,6},{8,11},{9,8},{10,9... | collective-permute-start | bytes 221192 | tf_op jit(solution)/shard_map/ppermute | solution.py:241
  16.0 40.0 %collective-permute-start.1 = (f32[2,4,3,768]{3,0,2,1:T(2,128)}, f32[2,4,3,768]{3,0,2,1:T(2,128)}, u32[]{:S(2)}, u32[]{:S(2)}) collective-permute-start(f32[2,4,3,768]{3,0,2,1:T(2,128)} %bitcast.7), channel_id=1, source_target_pairs={{0,2},{1,3},{2,0},{3,1},{4,6},{5,7},{6,4},{7,5},{8,10},{9,11},{10,... | collective-permute-start | bytes 221192 | tf_op jit(solution)/shard_map/ppermute | solution.py:241
  18.5 32.6 %collective-permute-start.14 = (f32[4,64]{1,0:T(4,128)}, f32[4,64]{1,0:T(4,128)}, u32[]{:S(2)}, u32[]{:S(2)}) collective-permute-start(f32[4,64]{1,0:T(4,128)} %bitcast.48), channel_id=1, source_target_pairs={{0,16},{16,0},{1,17},{17,1},{2,18},{18,2},{3,19},{19,3},{4,20},{20... | collective-permute-start | bytes 3080 | tf_op jit(solution)/shard_map/ppermute | solution.py:205
  54.2 46.5 %collective-permute-start.6 = (bf16[128,896]{1,0:T(8,128)(2,1)}, bf16[128,896]{1,0:T(8,128)(2,1)S(1)}, u32[]{:S(2)}, u32[]{:S(2)}) collective-permute-start(bf16[128,896]{1,0:T(8,128)(2,1)} %pad_maximum_fusion.17), channel_id=1, source_target_pairs={{0,3},{1,0},{2,1},{3,2},{4,7},{5,4},{6,5},{7,6},{8,11},{9,8},{10,9... | collective-permute-start | bytes 688136 | tf_op jit(solution)/shard_map/ppermute | solution.py:241
  98.3 43.2 %collective-permute-start.11 = (bf16[768,576]{0,1:T(8,128)(2,1)S(1)}, bf16[768,576]{0,1:T(8,128)(2,1)S(1)}, u32[]{:S(2)}, u32[]{:S(2)}) collective-permute-start(bf16[768,576]{0,1:T(8,128)(2,1)S(1)} %bitcast.297), channel_id=1, source_target_pairs={{0,2},{1,3},{2,0},{3,1},{4,6},{5,7},{6,4},{7,5},{8,10},{9,11},{10,... | collective-permute-start | bytes 2654216 | tf_op jit(solution)/shard_map/ppermute | solution.py:263
  102.3 39.1 %collective-permute-start.10 = (bf16[768,576]{0,1:T(8,128)(2,1)S(1)}, bf16[768,576]{0,1:T(8,128)(2,1)S(1)}, u32[]{:S(2)}, u32[]{:S(2)}) collective-permute-start(bf16[768,576]{0,1:T(8,128)(2,1)S(1)} %bitcast.296), channel_id=1, source_target_pairs={{0,1},{1,2},{2,3},{3,0},{4,5},{5,6},{6,7},{7,4},{8,9},{9,10},{10,1... | collective-permute-start | bytes 2654216 | tf_op jit(solution)/shard_map/ppermute | solution.py:263
  110.5 40.6 %collective-permute-start.15 = (bf16[128,896]{1,0:T(8,128)(2,1)}, bf16[128,896]{1,0:T(8,128)(2,1)S(1)}, u32[]{:S(2)}, u32[]{:S(2)}) collective-permute-start(bf16[128,896]{1,0:T(8,128)(2,1)} %pad_maximum_fusion.18), channel_id=1, source_target_pairs={{0,1},{1,2},{2,3},{3,0},{4,5},{5,6},{6,7},{7,4},{8,9},{9,10},{10,1... | collective-permute-start | bytes 688136 | tf_op jit(solution)/shard_map/ppermute | solution.py:241
  141.9 72.8 %collective-permute-start.13 = (bf16[3072,576]{0,1:T(8,128)(2,1)S(1)}, bf16[3072,576]{0,1:T(8,128)(2,1)S(1)}, u32[]{:S(2)}, u32[]{:S(2)}) collective-permute-start(bf16[3072,576]{0,1:T(8,128)(2,1)S(1)} %pad_maximum_fusion.4), channel_id=1, source_target_pairs={{0,16},{1,17},{2,18},{3,19},{4,20},{5,21},{6,22},{7,23},{8,24},{9,... | collective-permute-start | bytes 10616840 | tf_op jit(solution)/shard_map/ppermute | solution.py:266
  147.7 53.6 %collective-permute-start.22 = (bf16[768,768]{1,0:T(8,128)(2,1)S(1)}, bf16[768,768]{1,0:T(8,128)(2,1)S(1)}, u32[]{:S(2)}, u32[]{:S(2)}) collective-permute-start(bf16[768,768]{1,0:T(8,128)(2,1)S(1)} %get-tuple-element.160), channel_id=1, source_target_pairs={{0,2},{1,3},{2,0},{3,1},{4,6},{5,7},{6,4},{7,5},{8,10},{9,11},{10,... | collective-permute-start | bytes 3538952 | tf_op jit(solution)/shard_map/ppermute | solution.py:263
  151.0 51.7 %collective-permute-start.21 = (bf16[768,768]{1,0:T(8,128)(2,1)S(1)}, bf16[768,768]{1,0:T(8,128)(2,1)S(1)}, u32[]{:S(2)}, u32[]{:S(2)}) collective-permute-start(bf16[768,768]{1,0:T(8,128)(2,1)S(1)} %get-tuple-element.161), channel_id=1, source_target_pairs={{0,1},{1,2},{2,3},{3,0},{4,5},{5,6},{6,7},{7,4},{8,9},{9,10},{10,1... | collective-permute-start | bytes 3538952 | tf_op jit(solution)/shard_map/ppermute | solution.py:263
  158.6 51.9 %collective-permute-start.9 = (bf16[128,3072]{1,0:T(8,128)(2,1)S(1)}, bf16[128,3072]{1,0:T(8,128)(2,1)S(1)}, u32[]{:S(2)}, u32[]{:S(2)}) collective-permute-start(bf16[128,3072]{1,0:T(8,128)(2,1)S(1)} %fusion.99), channel_id=1, source_target_pairs={{0,12},{4,8},{8,4},{12,0},{1,13},{5,9},{9,5},{13,1},{2,14},{6,10},... | collective-permute-start | bytes 2359304 | tf_op jit(solution)/shard_map/ppermute | solution.py:227
  165.3 45.2 %collective-permute-start.8 = (bf16[128,3072]{1,0:T(8,128)(2,1)S(1)}, bf16[128,3072]{1,0:T(8,128)(2,1)S(1)}, u32[]{:S(2)}, u32[]{:S(2)}) collective-permute-start(bf16[128,3072]{1,0:T(8,128)(2,1)S(1)} %fusion.99), channel_id=1, source_target_pairs={{0,8},{4,12},{8,0},{12,4},{1,9},{5,13},{9,1},{13,5},{2,10},{6,14},... | collective-permute-start | bytes 2359304 | tf_op jit(solution)/shard_map/ppermute | solution.py:227
  205.3 106.5 %collective-permute-start.24 = (bf16[3072,768]{1,0:T(8,128)(2,1)}, bf16[3072,768]{1,0:T(8,128)(2,1)}, u32[]{:S(2)}, u32[]{:S(2)}) collective-permute-start(bf16[3072,768]{1,0:T(8,128)(2,1)} %pad_maximum_fusion), channel_id=1, source_target_pairs={{0,16},{1,17},{2,18},{3,19},{4,20},{5,21},{6,22},{7,23},{8,24},{9,... | collective-permute-start | bytes 14155784 | tf_op jit(solution)/shard_map/ppermute | solution.py:266
  210.5 130.2 %collective-permute-start.32 = (bf16[768,768]{1,0:T(8,128)(2,1)}, bf16[768,768]{1,0:T(8,128)(2,1)}, u32[]{:S(2)}, u32[]{:S(2)}) collective-permute-start(bf16[768,768]{1,0:T(8,128)(2,1)} %pad_maximum_fusion.6), channel_id=1, source_target_pairs={{0,16},{16,0},{1,17},{17,1},{2,18},{18,2},{3,19},{19,3},{4,20},{20... | collective-permute-start | bytes 3538952 | tf_op jit(solution)/shard_map/ppermute | solution.py:205
  213.2 35.0 %collective-permute-start.19 = (bf16[128,3072]{1,0:T(8,128)(2,1)S(1)}, bf16[128,3072]{1,0:T(8,128)(2,1)S(1)}, u32[]{:S(2)}, u32[]{:S(2)}) collective-permute-start(bf16[128,3072]{1,0:T(8,128)(2,1)S(1)} %fusion.101), channel_id=1, source_target_pairs={{0,8},{4,12},{8,0},{12,4},{1,9},{5,13},{9,1},{13,5},{2,10},{6,14},... | collective-permute-start | bytes 2359304 | tf_op jit(solution)/shard_map/ppermute | solution.py:227
  214.7 35.4 %collective-permute-start.18 = (bf16[128,3072]{1,0:T(8,128)(2,1)S(1)}, bf16[128,3072]{1,0:T(8,128)(2,1)S(1)}, u32[]{:S(2)}, u32[]{:S(2)}) collective-permute-start(bf16[128,3072]{1,0:T(8,128)(2,1)S(1)} %fusion.101), channel_id=1, source_target_pairs={{0,4},{4,0},{8,12},{12,8},{1,5},{5,1},{9,13},{13,9},{2,6},{6,2},{1... | collective-permute-start | bytes 2359304 | tf_op jit(solution)/shard_map/ppermute | solution.py:227
  248.3 50.5 %collective-permute-start.37 = (bf16[768,768]{1,0:T(8,128)(2,1)}, bf16[768,768]{1,0:T(8,128)(2,1)}, u32[]{:S(2)}, u32[]{:S(2)}) collective-permute-start(bf16[768,768]{1,0:T(8,128)(2,1)} %get-tuple-element.156), channel_id=1, source_target_pairs={{0,2},{1,3},{2,0},{3,1},{4,6},{5,7},{6,4},{7,5},{8,10},{9,11},{10,... | collective-permute-start | bytes 3538952 | tf_op jit(solution)/shard_map/ppermute | solution.py:263
  250.2 48.6 %collective-permute-start.36 = (bf16[768,768]{1,0:T(8,128)(2,1)}, bf16[768,768]{1,0:T(8,128)(2,1)}, u32[]{:S(2)}, u32[]{:S(2)}) collective-permute-start(bf16[768,768]{1,0:T(8,128)(2,1)} %get-tuple-element.157), channel_id=1, source_target_pairs={{0,1},{1,2},{2,3},{3,0},{4,5},{5,6},{6,7},{7,4},{8,9},{9,10},{10,1... | collective-permute-start | bytes 3538952 | tf_op jit(solution)/shard_map/ppermute | solution.py:263
  303.7 77.6 %collective-permute-start.39 = (bf16[768,3072]{1,0:T(8,128)(2,1)}, bf16[768,3072]{1,0:T(8,128)(2,1)}, u32[]{:S(2)}, u32[]{:S(2)}) collective-permute-start(bf16[768,3072]{1,0:T(8,128)(2,1)} %pad_maximum_fusion.1), channel_id=1, source_target_pairs={{0,16},{1,17},{2,18},{3,19},{4,20},{5,21},{6,22},{7,23},{8,24},{9,... | collective-permute-start | bytes 14155784 | tf_op jit(solution)/shard_map/ppermute | solution.py:266
  329.4 33.9 %collective-permute-start.30 = (bf16[512,192]{1,0:T(8,128)(2,1)S(1)}, bf16[512,192]{1,0:T(8,128)(2,1)S(1)}, u32[]{:S(2)}, u32[]{:S(2)}) collective-permute-start(bf16[512,192]{1,0:T(8,128)(2,1)S(1)} %attend.4), channel_id=1, source_target_pairs={{0,2},{1,3},{2,0},{3,1},{4,6},{5,7},{6,4},{7,5},{8,10},{9,11},{10,... | collective-permute-start | bytes 589832 | tf_op jit(solution)/shard_map/ppermute | solution.py:241
  329.4 33.9 %collective-permute-start.29 = (bf16[512,192]{1,0:T(8,128)(2,1)S(1)}, bf16[512,192]{1,0:T(8,128)(2,1)S(1)}, u32[]{:S(2)}, u32[]{:S(2)}) collective-permute-start(bf16[512,192]{1,0:T(8,128)(2,1)S(1)} %attend.4), channel_id=1, source_target_pairs={{0,1},{1,2},{2,3},{3,0},{4,5},{5,6},{6,7},{7,4},{8,9},{9,10},{10,1... | collective-permute-start | bytes 589832 | tf_op jit(solution)/shard_map/ppermute | solution.py:241
  340.8 33.6 %collective-permute-start.56 = (bf16[512,192]{1,0:T(8,128)(2,1)S(1)}, bf16[512,192]{1,0:T(8,128)(2,1)S(1)}, u32[]{:S(2)}, u32[]{:S(2)}) collective-permute-start(bf16[512,192]{1,0:T(8,128)(2,1)S(1)} %attend.5), channel_id=1, source_target_pairs={{0,2},{1,3},{2,0},{3,1},{4,6},{5,7},{6,4},{7,5},{8,10},{9,11},{10,... | collective-permute-start | bytes 589832 | tf_op jit(solution)/shard_map/ppermute | solution.py:241
  413.7 32.2 %collective-permute-start.47 = (bf16[128,3072]{1,0:T(8,128)(2,1)S(1)}, bf16[128,3072]{1,0:T(8,128)(2,1)S(1)}, u32[]{:S(2)}, u32[]{:S(2)}) collective-permute-start(bf16[128,3072]{1,0:T(8,128)(2,1)S(1)} %fusion.103), channel_id=1, source_target_pairs={{0,8},{4,12},{8,0},{12,4},{1,9},{5,13},{9,1},{13,5},{2,10},{6,14},... | collective-permute-start | bytes 2359304 | tf_op jit(solution)/shard_map/ppermute | solution.py:227
  414.9 31.8 %collective-permute-start.46 = (bf16[128,3072]{1,0:T(8,128)(2,1)S(1)}, bf16[128,3072]{1,0:T(8,128)(2,1)}, u32[]{:S(2)}, u32[]{:S(2)}) collective-permute-start(bf16[128,3072]{1,0:T(8,128)(2,1)S(1)} %fusion.103), channel_id=1, source_target_pairs={{0,4},{4,0},{8,12},{12,8},{1,5},{5,1},{9,13},{13,9},{2,6},{6,2},{1... | collective-permute-start | bytes 2359304 | tf_op jit(solution)/shard_map/ppermute | solution.py:227
  463.8 35.2 %collective-permute-start.50 = (bf16[128,3072]{1,0:T(8,128)(2,1)S(1)}, bf16[128,3072]{1,0:T(8,128)(2,1)S(1)}, u32[]{:S(2)}, u32[]{:S(2)}) collective-permute-start(bf16[128,3072]{1,0:T(8,128)(2,1)S(1)} %get-tuple-element.178), channel_id=1, source_target_pairs={{0,8},{4,12},{8,0},{12,4},{1,9},{5,13},{9,1},{13,5},{2,10},{6,14},... | collective-permute-start | bytes 2359304 | tf_op jit(solution)/shard_map/ppermute | solution.py:234
  465.2 34.0 %collective-permute-start.49 = (bf16[128,3072]{1,0:T(8,128)(2,1)S(1)}, bf16[128,3072]{1,0:T(8,128)(2,1)S(1)}, u32[]{:S(2)}, u32[]{:S(2)}) collective-permute-start(bf16[128,3072]{1,0:T(8,128)(2,1)S(1)} %get-tuple-element.176), channel_id=1, source_target_pairs={{0,4},{4,0},{8,12},{12,8},{1,5},{5,1},{9,13},{13,9},{2,6},{6,2},{1... | collective-permute-start | bytes 2359304 | tf_op jit(solution)/shard_map/ppermute | solution.py:234
  465.7 37.3 %collective-permute-start.69 = (bf16[768,576]{0,1:T(8,128)(2,1)S(1)}, bf16[768,576]{0,1:T(8,128)(2,1)S(1)}, u32[]{:S(2)}, u32[]{:S(2)}) collective-permute-start(bf16[768,576]{0,1:T(8,128)(2,1)S(1)} %get-tuple-element.163), channel_id=1, source_target_pairs={{16,19},{17,16},{18,17},{19,18},{20,23},{21,20},{22,21},{23,22},{2... | collective-permute-start | bytes 2654216 | tf_op jit(solution)/shard_map/ppermute | solution.py:263
  466.4 38.4 %collective-permute-start.68 = (bf16[768,576]{0,1:T(8,128)(2,1)S(1)}, bf16[768,576]{0,1:T(8,128)(2,1)S(1)}, u32[]{:S(2)}, u32[]{:S(2)}) collective-permute-start(bf16[768,576]{0,1:T(8,128)(2,1)S(1)} %get-tuple-element.164), channel_id=1, source_target_pairs={{16,18},{17,19},{18,16},{19,17},{20,22},{21,23},{22,20},{23,21},{2... | collective-permute-start | bytes 2654216 | tf_op jit(solution)/shard_map/ppermute | solution.py:263
  505.3 86.8 %collective-permute-start.70 = (bf16[3072,576]{0,1:T(8,128)(2,1)S(1)}, bf16[3072,576]{0,1:T(8,128)(2,1)S(1)}, u32[]{:S(2)}, u32[]{:S(2)}) collective-permute-start(bf16[3072,576]{0,1:T(8,128)(2,1)S(1)} %pad_maximum_fusion.5), channel_id=1, source_target_pairs={{16,0},{17,1},{18,2},{19,3},{20,4},{21,5},{22,6},{23,7},{24,8},{25... | collective-permute-start | bytes 10616840 | tf_op jit(solution)/shard_map/ppermute | solution.py:266
  525.1 31.8 %collective-permute-start.79 = (bf16[128,896]{1,0:T(8,128)(2,1)S(1)}, bf16[128,896]{1,0:T(8,128)(2,1)S(1)}, u32[]{:S(2)}, u32[]{:S(2)}) collective-permute-start(bf16[128,896]{1,0:T(8,128)(2,1)S(1)} %pad_maximum_fusion.21), channel_id=1, source_target_pairs={{0,3},{1,0},{2,1},{3,2},{4,7},{5,4},{6,5},{7,6},{8,11},{9,8},{10,9... | collective-permute-start | bytes 688136 | tf_op jit(solution)/shard_map/ppermute | solution.py:241
  529.2 35.1 %collective-permute-start.78 = (bf16[128,896]{1,0:T(8,128)(2,1)S(1)}, bf16[128,896]{1,0:T(8,128)(2,1)S(1)}, u32[]{:S(2)}, u32[]{:S(2)}) collective-permute-start(bf16[128,896]{1,0:T(8,128)(2,1)S(1)} %pad_maximum_fusion.21), channel_id=1, source_target_pairs={{0,2},{1,3},{2,0},{3,1},{4,6},{5,7},{6,4},{7,5},{8,10},{9,11},{10,... | collective-permute-start | bytes 688136 | tf_op jit(solution)/shard_map/ppermute | solution.py:241
  555.4 32.0 %collective-permute-start.65 = (bf16[128,3072]{1,0:T(8,128)(2,1)S(1)}, bf16[128,3072]{1,0:T(8,128)(2,1)S(1)}, u32[]{:S(2)}, u32[]{:S(2)}) collective-permute-start(bf16[128,3072]{1,0:T(8,128)(2,1)S(1)} %fusion.105), channel_id=1, source_target_pairs={{0,8},{4,12},{8,0},{12,4},{1,9},{5,13},{9,1},{13,5},{2,10},{6,14},... | collective-permute-start | bytes 2359304 | tf_op jit(solution)/shard_map/ppermute | solution.py:227
  556.9 30.5 %collective-permute-start.64 = (bf16[128,3072]{1,0:T(8,128)(2,1)S(1)}, bf16[128,3072]{1,0:T(8,128)(2,1)S(1)}, u32[]{:S(2)}, u32[]{:S(2)}) collective-permute-start(bf16[128,3072]{1,0:T(8,128)(2,1)S(1)} %fusion.105), channel_id=1, source_target_pairs={{0,4},{4,0},{8,12},{12,8},{1,5},{5,1},{9,13},{13,9},{2,6},{6,2},{1... | collective-permute-start | bytes 2359304 | tf_op jit(solution)/shard_map/ppermute | solution.py:227
  598.0 36.7 %collective-permute-start.72 = (bf16[128,3072]{1,0:T(8,128)(2,1)S(1)}, bf16[128,3072]{1,0:T(8,128)(2,1)S(1)}, u32[]{:S(2)}, u32[]{:S(2)}) collective-permute-start(bf16[128,3072]{1,0:T(8,128)(2,1)S(1)} %get-tuple-element.181), channel_id=1, source_target_pairs={{0,8},{4,12},{8,0},{12,4},{1,9},{5,13},{9,1},{13,5},{2,10},{6,14},... | collective-permute-start | bytes 2359304 | tf_op jit(solution)/shard_map/ppermute | solution.py:234
  599.4 36.0 %collective-permute-start.71 = (bf16[128,3072]{1,0:T(8,128)(2,1)S(1)}, bf16[128,3072]{1,0:T(8,128)(2,1)S(1)}, u32[]{:S(2)}, u32[]{:S(2)}) collective-permute-start(bf16[128,3072]{1,0:T(8,128)(2,1)S(1)} %get-tuple-element.179), channel_id=1, source_target_pairs={{0,4},{4,0},{8,12},{12,8},{1,5},{5,1},{9,13},{13,9},{2,6},{6,2},{1... | collective-permute-start | bytes 2359304 | tf_op jit(solution)/shard_map/ppermute | solution.py:234
  600.9 50.7 %collective-permute-start.82 = (bf16[128,3072]{1,0:T(8,128)(2,1)S(1)}, bf16[128,3072]{1,0:T(8,128)(2,1)S(1)}, u32[]{:S(2)}, u32[]{:S(2)}) collective-permute-start(bf16[128,3072]{1,0:T(8,128)(2,1)S(1)} %fusion.107), channel_id=1, source_target_pairs={{0,12},{4,8},{8,4},{12,0},{1,13},{5,9},{9,5},{13,1},{2,14},{6,10},... | collective-permute-start | bytes 2359304 | tf_op jit(solution)/shard_map/ppermute | solution.py:227
  602.5 64.9 %collective-permute-start.81 = (bf16[128,3072]{1,0:T(8,128)(2,1)S(1)}, bf16[128,3072]{1,0:T(8,128)(2,1)S(1)}, u32[]{:S(2)}, u32[]{:S(2)}) collective-permute-start(bf16[128,3072]{1,0:T(8,128)(2,1)S(1)} %fusion.107), channel_id=1, source_target_pairs={{0,8},{4,12},{8,0},{12,4},{1,9},{5,13},{9,1},{13,5},{2,10},{6,14},... | collective-permute-start | bytes 2359304 | tf_op jit(solution)/shard_map/ppermute | solution.py:227
  617.8 49.7 %collective-permute-start.80 = (bf16[128,3072]{1,0:T(8,128)(2,1)S(1)}, bf16[128,3072]{1,0:T(8,128)(2,1)S(1)}, u32[]{:S(2)}, u32[]{:S(2)}) collective-permute-start(bf16[128,3072]{1,0:T(8,128)(2,1)S(1)} %fusion.107), channel_id=1, source_target_pairs={{0,4},{4,0},{8,12},{12,8},{1,5},{5,1},{9,13},{13,9},{2,6},{6,2},{1... | collective-permute-start | bytes 2359304 | tf_op jit(solution)/shard_map/ppermute | solution.py:227
  634.7 82.4 %collective-permute-start.91 = (bf16[768,768]{1,0:T(8,128)(2,1)S(1)}, bf16[768,768]{1,0:T(8,128)(2,1)S(1)}, u32[]{:S(2)}, u32[]{:S(2)}) collective-permute-start(bf16[768,768]{1,0:T(8,128)(2,1)S(1)} %get-tuple-element.151), channel_id=1, source_target_pairs={{16,19},{17,16},{18,17},{19,18},{20,23},{21,20},{22,21},{23,22},{2... | collective-permute-start | bytes 3538952 | tf_op jit(solution)/shard_map/ppermute | solution.py:263
  636.0 43.8 %collective-permute-start.76 = (bf16[128,768]{1,0:T(8,128)(2,1)S(1)}, bf16[128,768]{1,0:T(8,128)(2,1)S(1)}, u32[]{:S(2)}, u32[]{:S(2)}) collective-permute-start(bf16[128,768]{1,0:T(8,128)(2,1)S(1)} %get-tuple-element.212), channel_id=1, source_target_pairs={{0,1},{1,2},{2,3},{3,0},{4,5},{5,6},{6,7},{7,4},{8,9},{9,10},{10,1... | collective-permute-start | bytes 589832 | tf_op jit(solution)/shard_map/ppermute | solution.py:250
  670.1 48.0 %collective-permute-start.90 = (bf16[768,768]{1,0:T(8,128)(2,1)S(1)}, bf16[768,768]{1,0:T(8,128)(2,1)S(1)}, u32[]{:S(2)}, u32[]{:S(2)}) collective-permute-start(bf16[768,768]{1,0:T(8,128)(2,1)S(1)} %get-tuple-element.152), channel_id=1, source_target_pairs={{16,18},{17,19},{18,16},{19,17},{20,22},{21,23},{22,20},{23,21},{2... | collective-permute-start | bytes 3538952 | tf_op jit(solution)/shard_map/ppermute | solution.py:263
  670.9 47.3 %collective-permute-start.89 = (bf16[768,768]{1,0:T(8,128)(2,1)S(1)}, bf16[768,768]{1,0:T(8,128)(2,1)S(1)}, u32[]{:S(2)}, u32[]{:S(2)}) collective-permute-start(bf16[768,768]{1,0:T(8,128)(2,1)S(1)} %get-tuple-element.153), channel_id=1, source_target_pairs={{16,17},{17,18},{18,19},{19,16},{20,21},{21,22},{22,23},{23,20},{2... | collective-permute-start | bytes 3538952 | tf_op jit(solution)/shard_map/ppermute | solution.py:263
  671.6 43.5 %collective-permute-start.75 = (bf16[128,768]{1,0:T(8,128)(2,1)S(1)}, bf16[128,768]{1,0:T(8,128)(2,1)S(1)}, u32[]{:S(2)}, u32[]{:S(2)}) collective-permute-start(bf16[128,768]{1,0:T(8,128)(2,1)S(1)} %get-tuple-element.213), channel_id=1, source_target_pairs={{0,2},{1,3},{2,0},{3,1},{4,6},{5,7},{6,4},{7,5},{8,10},{9,11},{10,... | collective-permute-start | bytes 589832 | tf_op jit(solution)/shard_map/ppermute | solution.py:250
  679.8 36.1 %collective-permute-start.74 = (bf16[128,768]{1,0:T(8,128)(2,1)S(1)}, bf16[128,768]{1,0:T(8,128)(2,1)S(1)}, u32[]{:S(2)}, u32[]{:S(2)}) collective-permute-start(bf16[128,768]{1,0:T(8,128)(2,1)S(1)} %get-tuple-element.211), channel_id=1, source_target_pairs={{0,3},{1,0},{2,1},{3,2},{4,7},{5,4},{6,5},{7,6},{8,11},{9,8},{10,9... | collective-permute-start | bytes 589832 | tf_op jit(solution)/shard_map/ppermute | solution.py:250
  721.1 53.4 %collective-permute-start.92 = (bf16[3072,768]{1,0:T(8,128)(2,1)}, bf16[3072,768]{1,0:T(8,128)(2,1)}, u32[]{:S(2)}, u32[]{:S(2)}) collective-permute-start(bf16[3072,768]{1,0:T(8,128)(2,1)} %pad_maximum_fusion.2), channel_id=1, source_target_pairs={{16,0},{17,1},{18,2},{19,3},{20,4},{21,5},{22,6},{23,7},{24,8},{25... | collective-permute-start | bytes 14155784 | tf_op jit(solution)/shard_map/ppermute | solution.py:266
  730.9 140.1 %collective-permute-start.103 = (bf16[768,3072]{1,0:T(8,128)(2,1)}, bf16[768,3072]{1,0:T(8,128)(2,1)}, u32[]{:S(2)}, u32[]{:S(2)}) collective-permute-start(bf16[768,3072]{1,0:T(8,128)(2,1)} %pad_maximum_fusion.3), channel_id=1, source_target_pairs={{16,0},{17,1},{18,2},{19,3},{20,4},{21,5},{22,6},{23,7},{24,8},{25... | collective-permute-start | bytes 14155784 | tf_op jit(solution)/shard_map/ppermute | solution.py:266
  782.4 74.6 %collective-permute-start.93 = (bf16[3,1024,128]{2,1,0:T(8,128)(2,1)S(1)}, bf16[3,1024,128]{2,1,0:T(8,128)(2,1)S(1)}, u32[]{:S(2)}, u32[]{:S(2)}) collective-permute-start(bf16[3,1024,128]{2,1,0:T(8,128)(2,1)S(1)} %bitcast_select_fusion), channel_id=1, source_target_pairs={{0,16},{16,0},{1,17},{17,1},{2,18},{18,2},{3,19},{19,3},{4,20},{20... | collective-permute-start | bytes 2359304 | tf_op jit(solution)/shard_map/ppermute | solution.py:205
  926.1 33.7 %collective-permute-start.127 = (bf16[128,896]{1,0:T(8,128)(2,1)S(1)}, bf16[128,896]{1,0:T(8,128)(2,1)S(1)}, u32[]{:S(2)}, u32[]{:S(2)}) collective-permute-start(bf16[128,896]{1,0:T(8,128)(2,1)S(1)} %pad_maximum_fusion.24), channel_id=1, source_target_pairs={{0,3},{1,0},{2,1},{3,2},{4,7},{5,4},{6,5},{7,6},{8,11},{9,8},{10,9... | collective-permute-start | bytes 688136 | tf_op jit(solution)/shard_map/ppermute | solution.py:241
  926.2 32.7 %collective-permute-start.126 = (bf16[128,896]{1,0:T(8,128)(2,1)S(1)}, bf16[128,896]{1,0:T(8,128)(2,1)S(1)}, u32[]{:S(2)}, u32[]{:S(2)}) collective-permute-start(bf16[128,896]{1,0:T(8,128)(2,1)S(1)} %pad_maximum_fusion.24), channel_id=1, source_target_pairs={{0,2},{1,3},{2,0},{3,1},{4,6},{5,7},{6,4},{7,5},{8,10},{9,11},{10,... | collective-permute-start | bytes 688136 | tf_op jit(solution)/shard_map/ppermute | solution.py:241
  932.6 38.8 %collective-permute-start.109 = (bf16[128,896]{1,0:T(8,128)(2,1)S(1)}, bf16[128,896]{1,0:T(8,128)(2,1)S(1)}, u32[]{:S(2)}, u32[]{:S(2)}) collective-permute-start(bf16[128,896]{1,0:T(8,128)(2,1)S(1)} %pad_maximum_fusion.23), channel_id=1, source_target_pairs={{0,3},{1,0},{2,1},{3,2},{4,7},{5,4},{6,5},{7,6},{8,11},{9,8},{10,9... | collective-permute-start | bytes 688136 | tf_op jit(solution)/shard_map/ppermute | solution.py:241
  934.5 34.7 %collective-permute-start.108 = (bf16[128,896]{1,0:T(8,128)(2,1)S(1)}, bf16[128,896]{1,0:T(8,128)(2,1)S(1)}, u32[]{:S(2)}, u32[]{:S(2)}) collective-permute-start(bf16[128,896]{1,0:T(8,128)(2,1)S(1)} %pad_maximum_fusion.23), channel_id=1, source_target_pairs={{0,2},{1,3},{2,0},{3,1},{4,6},{5,7},{6,4},{7,5},{8,10},{9,11},{10,... | collective-permute-start | bytes 688136 | tf_op jit(solution)/shard_map/ppermute | solution.py:241
  959.5 163.7 %collective-permute-start.138 = (bf16[256,12,128]{2,0,1:T(8,128)(2,1)}, bf16[256,12,128]{2,0,1:T(8,128)(2,1)}, u32[]{:S(2)}, u32[]{:S(2)}) collective-permute-start(bf16[256,12,128]{2,0,1:T(8,128)(2,1)} %broadcast_select_fusion.12), channel_id=1, source_target_pairs={{0,16},{16,0},{1,17},{17,1},{2,18},{18,2},{3,19},{19,3},{4,20},{20... | collective-permute-start | bytes 2359304 | tf_op jit(solution)/shard_map/ppermute | solution.py:205
  973.8 44.7 %collective-permute-start.112 = (bf16[128,3072]{1,0:T(8,128)(2,1)}, bf16[128,3072]{1,0:T(8,128)(2,1)}, u32[]{:S(2)}, u32[]{:S(2)}) collective-permute-start(bf16[128,3072]{1,0:T(8,128)(2,1)} %fusion.111), channel_id=1, source_target_pairs={{0,12},{4,8},{8,4},{12,0},{1,13},{5,9},{9,5},{13,1},{2,14},{6,10},... | collective-permute-start | bytes 2359304 | tf_op jit(solution)/shard_map/ppermute | solution.py:227
  982.7 50.7 %collective-permute-start.111 = (bf16[128,3072]{1,0:T(8,128)(2,1)}, bf16[128,3072]{1,0:T(8,128)(2,1)}, u32[]{:S(2)}, u32[]{:S(2)}) collective-permute-start(bf16[128,3072]{1,0:T(8,128)(2,1)} %fusion.111), channel_id=1, source_target_pairs={{0,8},{4,12},{8,0},{12,4},{1,9},{5,13},{9,1},{13,5},{2,10},{6,14},... | collective-permute-start | bytes 2359304 | tf_op jit(solution)/shard_map/ppermute | solution.py:227
  999.6 34.9 %collective-permute-start.110 = (bf16[128,3072]{1,0:T(8,128)(2,1)}, bf16[128,3072]{1,0:T(8,128)(2,1)}, u32[]{:S(2)}, u32[]{:S(2)}) collective-permute-start(bf16[128,3072]{1,0:T(8,128)(2,1)} %fusion.111), channel_id=1, source_target_pairs={{0,4},{4,0},{8,12},{12,8},{1,5},{5,1},{9,13},{13,9},{2,6},{6,2},{1... | collective-permute-start | bytes 2359304 | tf_op jit(solution)/shard_map/ppermute | solution.py:227
  1016.9 34.3 %collective-permute-start.133 = (bf16[128,3072]{1,0:T(8,128)(2,1)}, bf16[128,3072]{1,0:T(8,128)(2,1)}, u32[]{:S(2)}, u32[]{:S(2)}) collective-permute-start(bf16[128,3072]{1,0:T(8,128)(2,1)} %get-tuple-element.174), channel_id=1, source_target_pairs={{0,12},{4,8},{8,4},{12,0},{1,13},{5,9},{9,5},{13,1},{2,14},{6,10},... | collective-permute-start | bytes 2359304 | tf_op jit(solution)/shard_map/ppermute | solution.py:234
  1018.5 48.6 %collective-permute-start.132 = (bf16[128,3072]{1,0:T(8,128)(2,1)}, bf16[128,3072]{1,0:T(8,128)(2,1)}, u32[]{:S(2)}, u32[]{:S(2)}) collective-permute-start(bf16[128,3072]{1,0:T(8,128)(2,1)} %get-tuple-element.175), channel_id=1, source_target_pairs={{0,8},{4,12},{8,0},{12,4},{1,9},{5,13},{9,1},{13,5},{2,10},{6,14},... | collective-permute-start | bytes 2359304 | tf_op jit(solution)/shard_map/ppermute | solution.py:234
  1033.4 34.8 %collective-permute-start.131 = (bf16[128,3072]{1,0:T(8,128)(2,1)}, bf16[128,3072]{1,0:T(8,128)(2,1)}, u32[]{:S(2)}, u32[]{:S(2)}) collective-permute-start(bf16[128,3072]{1,0:T(8,128)(2,1)} %get-tuple-element.173), channel_id=1, source_target_pairs={{0,4},{4,0},{8,12},{12,8},{1,5},{5,1},{9,13},{13,9},{2,6},{6,2},{1... | collective-permute-start | bytes 2359304 | tf_op jit(solution)/shard_map/ppermute | solution.py:234
  1049.4 34.5 %collective-permute-start.115 = (bf16[128,3072]{1,0:T(8,128)(2,1)S(1)}, bf16[128,3072]{1,0:T(8,128)(2,1)S(1)}, u32[]{:S(2)}, u32[]{:S(2)}) collective-permute-start(bf16[128,3072]{1,0:T(8,128)(2,1)S(1)} %get-tuple-element.171), channel_id=1, source_target_pairs={{0,12},{4,8},{8,4},{12,0},{1,13},{5,9},{9,5},{13,1},{2,14},{6,10},... | collective-permute-start | bytes 2359304 | tf_op jit(solution)/shard_map/ppermute | solution.py:234
  1051.2 49.1 %collective-permute-start.114 = (bf16[128,3072]{1,0:T(8,128)(2,1)S(1)}, bf16[128,3072]{1,0:T(8,128)(2,1)S(1)}, u32[]{:S(2)}, u32[]{:S(2)}) collective-permute-start(bf16[128,3072]{1,0:T(8,128)(2,1)S(1)} %get-tuple-element.172), channel_id=1, source_target_pairs={{0,8},{4,12},{8,0},{12,4},{1,9},{5,13},{9,1},{13,5},{2,10},{6,14},... | collective-permute-start | bytes 2359304 | tf_op jit(solution)/shard_map/ppermute | solution.py:234
  1067.1 37.0 %collective-permute-start.113 = (bf16[128,3072]{1,0:T(8,128)(2,1)S(1)}, bf16[128,3072]{1,0:T(8,128)(2,1)S(1)}, u32[]{:S(2)}, u32[]{:S(2)}) collective-permute-start(bf16[128,3072]{1,0:T(8,128)(2,1)S(1)} %get-tuple-element.170), channel_id=1, source_target_pairs={{0,4},{4,0},{8,12},{12,8},{1,5},{5,1},{9,13},{13,9},{2,6},{6,2},{1... | collective-permute-start | bytes 2359304 | tf_op jit(solution)/shard_map/ppermute | solution.py:234
  1070.6 35.2 %collective-permute-start.136 = (bf16[128,768]{1,0:T(8,128)(2,1)S(1)}, bf16[128,768]{1,0:T(8,128)(2,1)S(1)}, u32[]{:S(2)}, u32[]{:S(2)}) collective-permute-start(bf16[128,768]{1,0:T(8,128)(2,1)S(1)} %get-tuple-element.196), channel_id=1, source_target_pairs={{0,1},{1,2},{2,3},{3,0},{4,5},{5,6},{6,7},{7,4},{8,9},{9,10},{10,1... | collective-permute-start | bytes 589832 | tf_op jit(solution)/shard_map/ppermute | solution.py:250
  (217 other events, 5537.7 us)

commit v6 on v3

--- a/solution.py
+++ b/solution.py
@@ -196,8 +196,8 @@
         w_down[0],
     )
     n_narrow = lax.axis_size("narrow")
-    if n_narrow == lax.axis_size("wide") and stale_cache.shape[3] % n_narrow == 0:
-        return in_halves(*operands)
+    if n_narrow == 4 and lax.axis_size("wide") == 4 and stale_cache.shape[3] % n_narrow == 0:
+        return in_pairs(*operands)
     return features_split(*operands)
 
 
@@ -235,37 +235,38 @@
     return total
 
 
-def gather_line(block):
+def gather_direct(block):
     n = lax.axis_size("narrow")
-    me = lax.axis_index("narrow")
-    from_left = [block]
-    from_right = [block]
-    for step in range(1, n):
-        right = [(i, i + 1) for i in range(step - 1, n - 1)]
-        left = [(i + 1, i) for i in range(0, n - step)]
-        from_left.append(lax.ppermute(from_left[-1], "narrow", right))
-        from_right.append(lax.ppermute(from_right[-1], "narrow", left))
     return [block] + [
-        jnp.where(me >= step, from_left[step], from_right[n - step]) for step in range(1, n)
+        lax.ppermute(block, "narrow", [(i, (i + step) % n) for i in range(n)]) for step in range(1, n)
     ]
 
 
-def line_norm(values, model_width):
-    n = lax.axis_size("narrow")
+def to_mate(value):
+    return lax.ppermute(value, "narrow", [(i, i ^ 1) for i in range(lax.axis_size("narrow"))])
+
+
+def to_partner(value):
+    return lax.ppermute(value, "narrow", [(i, i ^ 2) for i in range(lax.axis_size("narrow"))])
+
+
+def pair_norm(values, table, kinds):
     width = values.shape[1]
     mean = jnp.mean(values, axis=1)
     center = values - mean[:, None]
     own = jnp.stack([mean, jnp.sum(center * center, axis=1)])
-    parts = [own]
-    for step in range(1, n):
-        parts.append(lax.ppermute(own, "narrow", [(i, (i + step) % n) for i in range(n)]))
-    whole_mean = sum(part[0] for part in parts) / n
-    spread = sum(part[1] + width * (part[0] - whole_mean) ** 2 for part in parts)
-    scale = lax.rsqrt(spread / model_width + EPS_ROW)
-    return (values - whole_mean[:, None]) * scale[:, None]
-
-
-def in_halves(
+    far = to_partner(own)
+    whole_mean = 0.5 * (own[0] + far[0])
+    spread = own[1] + far[1] + width * ((own[0] - whole_mean) ** 2 + (far[0] - whole_mean) ** 2)
+    scale = lax.rsqrt(spread / (2 * width) + EPS_ROW)
+    return modulate((values - whole_mean[:, None]) * scale[:, None], table, kinds)
+
+
+def ordered(*values):
+    return lax.optimization_barrier(values)
+
+
+def in_pairs(
     hidden_in,
     row_kind,
     positions,
@@ -284,16 +285,20 @@
     narrow_idx = lax.axis_index("narrow")
     section = lax.axis_index("section")
     lead = section == 0
+    odd = narrow_idx % 2
+    high = narrow_idx // 2
+    lower = high == 0
     _, rows_a, feat_a = hidden_in.shape
     halves = 2
     part = rows_a // halves
     total_rows = rows_a * n_wide
+    chunk = total_rows // halves
     rows_b = total_rows // n_narrow
     heads_local = stale_cache.shape[3]
     heads = heads_local // n_narrow
     pair = stale_cache.shape[4]
     head_dim = pair // 2
-    model_width = feat_a * n_narrow
+    head_group = [0, 2, 1, 3]
 
     def both_layers(own):
         other = swap(own)
@@ -304,14 +309,46 @@
         order = [lax.dynamic_index_in_dim(blocks, wide_idx ^ step, 0, False) for step in range(n_wide)]
         return jnp.stack(order, axis=1).reshape(total_rows)
 
+    def qkv_part(own, parity):
+        size = own.shape[1] // 4
+        starts = [(2 * parity + 1 - high) * size, (2 * parity + high) * size]
+        return jnp.concatenate([lax.dynamic_slice_in_dim(own, at, size, 1) for at in starts], axis=1)
+
+    def qkv_of(layer, own):
+        pairs = [(layer * n_narrow + i, layer * n_narrow + (i ^ 1)) for i in range(n_narrow)]
+        got = lax.ppermute(qkv_part(own, 1 - odd), ("section", "narrow"), pairs)
+        joined = jnp.concatenate([qkv_part(own, odd), got], axis=0)
+        passed = lax.ppermute(joined, "section", [(layer, 1 - layer)])
+        return jnp.where(section == layer, joined, passed)
+
+    def up_of(own):
+        size = own.shape[1] // 2
+        got = to_mate(lax.dynamic_slice_in_dim(own, (1 - odd) * size, size, 1))
+        kept = lax.dynamic_slice_in_dim(own, odd * size, size, 1)
+        return both_layers(jnp.concatenate([kept, got], axis=0))
+
+    def down_of(own):
+        size = own.shape[0] // 2
+        got = to_mate(lax.dynamic_slice_in_dim(own, (1 - odd) * size, size, 0))
+        kept = lax.dynamic_slice_in_dim(own, odd * size, size, 0)
+        return both_layers(jnp.concatenate([kept, got], axis=1))
+
+    layer_in = lax.dynamic_index_in_dim(hidden_in, section, 0, False)
+    layer_in = jnp.concatenate([layer_in, to_mate(layer_in)], axis=1)
+    layer_in = [layer_in[h * part : (h + 1) * part] for h in range(halves)]
+    qkv_weight = qkv_of(0, w_qkv)
+
     activated = jax.nn.silu(time_features(timesteps, ada_weight.shape[1])).astype(BF)
     modulation = jnp.einsum("re,kesd->krsd", activated, ada_weight, preferred_element_type=F32)
-    tables = both_layers(modulation.reshape(2, 4, 3, feat_a))
-    qkv_weights = both_layers(w_qkv)
+    modulation = modulation.reshape(2, 4, 3, feat_a)
+    tables = both_layers(jnp.concatenate([modulation, to_mate(modulation)], axis=-1))
     norm_rows = both_layers(qk_norm)
-    out_weights = both_layers(w_out)
-    up_weights = both_layers(w_up)
-    down_weights = both_layers(w_down)
+    size = w_out.shape[0] // n_narrow
+    groups = jnp.array(head_group, jnp.int32)
+    starts = [groups[(narrow_idx + n_narrow - step) % n_narrow] * size for step in range(n_narrow)]
+    out_weights = both_layers(
+        jnp.concatenate([lax.dynamic_slice_in_dim(w_out, start, size, 0) for start in starts], axis=0)
+    )
 
     kinds = lax.dynamic_index_in_dim(row_kind, section, 0, False)
     kinds_other = lax.dynamic_index_in_dim(row_kind, 1 - section, 0, False)
@@ -323,10 +360,12 @@
     places = lax.dynamic_index_in_dim(positions, section, 1, False)
     places = jnp.stack([relative(places[i]) for i in range(3)])
     cosine, sine = rotary_tables(places, head_dim)
-    chunk = total_rows // halves
-
-    blocks = stale_cache[0, 1].reshape(rows_b, n_narrow, heads, pair).transpose(1, 2, 0, 3)
-    stale = exchange(blocks, "narrow").transpose(1, 0, 2, 3).reshape(heads, total_rows, pair)
+
+    def stale_heads(rows_part):
+        blocks = rows_part.reshape(rows_b, n_narrow, heads, pair)
+        blocks = jnp.stack([blocks[:, group] for group in head_group]).transpose(0, 2, 1, 3)
+        got = exchange(blocks, "narrow")
+        return got.transpose(1, 0, 2, 3).reshape(heads, total_rows, pair)
 
     def to_rows(fresh):
         blocks = [f.reshape(heads, n_wide, part, pair) for f in fresh]
@@ -335,10 +374,12 @@
             picked = [lax.dynamic_index_in_dim(b, wide_idx ^ there, 1, False) for b in blocks]
             per_narrow.append(jnp.concatenate(picked, axis=1))
         got = exchange(jnp.stack(per_narrow), "narrow")
+        got = jnp.stack([got[sender] for sender in head_group])
         return got.transpose(2, 0, 1, 3).reshape(rows_b, heads_local, pair)
 
-    layer_in = lax.dynamic_index_in_dim(hidden_in, section, 0, False)
-    layer_in = [layer_in[h * part : (h + 1) * part] for h in range(halves)]
+    def by_wide(terms):
+        return [terms[r * part : (r + 1) * part] for r in range(n_wide)]
+
     results = []
     caches = []
     for layer in range(2):
@@ -348,46 +389,70 @@
         queries = []
         fresh = []
         for h in range(halves):
-            entry = modulate(line_norm(x_in[h], model_width), table[0], kinds_h[h])
-            terms = jnp.dot(gather_wide(entry), qkv_weights[layer], preferred_element_type=F32)
-            qkv = lax.psum_scatter(terms.astype(BF), "narrow", scatter_dimension=1, tiled=True)
+            entry = pair_norm(x_in[h], table[0], kinds_h[h])
+            if layer == 0 and h == 0:
+                entry, w_up_now, stale = ordered(entry, w_up, stale_cache[0, 1])
+                up_weights = up_of(w_up_now)
+                stale = stale_heads(stale)
+            entry = gather_wide(entry)
+            width = qkv_weight.shape[1] // 2
+            theirs = jnp.dot(entry, qkv_weight[:, :width], preferred_element_type=F32).astype(BF)
+            if layer == 0 and h == 0:
+                theirs, w_down_now = ordered(theirs, w_down)
+                down_weights = down_of(w_down_now)
+            got = to_partner(theirs)
+            mine = jnp.dot(entry, qkv_weight[:, width:], preferred_element_type=F32)
+            qkv = mine + got.astype(F32)
             rows = slice(h * chunk, (h + 1) * chunk)
             q, pairs = prepare(
                 qkv, cosine[rows], sine[rows], kinds_r[rows], norm_pair, heads, head_dim
             )
             queries.append(q)
             fresh.append(pairs)
-        caches.append(to_rows(fresh))
         own = jnp.concatenate(fresh, axis=1)
         if layer == 0:
+            own, *up_weights = ordered(own, *up_weights)
             other = jnp.where(lead, stale, lax.ppermute(own, "section", [(0, 1)]))
         else:
             other = swap(jnp.where(lead, own, stale))
         after = []
         for h in range(halves):
             attended = attend(queries[h], own, other, own_mask, other_mask, head_dim)
-            attended = lax.all_gather(attended, "narrow", axis=1, tiled=True)
+            attended = jnp.concatenate(gather_direct(attended), axis=1)
             terms = jnp.dot(attended, out_weights[layer], preferred_element_type=F32).astype(BF)
-            projected = scatter_wide([terms[r * part : (r + 1) * part] for r in range(n_wide)])
+            if h == 0:
+                terms, *fresh = ordered(terms, *fresh)
+                cache = to_rows(fresh)
+            projected = scatter_wide(by_wide(terms)).astype(BF)
+            projected = jnp.concatenate([projected, to_mate(projected)], axis=1).astype(F32)
             after.append(x_in[h] + pick(table[0], kinds_h[h], 2) * projected)
+        if layer == 0:
+            after[0], *down_weights = ordered(after[0], *down_weights)
+        after[1], cache = ordered(after[1], cache)
+        caches.append(cache)
         inner = []
         for h in range(halves):
-            entry = modulate(line_norm(after[h], model_width), table[1], kinds_h[h])
-            terms = jnp.dot(gather_wide(entry), up_weights[layer], preferred_element_type=F32)
-            up = lax.psum_scatter(terms.astype(BF), "narrow", scatter_dimension=0, tiled=True)
-            inner.append(jax.nn.gelu(up.astype(F32), approximate=True).astype(BF))
+            entry = pair_norm(after[h], table[1], kinds_h[h])
+            if layer == 0 and h == 0:
+                entry, w_qkv_now = ordered(entry, w_qkv)
+                qkv_weight = qkv_of(1, w_qkv_now)
+            up = jnp.dot(gather_wide(entry), up_weights[layer], preferred_element_type=F32).astype(BF)
+            size = chunk // 2
+            got = to_partner(lax.dynamic_slice_in_dim(up, (1 - high) * size, size, 0))
+            up = lax.dynamic_slice_in_dim(up, high * size, size, 0).astype(F32) + got.astype(F32)
+            inner.append(jax.nn.gelu(up, approximate=True).astype(BF))
         layer_in = []
         for h in range(halves):
-            gathered = jnp.concatenate(gather_line(inner[h]), axis=0)
-            terms = jnp.dot(gathered, down_weights[layer], preferred_element_type=F32).astype(BF)
-            size = chunk // n_narrow
-            ordered = [
-                lax.dynamic_slice_in_dim(terms, (narrow_idx + n_narrow - r) % n_narrow * size, size, 0)
-                for r in range(n_narrow)
-            ]
-            down = scatter_wide(ordered)
+            got = to_partner(inner[h])
+            mine = jnp.dot(inner[h], down_weights[layer], preferred_element_type=F32).astype(BF)
+            theirs = jnp.dot(got, down_weights[layer], preferred_element_type=F32).astype(BF)
+            first = jnp.where(lower, mine, theirs)
+            second = jnp.where(lower, theirs, mine)
+            down = scatter_wide(by_wide(jnp.concatenate([first, second], axis=0))).astype(BF)
+            far = to_mate(jnp.concatenate([down[:, feat_a:], down[:, :feat_a]], axis=1))
+            down = down.astype(F32) + far.astype(F32)
             layer_in.append((after[h] + pick(table[1], kinds_h[h], 2) * down).astype(BF))
-        results.append(jnp.concatenate(layer_in, axis=0))
+        results.append(jnp.concatenate([block[:, :feat_a] for block in layer_in], axis=0))
     return (by_layer(results, lead), by_layer(caches, lead))
 
 

time: 972 us -> 968 us (level)
  blocking collectives: 90.9 us -> 0 us
  other arithmetic: 38.3 us -> 97.4 us
  waiting for transfers between devices: 468 us -> 519 us
  matrix products: 83.8 us -> 63.5 us
  local copies, waits for them, and re-layouts: 31.2 us -> 43 us
  between operations: 16.7 us -> 6.27 us
    ppermute x49, waiting for transfers between devices: 160 us -> 373 us  [the longest x20 325 us: to_partner(): lax.ppermute(value, 'narrow', [(i, i ^ 2) for i in range(lax.axis_size('n...]
    unnamed x12 -> x0, waiting for transfers between devices: 113 us -> none
    all_gather x4 -> x0, blocking collectives: 90.9 us -> none  [in_halves(): attended = lax.all_gather(attended, 'narrow', axis=1, tiled=True)]
    reduce_scatter x4 -> x0, waiting for transfers between devices: 67.2 us -> none  [in_halves(): lax.psum_scatter(terms.astype(BF), 'narrow', scatter_dimension=0, tiled=T...]
    ppermute x24, waiting for transfers between devices: 45.4 us -> 70.2 us  [gather_wide(): lax.ppermute(block, 'wide', wide_pairs(step))]
    ppermute x49, starting transfers between devices: 122 us -> 98.1 us  [the longest x12 35.6 us: gather_direct(): lax.ppermute(block, 'narrow', [(i, (i + step) % n) for i in range(n)])]
    ppermute x9, starting transfers between devices: 14.8 us -> 37.8 us  [exchange(): block = lax.ppermute(block, axis, [(i, (i + step) % n) for i in range(n)])]
    ppermute x9, waiting for transfers between devices: 40.8 us -> 18.8 us  [exchange(): block = lax.ppermute(block, axis, [(i, (i + step) % n) for i in range(n)])]
  transfers between devices with their start and end apart: 123 -> 114, of which waited for: 69 -> 61; matrix products, arithmetic and copies ran while one was open for 12% -> 19% of each run, Pallas kernels for 2% -> 3%
where the time goes in v6:
time: 968 us; the launch traced here: 960 us
  waiting for transfers between devices  519 us (54%)
  starting transfers between devices  193 us (20%)
  other arithmetic  97.4 us (10%)
  matrix products  63.5 us (7%)
  local copies, waits for them, and re-layouts  43 us (4%)
  Pallas kernels  37.6 us (4%)
    ppermute x20, waiting for transfers between devices, to_partner(): lax.ppermute(value, 'narrow', [(i, i ^ 2) for i in range(lax.axis_size('n...  325 us
    ppermute x24, waiting for transfers between devices, gather_wide(): lax.ppermute(block, 'wide', wide_pairs(step))  70.2 us
    ppermute x24, waiting for transfers between devices, scatter_wide(): total += lax.ppermute(terms[step], 'wide', wide_pairs(step)).astype(F32)  53 us
    ppermute x9, starting transfers between devices, exchange(): block = lax.ppermute(block, axis, [(i, (i + step) % n) for i in range(n)])  37.8 us
    ppermute x12, starting transfers between devices, gather_direct(): lax.ppermute(block, 'narrow', [(i, (i + step) % n) for i in range(n)])  35.6 us
    ppermute x24, starting transfers between devices, gather_wide(): lax.ppermute(block, 'wide', wide_pairs(step))  31 us
    ppermute x20, starting transfers between devices, to_partner(): lax.ppermute(value, 'narrow', [(i, i ^ 2) for i in range(lax.axis_size('n...  28.1 us
    ppermute x24, starting transfers between devices, scatter_wide(): total += lax.ppermute(terms[step], 'wide', wide_pairs(step)).astype(F32)  25.5 us
  transfers between devices with their start and end apart: 114, of which 61 were waited for; matrix products, arithmetic and copies ran while one was open for 19% of the time, Pallas kernels for 3%

profile of v6, /device:TPU:0, one launch (start us, length us, event | category | flops | bytes accessed | tf_op | source)
XLA Modules:
  0.0 959.6 jit_solution(17187568515812996183)
XLA Ops:
  6.4 5.0 fusion.104
  12.0 4.6 dynamic-slice_bitcast_fusion.1
  18.4 3.9 collective-permute-start.7
  66.5 40.3 %collective-permute-done.11 = f32[2,128]{1,0:T(2,128)S(1)} collective-permute-done((f32[2,128]{1,0:T(2,128)S(1)}, f32[2,128]{1,0:T(2,128)S(1)}, u32[]{:S(2)}, u32[]{:S(2)}) %collective-permute-start.11) | collective-permute-done | bytes 1056 | tf_op jit(solution)/shard_map/ppermute | solution.py:250
  117.5 8.9 collective-permute-done.6
  129.5 9.6 %broadcast_select_fusion.5 = bf16[1536,1152]{1,0:T(8,128)(2,1)S(1)} fusion(bf16[1536,1152]{1,0:T(8,128)(2,1)S(1)} %collective-permute-done.8, pred[]{:T(512)S(6)} %eq.132, bf16[768,1152]{1,0:T(8,128)(2,1)} %collective-permute-done.7, bf16[768,576]{1,0:T(8,128)(2,1)S(1)} %get-tuple-element.139, bf16[768,576]{1,0:T(8,128)(2,1)S(1)} %get-tuple-element.140), kind=kLoop, calls=%fused_computation.13 | loop fusion | flops 12386304 | bytes 10616833 | tf_op jit(solution)/shard_map/jit(_where)/select_n | solution.py:322
  139.2 6.0 collective-permute-done.13
  154.3 4.1 collective-permute-start.30
  158.4 31.2 %collective-permute-done.15 = bf16[512,576]{0,1:T(8,128)(2,1)} collective-permute-done((bf16[512,576]{0,1:T(8,128)(2,1)S(1)}, bf16[512,576]{0,1:T(8,128)(2,1)}, u32[]{:S(2)}, u32[]{:S(2)}) %collective-permute-start.15) | collective-permute-done | bytes 589856 | tf_op jit(solution)/shard_map/ppermute | solution.py:250
  194.4 4.4 prepare.5
  201.0 4.0 fusion.80.qkv_ref
  205.1 4.0 prepare.4
  209.3 7.3 broadcast_select_fusion.2
  225.9 8.9 collective-permute-done.18
  234.8 8.3 collective-permute-start.20
  247.7 5.2 attend.4
  253.0 4.7 collective-permute-start.23
  257.7 4.3 pad_maximum_fusion.1
  262.1 5.2 attend.5
  269.4 4.8 collective-permute-start.43
  274.2 15.1 %collective-permute-start.44 = (bf16[512,192]{1,0:T(8,128)(2,1)S(1)}, bf16[512,192]{1,0:T(8,128)(2,1)S(1)}, u32[]{:S(2)}, u32[]{:S(2)}) collective-permute-start(bf16[512,192]{1,0:T(8,128)(2,1)S(1)} %attend.5), channel_id=1, source_target_pairs={{0,3},{1,0},{2,1},{3,2},{4,7},{5,4},{6,5},{7,6},{8,11},{9,8},{10,9... | collective-permute-start | bytes 589832 | tf_op jit(solution)/shard_map/ppermute | solution.py:241
  293.2 5.6 collective-permute-done.43
  303.8 4.2 collective-permute-done.45
  309.5 3.9 collective-permute-done.46
  316.4 4.5 collective-permute-start.50
  324.3 6.3 collective-permute-start.48
  330.9 5.5 collective-permute-done.51
  357.7 8.7 collective-permute-done.53
  366.4 6.7 collective-permute-done.54
  373.1 5.3 convolution_convert_fusion.2
  382.5 31.6 %collective-permute-done.56 = bf16[256,1536]{1,0:T(8,128)(2,1)} collective-permute-done((bf16[256,1536]{1,0:T(8,128)(2,1)}, bf16[256,1536]{1,0:T(8,128)(2,1)}, u32[]{:S(2)}, u32[]{:S(2)}) %collective-permute-start.56) | collective-permute-done | bytes 786464 | tf_op jit(solution)/shard_map/ppermute | solution.py:250
  417.0 8.0 broadcast_select_fusion
  428.4 24.1 %collective-permute-done.57 = bf16[256,1536]{1,0:T(8,128)(2,1)} collective-permute-done((bf16[256,1536]{1,0:T(8,128)(2,1)}, bf16[256,1536]{1,0:T(8,128)(2,1)}, u32[]{:S(2)}, u32[]{:S(2)}) %collective-permute-start.57) | collective-permute-done | bytes 786464 | tf_op jit(solution)/shard_map/ppermute | solution.py:250
  452.5 4.0 convolution_convert_fusion.8
  464.2 5.9 collective-permute-done.33
  470.1 7.1 collective-permute-done.34
  487.6 27.4 %collective-permute-done.36 = bf16[256,1536]{1,0:T(8,128)(2,1)S(1)} collective-permute-done((bf16[256,1536]{1,0:T(8,128)(2,1)S(1)}, bf16[256,1536]{1,0:T(8,128)(2,1)S(1)}, u32[]{:S(2)}, u32[]{:S(2)}) %collective-permute-start.36) | collective-permute-done | bytes 786464 | tf_op jit(solution)/shard_map/ppermute | solution.py:250
  518.6 32.6 %collective-permute-done.37 = bf16[256,1536]{1,0:T(8,128)(2,1)S(1)} collective-permute-done((bf16[256,1536]{1,0:T(8,128)(2,1)S(1)}, bf16[256,1536]{1,0:T(8,128)(2,1)S(1)}, u32[]{:S(2)}, u32[]{:S(2)}) %collective-permute-start.37) | collective-permute-done | bytes 786464 | tf_op jit(solution)/shard_map/ppermute | solution.py:250
  561.6 10.6 %collective-permute-done.39 = bf16[128,1536]{1,0:T(8,128)(2,1)S(1)} collective-permute-done((bf16[128,1536]{1,0:T(8,128)(2,1)S(1)}, bf16[128,1536]{1,0:T(8,128)(2,1)S(1)}, u32[]{:S(2)}, u32[]{:S(2)}) %collective-permute-start.39) | collective-permute-done | bytes 393248 | tf_op jit(solution)/shard_map/ppermute | solution.py:234
  574.9 8.8 collective-permute-done.41
  597.5 12.4 %broadcast_select_fusion.4 = bf16[1536,1152]{1,0:T(8,128)(2,1)S(1)} fusion(bf16[1536,1152]{1,0:T(8,128)(2,1)} %collective-permute-done.67, pred[]{:T(512)S(6)} %eq.143, bf16[768,1152]{1,0:T(8,128)(2,1)S(1)} %copy-done.26, bf16[768,576]{1,0:T(8,128)(2,1)S(1)} %copy-done.16, bf16[768,576]{1,0:T(8,128)(2,1)S(1)} %copy-done.18), kind=kLoop, calls=%fused_computation.12 | loop fusion | flops 12386304 | bytes 10616833 | tf_op jit(solution)/shard_map/jit(_where)/select_n | solution.py:322
  620.9 4.7 collective-permute-done.65
  630.3 20.6 %collective-permute-done.73 = bf16[512,576]{0,1:T(8,128)(2,1)S(1)} collective-permute-done((bf16[512,576]{0,1:T(8,128)(2,1)S(1)}, bf16[512,576]{0,1:T(8,128)(2,1)S(1)}, u32[]{:S(2)}, u32[]{:S(2)}) %collective-permute-start.73) | collective-permute-done | bytes 589856 | tf_op jit(solution)/shard_map/ppermute | solution.py:250
  652.1 3.9 fusion.89.qkv_ref
  656.0 4.2 prepare.7
  664.9 3.9 fusion.86.qkv_ref
  668.8 4.0 prepare.6
  675.4 5.2 attend.6
  685.1 5.2 attend.7
  695.1 8.1 collective-permute-done.76
  705.9 17.5 %collective-permute-start.99 = (bf16[1,3,256,128]{3,2,0,1:T(8,128)(2,1)S(1)}, bf16[1,3,256,128]{3,2,0,1:T(8,128)(2,1)S(1)}, u32[]{:S(2)}, u32[]{:S(2)}) collective-permute-start(bf16[1,3,256,128]{3,2,0,1:T(8,128)(2,1)S(1)} %get-tuple-element.173), channel_id=1, source_target_pairs={{0,1},{1,2},{2,3},{3,0},{4,5},{5,6},{6,7},{7,4},{8,9},{9,10},{10,1... | collective-permute-start | bytes 589832 | tf_op jit(solution)/shard_map/ppermute | solution.py:167
  723.4 9.8 %collective-permute-done.93 = bf16[512,192]{1,0:T(8,128)(2,1)S(1)} collective-permute-done((bf16[512,192]{1,0:T(8,128)(2,1)S(1)}, bf16[512,192]{1,0:T(8,128)(2,1)S(1)}, u32[]{:S(2)}, u32[]{:S(2)}) %collective-permute-start.93) | collective-permute-done | bytes 196640 | tf_op jit(solution)/shard_map/ppermute | solution.py:241
  739.1 4.3 collective-permute-done.95
  752.4 6.3 collective-permute-start.98
  780.3 5.6 collective-permute-done.103
  787.2 8.0 collective-permute-done.104
  795.2 5.1 convolution_convert_fusion
  801.3 4.1 collective-permute-done.84
  808.9 46.6 %collective-permute-done.106 = bf16[256,1536]{1,0:T(8,128)(2,1)S(1)} collective-permute-done((bf16[256,1536]{1,0:T(8,128)(2,1)S(1)}, bf16[256,1536]{1,0:T(8,128)(2,1)S(1)}, u32[]{:S(2)}, u32[]{:S(2)}) %collective-permute-start.106) | collective-permute-done | bytes 786464 | tf_op jit(solution)/shard_map/ppermute | solution.py:250
  856.1 41.4 %collective-permute-done.86 = bf16[256,1536]{1,0:T(8,128)(2,1)S(1)} collective-permute-done((bf16[256,1536]{1,0:T(8,128)(2,1)S(1)}, bf16[256,1536]{1,0:T(8,128)(2,1)S(1)}, u32[]{:S(2)}, u32[]{:S(2)}) %collective-permute-start.86) | collective-permute-done | bytes 786464 | tf_op jit(solution)/shard_map/ppermute | solution.py:250
  898.3 16.1 %collective-permute-done.107 = bf16[256,1536]{1,0:T(8,128)(2,1)S(1)} collective-permute-done((bf16[256,1536]{1,0:T(8,128)(2,1)S(1)}, bf16[256,1536]{1,0:T(8,128)(2,1)S(1)}, u32[]{:S(2)}, u32[]{:S(2)}) %collective-permute-start.107) | collective-permute-done | bytes 786464 | tf_op jit(solution)/shard_map/ppermute | solution.py:250
  929.5 6.2 collective-permute-done.109
  937.5 8.7 collective-permute-done.89
  948.4 7.5 collective-permute-done.91
  (616 shorter events, 293.3 us)
Async XLA Ops:
  2.5 43.5 %collective-permute-start = (bf16[256,768]{1,0:T(8,128)(2,1)}, bf16[256,768]{1,0:T(8,128)(2,1)}, u32[]{:S(2)}, u32[]{:S(2)}) collective-permute-start(bf16[256,768]{1,0:T(8,128)(2,1)} %dynamic-slice_bitcast_fusion.4), channel_id=1, source_target_pairs={{0,1},{1,0},{2,3},{3,2},{4,5},{5,4},{6,7},{7,6},{8,9},{9,8},{10,11... | collective-permute-start | bytes 1179656 | tf_op jit(solution)/shard_map/ppermute | solution.py:246
  12.0 29.6 %collective-permute-start.1 = (f32[2,4,3,768]{3,0,2,1:T(2,128)}, f32[2,4,3,768]{3,0,2,1:T(2,128)}, u32[]{:S(2)}, u32[]{:S(2)}) collective-permute-start(f32[2,4,3,768]{3,0,2,1:T(2,128)} %bitcast.7), channel_id=1, source_target_pairs={{0,1},{1,0},{2,3},{3,2},{4,5},{5,4},{6,7},{7,6},{8,9},{9,8},{10,11... | collective-permute-start | bytes 221192 | tf_op jit(solution)/shard_map/ppermute | solution.py:246
  18.4 38.5 %collective-permute-start.7 = (bf16[768,1152]{1,0:T(8,128)(2,1)}, bf16[768,1152]{1,0:T(8,128)(2,1)}, u32[]{:S(2)}, u32[]{:S(2)}) collective-permute-start(bf16[768,1152]{1,0:T(8,128)(2,1)} %pad_maximum_fusion.4), channel_id=1, source_target_pairs={{0,1},{1,0},{2,3},{3,2},{4,5},{5,4},{6,7},{7,6},{8,9},{9,8},{10,11... | collective-permute-start | bytes 5308424 | tf_op jit(solution)/shard_map/ppermute | solution.py:319
  22.3 20.5 %collective-permute-start.10 = (f32[4,64]{1,0:T(4,128)}, f32[4,64]{1,0:T(4,128)}, u32[]{:S(2)}, u32[]{:S(2)}) collective-permute-start(f32[4,64]{1,0:T(4,128)} %bitcast.45), channel_id=1, source_target_pairs={{0,16},{16,0},{1,17},{17,1},{2,18},{18,2},{3,19},{19,3},{4,20},{20... | collective-permute-start | bytes 3080 | tf_op jit(solution)/shard_map/ppermute | solution.py:205
  29.0 238.4 %collective-permute-start.25 = (bf16[768,768]{1,0:T(8,128)(2,1)}, bf16[768,768]{1,0:T(8,128)(2,1)}, u32[]{:S(2)}, u32[]{:S(2)}) collective-permute-start(bf16[768,768]{1,0:T(8,128)(2,1)} %pad_maximum_fusion.9), channel_id=1, source_target_pairs={{0,16},{16,0},{1,17},{17,1},{2,18},{18,2},{3,19},{19,3},{4,20},{20... | collective-permute-start | bytes 3538952 | tf_op jit(solution)/shard_map/ppermute | solution.py:205
  56.7 52.8 %collective-permute-start.16 = (bf16[768,1536]{1,0:T(8,128)(2,1)S(1)}, bf16[768,1536]{1,0:T(8,128)(2,1)S(1)}, u32[]{:S(2)}, u32[]{:S(2)}) collective-permute-start(bf16[768,1536]{1,0:T(8,128)(2,1)S(1)} %get-tuple-element.133), channel_id=1, source_target_pairs={{0,1},{1,0},{2,3},{3,2},{4,5},{5,4},{6,7},{7,6},{8,9},{9,8},{10,11... | collective-permute-start | bytes 7077896 | tf_op jit(solution)/shard_map/ppermute | solution.py:246
  59.7 67.7 %collective-permute-start.8 = (bf16[1536,1152]{1,0:T(8,128)(2,1)S(1)}, bf16[1536,1152]{1,0:T(8,128)(2,1)S(1)}, u32[]{:S(2)}, u32[]{:S(2)}) collective-permute-start(bf16[1536,1152]{1,0:T(8,128)(2,1)S(1)} %fusion.3), channel_id=1, source_target_pairs={{0,16},{1,17},{2,18},{3,19},{4,20},{5,21},{6,22},{7,23},{8,24},{9,... | collective-permute-start | bytes 10616840 | tf_op jit(solution)/shard_map/ppermute | solution.py:321
  62.4 44.4 %collective-permute-start.11 = (f32[2,128]{1,0:T(2,128)S(1)}, f32[2,128]{1,0:T(2,128)S(1)}, u32[]{:S(2)}, u32[]{:S(2)}) collective-permute-start(f32[2,128]{1,0:T(2,128)S(1)} %pad_maximum_fusion.34), channel_id=1, source_target_pairs={{0,2},{1,3},{2,0},{3,1},{4,6},{5,7},{6,4},{7,5},{8,10},{9,11},{10,... | collective-permute-start | bytes 3080 | tf_op jit(solution)/shard_map/ppermute | solution.py:250
  65.0 48.6 %collective-permute-start.4 = (bf16[128,1536]{1,0:T(8,128)(2,1)S(1)}, bf16[128,1536]{1,0:T(8,128)(2,1)S(1)}, u32[]{:S(2)}, u32[]{:S(2)}) collective-permute-start(bf16[128,1536]{1,0:T(8,128)(2,1)S(1)} %fusion.112), channel_id=1, source_target_pairs={{0,4},{4,0},{8,12},{12,8},{1,5},{5,1},{9,13},{13,9},{2,6},{6,2},{1... | collective-permute-start | bytes 1179656 | tf_op jit(solution)/shard_map/ppermute | solution.py:227
  112.5 96.7 %collective-permute-start.17 = (bf16[1536,1536]{1,0:T(8,128)(2,1)}, bf16[1536,1536]{1,0:T(8,128)(2,1)}, u32[]{:S(2)}, u32[]{:S(2)}) collective-permute-start(bf16[1536,1536]{1,0:T(8,128)(2,1)} %pad_maximum_fusion), channel_id=1, source_target_pairs={{0,16},{16,0},{1,17},{17,1},{2,18},{18,2},{3,19},{19,3},{4,20},{20... | collective-permute-start | bytes 14155784 | tf_op jit(solution)/shard_map/ppermute | solution.py:205
  116.2 22.9 %collective-permute-start.12 = (bf16[128,1536]{1,0:T(8,128)(2,1)S(1)}, bf16[128,1536]{1,0:T(8,128)(2,1)S(1)}, u32[]{:S(2)}, u32[]{:S(2)}) collective-permute-start(bf16[128,1536]{1,0:T(8,128)(2,1)S(1)} %fusion.118), channel_id=1, source_target_pairs={{0,4},{4,0},{8,12},{12,8},{1,5},{5,1},{9,13},{13,9},{2,6},{6,2},{1... | collective-permute-start | bytes 1179656 | tf_op jit(solution)/shard_map/ppermute | solution.py:227
  126.4 18.8 %collective-permute-start.13 = (bf16[128,1536]{1,0:T(8,128)(2,1)S(1)}, bf16[128,1536]{1,0:T(8,128)(2,1)S(1)}, u32[]{:S(2)}, u32[]{:S(2)}) collective-permute-start(bf16[128,1536]{1,0:T(8,128)(2,1)S(1)} %fusion.118), channel_id=1, source_target_pairs={{0,8},{4,12},{8,0},{12,4},{1,9},{5,13},{9,1},{13,5},{2,10},{6,14},... | collective-permute-start | bytes 1179656 | tf_op jit(solution)/shard_map/ppermute | solution.py:227
  146.4 43.2 %collective-permute-start.15 = (bf16[512,576]{0,1:T(8,128)(2,1)S(1)}, bf16[512,576]{0,1:T(8,128)(2,1)}, u32[]{:S(2)}, u32[]{:S(2)}) collective-permute-start(bf16[512,576]{0,1:T(8,128)(2,1)S(1)} %fusion.95), channel_id=1, source_target_pairs={{0,2},{1,3},{2,0},{3,1},{4,6},{5,7},{6,4},{7,5},{8,10},{9,11},{10,... | collective-permute-start | bytes 1769480 | tf_op jit(solution)/shard_map/ppermute | solution.py:250
  151.8 48.0 %collective-permute-start.9 = (bf16[512,576]{0,1:T(8,128)(2,1)}, bf16[512,576]{0,1:T(8,128)(2,1)S(1)}, u32[]{:S(2)}, u32[]{:S(2)}) collective-permute-start(bf16[512,576]{0,1:T(8,128)(2,1)} %fusion.92), channel_id=1, source_target_pairs={{0,2},{1,3},{2,0},{3,1},{4,6},{5,7},{6,4},{7,5},{8,10},{9,11},{10,... | collective-permute-start | bytes 1769480 | tf_op jit(solution)/shard_map/ppermute | solution.py:250
  154.3 103.5 %collective-permute-start.30 = (bf16[1536,768]{1,0:T(8,128)(2,1)}, bf16[1536,768]{1,0:T(8,128)(2,1)}, u32[]{:S(2)}, u32[]{:S(2)}) collective-permute-start(bf16[1536,768]{1,0:T(8,128)(2,1)} %get-tuple-element.131), channel_id=1, source_target_pairs={{0,1},{1,0},{2,3},{3,2},{4,5},{5,4},{6,7},{7,6},{8,9},{9,8},{10,11... | collective-permute-start | bytes 7077896 | tf_op jit(solution)/shard_map/ppermute | solution.py:246
  216.6 30.1 %collective-permute-start.21 = (bf16[3,1024,128]{2,1,0:T(8,128)(2,1)S(1)}, bf16[3,1024,128]{2,1,0:T(8,128)(2,1)}, u32[]{:S(2)}, u32[]{:S(2)}) collective-permute-start(bf16[3,1024,128]{2,1,0:T(8,128)(2,1)S(1)} %pad_maximum_fusion.10.own_ref), channel_id=1, source_target_pairs={{0,16},{1,17},{2,18},{3,19},{4,20},{5,21},{6,22},{7,23},{8,24},{9,... | collective-permute-start | bytes 2359304 | tf_op jit(solution)/shard_map/ppermute | solution.py:415
  221.4 22.7 %collective-permute-start.19 = (bf16[1,3,256,128]{3,2,0,1:T(8,128)(2,1)}, bf16[1,3,256,128]{3,2,0,1:T(8,128)(2,1)S(1)}, u32[]{:S(2)}, u32[]{:S(2)}) collective-permute-start(bf16[1,3,256,128]{3,2,0,1:T(8,128)(2,1)} %get-tuple-element.197), channel_id=1, source_target_pairs={{0,2},{1,3},{2,0},{3,1},{4,6},{5,7},{6,4},{7,5},{8,10},{9,11},{10,... | collective-permute-start | bytes 589832 | tf_op jit(solution)/shard_map/ppermute | solution.py:167
  253.0 21.2 %collective-permute-start.23 = (bf16[512,192]{1,0:T(8,128)(2,1)S(1)}, bf16[512,192]{1,0:T(8,128)(2,1)S(1)}, u32[]{:S(2)}, u32[]{:S(2)}) collective-permute-start(bf16[512,192]{1,0:T(8,128)(2,1)S(1)} %attend.4), channel_id=1, source_target_pairs={{0,2},{1,3},{2,0},{3,1},{4,6},{5,7},{6,4},{7,5},{8,10},{9,11},{10,... | collective-permute-start | bytes 589832 | tf_op jit(solution)/shard_map/ppermute | solution.py:241
  257.7 31.6 %collective-permute-start.24 = (bf16[512,192]{1,0:T(8,128)(2,1)S(1)}, bf16[512,192]{1,0:T(8,128)(2,1)S(1)}, u32[]{:S(2)}, u32[]{:S(2)}) collective-permute-start(bf16[512,192]{1,0:T(8,128)(2,1)S(1)} %attend.4), channel_id=1, source_target_pairs={{0,3},{1,0},{2,1},{3,2},{4,7},{5,4},{6,5},{7,6},{8,11},{9,8},{10,9... | collective-permute-start | bytes 589832 | tf_op jit(solution)/shard_map/ppermute | solution.py:241
  262.0 155.0 %collective-permute-start.31 = (bf16[1536,1536]{1,0:T(8,128)(2,1)}, bf16[1536,1536]{1,0:T(8,128)(2,1)}, u32[]{:S(2)}, u32[]{:S(2)}) collective-permute-start(bf16[1536,1536]{1,0:T(8,128)(2,1)} %pad_maximum_fusion.1), channel_id=1, source_target_pairs={{0,16},{16,0},{1,17},{17,1},{2,18},{18,2},{3,19},{19,3},{4,20},{20... | collective-permute-start | bytes 14155784 | tf_op jit(solution)/shard_map/ppermute | solution.py:205
  267.4 25.9 %collective-permute-start.42 = (bf16[512,192]{1,0:T(8,128)(2,1)S(1)}, bf16[512,192]{1,0:T(8,128)(2,1)S(1)}, u32[]{:S(2)}, u32[]{:S(2)}) collective-permute-start(bf16[512,192]{1,0:T(8,128)(2,1)S(1)} %attend.5), channel_id=1, source_target_pairs={{0,1},{1,2},{2,3},{3,0},{4,5},{5,6},{6,7},{7,4},{8,9},{9,10},{10,1... | collective-permute-start | bytes 589832 | tf_op jit(solution)/shard_map/ppermute | solution.py:241
  269.4 29.4 %collective-permute-start.43 = (bf16[512,192]{1,0:T(8,128)(2,1)S(1)}, bf16[512,192]{1,0:T(8,128)(2,1)S(1)}, u32[]{:S(2)}, u32[]{:S(2)}) collective-permute-start(bf16[512,192]{1,0:T(8,128)(2,1)S(1)} %attend.5), channel_id=1, source_target_pairs={{0,2},{1,3},{2,0},{3,1},{4,6},{5,7},{6,4},{7,5},{8,10},{9,11},{10,... | collective-permute-start | bytes 589832 | tf_op jit(solution)/shard_map/ppermute | solution.py:241
  274.2 24.9 %collective-permute-start.44 = (bf16[512,192]{1,0:T(8,128)(2,1)S(1)}, bf16[512,192]{1,0:T(8,128)(2,1)S(1)}, u32[]{:S(2)}, u32[]{:S(2)}) collective-permute-start(bf16[512,192]{1,0:T(8,128)(2,1)S(1)} %attend.5), channel_id=1, source_target_pairs={{0,3},{1,0},{2,1},{3,2},{4,7},{5,4},{6,5},{7,6},{8,11},{9,8},{10,9... | collective-permute-start | bytes 589832 | tf_op jit(solution)/shard_map/ppermute | solution.py:241
  290.8 39.9 %collective-permute-start.49 = (bf16[1,3,256,128]{3,2,0,1:T(8,128)(2,1)S(1)}, bf16[1,3,256,128]{3,2,0,1:T(8,128)(2,1)S(1)}, u32[]{:S(2)}, u32[]{:S(2)}) collective-permute-start(bf16[1,3,256,128]{3,2,0,1:T(8,128)(2,1)S(1)} %get-tuple-element.191), channel_id=1, source_target_pairs={{0,1},{1,2},{2,3},{3,0},{4,5},{5,6},{6,7},{7,4},{8,9},{9,10},{10,1... | collective-permute-start | bytes 589832 | tf_op jit(solution)/shard_map/ppermute | solution.py:167
  380.5 33.6 %collective-permute-start.56 = (bf16[256,1536]{1,0:T(8,128)(2,1)}, bf16[256,1536]{1,0:T(8,128)(2,1)}, u32[]{:S(2)}, u32[]{:S(2)}) collective-permute-start(bf16[256,1536]{1,0:T(8,128)(2,1)} %constant_dynamic-slice_fusion.10), channel_id=1, source_target_pairs={{0,2},{1,3},{2,0},{3,1},{4,6},{5,7},{6,4},{7,5},{8,10},{9,11},{10,... | collective-permute-start | bytes 2359304 | tf_op jit(solution)/shard_map/ppermute | solution.py:250
  417.0 35.5 %collective-permute-start.57 = (bf16[256,1536]{1,0:T(8,128)(2,1)}, bf16[256,1536]{1,0:T(8,128)(2,1)}, u32[]{:S(2)}, u32[]{:S(2)}) collective-permute-start(bf16[256,1536]{1,0:T(8,128)(2,1)} %fusion.35), channel_id=1, source_target_pairs={{0,2},{1,3},{2,0},{3,1},{4,6},{5,7},{6,4},{7,5},{8,10},{9,11},{10,... | collective-permute-start | bytes 2359304 | tf_op jit(solution)/shard_map/ppermute | solution.py:250
  425.4 31.0 %collective-permute-start.32 = (f32[2,128]{1,0:T(2,128)S(1)}, f32[2,128]{1,0:T(2,128)S(1)}, u32[]{:S(2)}, u32[]{:S(2)}) collective-permute-start(f32[2,128]{1,0:T(2,128)S(1)} %pad_maximum_fusion.35), channel_id=1, source_target_pairs={{0,2},{1,3},{2,0},{3,1},{4,6},{5,7},{6,4},{7,5},{8,10},{9,11},{10,... | collective-permute-start | bytes 3080 | tf_op jit(solution)/shard_map/ppermute | solution.py:250
  479.9 35.1 %collective-permute-start.36 = (bf16[256,1536]{1,0:T(8,128)(2,1)S(1)}, bf16[256,1536]{1,0:T(8,128)(2,1)S(1)}, u32[]{:S(2)}, u32[]{:S(2)}) collective-permute-start(bf16[256,1536]{1,0:T(8,128)(2,1)S(1)} %constant_dynamic-slice_fusion.15), channel_id=1, source_target_pairs={{0,2},{1,3},{2,0},{3,1},{4,6},{5,7},{6,4},{7,5},{8,10},{9,11},{10,... | collective-permute-start | bytes 2359304 | tf_op jit(solution)/shard_map/ppermute | solution.py:250
  480.0 35.7 %collective-permute-start.59 = (bf16[128,1536]{1,0:T(8,128)(2,1)S(1)}, bf16[128,1536]{1,0:T(8,128)(2,1)S(1)}, u32[]{:S(2)}, u32[]{:S(2)}) collective-permute-start(bf16[128,1536]{1,0:T(8,128)(2,1)S(1)} %get-tuple-element.180), channel_id=1, source_target_pairs={{0,8},{4,12},{8,0},{12,4},{1,9},{5,13},{9,1},{13,5},{2,10},{6,14},... | collective-permute-start | bytes 1179656 | tf_op jit(solution)/shard_map/ppermute | solution.py:234
  480.4 35.4 %collective-permute-start.60 = (bf16[128,1536]{1,0:T(8,128)(2,1)S(1)}, bf16[128,1536]{1,0:T(8,128)(2,1)S(1)}, u32[]{:S(2)}, u32[]{:S(2)}) collective-permute-start(bf16[128,1536]{1,0:T(8,128)(2,1)S(1)} %get-tuple-element.181), channel_id=1, source_target_pairs={{0,12},{4,8},{8,4},{12,0},{1,13},{5,9},{9,5},{13,1},{2,14},{6,10},... | collective-permute-start | bytes 1179656 | tf_op jit(solution)/shard_map/ppermute | solution.py:234
  481.9 33.8 %collective-permute-start.58 = (bf16[128,1536]{1,0:T(8,128)(2,1)S(1)}, bf16[128,1536]{1,0:T(8,128)(2,1)S(1)}, u32[]{:S(2)}, u32[]{:S(2)}) collective-permute-start(bf16[128,1536]{1,0:T(8,128)(2,1)S(1)} %slice.741), channel_id=1, source_target_pairs={{0,4},{4,0},{8,12},{12,8},{1,5},{5,1},{9,13},{13,9},{2,6},{6,2},{1... | collective-permute-start | bytes 1179656 | tf_op jit(solution)/shard_map/ppermute | solution.py:234
  486.5 71.2 %collective-permute-start.66 = (bf16[768,1152]{1,0:T(8,128)(2,1)S(1)}, bf16[768,1152]{1,0:T(8,128)(2,1)S(1)}, u32[]{:S(2)}, u32[]{:S(2)}) collective-permute-start(bf16[768,1152]{1,0:T(8,128)(2,1)S(1)} %pad_maximum_fusion.5), channel_id=1, source_target_pairs={{16,17},{17,16},{18,19},{19,18},{20,21},{21,20},{22,23},{23,22},{2... | collective-permute-start | bytes 5308424 | tf_op jit(solution)/shard_map/ppermute | solution.py:319
  515.6 35.5 %collective-permute-start.37 = (bf16[256,1536]{1,0:T(8,128)(2,1)S(1)}, bf16[256,1536]{1,0:T(8,128)(2,1)S(1)}, u32[]{:S(2)}, u32[]{:S(2)}) collective-permute-start(bf16[256,1536]{1,0:T(8,128)(2,1)S(1)} %fusion.27), channel_id=1, source_target_pairs={{0,2},{1,3},{2,0},{3,1},{4,6},{5,7},{6,4},{7,5},{8,10},{9,11},{10,... | collective-permute-start | bytes 2359304 | tf_op jit(solution)/shard_map/ppermute | solution.py:250
  516.9 58.0 %collective-permute-start.61 = (bf16[128,1536]{1,0:T(8,128)(2,1)}, bf16[128,1536]{1,0:T(8,128)(2,1)}, u32[]{:S(2)}, u32[]{:S(2)}) collective-permute-start(bf16[128,1536]{1,0:T(8,128)(2,1)} %pad_maximum_fusion.17), channel_id=1, source_target_pairs={{0,1},{1,0},{2,3},{3,2},{4,5},{5,4},{6,7},{7,6},{8,9},{9,8},{10,11... | collective-permute-start | bytes 1179656 | tf_op jit(solution)/shard_map/ppermute | solution.py:246
  554.1 18.2 %collective-permute-start.39 = (bf16[128,1536]{1,0:T(8,128)(2,1)S(1)}, bf16[128,1536]{1,0:T(8,128)(2,1)S(1)}, u32[]{:S(2)}, u32[]{:S(2)}) collective-permute-start(bf16[128,1536]{1,0:T(8,128)(2,1)S(1)} %get-tuple-element.178), channel_id=1, source_target_pairs={{0,8},{4,12},{8,0},{12,4},{1,9},{5,13},{9,1},{13,5},{2,10},{6,14},... | collective-permute-start | bytes 1179656 | tf_op jit(solution)/shard_map/ppermute | solution.py:234
  554.1 18.1 %collective-permute-start.40 = (bf16[128,1536]{1,0:T(8,128)(2,1)S(1)}, bf16[128,1536]{1,0:T(8,128)(2,1)S(1)}, u32[]{:S(2)}, u32[]{:S(2)}) collective-permute-start(bf16[128,1536]{1,0:T(8,128)(2,1)S(1)} %get-tuple-element.179), channel_id=1, source_target_pairs={{0,12},{4,8},{8,4},{12,0},{1,13},{5,9},{9,5},{13,1},{2,14},{6,10},... | collective-permute-start | bytes 1179656 | tf_op jit(solution)/shard_map/ppermute | solution.py:234
  554.2 19.2 %collective-permute-start.38 = (bf16[128,1536]{1,0:T(8,128)(2,1)S(1)}, bf16[128,1536]{1,0:T(8,128)(2,1)S(1)}, u32[]{:S(2)}, u32[]{:S(2)}) collective-permute-start(bf16[128,1536]{1,0:T(8,128)(2,1)S(1)} %slice.726), channel_id=1, source_target_pairs={{0,4},{4,0},{8,12},{12,8},{1,5},{5,1},{9,13},{13,9},{2,6},{6,2},{1... | collective-permute-start | bytes 1179656 | tf_op jit(solution)/shard_map/ppermute | solution.py:234
  560.2 36.5 %collective-permute-start.67 = (bf16[1536,1152]{1,0:T(8,128)(2,1)}, bf16[1536,1152]{1,0:T(8,128)(2,1)}, u32[]{:S(2)}, u32[]{:S(2)}) collective-permute-start(bf16[1536,1152]{1,0:T(8,128)(2,1)} %fusion.2), channel_id=1, source_target_pairs={{16,0},{17,1},{18,2},{19,3},{20,4},{21,5},{22,6},{23,7},{24,8},{25... | collective-permute-start | bytes 10616840 | tf_op jit(solution)/shard_map/ppermute | solution.py:321
  591.9 18.0 %collective-permute-start.70 = (bf16[128,1536]{1,0:T(8,128)(2,1)S(1)}, bf16[128,1536]{1,0:T(8,128)(2,1)S(1)}, u32[]{:S(2)}, u32[]{:S(2)}) collective-permute-start(bf16[128,1536]{1,0:T(8,128)(2,1)S(1)} %fusion.130), channel_id=1, source_target_pairs={{0,4},{4,0},{8,12},{12,8},{1,5},{5,1},{9,13},{13,9},{2,6},{6,2},{1... | collective-permute-start | bytes 1179656 | tf_op jit(solution)/shard_map/ppermute | solution.py:227
  592.0 20.6 %collective-permute-start.71 = (bf16[128,1536]{1,0:T(8,128)(2,1)S(1)}, bf16[128,1536]{1,0:T(8,128)(2,1)S(1)}, u32[]{:S(2)}, u32[]{:S(2)}) collective-permute-start(bf16[128,1536]{1,0:T(8,128)(2,1)S(1)} %fusion.130), channel_id=1, source_target_pairs={{0,8},{4,12},{8,0},{12,4},{1,9},{5,13},{9,1},{13,5},{2,10},{6,14},... | collective-permute-start | bytes 1179656 | tf_op jit(solution)/shard_map/ppermute | solution.py:227
  592.9 19.8 %collective-permute-start.72 = (bf16[128,1536]{1,0:T(8,128)(2,1)S(1)}, bf16[128,1536]{1,0:T(8,128)(2,1)S(1)}, u32[]{:S(2)}, u32[]{:S(2)}) collective-permute-start(bf16[128,1536]{1,0:T(8,128)(2,1)S(1)} %fusion.130), channel_id=1, source_target_pairs={{0,12},{4,8},{8,4},{12,0},{1,13},{5,9},{9,5},{13,1},{2,14},{6,10},... | collective-permute-start | bytes 1179656 | tf_op jit(solution)/shard_map/ppermute | solution.py:227
  596.6 24.3 %collective-permute-start.63 = (bf16[128,1536]{1,0:T(8,128)(2,1)S(1)}, bf16[128,1536]{1,0:T(8,128)(2,1)S(1)}, u32[]{:S(2)}, u32[]{:S(2)}) collective-permute-start(bf16[128,1536]{1,0:T(8,128)(2,1)S(1)} %fusion.124), channel_id=1, source_target_pairs={{0,4},{4,0},{8,12},{12,8},{1,5},{5,1},{9,13},{13,9},{2,6},{6,2},{1... | collective-permute-start | bytes 1179656 | tf_op jit(solution)/shard_map/ppermute | solution.py:227
  596.7 24.2 %collective-permute-start.64 = (bf16[128,1536]{1,0:T(8,128)(2,1)S(1)}, bf16[128,1536]{1,0:T(8,128)(2,1)S(1)}, u32[]{:S(2)}, u32[]{:S(2)}) collective-permute-start(bf16[128,1536]{1,0:T(8,128)(2,1)S(1)} %fusion.124), channel_id=1, source_target_pairs={{0,8},{4,12},{8,0},{12,4},{1,9},{5,13},{9,1},{13,5},{2,10},{6,14},... | collective-permute-start | bytes 1179656 | tf_op jit(solution)/shard_map/ppermute | solution.py:227
  614.6 36.3 %collective-permute-start.73 = (bf16[512,576]{0,1:T(8,128)(2,1)S(1)}, bf16[512,576]{0,1:T(8,128)(2,1)S(1)}, u32[]{:S(2)}, u32[]{:S(2)}) collective-permute-start(bf16[512,576]{0,1:T(8,128)(2,1)S(1)} %fusion.101), channel_id=1, source_target_pairs={{0,2},{1,3},{2,0},{3,1},{4,6},{5,7},{6,4},{7,5},{8,10},{9,11},{10,... | collective-permute-start | bytes 1769480 | tf_op jit(solution)/shard_map/ppermute | solution.py:250
  627.6 34.9 %collective-permute-start.68 = (bf16[512,576]{0,1:T(8,128)(2,1)}, bf16[512,576]{0,1:T(8,128)(2,1)}, u32[]{:S(2)}, u32[]{:S(2)}) collective-permute-start(bf16[512,576]{0,1:T(8,128)(2,1)} %fusion.98), channel_id=1, source_target_pairs={{0,2},{1,3},{2,0},{3,1},{4,6},{5,7},{6,4},{7,5},{8,10},{9,11},{10,... | collective-permute-start | bytes 1769480 | tf_op jit(solution)/shard_map/ppermute | solution.py:250
  681.5 21.6 %collective-permute-start.76 = (bf16[512,192]{1,0:T(8,128)(2,1)S(1)}, bf16[512,192]{1,0:T(8,128)(2,1)S(1)}, u32[]{:S(2)}, u32[]{:S(2)}) collective-permute-start(bf16[512,192]{1,0:T(8,128)(2,1)S(1)} %attend.6), channel_id=1, source_target_pairs={{0,2},{1,3},{2,0},{3,1},{4,6},{5,7},{6,4},{7,5},{8,10},{9,11},{10,... | collective-permute-start | bytes 589832 | tf_op jit(solution)/shard_map/ppermute | solution.py:241
  684.9 18.3 %collective-permute-start.77 = (bf16[512,192]{1,0:T(8,128)(2,1)S(1)}, bf16[512,192]{1,0:T(8,128)(2,1)S(1)}, u32[]{:S(2)}, u32[]{:S(2)}) collective-permute-start(bf16[512,192]{1,0:T(8,128)(2,1)S(1)} %attend.6), channel_id=1, source_target_pairs={{0,3},{1,0},{2,1},{3,2},{4,7},{5,4},{6,5},{7,6},{8,11},{9,8},{10,9... | collective-permute-start | bytes 589832 | tf_op jit(solution)/shard_map/ppermute | solution.py:241
  690.3 33.0 %collective-permute-start.92 = (bf16[512,192]{1,0:T(8,128)(2,1)S(1)}, bf16[512,192]{1,0:T(8,128)(2,1)S(1)}, u32[]{:S(2)}, u32[]{:S(2)}) collective-permute-start(bf16[512,192]{1,0:T(8,128)(2,1)S(1)} %attend.7), channel_id=1, source_target_pairs={{0,1},{1,2},{2,3},{3,0},{4,5},{5,6},{6,7},{7,4},{8,9},{9,10},{10,1... | collective-permute-start | bytes 589832 | tf_op jit(solution)/shard_map/ppermute | solution.py:241
  692.4 40.8 %collective-permute-start.93 = (bf16[512,192]{1,0:T(8,128)(2,1)S(1)}, bf16[512,192]{1,0:T(8,128)(2,1)S(1)}, u32[]{:S(2)}, u32[]{:S(2)}) collective-permute-start(bf16[512,192]{1,0:T(8,128)(2,1)S(1)} %attend.7), channel_id=1, source_target_pairs={{0,2},{1,3},{2,0},{3,1},{4,6},{5,7},{6,4},{7,5},{8,10},{9,11},{10,... | collective-permute-start | bytes 589832 | tf_op jit(solution)/shard_map/ppermute | solution.py:241
  692.4 40.8 %collective-permute-start.94 = (bf16[512,192]{1,0:T(8,128)(2,1)S(1)}, bf16[512,192]{1,0:T(8,128)(2,1)S(1)}, u32[]{:S(2)}, u32[]{:S(2)}) collective-permute-start(bf16[512,192]{1,0:T(8,128)(2,1)S(1)} %attend.7), channel_id=1, source_target_pairs={{0,3},{1,0},{2,1},{3,2},{4,7},{5,4},{6,5},{7,6},{8,11},{9,8},{10,9... | collective-permute-start | bytes 589832 | tf_op jit(solution)/shard_map/ppermute | solution.py:241
  705.9 55.1 %collective-permute-start.99 = (bf16[1,3,256,128]{3,2,0,1:T(8,128)(2,1)S(1)}, bf16[1,3,256,128]{3,2,0,1:T(8,128)(2,1)S(1)}, u32[]{:S(2)}, u32[]{:S(2)}) collective-permute-start(bf16[1,3,256,128]{3,2,0,1:T(8,128)(2,1)S(1)} %get-tuple-element.173), channel_id=1, source_target_pairs={{0,1},{1,2},{2,3},{3,0},{4,5},{5,6},{6,7},{7,4},{8,9},{9,10},{10,1... | collective-permute-start | bytes 589832 | tf_op jit(solution)/shard_map/ppermute | solution.py:167
  723.4 37.7 %collective-permute-start.100 = (bf16[1,3,256,128]{3,2,0,1:T(8,128)(2,1)S(1)}, bf16[1,3,256,128]{3,2,0,1:T(8,128)(2,1)S(1)}, u32[]{:S(2)}, u32[]{:S(2)}) collective-permute-start(bf16[1,3,256,128]{3,2,0,1:T(8,128)(2,1)S(1)} %get-tuple-element.172), channel_id=1, source_target_pairs={{0,2},{1,3},{2,0},{3,1},{4,6},{5,7},{6,4},{7,5},{8,10},{9,11},{10,... | collective-permute-start | bytes 589832 | tf_op jit(solution)/shard_map/ppermute | solution.py:167
  774.7 20.5 %collective-permute-start.104 = (bf16[128,1536]{1,0:T(8,128)(2,1)S(1)}, bf16[128,1536]{1,0:T(8,128)(2,1)S(1)}, u32[]{:S(2)}, u32[]{:S(2)}) collective-permute-start(bf16[128,1536]{1,0:T(8,128)(2,1)S(1)} %add_convert_fusion.1), channel_id=1, source_target_pairs={{0,8},{4,12},{8,0},{12,4},{1,9},{5,13},{9,1},{13,5},{2,10},{6,14},... | collective-permute-start | bytes 1179656 | tf_op jit(solution)/shard_map/ppermute | solution.py:227
  775.7 19.5 %collective-permute-start.105 = (bf16[128,1536]{1,0:T(8,128)(2,1)S(1)}, bf16[128,1536]{1,0:T(8,128)(2,1)S(1)}, u32[]{:S(2)}, u32[]{:S(2)}) collective-permute-start(bf16[128,1536]{1,0:T(8,128)(2,1)S(1)} %add_convert_fusion.1), channel_id=1, source_target_pairs={{0,12},{4,8},{8,4},{12,0},{1,13},{5,9},{9,5},{13,1},{2,14},{6,10},... | collective-permute-start | bytes 1179656 | tf_op jit(solution)/shard_map/ppermute | solution.py:227
  778.3 23.0 %collective-permute-start.83 = (bf16[128,1536]{1,0:T(8,128)(2,1)S(1)}, bf16[128,1536]{1,0:T(8,128)(2,1)S(1)}, u32[]{:S(2)}, u32[]{:S(2)}) collective-permute-start(bf16[128,1536]{1,0:T(8,128)(2,1)S(1)} %add_convert_fusion.3), channel_id=1, source_target_pairs={{0,4},{4,0},{8,12},{12,8},{1,5},{5,1},{9,13},{13,9},{2,6},{6,2},{1... | collective-permute-start | bytes 1179656 | tf_op jit(solution)/shard_map/ppermute | solution.py:227
  779.3 26.1 %collective-permute-start.84 = (bf16[128,1536]{1,0:T(8,128)(2,1)S(1)}, bf16[128,1536]{1,0:T(8,128)(2,1)S(1)}, u32[]{:S(2)}, u32[]{:S(2)}) collective-permute-start(bf16[128,1536]{1,0:T(8,128)(2,1)S(1)} %add_convert_fusion.3), channel_id=1, source_target_pairs={{0,8},{4,12},{8,0},{12,4},{1,9},{5,13},{9,1},{13,5},{2,10},{6,14},... | collective-permute-start | bytes 1179656 | tf_op jit(solution)/shard_map/ppermute | solution.py:227
  785.8 19.6 %collective-permute-start.85 = (bf16[128,1536]{1,0:T(8,128)(2,1)S(1)}, bf16[128,1536]{1,0:T(8,128)(2,1)S(1)}, u32[]{:S(2)}, u32[]{:S(2)}) collective-permute-start(bf16[128,1536]{1,0:T(8,128)(2,1)S(1)} %add_convert_fusion.3), channel_id=1, source_target_pairs={{0,12},{4,8},{8,4},{12,0},{1,13},{5,9},{9,5},{13,1},{2,14},{6,10},... | collective-permute-start | bytes 1179656 | tf_op jit(solution)/shard_map/ppermute | solution.py:227
  800.4 55.1 %collective-permute-start.106 = (bf16[256,1536]{1,0:T(8,128)(2,1)S(1)}, bf16[256,1536]{1,0:T(8,128)(2,1)S(1)}, u32[]{:S(2)}, u32[]{:S(2)}) collective-permute-start(bf16[256,1536]{1,0:T(8,128)(2,1)S(1)} %constant_dynamic-slice_fusion.1), channel_id=1, source_target_pairs={{0,2},{1,3},{2,0},{3,1},{4,6},{5,7},{6,4},{7,5},{8,10},{9,11},{10,... | collective-permute-start | bytes 2359304 | tf_op jit(solution)/shard_map/ppermute | solution.py:250
  808.1 89.5 %collective-permute-start.86 = (bf16[256,1536]{1,0:T(8,128)(2,1)S(1)}, bf16[256,1536]{1,0:T(8,128)(2,1)S(1)}, u32[]{:S(2)}, u32[]{:S(2)}) collective-permute-start(bf16[256,1536]{1,0:T(8,128)(2,1)S(1)} %constant_dynamic-slice_fusion.5), channel_id=1, source_target_pairs={{0,2},{1,3},{2,0},{3,1},{4,6},{5,7},{6,4},{7,5},{8,10},{9,11},{10,... | collective-permute-start | bytes 2359304 | tf_op jit(solution)/shard_map/ppermute | solution.py:250
  856.1 58.3 %collective-permute-start.107 = (bf16[256,1536]{1,0:T(8,128)(2,1)S(1)}, bf16[256,1536]{1,0:T(8,128)(2,1)S(1)}, u32[]{:S(2)}, u32[]{:S(2)}) collective-permute-start(bf16[256,1536]{1,0:T(8,128)(2,1)S(1)} %fusion.51), channel_id=1, source_target_pairs={{0,2},{1,3},{2,0},{3,1},{4,6},{5,7},{6,4},{7,5},{8,10},{9,11},{10,... | collective-permute-start | bytes 2359304 | tf_op jit(solution)/shard_map/ppermute | solution.py:250
  898.2 26.2 %collective-permute-start.87 = (bf16[256,1536]{1,0:T(8,128)(2,1)S(1)}, bf16[256,1536]{1,0:T(8,128)(2,1)S(1)}, u32[]{:S(2)}, u32[]{:S(2)}) collective-permute-start(bf16[256,1536]{1,0:T(8,128)(2,1)S(1)} %fusion.43), channel_id=1, source_target_pairs={{0,2},{1,3},{2,0},{3,1},{4,6},{5,7},{6,4},{7,5},{8,10},{9,11},{10,... | collective-permute-start | bytes 2359304 | tf_op jit(solution)/shard_map/ppermute | solution.py:250
  917.2 18.4 %collective-permute-start.109 = (bf16[128,1536]{1,0:T(8,128)(2,1)S(1)}, bf16[128,1536]{1,0:T(8,128)(2,1)S(1)}, u32[]{:S(2)}, u32[]{:S(2)}) collective-permute-start(bf16[128,1536]{1,0:T(8,128)(2,1)S(1)} %get-tuple-element.165), channel_id=1, source_target_pairs={{0,8},{4,12},{8,0},{12,4},{1,9},{5,13},{9,1},{13,5},{2,10},{6,14},... | collective-permute-start | bytes 1179656 | tf_op jit(solution)/shard_map/ppermute | solution.py:234
  918.5 18.6 %collective-permute-start.108 = (bf16[128,1536]{1,0:T(8,128)(2,1)S(1)}, bf16[128,1536]{1,0:T(8,128)(2,1)S(1)}, u32[]{:S(2)}, u32[]{:S(2)}) collective-permute-start(bf16[128,1536]{1,0:T(8,128)(2,1)S(1)} %slice.797), channel_id=1, source_target_pairs={{0,4},{4,0},{8,12},{12,8},{1,5},{5,1},{9,13},{13,9},{2,6},{6,2},{1... | collective-permute-start | bytes 1179656 | tf_op jit(solution)/shard_map/ppermute | solution.py:234
  927.4 18.7 %collective-permute-start.89 = (bf16[128,1536]{1,0:T(8,128)(2,1)S(1)}, bf16[128,1536]{1,0:T(8,128)(2,1)S(1)}, u32[]{:S(2)}, u32[]{:S(2)}) collective-permute-start(bf16[128,1536]{1,0:T(8,128)(2,1)S(1)} %get-tuple-element.160), channel_id=1, source_target_pairs={{0,8},{4,12},{8,0},{12,4},{1,9},{5,13},{9,1},{13,5},{2,10},{6,14},... | collective-permute-start | bytes 1179656 | tf_op jit(solution)/shard_map/ppermute | solution.py:234
  (146 other events, 2213.8 us)

commit v7 on v6

--- a/solution.py
+++ b/solution.py
@@ -235,13 +235,6 @@
     return total
 
 
-def gather_direct(block):
-    n = lax.axis_size("narrow")
-    return [block] + [
-        lax.ppermute(block, "narrow", [(i, (i + step) % n) for i in range(n)]) for step in range(1, n)
-    ]
-
-
 def to_mate(value):
     return lax.ppermute(value, "narrow", [(i, i ^ 1) for i in range(lax.axis_size("narrow"))])
 
@@ -250,7 +243,7 @@
     return lax.ppermute(value, "narrow", [(i, i ^ 2) for i in range(lax.axis_size("narrow"))])
 
 
-def pair_norm(values, table, kinds):
+def statistics(values):
     width = values.shape[1]
     mean = jnp.mean(values, axis=1)
     center = values - mean[:, None]
@@ -258,8 +251,12 @@
     far = to_partner(own)
     whole_mean = 0.5 * (own[0] + far[0])
     spread = own[1] + far[1] + width * ((own[0] - whole_mean) ** 2 + (far[0] - whole_mean) ** 2)
-    scale = lax.rsqrt(spread / (2 * width) + EPS_ROW)
-    return modulate((values - whole_mean[:, None]) * scale[:, None], table, kinds)
+    return whole_mean, lax.rsqrt(spread / (2 * width) + EPS_ROW)
+
+
+def normed(values, moments, table, kinds):
+    mean, scale = moments
+    return modulate((values - mean[:, None]) * scale[:, None], table, kinds)
 
 
 def ordered(*values):
@@ -309,47 +306,51 @@
         order = [lax.dynamic_index_in_dim(blocks, wide_idx ^ step, 0, False) for step in range(n_wide)]
         return jnp.stack(order, axis=1).reshape(total_rows)
 
-    def qkv_part(own, parity):
+    def weight_of(layer, kept, sent, axis):
+        pairs = [(layer * n_narrow + i, layer * n_narrow + (i ^ 1)) for i in range(n_narrow)]
+        got = lax.ppermute(sent, ("section", "narrow"), pairs)
+        joined = jnp.concatenate([kept, got], axis=axis)
+        return joined, lax.ppermute(joined, "section", [(layer, 1 - layer)])
+
+    def select(layer, weight):
+        return jnp.where(section == layer, weight[0], weight[1])
+
+    def two_blocks(own, axis, size, first, second):
+        starts = [first * size, second * size]
+        return jnp.concatenate([lax.dynamic_slice_in_dim(own, at, size, axis) for at in starts], axis=axis)
+
+    def qkv_of(layer, own):
         size = own.shape[1] // 4
-        starts = [(2 * parity + 1 - high) * size, (2 * parity + high) * size]
-        return jnp.concatenate([lax.dynamic_slice_in_dim(own, at, size, 1) for at in starts], axis=1)
-
-    def qkv_of(layer, own):
-        pairs = [(layer * n_narrow + i, layer * n_narrow + (i ^ 1)) for i in range(n_narrow)]
-        got = lax.ppermute(qkv_part(own, 1 - odd), ("section", "narrow"), pairs)
-        joined = jnp.concatenate([qkv_part(own, odd), got], axis=0)
-        passed = lax.ppermute(joined, "section", [(layer, 1 - layer)])
-        return jnp.where(section == layer, joined, passed)
-
-    def up_of(own):
+        parts = [two_blocks(own, 1, size, 2 * p + 1 - high, 2 * p + high) for p in (odd, 1 - odd)]
+        return weight_of(layer, parts[0], parts[1], 0)
+
+    def out_of(layer, own):
+        size = own.shape[0] // 4
+        parts = [two_blocks(own, 0, size, 2 * p + high, 2 * p + 1 - high) for p in (odd, 1 - odd)]
+        return weight_of(layer, parts[0], parts[1], 1)
+
+    def up_of(layer, own):
         size = own.shape[1] // 2
-        got = to_mate(lax.dynamic_slice_in_dim(own, (1 - odd) * size, size, 1))
-        kept = lax.dynamic_slice_in_dim(own, odd * size, size, 1)
-        return both_layers(jnp.concatenate([kept, got], axis=0))
-
-    def down_of(own):
+        parts = [lax.dynamic_slice_in_dim(own, p * size, size, 1) for p in (odd, 1 - odd)]
+        return weight_of(layer, parts[0], parts[1], 0)
+
+    def down_of(layer, own):
         size = own.shape[0] // 2
-        got = to_mate(lax.dynamic_slice_in_dim(own, (1 - odd) * size, size, 0))
-        kept = lax.dynamic_slice_in_dim(own, odd * size, size, 0)
-        return both_layers(jnp.concatenate([kept, got], axis=1))
+        parts = [lax.dynamic_slice_in_dim(own, p * size, size, 0) for p in (odd, 1 - odd)]
+        return weight_of(layer, parts[0], parts[1], 1)
 
     layer_in = lax.dynamic_index_in_dim(hidden_in, section, 0, False)
     layer_in = jnp.concatenate([layer_in, to_mate(layer_in)], axis=1)
+    first_mean, first_scale = statistics(layer_in.astype(F32))
+    first_mean, w_qkv_now, stale = ordered(first_mean, w_qkv, stale_cache[0, 1])
+    qkv_weight = qkv_of(0, w_qkv_now)
     layer_in = [layer_in[h * part : (h + 1) * part] for h in range(halves)]
-    qkv_weight = qkv_of(0, w_qkv)
 
     activated = jax.nn.silu(time_features(timesteps, ada_weight.shape[1])).astype(BF)
     modulation = jnp.einsum("re,kesd->krsd", activated, ada_weight, preferred_element_type=F32)
     modulation = modulation.reshape(2, 4, 3, feat_a)
     tables = both_layers(jnp.concatenate([modulation, to_mate(modulation)], axis=-1))
     norm_rows = both_layers(qk_norm)
-    size = w_out.shape[0] // n_narrow
-    groups = jnp.array(head_group, jnp.int32)
-    starts = [groups[(narrow_idx + n_narrow - step) % n_narrow] * size for step in range(n_narrow)]
-    out_weights = both_layers(
-        jnp.concatenate([lax.dynamic_slice_in_dim(w_out, start, size, 0) for start in starts], axis=0)
-    )
-
     kinds = lax.dynamic_index_in_dim(row_kind, section, 0, False)
     kinds_other = lax.dynamic_index_in_dim(row_kind, 1 - section, 0, False)
     kinds_r = relative(kinds)
@@ -377,9 +378,12 @@
         got = jnp.stack([got[sender] for sender in head_group])
         return got.transpose(2, 0, 1, 3).reshape(rows_b, heads_local, pair)
 
-    def by_wide(terms):
-        return [terms[r * part : (r + 1) * part] for r in range(n_wide)]
-
+    def summed(terms):
+        total = scatter_wide([terms[r * part : (r + 1) * part] for r in range(n_wide)]).astype(BF)
+        far = to_mate(jnp.concatenate([total[:, feat_a:], total[:, :feat_a]], axis=1))
+        return total.astype(F32) + far.astype(F32)
+
+    stale = stale_heads(stale)
     results = []
     caches = []
     for layer in range(2):
@@ -389,20 +393,25 @@
         queries = []
         fresh = []
         for h in range(halves):
-            entry = pair_norm(x_in[h], table[0], kinds_h[h])
+            if layer == 0:
+                rows = slice(h * part, (h + 1) * part)
+                moments = (first_mean[rows], first_scale[rows])
+            else:
+                moments = statistics(x_in[h])
+            entry = normed(x_in[h], moments, table[0], kinds_h[h])
             if layer == 0 and h == 0:
-                entry, w_up_now, stale = ordered(entry, w_up, stale_cache[0, 1])
-                up_weights = up_of(w_up_now)
-                stale = stale_heads(stale)
-            entry = gather_wide(entry)
-            width = qkv_weight.shape[1] // 2
-            theirs = jnp.dot(entry, qkv_weight[:, :width], preferred_element_type=F32).astype(BF)
-            if layer == 0 and h == 0:
-                theirs, w_down_now = ordered(theirs, w_down)
-                down_weights = down_of(w_down_now)
-            got = to_partner(theirs)
-            mine = jnp.dot(entry, qkv_weight[:, width:], preferred_element_type=F32)
-            qkv = mine + got.astype(F32)
+                entry, w_out_now, w_up_now = ordered(entry, w_out, w_up)
+                out_weight = out_of(0, w_out_now)
+                up_weight = up_of(0, w_up_now)
+            terms = jnp.dot(gather_wide(entry), select(layer, qkv_weight), preferred_element_type=F32)
+            terms = terms.astype(BF)
+            if h == 0:
+                terms, w_down_now = ordered(terms, w_down)
+                down_weight = down_of(layer, w_down_now)
+                if layer == 0:
+                    terms, stale = ordered(terms, stale)
+            width = terms.shape[1] // 2
+            qkv = terms[:, width:].astype(F32) + to_partner(terms[:, :width]).astype(F32)
             rows = slice(h * chunk, (h + 1) * chunk)
             q, pairs = prepare(
                 qkv, cosine[rows], sine[rows], kinds_r[rows], norm_pair, heads, head_dim
@@ -410,48 +419,47 @@
             queries.append(q)
             fresh.append(pairs)
         own = jnp.concatenate(fresh, axis=1)
+        own, *weights = ordered(own, *out_weight, *up_weight)
+        out_weight, up_weight = weights[:2], weights[2:]
         if layer == 0:
-            own, *up_weights = ordered(own, *up_weights)
             other = jnp.where(lead, stale, lax.ppermute(own, "section", [(0, 1)]))
         else:
             other = swap(jnp.where(lead, own, stale))
         after = []
         for h in range(halves):
             attended = attend(queries[h], own, other, own_mask, other_mask, head_dim)
-            attended = jnp.concatenate(gather_direct(attended), axis=1)
-            terms = jnp.dot(attended, out_weights[layer], preferred_element_type=F32).astype(BF)
-            if h == 0:
+            attended = jnp.concatenate([attended, to_partner(attended)], axis=1)
+            terms = jnp.dot(attended, select(layer, out_weight), preferred_element_type=F32).astype(BF)
+            if h == 1:
                 terms, *fresh = ordered(terms, *fresh)
                 cache = to_rows(fresh)
-            projected = scatter_wide(by_wide(terms)).astype(BF)
-            projected = jnp.concatenate([projected, to_mate(projected)], axis=1).astype(F32)
-            after.append(x_in[h] + pick(table[0], kinds_h[h], 2) * projected)
-        if layer == 0:
-            after[0], *down_weights = ordered(after[0], *down_weights)
-        after[1], cache = ordered(after[1], cache)
-        caches.append(cache)
+            after.append(x_in[h] + pick(table[0], kinds_h[h], 2) * summed(terms))
         inner = []
         for h in range(halves):
-            entry = pair_norm(after[h], table[1], kinds_h[h])
+            entry = normed(after[h], statistics(after[h]), table[1], kinds_h[h])
             if layer == 0 and h == 0:
                 entry, w_qkv_now = ordered(entry, w_qkv)
                 qkv_weight = qkv_of(1, w_qkv_now)
-            up = jnp.dot(gather_wide(entry), up_weights[layer], preferred_element_type=F32).astype(BF)
+            entry = gather_wide(entry)
+            up = jnp.dot(entry, select(layer, up_weight), preferred_element_type=F32).astype(BF)
             size = chunk // 2
             got = to_partner(lax.dynamic_slice_in_dim(up, (1 - high) * size, size, 0))
             up = lax.dynamic_slice_in_dim(up, high * size, size, 0).astype(F32) + got.astype(F32)
             inner.append(jax.nn.gelu(up, approximate=True).astype(BF))
+        inner[0], cache, *down_weight = ordered(inner[0], cache, *down_weight)
+        caches.append(cache)
+        if layer == 0:
+            inner[0], w_out_now, w_up_now = ordered(inner[0], w_out, w_up)
+            out_weight = out_of(1, w_out_now)
+            up_weight = up_of(1, w_up_now)
         layer_in = []
         for h in range(halves):
             got = to_partner(inner[h])
-            mine = jnp.dot(inner[h], down_weights[layer], preferred_element_type=F32).astype(BF)
-            theirs = jnp.dot(got, down_weights[layer], preferred_element_type=F32).astype(BF)
-            first = jnp.where(lower, mine, theirs)
-            second = jnp.where(lower, theirs, mine)
-            down = scatter_wide(by_wide(jnp.concatenate([first, second], axis=0))).astype(BF)
-            far = to_mate(jnp.concatenate([down[:, feat_a:], down[:, :feat_a]], axis=1))
-            down = down.astype(F32) + far.astype(F32)
-            layer_in.append((after[h] + pick(table[1], kinds_h[h], 2) * down).astype(BF))
+            first = jnp.where(lower, inner[h], got)
+            second = jnp.where(lower, got, inner[h])
+            whole = jnp.concatenate([first, second], axis=0)
+            terms = jnp.dot(whole, select(layer, down_weight), preferred_element_type=F32).astype(BF)
+            layer_in.append((after[h] + pick(table[1], kinds_h[h], 2) * summed(terms)).astype(BF))
         results.append(jnp.concatenate([block[:, :feat_a] for block in layer_in], axis=0))
     return (by_layer(results, lead), by_layer(caches, lead))
 

time: 968 us -> 899 us (0.929)
  other arithmetic: 97.4 us -> 56.2 us
  starting transfers between devices: 193 us -> 174 us
    ppermute x20 -> x23, waiting for transfers between devices: 325 us -> 279 us  [to_partner(): lax.ppermute(value, 'narrow', [(i, i ^ 2) for i in range(lax.axis_size('n...]
    ppermute x24, waiting for transfers between devices: 53 us -> 93.2 us  [scatter_wide(): total += lax.ppermute(terms[step], 'wide', wide_pairs(step)).astype(F32)]
    ppermute x24, waiting for transfers between devices: 70.2 us -> 41.1 us  [gather_wide(): lax.ppermute(block, 'wide', wide_pairs(step))]
    ppermute x9, starting transfers between devices: 37.8 us -> 15.9 us  [exchange(): block = lax.ppermute(block, axis, [(i, (i + step) % n) for i in range(n)])]
    select_n x2 -> x4, other arithmetic: 22 us -> 0.43 us  [in_pairs(): first = jnp.where(lower, inner[h], got)]
    ppermute x12 -> x10, starting transfers between devices: 24.1 us -> 7.04 us  [to_mate(): lax.ppermute(value, 'narrow', [(i, i ^ 1) for i in range(lax.axis_size('n...]
    select_n x4 -> x2, other arithmetic: 17 us -> 0.82 us  [both_layers(): return (jnp.where(lead, own, other), jnp.where(lead, other, own))]
    ppermute x8 -> x5, starting transfers between devices: 0.94 us -> 15.8 us  [swap(): return lax.ppermute(value, 'section', [(0, 1), (1, 0)])]
  transfers between devices with their start and end apart: 114 -> 112, of which waited for: 61 -> 60; matrix products, arithmetic and copies ran while one was open for 19% -> 18% of each run, Pallas kernels for 3% -> 4%
where the time goes in v7:
time: 899 us; the launch traced here: 889 us
  waiting for transfers between devices  510 us (57%)
  starting transfers between devices  174 us (19%)
  matrix products  59.7 us (7%)
  other arithmetic  56.2 us (6%)
  local copies, waits for them, and re-layouts  48.3 us (5%)
  Pallas kernels  37.2 us (4%)
    ppermute x23, waiting for transfers between devices, to_partner(): lax.ppermute(value, 'narrow', [(i, i ^ 2) for i in range(lax.axis_size('n...  279 us
    ppermute x24, waiting for transfers between devices, scatter_wide(): total += lax.ppermute(terms[step], 'wide', wide_pairs(step)).astype(F32)  93.2 us
    ppermute x24, waiting for transfers between devices, gather_wide(): lax.ppermute(block, 'wide', wide_pairs(step))  41.1 us
    ppermute x10, waiting for transfers between devices, to_mate(): lax.ppermute(value, 'narrow', [(i, i ^ 1) for i in range(lax.axis_size('n...  38.4 us
    ppermute x24, starting transfers between devices, gather_wide(): lax.ppermute(block, 'wide', wide_pairs(step))  37 us
    ppermute x24, starting transfers between devices, scatter_wide(): total += lax.ppermute(terms[step], 'wide', wide_pairs(step)).astype(F32)  35.2 us
    ppermute x8, waiting for transfers between devices, weight_of(): got = lax.ppermute(sent, ('section', 'narrow'), pairs)  32.9 us
    ppermute x23, starting transfers between devices, to_partner(): lax.ppermute(value, 'narrow', [(i, i ^ 2) for i in range(lax.axis_size('n...  30.2 us
  transfers between devices with their start and end apart: 112, of which 60 were waited for; matrix products, arithmetic and copies ran while one was open for 18% of the time, Pallas kernels for 4%

profile of v7, /device:TPU:0, one launch (start us, length us, event | category | flops | bytes accessed | tf_op | source)
XLA Modules:
  0.0 889.0 jit_solution(2020660680085519363)
XLA Ops:
  2.0 5.0 fusion.106
  17.1 4.0 collective-permute-done
  26.2 4.7 constant_dynamic-slice_fusion.56
  45.1 10.9 %collective-permute-done.7 = bf16[768,1152]{1,0:T(8,128)(2,1)S(1)} collective-permute-done((bf16[768,1152]{1,0:T(8,128)(2,1)S(1)}, bf16[768,1152]{1,0:T(8,128)(2,1)S(1)}, u32[]{:S(2)}, u32[]{:S(2)}) %collective-permute-start.7) | collective-permute-done | bytes 1769504 | tf_op jit(solution)/shard_map/ppermute | solution.py:311
  65.6 22.0 %collective-permute-done.20 = bf16[768,1536]{1,0:T(8,128)(2,1)} collective-permute-done((bf16[768,1536]{1,0:T(8,128)(2,1)}, bf16[768,1536]{1,0:T(8,128)(2,1)}, u32[]{:S(2)}, u32[]{:S(2)}) %collective-permute-start.20) | collective-permute-done | bytes 2359328 | tf_op jit(solution)/shard_map/ppermute | solution.py:311
  87.6 4.9 pad_maximum_fusion
  96.2 3.8 collective-permute-start.11
  104.4 6.1 collective-permute-done.9
  110.5 5.9 collective-permute-start.10
  117.2 11.6 %collective-permute-done.10 = bf16[1,3,256,128]{3,2,0,1:T(8,128)(2,1)S(1)} collective-permute-done((bf16[1,3,256,128]{3,2,0,1:T(8,128)(2,1)S(1)}, bf16[1,3,256,128]{3,2,0,1:T(8,128)(2,1)S(1)}, u32[]{:S(2)}, u32[]{:S(2)}) %collective-permute-start.10) | collective-permute-done | bytes 196640 | tf_op jit(solution)/shard_map/ppermute | solution.py:167
  139.1 4.2 convolution_convert_fusion.3
  144.7 4.9 constant_dynamic-slice_fusion.20
  151.6 4.8 convolution_convert_fusion.2
  161.5 4.7 collective-permute-done.12
  168.9 4.0 prepare.4
  172.9 15.8 %collective-permute-done.17 = bf16[512,576]{0,1:T(8,128)(2,1)} collective-permute-done((bf16[512,576]{0,1:T(8,128)(2,1)}, bf16[512,576]{0,1:T(8,128)(2,1)}, u32[]{:S(2)}, u32[]{:S(2)}) %collective-permute-start.17) | collective-permute-done | bytes 589856 | tf_op jit(solution)/shard_map/ppermute | solution.py:243
  192.5 4.0 prepare.5
  200.1 5.2 attend.5
  210.8 5.2 attend.4
  216.1 11.0 %collective-permute-done.33 = bf16[512,192]{1,0:T(8,128)(2,1)S(1)} collective-permute-done((bf16[512,192]{1,0:T(8,128)(2,1)S(1)}, bf16[512,192]{1,0:T(8,128)(2,1)S(1)}, u32[]{:S(2)}, u32[]{:S(2)}) %collective-permute-start.33) | collective-permute-done | bytes 196640 | tf_op jit(solution)/shard_map/ppermute | solution.py:243
  235.9 7.1 collective-permute-start.45
  249.5 4.9 collective-permute-done.46
  262.0 7.3 collective-permute-done.26
  274.7 6.1 collective-permute-done.27
  287.4 9.7 %collective-permute-start.51 = (bf16[128,1536]{1,0:T(8,128)(2,1)S(1)}, bf16[128,1536]{1,0:T(8,128)(2,1)S(1)}, u32[]{:S(2)}, u32[]{:S(2)}) collective-permute-start(bf16[128,1536]{1,0:T(8,128)(2,1)S(1)} %add_convert_fusion.8), channel_id=1, source_target_pairs={{0,12},{4,8},{8,4},{12,0},{1,13},{5,9},{9,5},{13,1},{2,14},{6,10},... | collective-permute-start | bytes 1179656 | tf_op jit(solution)/shard_map/ppermute | solution.py:227
  308.2 7.5 collective-permute-done.50
  315.7 4.5 collective-permute-start.29
  320.1 5.0 convolution_convert_fusion.11
  325.4 4.3 collective-permute-done.30
  329.7 4.9 convolution_convert_fusion.14
  335.1 39.4 %collective-permute-done.52 = bf16[256,1536]{1,0:T(8,128)(2,1)S(1)} collective-permute-done((bf16[256,1536]{1,0:T(8,128)(2,1)S(1)}, bf16[256,1536]{1,0:T(8,128)(2,1)S(1)}, u32[]{:S(2)}, u32[]{:S(2)}) %collective-permute-start.52) | collective-permute-done | bytes 786464 | tf_op jit(solution)/shard_map/ppermute | solution.py:243
  376.7 31.5 %collective-permute-done.32 = bf16[256,1536]{1,0:T(8,128)(2,1)S(1)} collective-permute-done((bf16[256,1536]{1,0:T(8,128)(2,1)S(1)}, bf16[256,1536]{1,0:T(8,128)(2,1)S(1)}, u32[]{:S(2)}, u32[]{:S(2)}) %collective-permute-start.32) | collective-permute-done | bytes 786464 | tf_op jit(solution)/shard_map/ppermute | solution.py:243
  408.9 16.1 %collective-permute-done.53 = bf16[256,1536]{1,0:T(8,128)(2,1)S(1)} collective-permute-done((bf16[256,1536]{1,0:T(8,128)(2,1)S(1)}, bf16[256,1536]{1,0:T(8,128)(2,1)S(1)}, u32[]{:S(2)}, u32[]{:S(2)}) %collective-permute-start.53) | collective-permute-done | bytes 786464 | tf_op jit(solution)/shard_map/ppermute | solution.py:243
  434.1 6.4 collective-permute-done.54
  441.3 8.2 collective-permute-done.56
  452.2 6.6 collective-permute-done.39
  465.3 7.1 collective-permute-done.40
  473.2 8.3 collective-permute-done.42
  487.5 6.1 collective-permute-done.57
  493.6 8.4 collective-permute-done.43
  532.8 5.2 constant_dynamic-slice_fusion.3
  548.8 19.9 %collective-permute-done.64 = bf16[512,576]{0,1:T(8,128)(2,1)} collective-permute-done((bf16[512,576]{0,1:T(8,128)(2,1)}, bf16[512,576]{0,1:T(8,128)(2,1)}, u32[]{:S(2)}, u32[]{:S(2)}) %collective-permute-start.64) | collective-permute-done | bytes 589856 | tf_op jit(solution)/shard_map/ppermute | solution.py:243
  571.5 4.2 prepare.6
  575.7 5.7 collective-permute-done.69
  585.1 4.0 prepare.7
  589.3 14.9 %collective-permute-start.74 = (bf16[3,1024,128]{2,1,0:T(8,128)(2,1)S(1)}, bf16[3,1024,128]{2,1,0:T(8,128)(2,1)S(1)}, u32[]{:S(2)}, u32[]{:S(2)}) collective-permute-start(bf16[3,1024,128]{2,1,0:T(8,128)(2,1)S(1)} %broadcast_select_fusion.30), channel_id=1, source_target_pairs={{0,16},{16,0},{1,17},{17,1},{2,18},{18,2},{3,19},{19,3},{4,20},{20... | collective-permute-start | bytes 2359304 | tf_op jit(solution)/shard_map/ppermute | solution.py:205
  606.2 5.2 attend.7
  616.6 5.2 attend.6
  621.9 11.0 %collective-permute-done.85 = bf16[512,192]{1,0:T(8,128)(2,1)S(1)} collective-permute-done((bf16[512,192]{1,0:T(8,128)(2,1)S(1)}, bf16[512,192]{1,0:T(8,128)(2,1)S(1)}, u32[]{:S(2)}, u32[]{:S(2)}) %collective-permute-start.85) | collective-permute-done | bytes 196640 | tf_op jit(solution)/shard_map/ppermute | solution.py:243
  652.2 7.9 collective-permute-done.98
  662.4 5.5 collective-permute-done.76
  667.9 7.0 collective-permute-done.78
  678.2 7.1 collective-permute-done.79
  697.9 7.0 collective-permute-done.83
  705.8 11.0 %collective-permute-done.82 = bf16[128,1536]{1,0:T(8,128)(2,1)S(1)} collective-permute-done((bf16[128,1536]{1,0:T(8,128)(2,1)S(1)}, bf16[128,1536]{1,0:T(8,128)(2,1)S(1)}, u32[]{:S(2)}, u32[]{:S(2)}) %collective-permute-start.82) | collective-permute-done | bytes 393248 | tf_op jit(solution)/shard_map/ppermute | solution.py:227
  716.9 4.9 convolution_convert_fusion.8
  724.8 5.0 convolution_convert_fusion.5
  731.8 38.2 %collective-permute-done.84 = bf16[256,1536]{1,0:T(8,128)(2,1)S(1)} collective-permute-done((bf16[256,1536]{1,0:T(8,128)(2,1)S(1)}, bf16[256,1536]{1,0:T(8,128)(2,1)S(1)}, u32[]{:S(2)}, u32[]{:S(2)}) %collective-permute-start.84) | collective-permute-done | bytes 786464 | tf_op jit(solution)/shard_map/ppermute | solution.py:243
  770.7 33.0 %collective-permute-done.104 = bf16[256,1536]{1,0:T(8,128)(2,1)S(1)} collective-permute-done((bf16[256,1536]{1,0:T(8,128)(2,1)S(1)}, bf16[256,1536]{1,0:T(8,128)(2,1)S(1)}, u32[]{:S(2)}, u32[]{:S(2)}) %collective-permute-start.104) | collective-permute-done | bytes 786464 | tf_op jit(solution)/shard_map/ppermute | solution.py:243
  804.4 33.0 %collective-permute-done.91 = bf16[256,1536]{1,0:T(8,128)(2,1)S(1)} collective-permute-done((bf16[256,1536]{1,0:T(8,128)(2,1)S(1)}, bf16[256,1536]{1,0:T(8,128)(2,1)S(1)}, u32[]{:S(2)}, u32[]{:S(2)}) %collective-permute-start.91) | collective-permute-done | bytes 786464 | tf_op jit(solution)/shard_map/ppermute | solution.py:243
  844.1 9.0 %collective-permute-done.105 = bf16[256,1536]{1,0:T(8,128)(2,1)S(1)} collective-permute-done((bf16[256,1536]{1,0:T(8,128)(2,1)S(1)}, bf16[256,1536]{1,0:T(8,128)(2,1)S(1)}, u32[]{:S(2)}, u32[]{:S(2)}) %collective-permute-start.105) | collective-permute-done | bytes 786464 | tf_op jit(solution)/shard_map/ppermute | solution.py:243
  861.6 6.6 collective-permute-done.106
  868.2 7.1 collective-permute-done.108
  878.6 6.7 collective-permute-done.109
  (602 shorter events, 278.7 us)
Async XLA Ops:
  0.6 63.7 %collective-permute-start.13 = (f32[4,64]{1,0:T(4,128)}, f32[4,64]{1,0:T(4,128)}, u32[]{:S(2)}, u32[]{:S(2)}) collective-permute-start(f32[4,64]{1,0:T(4,128)} %bitcast.434), channel_id=1, source_target_pairs={{0,16},{16,0},{1,17},{17,1},{2,18},{18,2},{3,19},{19,3},{4,20},{20... | collective-permute-start | bytes 3080 | tf_op jit(solution)/shard_map/ppermute | solution.py:205
  31.5 24.4 %collective-permute-start.7 = (bf16[768,1152]{1,0:T(8,128)(2,1)S(1)}, bf16[768,1152]{1,0:T(8,128)(2,1)S(1)}, u32[]{:S(2)}, u32[]{:S(2)}) collective-permute-start(bf16[768,1152]{1,0:T(8,128)(2,1)S(1)} %pad_maximum_fusion.6), channel_id=1, source_target_pairs={{0,1},{1,0},{2,3},{3,2},{4,5},{5,4},{6,7},{7,6},{8,9},{9,8},{10,11... | collective-permute-start | bytes 5308424 | tf_op jit(solution)/shard_map/ppermute | solution.py:311
  39.4 48.2 %collective-permute-start.20 = (bf16[768,1536]{1,0:T(8,128)(2,1)}, bf16[768,1536]{1,0:T(8,128)(2,1)}, u32[]{:S(2)}, u32[]{:S(2)}) collective-permute-start(bf16[768,1536]{1,0:T(8,128)(2,1)} %get-tuple-element.171), channel_id=1, source_target_pairs={{0,1},{1,0},{2,3},{3,2},{4,5},{5,4},{6,7},{7,6},{8,9},{9,8},{10,11... | collective-permute-start | bytes 7077896 | tf_op jit(solution)/shard_map/ppermute | solution.py:311
  58.5 78.2 %collective-permute-start.8 = (bf16[1536,1152]{1,0:T(8,128)(2,1)}, bf16[1536,1152]{1,0:T(8,128)(2,1)}, u32[]{:S(2)}, u32[]{:S(2)}) collective-permute-start(bf16[1536,1152]{1,0:T(8,128)(2,1)} %fusion.3), channel_id=1, source_target_pairs={{0,16},{1,17},{2,18},{3,19},{4,20},{5,21},{6,22},{7,23},{8,24},{9,... | collective-permute-start | bytes 10616840 | tf_op jit(solution)/shard_map/ppermute | solution.py:313
  92.5 104.1 %collective-permute-start.21 = (bf16[1536,1536]{1,0:T(8,128)(2,1)}, bf16[1536,1536]{1,0:T(8,128)(2,1)}, u32[]{:S(2)}, u32[]{:S(2)}) collective-permute-start(bf16[1536,1536]{1,0:T(8,128)(2,1)} %pad_maximum_fusion), channel_id=1, source_target_pairs={{0,16},{1,17},{2,18},{3,19},{4,20},{5,21},{6,22},{7,23},{8,24},{9,... | collective-permute-start | bytes 14155784 | tf_op jit(solution)/shard_map/ppermute | solution.py:313
  96.2 20.4 %collective-permute-start.11 = (bf16[1,3,256,128]{3,2,0,1:T(8,128)(2,1)S(1)}, bf16[1,3,256,128]{3,2,0,1:T(8,128)(2,1)S(1)}, u32[]{:S(2)}, u32[]{:S(2)}) collective-permute-start(bf16[1,3,256,128]{3,2,0,1:T(8,128)(2,1)S(1)} %get-tuple-element.244), channel_id=1, source_target_pairs={{0,3},{1,0},{2,1},{3,2},{4,7},{5,4},{6,5},{7,6},{8,11},{9,8},{10,9... | collective-permute-start | bytes 589832 | tf_op jit(solution)/shard_map/ppermute | solution.py:167
  100.3 28.5 %collective-permute-start.18 = (bf16[384,768]{1,0:T(8,128)(2,1)S(1)}, bf16[384,768]{1,0:T(8,128)(2,1)S(1)}, u32[]{:S(2)}, u32[]{:S(2)}) collective-permute-start(bf16[384,768]{1,0:T(8,128)(2,1)S(1)} %pad_maximum_fusion.16), channel_id=1, source_target_pairs={{0,1},{1,0},{2,3},{3,2},{4,5},{5,4},{6,7},{7,6},{8,9},{9,8},{10,11... | collective-permute-start | bytes 1769480 | tf_op jit(solution)/shard_map/ppermute | solution.py:311
  110.5 18.3 %collective-permute-start.10 = (bf16[1,3,256,128]{3,2,0,1:T(8,128)(2,1)S(1)}, bf16[1,3,256,128]{3,2,0,1:T(8,128)(2,1)S(1)}, u32[]{:S(2)}, u32[]{:S(2)}) collective-permute-start(bf16[1,3,256,128]{3,2,0,1:T(8,128)(2,1)S(1)} %get-tuple-element.245), channel_id=1, source_target_pairs={{0,2},{1,3},{2,0},{3,1},{4,6},{5,7},{6,4},{7,5},{8,10},{9,11},{10,... | collective-permute-start | bytes 589832 | tf_op jit(solution)/shard_map/ppermute | solution.py:167
  130.2 19.4 %collective-permute-start.16 = (bf16[128,1536]{1,0:T(8,128)(2,1)}, bf16[128,1536]{1,0:T(8,128)(2,1)}, u32[]{:S(2)}, u32[]{:S(2)}) collective-permute-start(bf16[128,1536]{1,0:T(8,128)(2,1)} %fusion.116), channel_id=1, source_target_pairs={{0,12},{4,8},{8,4},{12,0},{1,13},{5,9},{9,5},{13,1},{2,14},{6,10},... | collective-permute-start | bytes 1179656 | tf_op jit(solution)/shard_map/ppermute | solution.py:227
  136.7 59.9 %collective-permute-start.19 = (bf16[384,1536]{1,0:T(8,128)(2,1)}, bf16[384,1536]{1,0:T(8,128)(2,1)}, u32[]{:S(2)}, u32[]{:S(2)}) collective-permute-start(bf16[384,1536]{1,0:T(8,128)(2,1)} %pad_maximum_fusion.8), channel_id=1, source_target_pairs={{0,16},{1,17},{2,18},{3,19},{4,20},{5,21},{6,22},{7,23},{8,24},{9,... | collective-permute-start | bytes 3538952 | tf_op jit(solution)/shard_map/ppermute | solution.py:313
  149.5 59.3 %collective-permute-start.37 = (bf16[1536,768]{1,0:T(8,128)(2,1)}, bf16[1536,768]{1,0:T(8,128)(2,1)}, u32[]{:S(2)}, u32[]{:S(2)}) collective-permute-start(bf16[1536,768]{1,0:T(8,128)(2,1)} %get-tuple-element.169), channel_id=1, source_target_pairs={{0,1},{1,0},{2,3},{3,2},{4,5},{5,4},{6,7},{7,6},{8,9},{9,8},{10,11... | collective-permute-start | bytes 7077896 | tf_op jit(solution)/shard_map/ppermute | solution.py:311
  158.5 30.2 %collective-permute-start.17 = (bf16[512,576]{0,1:T(8,128)(2,1)}, bf16[512,576]{0,1:T(8,128)(2,1)}, u32[]{:S(2)}, u32[]{:S(2)}) collective-permute-start(bf16[512,576]{0,1:T(8,128)(2,1)} %copy.50), channel_id=1, source_target_pairs={{0,2},{1,3},{2,0},{3,1},{4,6},{5,7},{6,4},{7,5},{8,10},{9,11},{10,... | collective-permute-start | bytes 1769480 | tf_op jit(solution)/shard_map/ppermute | solution.py:243
  205.4 21.7 %collective-permute-start.33 = (bf16[512,192]{1,0:T(8,128)(2,1)S(1)}, bf16[512,192]{1,0:T(8,128)(2,1)S(1)}, u32[]{:S(2)}, u32[]{:S(2)}) collective-permute-start(bf16[512,192]{1,0:T(8,128)(2,1)S(1)} %attend.5), channel_id=1, source_target_pairs={{0,2},{1,3},{2,0},{3,1},{4,6},{5,7},{6,4},{7,5},{8,10},{9,11},{10,... | collective-permute-start | bytes 589832 | tf_op jit(solution)/shard_map/ppermute | solution.py:243
  216.0 19.9 %collective-permute-start.23 = (bf16[512,192]{1,0:T(8,128)(2,1)S(1)}, bf16[512,192]{1,0:T(8,128)(2,1)S(1)}, u32[]{:S(2)}, u32[]{:S(2)}) collective-permute-start(bf16[512,192]{1,0:T(8,128)(2,1)S(1)} %attend.4), channel_id=1, source_target_pairs={{0,2},{1,3},{2,0},{3,1},{4,6},{5,7},{6,4},{7,5},{8,10},{9,11},{10,... | collective-permute-start | bytes 589832 | tf_op jit(solution)/shard_map/ppermute | solution.py:243
  229.9 17.2 %collective-permute-start.35 = (bf16[1,3,256,128]{3,2,0,1:T(8,128)(2,1)S(1)}, bf16[1,3,256,128]{3,2,0,1:T(8,128)(2,1)S(1)}, u32[]{:S(2)}, u32[]{:S(2)}) collective-permute-start(bf16[1,3,256,128]{3,2,0,1:T(8,128)(2,1)S(1)} %get-tuple-element.241), channel_id=1, source_target_pairs={{0,2},{1,3},{2,0},{3,1},{4,6},{5,7},{6,4},{7,5},{8,10},{9,11},{10,... | collective-permute-start | bytes 589832 | tf_op jit(solution)/shard_map/ppermute | solution.py:167
  234.4 20.0 %collective-permute-start.46 = (bf16[128,1536]{1,0:T(8,128)(2,1)S(1)}, bf16[128,1536]{1,0:T(8,128)(2,1)S(1)}, u32[]{:S(2)}, u32[]{:S(2)}) collective-permute-start(bf16[128,1536]{1,0:T(8,128)(2,1)S(1)} %get-tuple-element.212), channel_id=1, source_target_pairs={{0,12},{4,8},{8,4},{12,0},{1,13},{5,9},{9,5},{13,1},{2,14},{6,10},... | collective-permute-start | bytes 1179656 | tf_op jit(solution)/shard_map/ppermute | solution.py:234
  235.9 21.4 %collective-permute-start.45 = (bf16[128,1536]{1,0:T(8,128)(2,1)S(1)}, bf16[128,1536]{1,0:T(8,128)(2,1)S(1)}, u32[]{:S(2)}, u32[]{:S(2)}) collective-permute-start(bf16[128,1536]{1,0:T(8,128)(2,1)S(1)} %get-tuple-element.213), channel_id=1, source_target_pairs={{0,8},{4,12},{8,0},{12,4},{1,9},{5,13},{9,1},{13,5},{2,10},{6,14},... | collective-permute-start | bytes 1179656 | tf_op jit(solution)/shard_map/ppermute | solution.py:234
  245.5 179.7 %collective-permute-start.38 = (bf16[1536,1536]{1,0:T(8,128)(2,1)S(1)}, bf16[1536,1536]{1,0:T(8,128)(2,1)S(1)}, u32[]{:S(2)}, u32[]{:S(2)}) collective-permute-start(bf16[1536,1536]{1,0:T(8,128)(2,1)S(1)} %pad_maximum_fusion.1), channel_id=1, source_target_pairs={{0,16},{1,17},{2,18},{3,19},{4,20},{5,21},{6,22},{7,23},{8,24},{9,... | collective-permute-start | bytes 14155784 | tf_op jit(solution)/shard_map/ppermute | solution.py:313
  247.1 26.3 %collective-permute-start.36 = (bf16[1,3,256,128]{3,2,0,1:T(8,128)(2,1)S(1)}, bf16[1,3,256,128]{3,2,0,1:T(8,128)(2,1)S(1)}, u32[]{:S(2)}, u32[]{:S(2)}) collective-permute-start(bf16[1,3,256,128]{3,2,0,1:T(8,128)(2,1)S(1)} %get-tuple-element.240), channel_id=1, source_target_pairs={{0,3},{1,0},{2,1},{3,2},{4,7},{5,4},{6,5},{7,6},{8,11},{9,8},{10,9... | collective-permute-start | bytes 589832 | tf_op jit(solution)/shard_map/ppermute | solution.py:167
  287.4 19.8 %collective-permute-start.51 = (bf16[128,1536]{1,0:T(8,128)(2,1)S(1)}, bf16[128,1536]{1,0:T(8,128)(2,1)S(1)}, u32[]{:S(2)}, u32[]{:S(2)}) collective-permute-start(bf16[128,1536]{1,0:T(8,128)(2,1)S(1)} %add_convert_fusion.8), channel_id=1, source_target_pairs={{0,12},{4,8},{8,4},{12,0},{1,13},{5,9},{9,5},{13,1},{2,14},{6,10},... | collective-permute-start | bytes 1179656 | tf_op jit(solution)/shard_map/ppermute | solution.py:227
  297.1 18.6 %collective-permute-start.50 = (bf16[128,1536]{1,0:T(8,128)(2,1)S(1)}, bf16[128,1536]{1,0:T(8,128)(2,1)S(1)}, u32[]{:S(2)}, u32[]{:S(2)}) collective-permute-start(bf16[128,1536]{1,0:T(8,128)(2,1)S(1)} %add_convert_fusion.8), channel_id=1, source_target_pairs={{0,8},{4,12},{8,0},{12,4},{1,9},{5,13},{9,1},{13,5},{2,10},{6,14},... | collective-permute-start | bytes 1179656 | tf_op jit(solution)/shard_map/ppermute | solution.py:227
  298.1 22.0 %collective-permute-start.49 = (bf16[128,1536]{1,0:T(8,128)(2,1)S(1)}, bf16[128,1536]{1,0:T(8,128)(2,1)S(1)}, u32[]{:S(2)}, u32[]{:S(2)}) collective-permute-start(bf16[128,1536]{1,0:T(8,128)(2,1)S(1)} %add_convert_fusion.8), channel_id=1, source_target_pairs={{0,4},{4,0},{8,12},{12,8},{1,5},{5,1},{9,13},{13,9},{2,6},{6,2},{1... | collective-permute-start | bytes 1179656 | tf_op jit(solution)/shard_map/ppermute | solution.py:227
  299.1 26.3 %collective-permute-start.31 = (bf16[128,1536]{1,0:T(8,128)(2,1)S(1)}, bf16[128,1536]{1,0:T(8,128)(2,1)S(1)}, u32[]{:S(2)}, u32[]{:S(2)}) collective-permute-start(bf16[128,1536]{1,0:T(8,128)(2,1)S(1)} %add_convert_fusion.12), channel_id=1, source_target_pairs={{0,12},{4,8},{8,4},{12,0},{1,13},{5,9},{9,5},{13,1},{2,14},{6,10},... | collective-permute-start | bytes 1179656 | tf_op jit(solution)/shard_map/ppermute | solution.py:227
  307.2 22.5 %collective-permute-start.30 = (bf16[128,1536]{1,0:T(8,128)(2,1)S(1)}, bf16[128,1536]{1,0:T(8,128)(2,1)S(1)}, u32[]{:S(2)}, u32[]{:S(2)}) collective-permute-start(bf16[128,1536]{1,0:T(8,128)(2,1)S(1)} %add_convert_fusion.12), channel_id=1, source_target_pairs={{0,8},{4,12},{8,0},{12,4},{1,9},{5,13},{9,1},{13,5},{2,10},{6,14},... | collective-permute-start | bytes 1179656 | tf_op jit(solution)/shard_map/ppermute | solution.py:227
  325.2 49.2 %collective-permute-start.52 = (bf16[256,1536]{1,0:T(8,128)(2,1)S(1)}, bf16[256,1536]{1,0:T(8,128)(2,1)S(1)}, u32[]{:S(2)}, u32[]{:S(2)}) collective-permute-start(bf16[256,1536]{1,0:T(8,128)(2,1)S(1)} %constant_dynamic-slice_fusion.18), channel_id=1, source_target_pairs={{0,2},{1,3},{2,0},{3,1},{4,6},{5,7},{6,4},{7,5},{8,10},{9,11},{10,... | collective-permute-start | bytes 2359304 | tf_op jit(solution)/shard_map/ppermute | solution.py:243
  334.7 73.6 %collective-permute-start.32 = (bf16[256,1536]{1,0:T(8,128)(2,1)S(1)}, bf16[256,1536]{1,0:T(8,128)(2,1)S(1)}, u32[]{:S(2)}, u32[]{:S(2)}) collective-permute-start(bf16[256,1536]{1,0:T(8,128)(2,1)S(1)} %constant_dynamic-slice_fusion.25), channel_id=1, source_target_pairs={{0,2},{1,3},{2,0},{3,1},{4,6},{5,7},{6,4},{7,5},{8,10},{9,11},{10,... | collective-permute-start | bytes 2359304 | tf_op jit(solution)/shard_map/ppermute | solution.py:243
  375.1 49.9 %collective-permute-start.53 = (bf16[256,1536]{1,0:T(8,128)(2,1)S(1)}, bf16[256,1536]{1,0:T(8,128)(2,1)S(1)}, u32[]{:S(2)}, u32[]{:S(2)}) collective-permute-start(bf16[256,1536]{1,0:T(8,128)(2,1)S(1)} %fusion.21), channel_id=1, source_target_pairs={{0,2},{1,3},{2,0},{3,1},{4,6},{5,7},{6,4},{7,5},{8,10},{9,11},{10,... | collective-permute-start | bytes 2359304 | tf_op jit(solution)/shard_map/ppermute | solution.py:243
  375.9 108.4 %collective-permute-start.62 = (bf16[768,1152]{1,0:T(8,128)(2,1)S(1)}, bf16[768,1152]{1,0:T(8,128)(2,1)S(1)}, u32[]{:S(2)}, u32[]{:S(2)}) collective-permute-start(bf16[768,1152]{1,0:T(8,128)(2,1)S(1)} %pad_maximum_fusion.7), channel_id=1, source_target_pairs={{16,17},{17,16},{18,19},{19,18},{20,21},{21,20},{22,23},{23,22},{2... | collective-permute-start | bytes 5308424 | tf_op jit(solution)/shard_map/ppermute | solution.py:311
  425.1 33.7 %collective-permute-start.39 = (bf16[256,1536]{1,0:T(8,128)(2,1)S(1)}, bf16[256,1536]{1,0:T(8,128)(2,1)S(1)}, u32[]{:S(2)}, u32[]{:S(2)}) collective-permute-start(bf16[256,1536]{1,0:T(8,128)(2,1)S(1)} %fusion.13), channel_id=1, source_target_pairs={{0,2},{1,3},{2,0},{3,1},{4,6},{5,7},{6,4},{7,5},{8,10},{9,11},{10,... | collective-permute-start | bytes 2359304 | tf_op jit(solution)/shard_map/ppermute | solution.py:243
  431.8 17.7 %collective-permute-start.56 = (bf16[128,1536]{1,0:T(8,128)(2,1)S(1)}, bf16[128,1536]{1,0:T(8,128)(2,1)S(1)}, u32[]{:S(2)}, u32[]{:S(2)}) collective-permute-start(bf16[128,1536]{1,0:T(8,128)(2,1)S(1)} %get-tuple-element.204), channel_id=1, source_target_pairs={{0,12},{4,8},{8,4},{12,0},{1,13},{5,9},{9,5},{13,1},{2,14},{6,10},... | collective-permute-start | bytes 1179656 | tf_op jit(solution)/shard_map/ppermute | solution.py:234
  432.6 19.4 %collective-permute-start.55 = (bf16[128,1536]{1,0:T(8,128)(2,1)S(1)}, bf16[128,1536]{1,0:T(8,128)(2,1)S(1)}, u32[]{:S(2)}, u32[]{:S(2)}) collective-permute-start(bf16[128,1536]{1,0:T(8,128)(2,1)S(1)} %get-tuple-element.205), channel_id=1, source_target_pairs={{0,8},{4,12},{8,0},{12,4},{1,9},{5,13},{9,1},{13,5},{2,10},{6,14},... | collective-permute-start | bytes 1179656 | tf_op jit(solution)/shard_map/ppermute | solution.py:234
  440.6 45.8 %collective-permute-start.70 = (bf16[384,768]{1,0:T(8,128)(2,1)S(1)}, bf16[384,768]{1,0:T(8,128)(2,1)S(1)}, u32[]{:S(2)}, u32[]{:S(2)}) collective-permute-start(bf16[384,768]{1,0:T(8,128)(2,1)S(1)} %pad_maximum_fusion.17), channel_id=1, source_target_pairs={{16,17},{17,16},{18,19},{19,18},{20,21},{21,20},{22,23},{23,22},{2... | collective-permute-start | bytes 1769480 | tf_op jit(solution)/shard_map/ppermute | solution.py:311
  463.5 18.0 %collective-permute-start.42 = (bf16[128,1536]{1,0:T(8,128)(2,1)S(1)}, bf16[128,1536]{1,0:T(8,128)(2,1)S(1)}, u32[]{:S(2)}, u32[]{:S(2)}) collective-permute-start(bf16[128,1536]{1,0:T(8,128)(2,1)S(1)} %get-tuple-element.199), channel_id=1, source_target_pairs={{0,12},{4,8},{8,4},{12,0},{1,13},{5,9},{9,5},{13,1},{2,14},{6,10},... | collective-permute-start | bytes 1179656 | tf_op jit(solution)/shard_map/ppermute | solution.py:234
  464.4 19.6 %collective-permute-start.41 = (bf16[128,1536]{1,0:T(8,128)(2,1)S(1)}, bf16[128,1536]{1,0:T(8,128)(2,1)S(1)}, u32[]{:S(2)}, u32[]{:S(2)}) collective-permute-start(bf16[128,1536]{1,0:T(8,128)(2,1)S(1)} %get-tuple-element.200), channel_id=1, source_target_pairs={{0,8},{4,12},{8,0},{12,4},{1,9},{5,13},{9,1},{13,5},{2,10},{6,14},... | collective-permute-start | bytes 1179656 | tf_op jit(solution)/shard_map/ppermute | solution.py:234
  472.4 30.5 %collective-permute-start.72 = (bf16[768,1536]{1,0:T(8,128)(2,1)S(1)}, bf16[768,1536]{1,0:T(8,128)(2,1)S(1)}, u32[]{:S(2)}, u32[]{:S(2)}) collective-permute-start(bf16[768,1536]{1,0:T(8,128)(2,1)S(1)} %get-tuple-element.167), channel_id=1, source_target_pairs={{16,17},{17,16},{18,19},{19,18},{20,21},{21,20},{22,23},{23,22},{2... | collective-permute-start | bytes 7077896 | tf_op jit(solution)/shard_map/ppermute | solution.py:311
  484.3 17.7 %collective-permute-start.43 = (bf16[128,1536]{1,0:T(8,128)(2,1)S(1)}, bf16[128,1536]{1,0:T(8,128)(2,1)S(1)}, u32[]{:S(2)}, u32[]{:S(2)}) collective-permute-start(bf16[128,1536]{1,0:T(8,128)(2,1)S(1)} %pad_maximum_fusion.20), channel_id=1, source_target_pairs={{0,1},{1,0},{2,3},{3,2},{4,5},{5,4},{6,7},{7,6},{8,9},{9,8},{10,11... | collective-permute-start | bytes 1179656 | tf_op jit(solution)/shard_map/ppermute | solution.py:239
  485.0 32.3 %collective-permute-start.63 = (bf16[1536,1152]{1,0:T(8,128)(2,1)S(1)}, bf16[1536,1152]{1,0:T(8,128)(2,1)S(1)}, u32[]{:S(2)}, u32[]{:S(2)}) collective-permute-start(bf16[1536,1152]{1,0:T(8,128)(2,1)S(1)} %fusion.2), channel_id=1, source_target_pairs={{16,0},{17,1},{18,2},{19,3},{20,4},{21,5},{22,6},{23,7},{24,8},{25... | collective-permute-start | bytes 10616840 | tf_op jit(solution)/shard_map/ppermute | solution.py:313
  505.4 83.8 %collective-permute-start.73 = (bf16[1536,1536]{1,0:T(8,128)(2,1)}, bf16[1536,1536]{1,0:T(8,128)(2,1)}, u32[]{:S(2)}, u32[]{:S(2)}) collective-permute-start(bf16[1536,1536]{1,0:T(8,128)(2,1)} %pad_maximum_fusion.2), channel_id=1, source_target_pairs={{16,0},{17,1},{18,2},{19,3},{20,4},{21,5},{22,6},{23,7},{24,8},{25... | collective-permute-start | bytes 14155784 | tf_op jit(solution)/shard_map/ppermute | solution.py:313
  517.4 71.8 %collective-permute-start.71 = (bf16[384,1536]{1,0:T(8,128)(2,1)}, bf16[384,1536]{1,0:T(8,128)(2,1)}, u32[]{:S(2)}, u32[]{:S(2)}) collective-permute-start(bf16[384,1536]{1,0:T(8,128)(2,1)} %pad_maximum_fusion.9), channel_id=1, source_target_pairs={{16,0},{17,1},{18,2},{19,3},{20,4},{21,5},{22,6},{23,7},{24,8},{25... | collective-permute-start | bytes 3538952 | tf_op jit(solution)/shard_map/ppermute | solution.py:313
  538.0 30.7 %collective-permute-start.64 = (bf16[512,576]{0,1:T(8,128)(2,1)}, bf16[512,576]{0,1:T(8,128)(2,1)}, u32[]{:S(2)}, u32[]{:S(2)}) collective-permute-start(bf16[512,576]{0,1:T(8,128)(2,1)} %copy.56), channel_id=1, source_target_pairs={{0,2},{1,3},{2,0},{3,1},{4,6},{5,7},{6,4},{7,5},{8,10},{9,11},{10,... | collective-permute-start | bytes 1769480 | tf_op jit(solution)/shard_map/ppermute | solution.py:243
  539.8 74.8 %collective-permute-start.89 = (bf16[1536,768]{1,0:T(8,128)(2,1)}, bf16[1536,768]{1,0:T(8,128)(2,1)}, u32[]{:S(2)}, u32[]{:S(2)}) collective-permute-start(bf16[1536,768]{1,0:T(8,128)(2,1)} %get-tuple-element.165), channel_id=1, source_target_pairs={{16,17},{17,16},{18,19},{19,18},{20,21},{21,20},{22,23},{23,22},{2... | collective-permute-start | bytes 7077896 | tf_op jit(solution)/shard_map/ppermute | solution.py:311
  547.6 33.8 %collective-permute-start.69 = (bf16[512,576]{0,1:T(8,128)(2,1)}, bf16[512,576]{0,1:T(8,128)(2,1)}, u32[]{:S(2)}, u32[]{:S(2)}) collective-permute-start(bf16[512,576]{0,1:T(8,128)(2,1)} %copy.59), channel_id=1, source_target_pairs={{0,2},{1,3},{2,0},{3,1},{4,6},{5,7},{6,4},{7,5},{8,10},{9,11},{10,... | collective-permute-start | bytes 1769480 | tf_op jit(solution)/shard_map/ppermute | solution.py:243
  589.3 16.9 %collective-permute-start.74 = (bf16[3,1024,128]{2,1,0:T(8,128)(2,1)S(1)}, bf16[3,1024,128]{2,1,0:T(8,128)(2,1)S(1)}, u32[]{:S(2)}, u32[]{:S(2)}) collective-permute-start(bf16[3,1024,128]{2,1,0:T(8,128)(2,1)S(1)} %broadcast_select_fusion.30), channel_id=1, source_target_pairs={{0,16},{16,0},{1,17},{17,1},{2,18},{18,2},{3,19},{19,3},{4,20},{20... | collective-permute-start | bytes 2359304 | tf_op jit(solution)/shard_map/ppermute | solution.py:205
  611.4 21.5 %collective-permute-start.85 = (bf16[512,192]{1,0:T(8,128)(2,1)S(1)}, bf16[512,192]{1,0:T(8,128)(2,1)S(1)}, u32[]{:S(2)}, u32[]{:S(2)}) collective-permute-start(bf16[512,192]{1,0:T(8,128)(2,1)S(1)} %attend.7), channel_id=1, source_target_pairs={{0,2},{1,3},{2,0},{3,1},{4,6},{5,7},{6,4},{7,5},{8,10},{9,11},{10,... | collective-permute-start | bytes 589832 | tf_op jit(solution)/shard_map/ppermute | solution.py:243
  621.8 19.7 %collective-permute-start.75 = (bf16[512,192]{1,0:T(8,128)(2,1)S(1)}, bf16[512,192]{1,0:T(8,128)(2,1)S(1)}, u32[]{:S(2)}, u32[]{:S(2)}) collective-permute-start(bf16[512,192]{1,0:T(8,128)(2,1)S(1)} %attend.6), channel_id=1, source_target_pairs={{0,2},{1,3},{2,0},{3,1},{4,6},{5,7},{6,4},{7,5},{8,10},{9,11},{10,... | collective-permute-start | bytes 589832 | tf_op jit(solution)/shard_map/ppermute | solution.py:243
  639.8 20.2 %collective-permute-start.98 = (bf16[128,1536]{1,0:T(8,128)(2,1)S(1)}, bf16[128,1536]{1,0:T(8,128)(2,1)S(1)}, u32[]{:S(2)}, u32[]{:S(2)}) collective-permute-start(bf16[128,1536]{1,0:T(8,128)(2,1)S(1)} %get-tuple-element.196), channel_id=1, source_target_pairs={{0,12},{4,8},{8,4},{12,0},{1,13},{5,9},{9,5},{13,1},{2,14},{6,10},... | collective-permute-start | bytes 1179656 | tf_op jit(solution)/shard_map/ppermute | solution.py:234
  641.6 19.7 %collective-permute-start.97 = (bf16[128,1536]{1,0:T(8,128)(2,1)S(1)}, bf16[128,1536]{1,0:T(8,128)(2,1)S(1)}, u32[]{:S(2)}, u32[]{:S(2)}) collective-permute-start(bf16[128,1536]{1,0:T(8,128)(2,1)S(1)} %get-tuple-element.197), channel_id=1, source_target_pairs={{0,8},{4,12},{8,0},{12,4},{1,9},{5,13},{9,1},{13,5},{2,10},{6,14},... | collective-permute-start | bytes 1179656 | tf_op jit(solution)/shard_map/ppermute | solution.py:234
  647.1 123.6 %collective-permute-start.90 = (bf16[1536,1536]{1,0:T(8,128)(2,1)S(1)}, bf16[1536,1536]{1,0:T(8,128)(2,1)S(1)}, u32[]{:S(2)}, u32[]{:S(2)}) collective-permute-start(bf16[1536,1536]{1,0:T(8,128)(2,1)S(1)} %pad_maximum_fusion.3), channel_id=1, source_target_pairs={{16,0},{17,1},{18,2},{19,3},{20,4},{21,5},{22,6},{23,7},{24,8},{25... | collective-permute-start | bytes 14155784 | tf_op jit(solution)/shard_map/ppermute | solution.py:313
  651.2 26.6 %collective-permute-start.88 = (bf16[1,3,256,128]{3,2,0,1:T(8,128)(2,1)S(1)}, bf16[1,3,256,128]{3,2,0,1:T(8,128)(2,1)S(1)}, u32[]{:S(2)}, u32[]{:S(2)}) collective-permute-start(bf16[1,3,256,128]{3,2,0,1:T(8,128)(2,1)S(1)} %get-tuple-element.232), channel_id=1, source_target_pairs={{0,3},{1,0},{2,1},{3,2},{4,7},{5,4},{6,5},{7,6},{8,11},{9,8},{10,9... | collective-permute-start | bytes 589832 | tf_op jit(solution)/shard_map/ppermute | solution.py:167
  651.2 16.7 %collective-permute-start.76 = (bf16[128,1536]{1,0:T(8,128)(2,1)S(1)}, bf16[128,1536]{1,0:T(8,128)(2,1)S(1)}, u32[]{:S(2)}, u32[]{:S(2)}) collective-permute-start(bf16[128,1536]{1,0:T(8,128)(2,1)S(1)} %get-tuple-element.192), channel_id=1, source_target_pairs={{0,4},{4,0},{8,12},{12,8},{1,5},{5,1},{9,13},{13,9},{2,6},{6,2},{1... | collective-permute-start | bytes 1179656 | tf_op jit(solution)/shard_map/ppermute | solution.py:234
  693.4 23.5 %collective-permute-start.82 = (bf16[128,1536]{1,0:T(8,128)(2,1)S(1)}, bf16[128,1536]{1,0:T(8,128)(2,1)S(1)}, u32[]{:S(2)}, u32[]{:S(2)}) collective-permute-start(bf16[128,1536]{1,0:T(8,128)(2,1)S(1)} %add_convert_fusion.4), channel_id=1, source_target_pairs={{0,8},{4,12},{8,0},{12,4},{1,9},{5,13},{9,1},{13,5},{2,10},{6,14},... | collective-permute-start | bytes 1179656 | tf_op jit(solution)/shard_map/ppermute | solution.py:227
  694.3 22.6 %collective-permute-start.81 = (bf16[128,1536]{1,0:T(8,128)(2,1)S(1)}, bf16[128,1536]{1,0:T(8,128)(2,1)S(1)}, u32[]{:S(2)}, u32[]{:S(2)}) collective-permute-start(bf16[128,1536]{1,0:T(8,128)(2,1)S(1)} %add_convert_fusion.4), channel_id=1, source_target_pairs={{0,4},{4,0},{8,12},{12,8},{1,5},{5,1},{9,13},{13,9},{2,6},{6,2},{1... | collective-permute-start | bytes 1179656 | tf_op jit(solution)/shard_map/ppermute | solution.py:227
  696.4 28.3 %collective-permute-start.103 = (bf16[128,1536]{1,0:T(8,128)(2,1)S(1)}, bf16[128,1536]{1,0:T(8,128)(2,1)S(1)}, u32[]{:S(2)}, u32[]{:S(2)}) collective-permute-start(bf16[128,1536]{1,0:T(8,128)(2,1)S(1)} %add_convert_fusion.1), channel_id=1, source_target_pairs={{0,12},{4,8},{8,4},{12,0},{1,13},{5,9},{9,5},{13,1},{2,14},{6,10},... | collective-permute-start | bytes 1179656 | tf_op jit(solution)/shard_map/ppermute | solution.py:227
  705.0 19.8 %collective-permute-start.102 = (bf16[128,1536]{1,0:T(8,128)(2,1)S(1)}, bf16[128,1536]{1,0:T(8,128)(2,1)S(1)}, u32[]{:S(2)}, u32[]{:S(2)}) collective-permute-start(bf16[128,1536]{1,0:T(8,128)(2,1)S(1)} %add_convert_fusion.1), channel_id=1, source_target_pairs={{0,8},{4,12},{8,0},{12,4},{1,9},{5,13},{9,1},{13,5},{2,10},{6,14},... | collective-permute-start | bytes 1179656 | tf_op jit(solution)/shard_map/ppermute | solution.py:227
  721.9 48.1 %collective-permute-start.84 = (bf16[256,1536]{1,0:T(8,128)(2,1)S(1)}, bf16[256,1536]{1,0:T(8,128)(2,1)S(1)}, u32[]{:S(2)}, u32[]{:S(2)}) collective-permute-start(bf16[256,1536]{1,0:T(8,128)(2,1)S(1)} %constant_dynamic-slice_fusion.7), channel_id=1, source_target_pairs={{0,2},{1,3},{2,0},{3,1},{4,6},{5,7},{6,4},{7,5},{8,10},{9,11},{10,... | collective-permute-start | bytes 2359304 | tf_op jit(solution)/shard_map/ppermute | solution.py:243
  729.8 73.9 %collective-permute-start.104 = (bf16[256,1536]{1,0:T(8,128)(2,1)S(1)}, bf16[256,1536]{1,0:T(8,128)(2,1)S(1)}, u32[]{:S(2)}, u32[]{:S(2)}) collective-permute-start(bf16[256,1536]{1,0:T(8,128)(2,1)S(1)} %constant_dynamic-slice_fusion.1), channel_id=1, source_target_pairs={{0,2},{1,3},{2,0},{3,1},{4,6},{5,7},{6,4},{7,5},{8,10},{9,11},{10,... | collective-permute-start | bytes 2359304 | tf_op jit(solution)/shard_map/ppermute | solution.py:243
  770.6 66.8 %collective-permute-start.91 = (bf16[256,1536]{1,0:T(8,128)(2,1)S(1)}, bf16[256,1536]{1,0:T(8,128)(2,1)S(1)}, u32[]{:S(2)}, u32[]{:S(2)}) collective-permute-start(bf16[256,1536]{1,0:T(8,128)(2,1)S(1)} %fusion.29), channel_id=1, source_target_pairs={{0,2},{1,3},{2,0},{3,1},{4,6},{5,7},{6,4},{7,5},{8,10},{9,11},{10,... | collective-permute-start | bytes 2359304 | tf_op jit(solution)/shard_map/ppermute | solution.py:243
  804.3 48.8 %collective-permute-start.105 = (bf16[256,1536]{1,0:T(8,128)(2,1)S(1)}, bf16[256,1536]{1,0:T(8,128)(2,1)S(1)}, u32[]{:S(2)}, u32[]{:S(2)}) collective-permute-start(bf16[256,1536]{1,0:T(8,128)(2,1)S(1)} %fusion.37), channel_id=1, source_target_pairs={{0,2},{1,3},{2,0},{3,1},{4,6},{5,7},{6,4},{7,5},{8,10},{9,11},{10,... | collective-permute-start | bytes 2359304 | tf_op jit(solution)/shard_map/ppermute | solution.py:243
  840.6 18.0 %collective-permute-start.92 = (bf16[128,1536]{1,0:T(8,128)(2,1)S(1)}, bf16[128,1536]{1,0:T(8,128)(2,1)S(1)}, u32[]{:S(2)}, u32[]{:S(2)}) collective-permute-start(bf16[128,1536]{1,0:T(8,128)(2,1)S(1)} %get-tuple-element.182), channel_id=1, source_target_pairs={{0,4},{4,0},{8,12},{12,8},{1,5},{5,1},{9,13},{13,9},{2,6},{6,2},{1... | collective-permute-start | bytes 1179656 | tf_op jit(solution)/shard_map/ppermute | solution.py:234
  842.0 17.6 %collective-permute-start.94 = (bf16[128,1536]{1,0:T(8,128)(2,1)S(1)}, bf16[128,1536]{1,0:T(8,128)(2,1)S(1)}, u32[]{:S(2)}, u32[]{:S(2)}) collective-permute-start(bf16[128,1536]{1,0:T(8,128)(2,1)S(1)} %get-tuple-element.183), channel_id=1, source_target_pairs={{0,12},{4,8},{8,4},{12,0},{1,13},{5,9},{9,5},{13,1},{2,14},{6,10},... | collective-permute-start | bytes 1179656 | tf_op jit(solution)/shard_map/ppermute | solution.py:234
  843.2 16.9 %collective-permute-start.93 = (bf16[128,1536]{1,0:T(8,128)(2,1)S(1)}, bf16[128,1536]{1,0:T(8,128)(2,1)S(1)}, u32[]{:S(2)}, u32[]{:S(2)}) collective-permute-start(bf16[128,1536]{1,0:T(8,128)(2,1)S(1)} %get-tuple-element.184), channel_id=1, source_target_pairs={{0,8},{4,12},{8,0},{12,4},{1,9},{5,13},{9,1},{13,5},{2,10},{6,14},... | collective-permute-start | bytes 1179656 | tf_op jit(solution)/shard_map/ppermute | solution.py:234
  857.4 17.9 %collective-permute-start.108 = (bf16[128,1536]{1,0:T(8,128)(2,1)S(1)}, bf16[128,1536]{1,0:T(8,128)(2,1)S(1)}, u32[]{:S(2)}, u32[]{:S(2)}) collective-permute-start(bf16[128,1536]{1,0:T(8,128)(2,1)S(1)} %get-tuple-element.188), channel_id=1, source_target_pairs={{0,12},{4,8},{8,4},{12,0},{1,13},{5,9},{9,5},{13,1},{2,14},{6,10},... | collective-permute-start | bytes 1179656 | tf_op jit(solution)/shard_map/ppermute | solution.py:234
  858.6 18.1 %collective-permute-start.107 = (bf16[128,1536]{1,0:T(8,128)(2,1)S(1)}, bf16[128,1536]{1,0:T(8,128)(2,1)S(1)}, u32[]{:S(2)}, u32[]{:S(2)}) collective-permute-start(bf16[128,1536]{1,0:T(8,128)(2,1)S(1)} %get-tuple-element.189), channel_id=1, source_target_pairs={{0,8},{4,12},{8,0},{12,4},{1,9},{5,13},{9,1},{13,5},{2,10},{6,14},... | collective-permute-start | bytes 1179656 | tf_op jit(solution)/shard_map/ppermute | solution.py:234
  860.3 18.2 %collective-permute-start.95 = (bf16[128,1536]{1,0:T(8,128)(2,1)S(1)}, bf16[128,1536]{1,0:T(8,128)(2,1)S(1)}, u32[]{:S(2)}, u32[]{:S(2)}) collective-permute-start(bf16[128,1536]{1,0:T(8,128)(2,1)S(1)} %pad_maximum_fusion.25), channel_id=1, source_target_pairs={{0,1},{1,0},{2,3},{3,2},{4,5},{5,4},{6,7},{7,6},{8,9},{9,8},{10,11... | collective-permute-start | bytes 1179656 | tf_op jit(solution)/shard_map/ppermute | solution.py:239
  (138 other events, 1287.1 us)

commit v8 on v7

--- a/solution.py
+++ b/solution.py
@@ -306,11 +306,19 @@
         order = [lax.dynamic_index_in_dim(blocks, wide_idx ^ step, 0, False) for step in range(n_wide)]
         return jnp.stack(order, axis=1).reshape(total_rows)
 
-    def weight_of(layer, kept, sent, axis):
+    def mate_half(layer, sent):
         pairs = [(layer * n_narrow + i, layer * n_narrow + (i ^ 1)) for i in range(n_narrow)]
-        got = lax.ppermute(sent, ("section", "narrow"), pairs)
+        return lax.ppermute(sent, ("section", "narrow"), pairs)
+
+    def passed(layer, value):
+        return lax.ppermute(value, "section", [(layer, 1 - layer)])
+
+    def pass_on(layer, kept, got, axis):
         joined = jnp.concatenate([kept, got], axis=axis)
-        return joined, lax.ppermute(joined, "section", [(layer, 1 - layer)])
+        return joined, passed(layer, joined)
+
+    def weight_of(layer, parts, axis):
+        return pass_on(layer, parts[0], mate_half(layer, parts[1]), axis)
 
     def select(layer, weight):
         return jnp.where(section == layer, weight[0], weight[1])
@@ -319,38 +327,46 @@
         starts = [first * size, second * size]
         return jnp.concatenate([lax.dynamic_slice_in_dim(own, at, size, axis) for at in starts], axis=axis)
 
-    def qkv_of(layer, own):
-        size = own.shape[1] // 4
-        parts = [two_blocks(own, 1, size, 2 * p + 1 - high, 2 * p + high) for p in (odd, 1 - odd)]
-        return weight_of(layer, parts[0], parts[1], 0)
-
-    def out_of(layer, own):
-        size = own.shape[0] // 4
-        parts = [two_blocks(own, 0, size, 2 * p + high, 2 * p + 1 - high) for p in (odd, 1 - odd)]
-        return weight_of(layer, parts[0], parts[1], 1)
-
-    def up_of(layer, own):
-        size = own.shape[1] // 2
-        parts = [lax.dynamic_slice_in_dim(own, p * size, size, 1) for p in (odd, 1 - odd)]
-        return weight_of(layer, parts[0], parts[1], 0)
-
-    def down_of(layer, own):
-        size = own.shape[0] // 2
-        parts = [lax.dynamic_slice_in_dim(own, p * size, size, 0) for p in (odd, 1 - odd)]
-        return weight_of(layer, parts[0], parts[1], 1)
+    size = w_qkv.shape[1] // 4
+    qkv_parts = [two_blocks(w_qkv, 1, size, 2 * p + 1 - high, 2 * p + high) for p in (odd, 1 - odd)]
+    size = w_out.shape[0] // 4
+    out_parts = [two_blocks(w_out, 0, size, 2 * p + high, 2 * p + 1 - high) for p in (odd, 1 - odd)]
+    size = w_up.shape[1] // 2
+    up_parts = [lax.dynamic_slice_in_dim(w_up, p * size, size, 1) for p in (odd, 1 - odd)]
+    size = w_down.shape[0] // 2
+    down_parts = [lax.dynamic_slice_in_dim(w_down, p * size, size, 0) for p in (odd, 1 - odd)]
+
+    def ordered_parts(value, parts):
+        value, sent = ordered(value, parts[1])
+        return value, (parts[0], sent)
 
     layer_in = lax.dynamic_index_in_dim(hidden_in, section, 0, False)
     layer_in = jnp.concatenate([layer_in, to_mate(layer_in)], axis=1)
+    layer_in, sent, timesteps, stale = ordered(layer_in, qkv_parts[1], timesteps, stale_cache[0, 1])
+    got = mate_half(0, sent)
+    kept = passed(0, qkv_parts[0])
+    layer_in, kept = ordered(layer_in, kept)
+    qkv_now = jnp.concatenate(
+        [
+            jnp.where(lead, qkv_parts[0], kept),
+            jnp.where(lead, got, passed(0, got)),
+        ],
+        axis=0,
+    )
     first_mean, first_scale = statistics(layer_in.astype(F32))
-    first_mean, w_qkv_now, stale = ordered(first_mean, w_qkv, stale_cache[0, 1])
-    qkv_weight = qkv_of(0, w_qkv_now)
     layer_in = [layer_in[h * part : (h + 1) * part] for h in range(halves)]
 
     activated = jax.nn.silu(time_features(timesteps, ada_weight.shape[1])).astype(BF)
     modulation = jnp.einsum("re,kesd->krsd", activated, ada_weight, preferred_element_type=F32)
     modulation = modulation.reshape(2, 4, 3, feat_a)
-    tables = both_layers(jnp.concatenate([modulation, to_mate(modulation)], axis=-1))
-    norm_rows = both_layers(qk_norm)
+    modulation = jnp.concatenate([modulation, to_mate(modulation)], axis=-1)
+    shape = modulation.shape
+    width = shape[-1]
+    rows = modulation.reshape(-1, width)
+    last = jnp.concatenate([qk_norm.reshape(-1), jnp.zeros((width - qk_norm.size,), F32)])
+    both = both_layers(jnp.concatenate([rows, last[None]], axis=0))
+    tables = [table[:-1].reshape(shape) for table in both]
+    norm_rows = [table[-1, : qk_norm.size].reshape(qk_norm.shape) for table in both]
     kinds = lax.dynamic_index_in_dim(row_kind, section, 0, False)
     kinds_other = lax.dynamic_index_in_dim(row_kind, 1 - section, 0, False)
     kinds_r = relative(kinds)
@@ -383,7 +399,6 @@
         far = to_mate(jnp.concatenate([total[:, feat_a:], total[:, :feat_a]], axis=1))
         return total.astype(F32) + far.astype(F32)
 
-    stale = stale_heads(stale)
     results = []
     caches = []
     for layer in range(2):
@@ -400,16 +415,15 @@
                 moments = statistics(x_in[h])
             entry = normed(x_in[h], moments, table[0], kinds_h[h])
             if layer == 0 and h == 0:
-                entry, w_out_now, w_up_now = ordered(entry, w_out, w_up)
-                out_weight = out_of(0, w_out_now)
-                up_weight = up_of(0, w_up_now)
-            terms = jnp.dot(gather_wide(entry), select(layer, qkv_weight), preferred_element_type=F32)
-            terms = terms.astype(BF)
-            if h == 0:
-                terms, w_down_now = ordered(terms, w_down)
-                down_weight = down_of(layer, w_down_now)
-                if layer == 0:
-                    terms, stale = ordered(terms, stale)
+                entry, stale = ordered(entry, stale_heads(stale))
+            terms = jnp.dot(gather_wide(entry), qkv_now, preferred_element_type=F32).astype(BF)
+            if layer == 0 and h == 0:
+                terms, out_sent, up_sent = ordered(terms, out_parts[1], up_parts[1])
+                out_got, up_got = mate_half(0, out_sent), mate_half(0, up_sent)
+            if layer == 0 and h == 1:
+                terms, out_got, up_got = ordered(terms, out_got, up_got)
+                out_weight = pass_on(0, out_parts[0], out_got, 1)
+                up_weight = pass_on(0, up_parts[0], up_got, 0)
             width = terms.shape[1] // 2
             qkv = terms[:, width:].astype(F32) + to_partner(terms[:, :width]).astype(F32)
             rows = slice(h * chunk, (h + 1) * chunk)
@@ -428,30 +442,45 @@
         after = []
         for h in range(halves):
             attended = attend(queries[h], own, other, own_mask, other_mask, head_dim)
+            if h == 1:
+                attended, first_terms = ordered(attended, first_terms)
             attended = jnp.concatenate([attended, to_partner(attended)], axis=1)
             terms = jnp.dot(attended, select(layer, out_weight), preferred_element_type=F32).astype(BF)
-            if h == 1:
+            if h == 0:
+                first_terms = terms
+            else:
                 terms, *fresh = ordered(terms, *fresh)
                 cache = to_rows(fresh)
             after.append(x_in[h] + pick(table[0], kinds_h[h], 2) * summed(terms))
+        after[0], cache = ordered(after[0], cache)
+        caches.append(cache)
         inner = []
+        mean, scale = statistics(jnp.concatenate(after, axis=0))
         for h in range(halves):
-            entry = normed(after[h], statistics(after[h]), table[1], kinds_h[h])
+            rows = slice(h * part, (h + 1) * part)
+            entry = normed(after[h], (mean[rows], scale[rows]), table[1], kinds_h[h])
             if layer == 0 and h == 0:
-                entry, w_qkv_now = ordered(entry, w_qkv)
-                qkv_weight = qkv_of(1, w_qkv_now)
+                entry, parts = ordered_parts(entry, qkv_parts)
+                qkv_weight = weight_of(1, parts, 0)
+            if h == 0:
+                entry, down_sent = ordered(entry, down_parts[1])
+                down_got = mate_half(layer, down_sent)
             entry = gather_wide(entry)
             up = jnp.dot(entry, select(layer, up_weight), preferred_element_type=F32).astype(BF)
+            if h == 1:
+                up, down_got = ordered(up, down_got)
+                down_weight = pass_on(layer, down_parts[0], down_got, 1)
             size = chunk // 2
             got = to_partner(lax.dynamic_slice_in_dim(up, (1 - high) * size, size, 0))
             up = lax.dynamic_slice_in_dim(up, high * size, size, 0).astype(F32) + got.astype(F32)
             inner.append(jax.nn.gelu(up, approximate=True).astype(BF))
-        inner[0], cache, *down_weight = ordered(inner[0], cache, *down_weight)
-        caches.append(cache)
+        inner[0], *down_weight = ordered(inner[0], *down_weight)
         if layer == 0:
-            inner[0], w_out_now, w_up_now = ordered(inner[0], w_out, w_up)
-            out_weight = out_of(1, w_out_now)
-            up_weight = up_of(1, w_up_now)
+            inner[0], parts = ordered_parts(inner[0], out_parts)
+            out_weight = weight_of(1, parts, 1)
+            inner[0], parts = ordered_parts(inner[0], up_parts)
+            up_weight = weight_of(1, parts, 0)
+            qkv_now = select(1, qkv_weight)
         layer_in = []
         for h in range(halves):
             got = to_partner(inner[h])

time: 899 us -> 951 us (1.058)
  waiting for transfers between devices: 510 us -> 550 us
  starting transfers between devices: 174 us -> 148 us
  local copies, waits for them, and re-layouts: 48.3 us -> 69 us
  other arithmetic: 56.2 us -> 66.6 us
    ppermute x24, waiting for transfers between devices: 41.1 us -> 98.1 us  [gather_wide(): lax.ppermute(block, 'wide', wide_pairs(step))]
    ppermute x24, waiting for transfers between devices: 93.2 us -> 59.6 us  [scatter_wide(): total += lax.ppermute(terms[step], 'wide', wide_pairs(step)).astype(F32)]
    ppermute x10, waiting for transfers between devices: 38.4 us -> 69.3 us  [to_mate(): lax.ppermute(value, 'narrow', [(i, i ^ 1) for i in range(lax.axis_size('n...]
    ppermute x16 -> x17, waiting for transfers between devices: 32.9 us -> 16.1 us  [the longest x8 16.1 us: mate_half(): return lax.ppermute(sent, ('section', 'narrow'), pairs)]
    ppermute x5 -> x4, starting transfers between devices: 15.8 us -> 1.52 us  [swap(): return lax.ppermute(value, 'section', [(0, 1), (1, 0)])]
    ppermute x24, starting transfers between devices: 37 us -> 27.3 us  [gather_wide(): lax.ppermute(block, 'wide', wide_pairs(step))]
    ppermute x23 -> x21, waiting for transfers between devices: 279 us -> 274 us  [to_partner(): lax.ppermute(value, 'narrow', [(i, i ^ 2) for i in range(lax.axis_size('n...]
    ppermute x16 -> x17, starting transfers between devices: 30.6 us -> 34.2 us  [the longest x9 21.1 us: passed(): return lax.ppermute(value, 'section', [(layer, 1 - layer)])]
  transfers between devices with their start and end apart: 112 -> 110, of which waited for: 60 -> 69; matrix products, arithmetic and copies ran while one was open for 18% -> 17% of each run, Pallas kernels for 4% -> 3%
where the time goes in v8:
time: 951 us; the launch traced here: 943 us
  waiting for transfers between devices  550 us (58%)
  starting transfers between devices  148 us (16%)
  local copies, waits for them, and re-layouts  69 us (7%)
  matrix products  67.8 us (7%)
  other arithmetic  66.6 us (7%)
  Pallas kernels  37.9 us (4%)
    ppermute x21, waiting for transfers between devices, to_partner(): lax.ppermute(value, 'narrow', [(i, i ^ 2) for i in range(lax.axis_size('n...  274 us
    ppermute x24, waiting for transfers between devices, gather_wide(): lax.ppermute(block, 'wide', wide_pairs(step))  98.1 us
    ppermute x10, waiting for transfers between devices, to_mate(): lax.ppermute(value, 'narrow', [(i, i ^ 1) for i in range(lax.axis_size('n...  69.3 us
    ppermute x24, waiting for transfers between devices, scatter_wide(): total += lax.ppermute(terms[step], 'wide', wide_pairs(step)).astype(F32)  59.6 us
    ppermute x9, waiting for transfers between devices, exchange(): block = lax.ppermute(block, axis, [(i, (i + step) % n) for i in range(n)])  29.6 us
    ppermute x21, starting transfers between devices, to_partner(): lax.ppermute(value, 'narrow', [(i, i ^ 2) for i in range(lax.axis_size('n...  29.3 us
    ppermute x24, starting transfers between devices, scatter_wide(): total += lax.ppermute(terms[step], 'wide', wide_pairs(step)).astype(F32)  28.5 us
    ppermute x24, starting transfers between devices, gather_wide(): lax.ppermute(block, 'wide', wide_pairs(step))  27.3 us
  transfers between devices with their start and end apart: 110, of which 69 were waited for; matrix products, arithmetic and copies ran while one was open for 17% of the time, Pallas kernels for 3%

profile of v8, /device:TPU:0, one launch (start us, length us, event | category | flops | bytes accessed | tf_op | source)
XLA Modules:
  0.0 942.7 jit_solution(13253076944109495724)
XLA Ops:
  5.6 4.6 dynamic-slice_bitcast_fusion.5
  31.2 5.1 fusion.106
  47.9 15.7 %collective-permute-done.2 = f32[2,4,3,768]{3,0,2,1:T(2,128)} collective-permute-done((f32[2,4,3,768]{3,0,2,1:T(2,128)}, f32[2,4,3,768]{3,0,2,1:T(2,128)}, u32[]{:S(2)}, u32[]{:S(2)}) %collective-permute-start.2) | collective-permute-done | bytes 73760 | tf_op jit(solution)/shard_map/ppermute | solution.py:239
  94.9 7.8 collective-permute-done.10
  102.7 5.5 collective-permute-done.9
  122.0 5.5 collective-permute-done.16
  127.6 6.2 collective-permute-done.15
  137.2 11.4 %collective-permute-done.17 = bf16[384,768]{1,0:T(8,128)(2,1)S(1)} collective-permute-done((bf16[384,768]{1,0:T(8,128)(2,1)S(1)}, bf16[384,768]{1,0:T(8,128)(2,1)S(1)}, u32[]{:S(2)}, u32[]{:S(2)}) %collective-permute-start.17) | collective-permute-done | bytes 589856 | tf_op jit(solution)/shard_map/ppermute | solution.py:311
  172.3 19.1 %collective-permute-done.13 = bf16[512,576]{0,1:T(8,128)(2,1)} collective-permute-done((bf16[512,576]{0,1:T(8,128)(2,1)}, bf16[512,576]{0,1:T(8,128)(2,1)}, u32[]{:S(2)}, u32[]{:S(2)}) %collective-permute-start.13) | collective-permute-done | bytes 589856 | tf_op jit(solution)/shard_map/ppermute | solution.py:243
  212.9 5.9 attend.4
  218.8 4.9 dynamic-slice_bitcast_fusion
  226.2 5.2 attend.5
  240.6 9.0 collective-permute-done.28
  259.8 6.6 collective-permute-done.29
  266.6 7.0 collective-permute-done.30
  279.5 7.2 collective-permute-done.27
  286.7 7.5 collective-permute-done.35
  295.5 4.1 collective-permute-start.36
  309.5 9.1 collective-permute-done.43
  318.5 4.1 collective-permute-done.42
  322.9 6.1 convolution_convert_fusion.12
  329.0 4.7 collective-permute-done.44
  349.0 4.1 collective-permute-done.38
  353.3 5.4 convolution_convert_fusion.13
  362.7 36.7 %collective-permute-done.51 = bf16[256,1536]{1,0:T(8,128)(2,1)S(1)} collective-permute-done((bf16[256,1536]{1,0:T(8,128)(2,1)S(1)}, bf16[256,1536]{1,0:T(8,128)(2,1)S(1)}, u32[]{:S(2)}, u32[]{:S(2)}) %collective-permute-start.51) | collective-permute-done | bytes 786464 | tf_op jit(solution)/shard_map/ppermute | solution.py:243
  400.9 23.8 %collective-permute-done.40 = bf16[256,1536]{1,0:T(8,128)(2,1)} collective-permute-done((bf16[256,1536]{1,0:T(8,128)(2,1)}, bf16[256,1536]{1,0:T(8,128)(2,1)}, u32[]{:S(2)}, u32[]{:S(2)}) %collective-permute-start.40) | collective-permute-done | bytes 786464 | tf_op jit(solution)/shard_map/ppermute | solution.py:243
  427.6 10.3 %collective-permute-done.52 = bf16[256,1536]{1,0:T(8,128)(2,1)} collective-permute-done((bf16[256,1536]{1,0:T(8,128)(2,1)}, bf16[256,1536]{1,0:T(8,128)(2,1)}, u32[]{:S(2)}, u32[]{:S(2)}) %collective-permute-start.52) | collective-permute-done | bytes 786464 | tf_op jit(solution)/shard_map/ppermute | solution.py:243
  439.4 5.0 convolution_convert_fusion.10
  452.6 6.9 collective-permute-done.55
  465.2 17.3 %collective-permute-done.46 = bf16[256,1536]{1,0:T(8,128)(2,1)} collective-permute-done((bf16[256,1536]{1,0:T(8,128)(2,1)}, bf16[256,1536]{1,0:T(8,128)(2,1)}, u32[]{:S(2)}, u32[]{:S(2)}) %collective-permute-start.46) | collective-permute-done | bytes 786464 | tf_op jit(solution)/shard_map/ppermute | solution.py:243
  483.9 5.1 convolution_convert_fusion.11
  492.7 9.4 collective-permute-done.49
  502.8 6.7 collective-permute-done.48
  517.2 4.4 collective-permute-done.56
  521.6 8.4 collective-permute-done.50
  551.4 12.6 %collective-permute-done.66 = bf16[128,1536]{1,0:T(8,128)(2,1)S(1)} collective-permute-done((bf16[128,1536]{1,0:T(8,128)(2,1)S(1)}, bf16[128,1536]{1,0:T(8,128)(2,1)S(1)}, u32[]{:S(2)}, u32[]{:S(2)}) %collective-permute-start.66) | collective-permute-done | bytes 393248 | tf_op jit(solution)/shard_map/ppermute | solution.py:227
  571.3 8.4 collective-permute-done.59
  579.6 5.7 convolution_convert_fusion.1
  588.1 24.2 %collective-permute-done.68 = bf16[512,576]{0,1:T(8,128)(2,1)} collective-permute-done((bf16[512,576]{0,1:T(8,128)(2,1)S(1)}, bf16[512,576]{0,1:T(8,128)(2,1)}, u32[]{:S(2)}, u32[]{:S(2)}) %collective-permute-start.68) | collective-permute-done | bytes 589856 | tf_op jit(solution)/shard_map/ppermute | solution.py:243
  615.1 4.2 prepare.7
  619.4 5.6 collective-permute-done.63
  636.2 5.2 attend.6
  641.6 5.2 attend.7
  646.8 9.5 %collective-permute-done.74 = bf16[512,192]{1,0:T(8,128)(2,1)} collective-permute-done((bf16[512,192]{1,0:T(8,128)(2,1)S(1)}, bf16[512,192]{1,0:T(8,128)(2,1)}, u32[]{:S(2)}, u32[]{:S(2)}) %collective-permute-start.74) | collective-permute-done | bytes 196640 | tf_op jit(solution)/shard_map/ppermute | solution.py:243
  662.4 10.1 %collective-permute-done.79 = bf16[512,192]{1,0:T(8,128)(2,1)S(1)} collective-permute-done((bf16[512,192]{1,0:T(8,128)(2,1)S(1)}, bf16[512,192]{1,0:T(8,128)(2,1)S(1)}, u32[]{:S(2)}, u32[]{:S(2)}) %collective-permute-start.79) | collective-permute-done | bytes 196640 | tf_op jit(solution)/shard_map/ppermute | solution.py:243
  683.6 6.3 collective-permute-done.80
  690.1 7.0 collective-permute-done.81
  702.8 8.1 collective-permute-done.78
  711.0 7.3 collective-permute-done.86
  731.4 9.5 %collective-permute-done.94 = bf16[128,1536]{1,0:T(8,128)(2,1)S(1)} collective-permute-done((bf16[128,1536]{1,0:T(8,128)(2,1)S(1)}, bf16[128,1536]{1,0:T(8,128)(2,1)S(1)}, u32[]{:S(2)}, u32[]{:S(2)}) %collective-permute-start.94) | collective-permute-done | bytes 393248 | tf_op jit(solution)/shard_map/ppermute | solution.py:227
  740.9 5.2 collective-permute-done.93
  746.8 5.1 convolution_convert_fusion.6
  760.2 6.2 collective-permute-done.90
  766.4 8.2 collective-permute-done.89
  774.6 5.1 convolution_convert_fusion.7
  782.4 30.1 %collective-permute-done.102 = bf16[256,1536]{1,0:T(8,128)(2,1)S(1)} collective-permute-done((bf16[256,1536]{1,0:T(8,128)(2,1)S(1)}, bf16[256,1536]{1,0:T(8,128)(2,1)S(1)}, u32[]{:S(2)}, u32[]{:S(2)}) %collective-permute-start.102) | collective-permute-done | bytes 786464 | tf_op jit(solution)/shard_map/ppermute | solution.py:243
  813.3 33.0 %collective-permute-done.91 = bf16[256,1536]{1,0:T(8,128)(2,1)S(1)} collective-permute-done((bf16[256,1536]{1,0:T(8,128)(2,1)S(1)}, bf16[256,1536]{1,0:T(8,128)(2,1)S(1)}, u32[]{:S(2)}, u32[]{:S(2)}) %collective-permute-start.91) | collective-permute-done | bytes 786464 | tf_op jit(solution)/shard_map/ppermute | solution.py:243
  846.9 15.9 %collective-permute-done.103 = bf16[256,1536]{1,0:T(8,128)(2,1)S(1)} collective-permute-done((bf16[256,1536]{1,0:T(8,128)(2,1)S(1)}, bf16[256,1536]{1,0:T(8,128)(2,1)S(1)}, u32[]{:S(2)}, u32[]{:S(2)}) %collective-permute-start.103) | collective-permute-done | bytes 786464 | tf_op jit(solution)/shard_map/ppermute | solution.py:243
  869.4 9.4 collective-permute-done.106
  878.8 6.8 collective-permute-done.105
  885.8 19.7 %collective-permute-done.97 = bf16[256,1536]{1,0:T(8,128)(2,1)S(1)} collective-permute-done((bf16[256,1536]{1,0:T(8,128)(2,1)S(1)}, bf16[256,1536]{1,0:T(8,128)(2,1)S(1)}, u32[]{:S(2)}, u32[]{:S(2)}) %collective-permute-start.97) | collective-permute-done | bytes 786464 | tf_op jit(solution)/shard_map/ppermute | solution.py:243
  912.2 9.3 collective-permute-done.100
  921.5 6.1 collective-permute-done.99
  928.2 10.6 %collective-permute-done.101 = bf16[128,1536]{1,0:T(8,128)(2,1)S(1)} collective-permute-done((bf16[128,1536]{1,0:T(8,128)(2,1)S(1)}, bf16[128,1536]{1,0:T(8,128)(2,1)S(1)}, u32[]{:S(2)}, u32[]{:S(2)}) %collective-permute-start.101) | collective-permute-done | bytes 393248 | tf_op jit(solution)/shard_map/ppermute | solution.py:239
  (593 shorter events, 333.8 us)
Async XLA Ops:
  2.6 24.5 %collective-permute-start = (bf16[256,768]{1,0:T(8,128)(2,1)}, bf16[256,768]{1,0:T(8,128)(2,1)}, u32[]{:S(2)}, u32[]{:S(2)}) collective-permute-start(bf16[256,768]{1,0:T(8,128)(2,1)} %dynamic-slice_bitcast_fusion.8), channel_id=1, source_target_pairs={{0,1},{1,0},{2,3},{3,2},{4,5},{5,4},{6,7},{7,6},{8,9},{9,8},{10,11... | collective-permute-start | bytes 1179656 | tf_op jit(solution)/shard_map/ppermute | solution.py:239
  12.0 68.7 %collective-permute-start.1 = (bf16[768,1152]{1,0:T(8,128)(2,1)}, bf16[768,1152]{1,0:T(8,128)(2,1)}, u32[]{:S(2)}, u32[]{:S(2)}) collective-permute-start(bf16[768,1152]{1,0:T(8,128)(2,1)} %pad_maximum_fusion.9), channel_id=1, source_target_pairs={{0,16},{1,17},{2,18},{3,19},{4,20},{5,21},{6,22},{7,23},{8,24},{9,... | collective-permute-start | bytes 5308424 | tf_op jit(solution)/shard_map/ppermute | solution.py:314
  28.8 52.5 %collective-permute-start.11 = (bf16[768,1152]{1,0:T(8,128)(2,1)}, bf16[768,1152]{1,0:T(8,128)(2,1)}, u32[]{:S(2)}, u32[]{:S(2)}) collective-permute-start(bf16[768,1152]{1,0:T(8,128)(2,1)} %pad_maximum_fusion.8), channel_id=1, source_target_pairs={{0,1},{1,0},{2,3},{3,2},{4,5},{5,4},{6,7},{7,6},{8,9},{9,8},{10,11... | collective-permute-start | bytes 5308424 | tf_op jit(solution)/shard_map/ppermute | solution.py:311
  36.9 26.7 %collective-permute-start.2 = (f32[2,4,3,768]{3,0,2,1:T(2,128)}, f32[2,4,3,768]{3,0,2,1:T(2,128)}, u32[]{:S(2)}, u32[]{:S(2)}) collective-permute-start(f32[2,4,3,768]{3,0,2,1:T(2,128)} %bitcast.12), channel_id=1, source_target_pairs={{0,1},{1,0},{2,3},{3,2},{4,5},{5,4},{6,7},{7,6},{8,9},{9,8},{10,11... | collective-permute-start | bytes 221192 | tf_op jit(solution)/shard_map/ppermute | solution.py:239
  42.1 27.9 %collective-permute-start.5 = (bf16[1,3,256,128]{3,2,0,1:T(8,128)(2,1)}, bf16[1,3,256,128]{3,2,0,1:T(8,128)(2,1)}, u32[]{:S(2)}, u32[]{:S(2)}) collective-permute-start(bf16[1,3,256,128]{3,2,0,1:T(8,128)(2,1)} %get-tuple-element.256), channel_id=1, source_target_pairs={{0,1},{1,2},{2,3},{3,0},{4,5},{5,6},{6,7},{7,4},{8,9},{9,10},{10,1... | collective-permute-start | bytes 589832 | tf_op jit(solution)/shard_map/ppermute | solution.py:167
  42.5 29.3 %collective-permute-start.6 = (bf16[1,3,256,128]{3,2,0,1:T(8,128)(2,1)}, bf16[1,3,256,128]{3,2,0,1:T(8,128)(2,1)}, u32[]{:S(2)}, u32[]{:S(2)}) collective-permute-start(bf16[1,3,256,128]{3,2,0,1:T(8,128)(2,1)} %get-tuple-element.255), channel_id=1, source_target_pairs={{0,2},{1,3},{2,0},{3,1},{4,6},{5,7},{6,4},{7,5},{8,10},{9,11},{10,... | collective-permute-start | bytes 589832 | tf_op jit(solution)/shard_map/ppermute | solution.py:167
  92.1 16.0 %collective-permute-start.9 = (bf16[128,1536]{1,0:T(8,128)(2,1)S(1)}, bf16[128,1536]{1,0:T(8,128)(2,1)S(1)}, u32[]{:S(2)}, u32[]{:S(2)}) collective-permute-start(bf16[128,1536]{1,0:T(8,128)(2,1)S(1)} %fusion.112), channel_id=1, source_target_pairs={{0,8},{4,12},{8,0},{12,4},{1,9},{5,13},{9,1},{13,5},{2,10},{6,14},... | collective-permute-start | bytes 1179656 | tf_op jit(solution)/shard_map/ppermute | solution.py:227
  111.5 37.1 %collective-permute-start.18 = (bf16[768,1536]{1,0:T(8,128)(2,1)S(1)}, bf16[768,1536]{1,0:T(8,128)(2,1)S(1)}, u32[]{:S(2)}, u32[]{:S(2)}) collective-permute-start(bf16[768,1536]{1,0:T(8,128)(2,1)S(1)} %copy-done.37), channel_id=1, source_target_pairs={{0,1},{1,0},{2,3},{3,2},{4,5},{5,4},{6,7},{7,6},{8,9},{9,8},{10,11... | collective-permute-start | bytes 7077896 | tf_op jit(solution)/shard_map/ppermute | solution.py:311
  116.3 17.5 %collective-permute-start.15 = (bf16[128,1536]{1,0:T(8,128)(2,1)S(1)}, bf16[128,1536]{1,0:T(8,128)(2,1)S(1)}, u32[]{:S(2)}, u32[]{:S(2)}) collective-permute-start(bf16[128,1536]{1,0:T(8,128)(2,1)S(1)} %fusion.116), channel_id=1, source_target_pairs={{0,8},{4,12},{8,0},{12,4},{1,9},{5,13},{9,1},{13,5},{2,10},{6,14},... | collective-permute-start | bytes 1179656 | tf_op jit(solution)/shard_map/ppermute | solution.py:227
  117.6 16.3 %collective-permute-start.14 = (bf16[128,1536]{1,0:T(8,128)(2,1)S(1)}, bf16[128,1536]{1,0:T(8,128)(2,1)S(1)}, u32[]{:S(2)}, u32[]{:S(2)}) collective-permute-start(bf16[128,1536]{1,0:T(8,128)(2,1)S(1)} %fusion.116), channel_id=1, source_target_pairs={{0,4},{4,0},{8,12},{12,8},{1,5},{5,1},{9,13},{13,9},{2,6},{6,2},{1... | collective-permute-start | bytes 1179656 | tf_op jit(solution)/shard_map/ppermute | solution.py:227
  118.1 30.5 %collective-permute-start.17 = (bf16[384,768]{1,0:T(8,128)(2,1)S(1)}, bf16[384,768]{1,0:T(8,128)(2,1)S(1)}, u32[]{:S(2)}, u32[]{:S(2)}) collective-permute-start(bf16[384,768]{1,0:T(8,128)(2,1)S(1)} %copy-done.48), channel_id=1, source_target_pairs={{0,1},{1,0},{2,3},{3,2},{4,5},{5,4},{6,7},{7,6},{8,9},{9,8},{10,11... | collective-permute-start | bytes 1769480 | tf_op jit(solution)/shard_map/ppermute | solution.py:311
  151.1 57.2 %collective-permute-start.21 = (bf16[1536,1536]{1,0:T(8,128)(2,1)}, bf16[1536,1536]{1,0:T(8,128)(2,1)}, u32[]{:S(2)}, u32[]{:S(2)}) collective-permute-start(bf16[1536,1536]{1,0:T(8,128)(2,1)} %pad_maximum_fusion.1), channel_id=1, source_target_pairs={{0,16},{1,17},{2,18},{3,19},{4,20},{5,21},{6,22},{7,23},{8,24},{9,... | collective-permute-start | bytes 14155784 | tf_op jit(solution)/shard_map/ppermute | solution.py:314
  161.7 29.7 %collective-permute-start.13 = (bf16[512,576]{0,1:T(8,128)(2,1)}, bf16[512,576]{0,1:T(8,128)(2,1)}, u32[]{:S(2)}, u32[]{:S(2)}) collective-permute-start(bf16[512,576]{0,1:T(8,128)(2,1)} %copy.36), channel_id=1, source_target_pairs={{0,2},{1,3},{2,0},{3,1},{4,6},{5,7},{6,4},{7,5},{8,10},{9,11},{10,... | collective-permute-start | bytes 1769480 | tf_op jit(solution)/shard_map/ppermute | solution.py:243
  165.8 42.5 %collective-permute-start.20 = (bf16[384,1536]{1,0:T(8,128)(2,1)}, bf16[384,1536]{1,0:T(8,128)(2,1)}, u32[]{:S(2)}, u32[]{:S(2)}) collective-permute-start(bf16[384,1536]{1,0:T(8,128)(2,1)} %pad_maximum_fusion.12), channel_id=1, source_target_pairs={{0,16},{1,17},{2,18},{3,19},{4,20},{5,21},{6,22},{7,23},{8,24},{9,... | collective-permute-start | bytes 3538952 | tf_op jit(solution)/shard_map/ppermute | solution.py:314
  171.1 29.6 %collective-permute-start.19 = (bf16[512,576]{0,1:T(8,128)(2,1)}, bf16[512,576]{0,1:T(8,128)(2,1)}, u32[]{:S(2)}, u32[]{:S(2)}) collective-permute-start(bf16[512,576]{0,1:T(8,128)(2,1)} %copy.39), channel_id=1, source_target_pairs={{0,2},{1,3},{2,0},{3,1},{4,6},{5,7},{6,4},{7,5},{8,10},{9,11},{10,... | collective-permute-start | bytes 1769480 | tf_op jit(solution)/shard_map/ppermute | solution.py:243
  237.0 18.7 %collective-permute-start.26 = (bf16[128,1536]{1,0:T(8,128)(2,1)S(1)}, bf16[128,1536]{1,0:T(8,128)(2,1)S(1)}, u32[]{:S(2)}, u32[]{:S(2)}) collective-permute-start(bf16[128,1536]{1,0:T(8,128)(2,1)S(1)} %get-tuple-element.223), channel_id=1, source_target_pairs={{0,12},{4,8},{8,4},{12,0},{1,13},{5,9},{9,5},{13,1},{2,14},{6,10},... | collective-permute-start | bytes 1179656 | tf_op jit(solution)/shard_map/ppermute | solution.py:234
  238.6 18.1 %collective-permute-start.25 = (bf16[128,1536]{1,0:T(8,128)(2,1)S(1)}, bf16[128,1536]{1,0:T(8,128)(2,1)S(1)}, u32[]{:S(2)}, u32[]{:S(2)}) collective-permute-start(bf16[128,1536]{1,0:T(8,128)(2,1)S(1)} %get-tuple-element.224), channel_id=1, source_target_pairs={{0,8},{4,12},{8,0},{12,4},{1,9},{5,13},{9,1},{13,5},{2,10},{6,14},... | collective-permute-start | bytes 1179656 | tf_op jit(solution)/shard_map/ppermute | solution.py:234
  240.2 18.8 %collective-permute-start.24 = (bf16[128,1536]{1,0:T(8,128)(2,1)S(1)}, bf16[128,1536]{1,0:T(8,128)(2,1)S(1)}, u32[]{:S(2)}, u32[]{:S(2)}) collective-permute-start(bf16[128,1536]{1,0:T(8,128)(2,1)S(1)} %get-tuple-element.222), channel_id=1, source_target_pairs={{0,4},{4,0},{8,12},{12,8},{1,5},{5,1},{9,13},{13,9},{2,6},{6,2},{1... | collective-permute-start | bytes 1179656 | tf_op jit(solution)/shard_map/ppermute | solution.py:234
  252.0 24.7 %collective-permute-start.34 = (bf16[128,1536]{1,0:T(8,128)(2,1)S(1)}, bf16[128,1536]{1,0:T(8,128)(2,1)S(1)}, u32[]{:S(2)}, u32[]{:S(2)}) collective-permute-start(bf16[128,1536]{1,0:T(8,128)(2,1)S(1)} %get-tuple-element.226), channel_id=1, source_target_pairs={{0,12},{4,8},{8,4},{12,0},{1,13},{5,9},{9,5},{13,1},{2,14},{6,10},... | collective-permute-start | bytes 1179656 | tf_op jit(solution)/shard_map/ppermute | solution.py:234
  252.7 24.1 %collective-permute-start.33 = (bf16[128,1536]{1,0:T(8,128)(2,1)S(1)}, bf16[128,1536]{1,0:T(8,128)(2,1)S(1)}, u32[]{:S(2)}, u32[]{:S(2)}) collective-permute-start(bf16[128,1536]{1,0:T(8,128)(2,1)S(1)} %get-tuple-element.227), channel_id=1, source_target_pairs={{0,8},{4,12},{8,0},{12,4},{1,9},{5,13},{9,1},{13,5},{2,10},{6,14},... | collective-permute-start | bytes 1179656 | tf_op jit(solution)/shard_map/ppermute | solution.py:234
  255.7 21.1 %collective-permute-start.32 = (bf16[128,1536]{1,0:T(8,128)(2,1)S(1)}, bf16[128,1536]{1,0:T(8,128)(2,1)S(1)}, u32[]{:S(2)}, u32[]{:S(2)}) collective-permute-start(bf16[128,1536]{1,0:T(8,128)(2,1)S(1)} %get-tuple-element.225), channel_id=1, source_target_pairs={{0,4},{4,0},{8,12},{12,8},{1,5},{5,1},{9,13},{13,9},{2,6},{6,2},{1... | collective-permute-start | bytes 1179656 | tf_op jit(solution)/shard_map/ppermute | solution.py:234
  277.0 17.2 %collective-permute-start.35 = (bf16[128,1536]{1,0:T(8,128)(2,1)S(1)}, bf16[128,1536]{1,0:T(8,128)(2,1)S(1)}, u32[]{:S(2)}, u32[]{:S(2)}) collective-permute-start(bf16[128,1536]{1,0:T(8,128)(2,1)S(1)} %pad_maximum_fusion.24), channel_id=1, source_target_pairs={{0,1},{1,0},{2,3},{3,2},{4,5},{5,4},{6,7},{7,6},{8,9},{9,8},{10,11... | collective-permute-start | bytes 1179656 | tf_op jit(solution)/shard_map/ppermute | solution.py:239
  302.9 30.7 %collective-permute-start.44 = (bf16[1536,768]{1,0:T(8,128)(2,1)S(1)}, bf16[1536,768]{1,0:T(8,128)(2,1)S(1)}, u32[]{:S(2)}, u32[]{:S(2)}) collective-permute-start(bf16[1536,768]{1,0:T(8,128)(2,1)S(1)} %copy-done.38), channel_id=1, source_target_pairs={{0,1},{1,0},{2,3},{3,2},{4,5},{5,4},{6,7},{7,6},{8,9},{9,8},{10,11... | collective-permute-start | bytes 7077896 | tf_op jit(solution)/shard_map/ppermute | solution.py:311
  306.7 16.0 %collective-permute-start.42 = (bf16[128,1536]{1,0:T(8,128)(2,1)S(1)}, bf16[128,1536]{1,0:T(8,128)(2,1)S(1)}, u32[]{:S(2)}, u32[]{:S(2)}) collective-permute-start(bf16[128,1536]{1,0:T(8,128)(2,1)S(1)} %add_convert_fusion.10), channel_id=1, source_target_pairs={{0,8},{4,12},{8,0},{12,4},{1,9},{5,13},{9,1},{13,5},{2,10},{6,14},... | collective-permute-start | bytes 1179656 | tf_op jit(solution)/shard_map/ppermute | solution.py:227
  336.2 103.1 %collective-permute-start.45 = (bf16[1536,1536]{1,0:T(8,128)(2,1)}, bf16[1536,1536]{1,0:T(8,128)(2,1)}, u32[]{:S(2)}, u32[]{:S(2)}) collective-permute-start(bf16[1536,1536]{1,0:T(8,128)(2,1)} %pad_maximum_fusion.3), channel_id=1, source_target_pairs={{0,16},{1,17},{2,18},{3,19},{4,20},{5,21},{6,22},{7,23},{8,24},{9,... | collective-permute-start | bytes 14155784 | tf_op jit(solution)/shard_map/ppermute | solution.py:314
  344.6 54.8 %collective-permute-start.51 = (bf16[256,1536]{1,0:T(8,128)(2,1)S(1)}, bf16[256,1536]{1,0:T(8,128)(2,1)S(1)}, u32[]{:S(2)}, u32[]{:S(2)}) collective-permute-start(bf16[256,1536]{1,0:T(8,128)(2,1)S(1)} %constant_dynamic-slice_fusion.6), channel_id=1, source_target_pairs={{0,2},{1,3},{2,0},{3,1},{4,6},{5,7},{6,4},{7,5},{8,10},{9,11},{10,... | collective-permute-start | bytes 2359304 | tf_op jit(solution)/shard_map/ppermute | solution.py:243
  359.8 65.0 %collective-permute-start.40 = (bf16[256,1536]{1,0:T(8,128)(2,1)}, bf16[256,1536]{1,0:T(8,128)(2,1)}, u32[]{:S(2)}, u32[]{:S(2)}) collective-permute-start(bf16[256,1536]{1,0:T(8,128)(2,1)} %constant_dynamic-slice_fusion.7), channel_id=1, source_target_pairs={{0,2},{1,3},{2,0},{3,1},{4,6},{5,7},{6,4},{7,5},{8,10},{9,11},{10,... | collective-permute-start | bytes 2359304 | tf_op jit(solution)/shard_map/ppermute | solution.py:243
  400.9 37.0 %collective-permute-start.52 = (bf16[256,1536]{1,0:T(8,128)(2,1)}, bf16[256,1536]{1,0:T(8,128)(2,1)}, u32[]{:S(2)}, u32[]{:S(2)}) collective-permute-start(bf16[256,1536]{1,0:T(8,128)(2,1)} %fusion.19), channel_id=1, source_target_pairs={{0,2},{1,3},{2,0},{3,1},{4,6},{5,7},{6,4},{7,5},{8,10},{9,11},{10,... | collective-permute-start | bytes 2359304 | tf_op jit(solution)/shard_map/ppermute | solution.py:243
  450.0 32.4 %collective-permute-start.46 = (bf16[256,1536]{1,0:T(8,128)(2,1)}, bf16[256,1536]{1,0:T(8,128)(2,1)}, u32[]{:S(2)}, u32[]{:S(2)}) collective-permute-start(bf16[256,1536]{1,0:T(8,128)(2,1)} %fusion.11), channel_id=1, source_target_pairs={{0,2},{1,3},{2,0},{3,1},{4,6},{5,7},{6,4},{7,5},{8,10},{9,11},{10,... | collective-permute-start | bytes 2359304 | tf_op jit(solution)/shard_map/ppermute | solution.py:243
  451.8 60.1 %collective-permute-start.61 = (bf16[768,1152]{1,0:T(8,128)(2,1)}, bf16[768,1152]{1,0:T(8,128)(2,1)S(1)}, u32[]{:S(2)}, u32[]{:S(2)}) collective-permute-start(bf16[768,1152]{1,0:T(8,128)(2,1)} %pad_maximum_fusion.8), channel_id=1, source_target_pairs={{16,17},{17,16},{18,19},{19,18},{20,21},{21,20},{22,23},{23,22},{2... | collective-permute-start | bytes 5308424 | tf_op jit(solution)/shard_map/ppermute | solution.py:311
  459.5 71.3 %collective-permute-start.71 = (bf16[768,1536]{1,0:T(8,128)(2,1)}, bf16[768,1536]{1,0:T(8,128)(2,1)S(1)}, u32[]{:S(2)}, u32[]{:S(2)}) collective-permute-start(bf16[768,1536]{1,0:T(8,128)(2,1)} %get-tuple-element.109), channel_id=1, source_target_pairs={{16,17},{17,16},{18,19},{19,18},{20,21},{21,20},{22,23},{23,22},{2... | collective-permute-start | bytes 7077896 | tf_op jit(solution)/shard_map/ppermute | solution.py:311
  490.4 19.1 %collective-permute-start.48 = (bf16[128,1536]{1,0:T(8,128)(2,1)S(1)}, bf16[128,1536]{1,0:T(8,128)(2,1)S(1)}, u32[]{:S(2)}, u32[]{:S(2)}) collective-permute-start(bf16[128,1536]{1,0:T(8,128)(2,1)S(1)} %get-tuple-element.214), channel_id=1, source_target_pairs={{0,8},{4,12},{8,0},{12,4},{1,9},{5,13},{9,1},{13,5},{2,10},{6,14},... | collective-permute-start | bytes 1179656 | tf_op jit(solution)/shard_map/ppermute | solution.py:234
  491.8 17.7 %collective-permute-start.47 = (bf16[128,1536]{1,0:T(8,128)(2,1)S(1)}, bf16[128,1536]{1,0:T(8,128)(2,1)S(1)}, u32[]{:S(2)}, u32[]{:S(2)}) collective-permute-start(bf16[128,1536]{1,0:T(8,128)(2,1)S(1)} %get-tuple-element.212), channel_id=1, source_target_pairs={{0,4},{4,0},{8,12},{12,8},{1,5},{5,1},{9,13},{13,9},{2,6},{6,2},{1... | collective-permute-start | bytes 1179656 | tf_op jit(solution)/shard_map/ppermute | solution.py:234
  509.8 20.2 %collective-permute-start.50 = (bf16[128,1536]{1,0:T(8,128)(2,1)S(1)}, bf16[128,1536]{1,0:T(8,128)(2,1)S(1)}, u32[]{:S(2)}, u32[]{:S(2)}) collective-permute-start(bf16[128,1536]{1,0:T(8,128)(2,1)S(1)} %pad_maximum_fusion.25), channel_id=1, source_target_pairs={{0,1},{1,0},{2,3},{3,2},{4,5},{5,4},{6,7},{7,6},{8,9},{9,8},{10,11... | collective-permute-start | bytes 1179656 | tf_op jit(solution)/shard_map/ppermute | solution.py:239
  514.4 31.6 %collective-permute-start.62 = (bf16[1536,1152]{1,0:T(8,128)(2,1)S(1)}, bf16[1536,1152]{1,0:T(8,128)(2,1)S(1)}, u32[]{:S(2)}, u32[]{:S(2)}) collective-permute-start(bf16[1536,1152]{1,0:T(8,128)(2,1)S(1)} %pad_maximum_fusion.5), channel_id=1, source_target_pairs={{16,0},{17,1},{18,2},{19,3},{20,4},{21,5},{22,6},{23,7},{24,8},{25... | collective-permute-start | bytes 10616840 | tf_op jit(solution)/shard_map/ppermute | solution.py:314
  534.2 98.7 %collective-permute-start.72 = (bf16[1536,1536]{1,0:T(8,128)(2,1)}, bf16[1536,1536]{1,0:T(8,128)(2,1)}, u32[]{:S(2)}, u32[]{:S(2)}) collective-permute-start(bf16[1536,1536]{1,0:T(8,128)(2,1)} %pad_maximum_fusion), channel_id=1, source_target_pairs={{16,0},{17,1},{18,2},{19,3},{20,4},{21,5},{22,6},{23,7},{24,8},{25... | collective-permute-start | bytes 14155784 | tf_op jit(solution)/shard_map/ppermute | solution.py:314
  542.6 21.4 %collective-permute-start.66 = (bf16[128,1536]{1,0:T(8,128)(2,1)S(1)}, bf16[128,1536]{1,0:T(8,128)(2,1)S(1)}, u32[]{:S(2)}, u32[]{:S(2)}) collective-permute-start(bf16[128,1536]{1,0:T(8,128)(2,1)S(1)} %fusion.128), channel_id=1, source_target_pairs={{0,8},{4,12},{8,0},{12,4},{1,9},{5,13},{9,1},{13,5},{2,10},{6,14},... | collective-permute-start | bytes 1179656 | tf_op jit(solution)/shard_map/ppermute | solution.py:227
  544.1 21.1 %collective-permute-start.65 = (bf16[128,1536]{1,0:T(8,128)(2,1)S(1)}, bf16[128,1536]{1,0:T(8,128)(2,1)S(1)}, u32[]{:S(2)}, u32[]{:S(2)}) collective-permute-start(bf16[128,1536]{1,0:T(8,128)(2,1)S(1)} %fusion.128), channel_id=1, source_target_pairs={{0,4},{4,0},{8,12},{12,8},{1,5},{5,1},{9,13},{13,9},{2,6},{6,2},{1... | collective-permute-start | bytes 1179656 | tf_op jit(solution)/shard_map/ppermute | solution.py:227
  546.0 86.9 %collective-permute-start.70 = (bf16[384,1536]{1,0:T(8,128)(2,1)}, bf16[384,1536]{1,0:T(8,128)(2,1)}, u32[]{:S(2)}, u32[]{:S(2)}) collective-permute-start(bf16[384,1536]{1,0:T(8,128)(2,1)} %pad_maximum_fusion.14), channel_id=1, source_target_pairs={{16,0},{17,1},{18,2},{19,3},{20,4},{21,5},{22,6},{23,7},{24,8},{25... | collective-permute-start | bytes 3538952 | tf_op jit(solution)/shard_map/ppermute | solution.py:314
  550.2 20.2 %collective-permute-start.60 = (bf16[128,1536]{1,0:T(8,128)(2,1)S(1)}, bf16[128,1536]{1,0:T(8,128)(2,1)}, u32[]{:S(2)}, u32[]{:S(2)}) collective-permute-start(bf16[128,1536]{1,0:T(8,128)(2,1)S(1)} %fusion.122), channel_id=1, source_target_pairs={{0,12},{4,8},{8,4},{12,0},{1,13},{5,9},{9,5},{13,1},{2,14},{6,10},... | collective-permute-start | bytes 1179656 | tf_op jit(solution)/shard_map/ppermute | solution.py:227
  570.4 42.0 %collective-permute-start.68 = (bf16[512,576]{0,1:T(8,128)(2,1)S(1)}, bf16[512,576]{0,1:T(8,128)(2,1)}, u32[]{:S(2)}, u32[]{:S(2)}) collective-permute-start(bf16[512,576]{0,1:T(8,128)(2,1)S(1)} %copy.46), channel_id=1, source_target_pairs={{0,2},{1,3},{2,0},{3,1},{4,6},{5,7},{6,4},{7,5},{8,10},{9,11},{10,... | collective-permute-start | bytes 1769480 | tf_op jit(solution)/shard_map/ppermute | solution.py:243
  587.5 37.5 %collective-permute-start.63 = (bf16[512,576]{0,1:T(8,128)(2,1)}, bf16[512,576]{0,1:T(8,128)(2,1)}, u32[]{:S(2)}, u32[]{:S(2)}) collective-permute-start(bf16[512,576]{0,1:T(8,128)(2,1)} %copy.43), channel_id=1, source_target_pairs={{0,2},{1,3},{2,0},{3,1},{4,6},{5,7},{6,4},{7,5},{8,10},{9,11},{10,... | collective-permute-start | bytes 1769480 | tf_op jit(solution)/shard_map/ppermute | solution.py:243
  658.9 20.1 %collective-permute-start.77 = (bf16[128,1536]{1,0:T(8,128)(2,1)S(1)}, bf16[128,1536]{1,0:T(8,128)(2,1)S(1)}, u32[]{:S(2)}, u32[]{:S(2)}) collective-permute-start(bf16[128,1536]{1,0:T(8,128)(2,1)S(1)} %get-tuple-element.207), channel_id=1, source_target_pairs={{0,12},{4,8},{8,4},{12,0},{1,13},{5,9},{9,5},{13,1},{2,14},{6,10},... | collective-permute-start | bytes 1179656 | tf_op jit(solution)/shard_map/ppermute | solution.py:234
  660.9 19.3 %collective-permute-start.76 = (bf16[128,1536]{1,0:T(8,128)(2,1)S(1)}, bf16[128,1536]{1,0:T(8,128)(2,1)S(1)}, u32[]{:S(2)}, u32[]{:S(2)}) collective-permute-start(bf16[128,1536]{1,0:T(8,128)(2,1)S(1)} %get-tuple-element.208), channel_id=1, source_target_pairs={{0,8},{4,12},{8,0},{12,4},{1,9},{5,13},{9,1},{13,5},{2,10},{6,14},... | collective-permute-start | bytes 1179656 | tf_op jit(solution)/shard_map/ppermute | solution.py:234
  662.1 20.4 %collective-permute-start.75 = (bf16[128,1536]{1,0:T(8,128)(2,1)S(1)}, bf16[128,1536]{1,0:T(8,128)(2,1)S(1)}, u32[]{:S(2)}, u32[]{:S(2)}) collective-permute-start(bf16[128,1536]{1,0:T(8,128)(2,1)S(1)} %get-tuple-element.206), channel_id=1, source_target_pairs={{0,4},{4,0},{8,12},{12,8},{1,5},{5,1},{9,13},{13,9},{2,6},{6,2},{1... | collective-permute-start | bytes 1179656 | tf_op jit(solution)/shard_map/ppermute | solution.py:234
  675.0 25.7 %collective-permute-start.85 = (bf16[128,1536]{1,0:T(8,128)(2,1)S(1)}, bf16[128,1536]{1,0:T(8,128)(2,1)S(1)}, u32[]{:S(2)}, u32[]{:S(2)}) collective-permute-start(bf16[128,1536]{1,0:T(8,128)(2,1)S(1)} %get-tuple-element.210), channel_id=1, source_target_pairs={{0,12},{4,8},{8,4},{12,0},{1,13},{5,9},{9,5},{13,1},{2,14},{6,10},... | collective-permute-start | bytes 1179656 | tf_op jit(solution)/shard_map/ppermute | solution.py:234
  677.2 23.4 %collective-permute-start.84 = (bf16[128,1536]{1,0:T(8,128)(2,1)S(1)}, bf16[128,1536]{1,0:T(8,128)(2,1)S(1)}, u32[]{:S(2)}, u32[]{:S(2)}) collective-permute-start(bf16[128,1536]{1,0:T(8,128)(2,1)S(1)} %get-tuple-element.211), channel_id=1, source_target_pairs={{0,8},{4,12},{8,0},{12,4},{1,9},{5,13},{9,1},{13,5},{2,10},{6,14},... | collective-permute-start | bytes 1179656 | tf_op jit(solution)/shard_map/ppermute | solution.py:234
  679.0 21.6 %collective-permute-start.83 = (bf16[128,1536]{1,0:T(8,128)(2,1)S(1)}, bf16[128,1536]{1,0:T(8,128)(2,1)S(1)}, u32[]{:S(2)}, u32[]{:S(2)}) collective-permute-start(bf16[128,1536]{1,0:T(8,128)(2,1)S(1)} %get-tuple-element.209), channel_id=1, source_target_pairs={{0,4},{4,0},{8,12},{12,8},{1,5},{5,1},{9,13},{13,9},{2,6},{6,2},{1... | collective-permute-start | bytes 1179656 | tf_op jit(solution)/shard_map/ppermute | solution.py:234
  700.9 17.4 %collective-permute-start.86 = (bf16[128,1536]{1,0:T(8,128)(2,1)S(1)}, bf16[128,1536]{1,0:T(8,128)(2,1)S(1)}, u32[]{:S(2)}, u32[]{:S(2)}) collective-permute-start(bf16[128,1536]{1,0:T(8,128)(2,1)S(1)} %pad_maximum_fusion.29), channel_id=1, source_target_pairs={{0,1},{1,0},{2,3},{3,2},{4,5},{5,4},{6,7},{7,6},{8,9},{9,8},{10,11... | collective-permute-start | bytes 1179656 | tf_op jit(solution)/shard_map/ppermute | solution.py:239
  726.1 25.8 %collective-permute-start.95 = (bf16[1536,768]{1,0:T(8,128)(2,1)S(1)}, bf16[1536,768]{1,0:T(8,128)(2,1)S(1)}, u32[]{:S(2)}, u32[]{:S(2)}) collective-permute-start(bf16[1536,768]{1,0:T(8,128)(2,1)S(1)} %copy-done.39), channel_id=1, source_target_pairs={{16,17},{17,16},{18,19},{19,18},{20,21},{21,20},{22,23},{23,22},{2... | collective-permute-start | bytes 7077896 | tf_op jit(solution)/shard_map/ppermute | solution.py:311
  728.0 18.1 %collective-permute-start.93 = (bf16[128,1536]{1,0:T(8,128)(2,1)S(1)}, bf16[128,1536]{1,0:T(8,128)(2,1)S(1)}, u32[]{:S(2)}, u32[]{:S(2)}) collective-permute-start(bf16[128,1536]{1,0:T(8,128)(2,1)S(1)} %add_convert_fusion.2), channel_id=1, source_target_pairs={{0,8},{4,12},{8,0},{12,4},{1,9},{5,13},{9,1},{13,5},{2,10},{6,14},... | collective-permute-start | bytes 1179656 | tf_op jit(solution)/shard_map/ppermute | solution.py:227
  730.6 16.2 %collective-permute-start.92 = (bf16[128,1536]{1,0:T(8,128)(2,1)S(1)}, bf16[128,1536]{1,0:T(8,128)(2,1)S(1)}, u32[]{:S(2)}, u32[]{:S(2)}) collective-permute-start(bf16[128,1536]{1,0:T(8,128)(2,1)S(1)} %add_convert_fusion.2), channel_id=1, source_target_pairs={{0,4},{4,0},{8,12},{12,8},{1,5},{5,1},{9,13},{13,9},{2,6},{6,2},{1... | collective-permute-start | bytes 1179656 | tf_op jit(solution)/shard_map/ppermute | solution.py:227
  752.3 110.6 %collective-permute-start.96 = (bf16[1536,1536]{1,0:T(8,128)(2,1)S(1)}, bf16[1536,1536]{1,0:T(8,128)(2,1)S(1)}, u32[]{:S(2)}, u32[]{:S(2)}) collective-permute-start(bf16[1536,1536]{1,0:T(8,128)(2,1)S(1)} %pad_maximum_fusion.2), channel_id=1, source_target_pairs={{16,0},{17,1},{18,2},{19,3},{20,4},{21,5},{22,6},{23,7},{24,8},{25... | collective-permute-start | bytes 14155784 | tf_op jit(solution)/shard_map/ppermute | solution.py:314
  754.4 20.2 %collective-permute-start.89 = (bf16[128,1536]{1,0:T(8,128)(2,1)S(1)}, bf16[128,1536]{1,0:T(8,128)(2,1)S(1)}, u32[]{:S(2)}, u32[]{:S(2)}) collective-permute-start(bf16[128,1536]{1,0:T(8,128)(2,1)S(1)} %add_convert_fusion.3), channel_id=1, source_target_pairs={{0,8},{4,12},{8,0},{12,4},{1,9},{5,13},{9,1},{13,5},{2,10},{6,14},... | collective-permute-start | bytes 1179656 | tf_op jit(solution)/shard_map/ppermute | solution.py:227
  755.8 18.8 %collective-permute-start.88 = (bf16[128,1536]{1,0:T(8,128)(2,1)S(1)}, bf16[128,1536]{1,0:T(8,128)(2,1)S(1)}, u32[]{:S(2)}, u32[]{:S(2)}) collective-permute-start(bf16[128,1536]{1,0:T(8,128)(2,1)S(1)} %add_convert_fusion.3), channel_id=1, source_target_pairs={{0,4},{4,0},{8,12},{12,8},{1,5},{5,1},{9,13},{13,9},{2,6},{6,2},{1... | collective-permute-start | bytes 1179656 | tf_op jit(solution)/shard_map/ppermute | solution.py:227
  757.5 55.1 %collective-permute-start.102 = (bf16[256,1536]{1,0:T(8,128)(2,1)S(1)}, bf16[256,1536]{1,0:T(8,128)(2,1)S(1)}, u32[]{:S(2)}, u32[]{:S(2)}) collective-permute-start(bf16[256,1536]{1,0:T(8,128)(2,1)S(1)} %constant_dynamic-slice_fusion.1), channel_id=1, source_target_pairs={{0,2},{1,3},{2,0},{3,1},{4,6},{5,7},{6,4},{7,5},{8,10},{9,11},{10,... | collective-permute-start | bytes 2359304 | tf_op jit(solution)/shard_map/ppermute | solution.py:243
  779.7 66.5 %collective-permute-start.91 = (bf16[256,1536]{1,0:T(8,128)(2,1)S(1)}, bf16[256,1536]{1,0:T(8,128)(2,1)S(1)}, u32[]{:S(2)}, u32[]{:S(2)}) collective-permute-start(bf16[256,1536]{1,0:T(8,128)(2,1)S(1)} %constant_dynamic-slice_fusion.2), channel_id=1, source_target_pairs={{0,2},{1,3},{2,0},{3,1},{4,6},{5,7},{6,4},{7,5},{8,10},{9,11},{10,... | collective-permute-start | bytes 2359304 | tf_op jit(solution)/shard_map/ppermute | solution.py:243
  813.2 49.6 %collective-permute-start.103 = (bf16[256,1536]{1,0:T(8,128)(2,1)S(1)}, bf16[256,1536]{1,0:T(8,128)(2,1)S(1)}, u32[]{:S(2)}, u32[]{:S(2)}) collective-permute-start(bf16[256,1536]{1,0:T(8,128)(2,1)S(1)} %fusion.35), channel_id=1, source_target_pairs={{0,2},{1,3},{2,0},{3,1},{4,6},{5,7},{6,4},{7,5},{8,10},{9,11},{10,... | collective-permute-start | bytes 2359304 | tf_op jit(solution)/shard_map/ppermute | solution.py:243
  866.3 19.3 %collective-permute-start.105 = (bf16[128,1536]{1,0:T(8,128)(2,1)S(1)}, bf16[128,1536]{1,0:T(8,128)(2,1)S(1)}, u32[]{:S(2)}, u32[]{:S(2)}) collective-permute-start(bf16[128,1536]{1,0:T(8,128)(2,1)S(1)} %get-tuple-element.203), channel_id=1, source_target_pairs={{0,8},{4,12},{8,0},{12,4},{1,9},{5,13},{9,1},{13,5},{2,10},{6,14},... | collective-permute-start | bytes 1179656 | tf_op jit(solution)/shard_map/ppermute | solution.py:234
  867.6 18.0 %collective-permute-start.104 = (bf16[128,1536]{1,0:T(8,128)(2,1)S(1)}, bf16[128,1536]{1,0:T(8,128)(2,1)S(1)}, u32[]{:S(2)}, u32[]{:S(2)}) collective-permute-start(bf16[128,1536]{1,0:T(8,128)(2,1)S(1)} %get-tuple-element.201), channel_id=1, source_target_pairs={{0,4},{4,0},{8,12},{12,8},{1,5},{5,1},{9,13},{13,9},{2,6},{6,2},{1... | collective-permute-start | bytes 1179656 | tf_op jit(solution)/shard_map/ppermute | solution.py:234
  869.3 36.2 %collective-permute-start.97 = (bf16[256,1536]{1,0:T(8,128)(2,1)S(1)}, bf16[256,1536]{1,0:T(8,128)(2,1)S(1)}, u32[]{:S(2)}, u32[]{:S(2)}) collective-permute-start(bf16[256,1536]{1,0:T(8,128)(2,1)S(1)} %fusion.27), channel_id=1, source_target_pairs={{0,2},{1,3},{2,0},{3,1},{4,6},{5,7},{6,4},{7,5},{8,10},{9,11},{10,... | collective-permute-start | bytes 2359304 | tf_op jit(solution)/shard_map/ppermute | solution.py:243
  909.3 18.3 %collective-permute-start.99 = (bf16[128,1536]{1,0:T(8,128)(2,1)S(1)}, bf16[128,1536]{1,0:T(8,128)(2,1)S(1)}, u32[]{:S(2)}, u32[]{:S(2)}) collective-permute-start(bf16[128,1536]{1,0:T(8,128)(2,1)S(1)} %get-tuple-element.198), channel_id=1, source_target_pairs={{0,8},{4,12},{8,0},{12,4},{1,9},{5,13},{9,1},{13,5},{2,10},{6,14},... | collective-permute-start | bytes 1179656 | tf_op jit(solution)/shard_map/ppermute | solution.py:234
  910.4 17.3 %collective-permute-start.98 = (bf16[128,1536]{1,0:T(8,128)(2,1)S(1)}, bf16[128,1536]{1,0:T(8,128)(2,1)S(1)}, u32[]{:S(2)}, u32[]{:S(2)}) collective-permute-start(bf16[128,1536]{1,0:T(8,128)(2,1)S(1)} %get-tuple-element.196), channel_id=1, source_target_pairs={{0,4},{4,0},{8,12},{12,8},{1,5},{5,1},{9,13},{13,9},{2,6},{6,2},{1... | collective-permute-start | bytes 1179656 | tf_op jit(solution)/shard_map/ppermute | solution.py:234
  912.1 16.1 %collective-permute-start.107 = (bf16[128,1536]{1,0:T(8,128)(2,1)S(1)}, bf16[128,1536]{1,0:T(8,128)(2,1)S(1)}, u32[]{:S(2)}, u32[]{:S(2)}) collective-permute-start(bf16[128,1536]{1,0:T(8,128)(2,1)S(1)} %pad_maximum_fusion.31), channel_id=1, source_target_pairs={{0,1},{1,0},{2,3},{3,2},{4,5},{5,4},{6,7},{7,6},{8,9},{9,8},{10,11... | collective-permute-start | bytes 1179656 | tf_op jit(solution)/shard_map/ppermute | solution.py:239
  (134 other events, 1965.8 us)

commit v9 on v8

--- a/solution.py
+++ b/solution.py
@@ -342,24 +342,19 @@
 
     layer_in = lax.dynamic_index_in_dim(hidden_in, section, 0, False)
     layer_in = jnp.concatenate([layer_in, to_mate(layer_in)], axis=1)
-    layer_in, sent, timesteps, stale = ordered(layer_in, qkv_parts[1], timesteps, stale_cache[0, 1])
-    got = mate_half(0, sent)
-    kept = passed(0, qkv_parts[0])
-    layer_in, kept = ordered(layer_in, kept)
-    qkv_now = jnp.concatenate(
-        [
-            jnp.where(lead, qkv_parts[0], kept),
-            jnp.where(lead, got, passed(0, got)),
-        ],
-        axis=0,
-    )
+    layer_in, timesteps = ordered(layer_in, timesteps)
     first_mean, first_scale = statistics(layer_in.astype(F32))
     layer_in = [layer_in[h * part : (h + 1) * part] for h in range(halves)]
-
     activated = jax.nn.silu(time_features(timesteps, ada_weight.shape[1])).astype(BF)
     modulation = jnp.einsum("re,kesd->krsd", activated, ada_weight, preferred_element_type=F32)
     modulation = modulation.reshape(2, 4, 3, feat_a)
     modulation = jnp.concatenate([modulation, to_mate(modulation)], axis=-1)
+    kept = passed(0, qkv_parts[0])
+    modulation, first_mean, sent, kept = ordered(modulation, first_mean, qkv_parts[1], kept)
+    got = mate_half(0, sent)
+    qkv_now = jnp.concatenate(
+        [jnp.where(lead, qkv_parts[0], kept), jnp.where(lead, got, passed(0, got))], axis=0
+    )
     shape = modulation.shape
     width = shape[-1]
     rows = modulation.reshape(-1, width)
@@ -367,6 +362,7 @@
     both = both_layers(jnp.concatenate([rows, last[None]], axis=0))
     tables = [table[:-1].reshape(shape) for table in both]
     norm_rows = [table[-1, : qk_norm.size].reshape(qk_norm.shape) for table in both]
+
     kinds = lax.dynamic_index_in_dim(row_kind, section, 0, False)
     kinds_other = lax.dynamic_index_in_dim(row_kind, 1 - section, 0, False)
     kinds_r = relative(kinds)
@@ -415,15 +411,15 @@
                 moments = statistics(x_in[h])
             entry = normed(x_in[h], moments, table[0], kinds_h[h])
             if layer == 0 and h == 0:
-                entry, stale = ordered(entry, stale_heads(stale))
+                entry, stale = ordered(entry, stale_cache[0, 1])
+                stale = stale_heads(stale)
+                entry, out_sent = ordered(entry, out_parts[1])
+                out_got = mate_half(0, out_sent)
             terms = jnp.dot(gather_wide(entry), qkv_now, preferred_element_type=F32).astype(BF)
-            if layer == 0 and h == 0:
-                terms, out_sent, up_sent = ordered(terms, out_parts[1], up_parts[1])
-                out_got, up_got = mate_half(0, out_sent), mate_half(0, up_sent)
             if layer == 0 and h == 1:
-                terms, out_got, up_got = ordered(terms, out_got, up_got)
+                terms, stale, out_got, up_sent = ordered(terms, stale, out_got, up_parts[1])
                 out_weight = pass_on(0, out_parts[0], out_got, 1)
-                up_weight = pass_on(0, up_parts[0], up_got, 0)
+                up_got = mate_half(0, up_sent)
             width = terms.shape[1] // 2
             qkv = terms[:, width:].astype(F32) + to_partner(terms[:, :width]).astype(F32)
             rows = slice(h * chunk, (h + 1) * chunk)
@@ -433,8 +429,7 @@
             queries.append(q)
             fresh.append(pairs)
         own = jnp.concatenate(fresh, axis=1)
-        own, *weights = ordered(own, *out_weight, *up_weight)
-        out_weight, up_weight = weights[:2], weights[2:]
+        own, *out_weight = ordered(own, *out_weight)
         if layer == 0:
             other = jnp.where(lead, stale, lax.ppermute(own, "section", [(0, 1)]))
         else:
@@ -442,52 +437,44 @@
         after = []
         for h in range(halves):
             attended = attend(queries[h], own, other, own_mask, other_mask, head_dim)
-            if h == 1:
-                attended, first_terms = ordered(attended, first_terms)
             attended = jnp.concatenate([attended, to_partner(attended)], axis=1)
             terms = jnp.dot(attended, select(layer, out_weight), preferred_element_type=F32).astype(BF)
-            if h == 0:
-                first_terms = terms
-            else:
-                terms, *fresh = ordered(terms, *fresh)
+            if layer == 0 and h == 0:
+                terms, up_got = ordered(terms, up_got)
+                up_weight = pass_on(0, up_parts[0], up_got, 0)
+            if h == 1:
+                terms, down_sent, *fresh = ordered(terms, down_parts[1], *fresh)
                 cache = to_rows(fresh)
+                down_weight = weight_of(layer, (down_parts[0], down_sent), 1)
             after.append(x_in[h] + pick(table[0], kinds_h[h], 2) * summed(terms))
-        after[0], cache = ordered(after[0], cache)
-        caches.append(cache)
         inner = []
-        mean, scale = statistics(jnp.concatenate(after, axis=0))
         for h in range(halves):
-            rows = slice(h * part, (h + 1) * part)
-            entry = normed(after[h], (mean[rows], scale[rows]), table[1], kinds_h[h])
+            entry = normed(after[h], statistics(after[h]), table[1], kinds_h[h])
             if layer == 0 and h == 0:
                 entry, parts = ordered_parts(entry, qkv_parts)
                 qkv_weight = weight_of(1, parts, 0)
-            if h == 0:
-                entry, down_sent = ordered(entry, down_parts[1])
-                down_got = mate_half(layer, down_sent)
             entry = gather_wide(entry)
             up = jnp.dot(entry, select(layer, up_weight), preferred_element_type=F32).astype(BF)
-            if h == 1:
-                up, down_got = ordered(up, down_got)
-                down_weight = pass_on(layer, down_parts[0], down_got, 1)
             size = chunk // 2
             got = to_partner(lax.dynamic_slice_in_dim(up, (1 - high) * size, size, 0))
             up = lax.dynamic_slice_in_dim(up, high * size, size, 0).astype(F32) + got.astype(F32)
             inner.append(jax.nn.gelu(up, approximate=True).astype(BF))
-        inner[0], *down_weight = ordered(inner[0], *down_weight)
-        if layer == 0:
-            inner[0], parts = ordered_parts(inner[0], out_parts)
-            out_weight = weight_of(1, parts, 1)
-            inner[0], parts = ordered_parts(inner[0], up_parts)
-            up_weight = weight_of(1, parts, 0)
-            qkv_now = select(1, qkv_weight)
         layer_in = []
         for h in range(halves):
             got = to_partner(inner[h])
+            if h == 1:
+                got, cache = ordered(got, cache)
+                caches.append(cache)
             first = jnp.where(lower, inner[h], got)
             second = jnp.where(lower, got, inner[h])
             whole = jnp.concatenate([first, second], axis=0)
             terms = jnp.dot(whole, select(layer, down_weight), preferred_element_type=F32).astype(BF)
+            if layer == 0 and h == 0:
+                terms, parts = ordered_parts(terms, out_parts)
+                out_weight = weight_of(1, parts, 1)
+                terms, parts = ordered_parts(terms, up_parts)
+                up_weight = weight_of(1, parts, 0)
+                qkv_now = select(1, qkv_weight)
             layer_in.append((after[h] + pick(table[1], kinds_h[h], 2) * summed(terms)).astype(BF))
         results.append(jnp.concatenate([block[:, :feat_a] for block in layer_in], axis=0))
     return (by_layer(results, lead), by_layer(caches, lead))

time: 951 us -> 865 us (0.910)
  waiting for transfers between devices: 550 us -> 472 us
  local copies, waits for them, and re-layouts: 69 us -> 58.5 us
    ppermute x24, waiting for transfers between devices: 98.1 us -> 18.5 us  [gather_wide(): lax.ppermute(block, 'wide', wide_pairs(step))]
    ppermute x21 -> x23, waiting for transfers between devices: 274 us -> 316 us  [to_partner(): lax.ppermute(value, 'narrow', [(i, i ^ 2) for i in range(lax.axis_size('n...]
    ppermute x10, waiting for transfers between devices: 69.3 us -> 27.6 us  [to_mate(): lax.ppermute(value, 'narrow', [(i, i ^ 1) for i in range(lax.axis_size('n...]
    ppermute x8, waiting for transfers between devices: 16.1 us -> 30.3 us  [mate_half(): return lax.ppermute(sent, ('section', 'narrow'), pairs)]
    ppermute x9, waiting for transfers between devices: 29.6 us -> 18.1 us  [exchange(): block = lax.ppermute(block, axis, [(i, (i + step) % n) for i in range(n)])]
    ppermute x21 -> x23, starting transfers between devices: 29.3 us -> 32.6 us  [to_partner(): lax.ppermute(value, 'narrow', [(i, i ^ 2) for i in range(lax.axis_size('n...]
  transfers between devices with their start and end apart: 110 -> 112, of which waited for: 69 -> 54; matrix products, arithmetic and copies ran while one was open for 17% -> 20% of each run, Pallas kernels for 3% -> 4%
where the time goes in v9:
time: 865 us; the launch traced here: 856 us
  waiting for transfers between devices  472 us (55%)
  starting transfers between devices  154 us (18%)
  other arithmetic  66.3 us (8%)
  matrix products  63 us (7%)
  local copies, waits for them, and re-layouts  58.5 us (7%)
  Pallas kernels  37.9 us (4%)
    ppermute x23, waiting for transfers between devices, to_partner(): lax.ppermute(value, 'narrow', [(i, i ^ 2) for i in range(lax.axis_size('n...  316 us
    ppermute x24, waiting for transfers between devices, scatter_wide(): total += lax.ppermute(terms[step], 'wide', wide_pairs(step)).astype(F32)  59.7 us
    ppermute x23, starting transfers between devices, to_partner(): lax.ppermute(value, 'narrow', [(i, i ^ 2) for i in range(lax.axis_size('n...  32.6 us
    ppermute x24, starting transfers between devices, scatter_wide(): total += lax.ppermute(terms[step], 'wide', wide_pairs(step)).astype(F32)  31 us
    ppermute x8, waiting for transfers between devices, mate_half(): return lax.ppermute(sent, ('section', 'narrow'), pairs)  30.3 us
    ppermute x24, starting transfers between devices, gather_wide(): lax.ppermute(block, 'wide', wide_pairs(step))  28.5 us
    ppermute x10, waiting for transfers between devices, to_mate(): lax.ppermute(value, 'narrow', [(i, i ^ 1) for i in range(lax.axis_size('n...  27.6 us
    pallas_call x4, Pallas kernels, attend(): pl.pallas_call(functools.partial(attend_kernel, heads, head_dim), grid=(r...  21.6 us
  transfers between devices with their start and end apart: 112, of which 54 were waited for; matrix products, arithmetic and copies ran while one was open for 20% of the time, Pallas kernels for 4%

profile of v9, /device:TPU:0, one launch (start us, length us, event | category | flops | bytes accessed | tf_op | source)
XLA Modules:
  0.0 855.8 jit_solution(17175531641357227636)
XLA Ops:
  2.6 3.0 collective-permute-start
  5.6 5.5 dynamic-slice_bitcast_fusion.5
  31.9 4.9 dynamic-slice_bitcast_fusion.2
  41.4 5.0 fusion.104
  48.1 2.8 collective-permute-done.1
  56.0 3.2 broadcast_select_fusion.14
  64.9 10.8 %collective-permute-done.8 = bf16[768,1152]{1,0:T(8,128)(2,1)} collective-permute-done((bf16[768,1152]{1,0:T(8,128)(2,1)}, bf16[768,1152]{1,0:T(8,128)(2,1)}, u32[]{:S(2)}, u32[]{:S(2)}) %collective-permute-start.8) | collective-permute-done | bytes 1769504 | tf_op jit(solution)/shard_map/ppermute | solution.py:311
  86.4 6.0 collective-permute-done.14
  92.4 4.1 collective-permute-done.15
  108.8 8.1 collective-permute-done.17
  123.5 4.0 convolution_convert_fusion.3
  129.7 2.8 collective-permute-start.10
  132.7 12.1 %collective-permute-done.18 = bf16[512,576]{0,1:T(8,128)(2,1)S(1)} collective-permute-done((bf16[512,576]{0,1:T(8,128)(2,1)}, bf16[512,576]{0,1:T(8,128)(2,1)S(1)}, u32[]{:S(2)}, u32[]{:S(2)}) %collective-permute-start.18) | collective-permute-done | bytes 589856 | tf_op jit(solution)/shard_map/ppermute | solution.py:243
  146.4 4.0 prepare.5
  154.9 4.0 prepare.4
  164.1 5.9 attend.5
  171.8 4.8 dynamic-slice_bitcast_fusion.1
  178.3 5.2 attend.4
  184.7 18.6 %collective-permute-done.34 = bf16[512,192]{1,0:T(8,128)(2,1)} collective-permute-done((bf16[512,192]{1,0:T(8,128)(2,1)}, bf16[512,192]{1,0:T(8,128)(2,1)}, u32[]{:S(2)}, u32[]{:S(2)}) %collective-permute-start.34) | collective-permute-done | bytes 196640 | tf_op jit(solution)/shard_map/ppermute | solution.py:243
  222.1 4.9 collective-permute-done.25
  227.0 3.5 collective-permute-start.31
  233.6 2.8 collective-permute-start.53
  238.6 6.5 collective-permute-done.53
  249.6 39.9 %collective-permute-done.45 = f32[2,128]{1,0:T(2,128)S(1)} collective-permute-done((f32[2,128]{1,0:T(2,128)S(1)}, f32[2,128]{1,0:T(2,128)S(1)}, u32[]{:S(2)}, u32[]{:S(2)}) %collective-permute-start.45) | collective-permute-done | bytes 1056 | tf_op jit(solution)/shard_map/ppermute | solution.py:243
  295.0 11.4 %collective-permute-done.35 = bf16[1536,768]{1,0:T(8,128)(2,1)S(1)} collective-permute-done((bf16[1536,768]{1,0:T(8,128)(2,1)S(1)}, bf16[1536,768]{1,0:T(8,128)(2,1)S(1)}, u32[]{:S(2)}, u32[]{:S(2)}) %collective-permute-start.35) | collective-permute-done | bytes 2359328 | tf_op jit(solution)/shard_map/ppermute | solution.py:311
  312.8 4.7 convolution_convert_fusion.11
  319.3 4.6 convolution_convert_fusion.14
  326.4 31.6 %collective-permute-done.49 = bf16[256,1536]{1,0:T(8,128)(2,1)S(1)} collective-permute-done((bf16[256,1536]{1,0:T(8,128)(2,1)S(1)}, bf16[256,1536]{1,0:T(8,128)(2,1)S(1)}, u32[]{:S(2)}, u32[]{:S(2)}) %collective-permute-start.49) | collective-permute-done | bytes 786464 | tf_op jit(solution)/shard_map/ppermute | solution.py:243
  358.7 24.5 %collective-permute-done.32 = bf16[256,1536]{1,0:T(8,128)(2,1)S(1)} collective-permute-done((bf16[256,1536]{1,0:T(8,128)(2,1)S(1)}, bf16[256,1536]{1,0:T(8,128)(2,1)S(1)}, u32[]{:S(2)}, u32[]{:S(2)}) %collective-permute-start.32) | collective-permute-done | bytes 786464 | tf_op jit(solution)/shard_map/ppermute | solution.py:243
  384.0 4.2 pad_maximum_fusion.5
  389.9 10.2 %collective-permute-done.50 = bf16[256,1536]{1,0:T(8,128)(2,1)S(1)} collective-permute-done((bf16[256,1536]{1,0:T(8,128)(2,1)S(1)}, bf16[256,1536]{1,0:T(8,128)(2,1)S(1)}, u32[]{:S(2)}, u32[]{:S(2)}) %collective-permute-start.50) | collective-permute-done | bytes 786464 | tf_op jit(solution)/shard_map/ppermute | solution.py:243
  400.2 8.3 collective-permute-done.33
  443.9 5.5 collective-permute-done.57
  451.7 3.4 collective-permute-start.65
  467.9 2.7 collective-permute-done.67
  472.6 4.9 convolution_convert_fusion
  479.8 3.0 collective-permute-start.69
  482.8 5.3 collective-permute-done.60
  488.1 5.8 convolution_convert_fusion.1
  496.1 3.0 collective-permute-start.64
  502.1 4.2 prepare.7
  506.3 25.5 %collective-permute-done.64 = bf16[512,576]{0,1:T(8,128)(2,1)} collective-permute-done((bf16[512,576]{0,1:T(8,128)(2,1)}, bf16[512,576]{0,1:T(8,128)(2,1)}, u32[]{:S(2)}, u32[]{:S(2)}) %collective-permute-start.64) | collective-permute-done | bytes 589856 | tf_op jit(solution)/shard_map/ppermute | solution.py:243
  535.5 4.0 prepare.6
  541.3 4.7 collective-permute-start.72
  549.1 5.2 attend.6
  557.8 5.2 attend.7
  563.0 3.0 collective-permute-start.86
  574.4 4.5 collective-permute-done.86
  585.3 7.0 collective-permute-done.75
  595.0 5.7 collective-permute-done.95
  600.7 8.0 collective-permute-done.94
  612.7 8.4 collective-permute-done.96
  632.7 3.8 collective-permute-done.100
  638.1 2.7 collective-permute-done.99
  644.1 5.9 convolution_convert_fusion.5
  654.8 5.8 convolution_convert_fusion.8
  661.9 53.2 %collective-permute-done.101 = bf16[256,1536]{1,0:T(8,128)(2,1)S(1)} collective-permute-done((bf16[256,1536]{1,0:T(8,128)(2,1)S(1)}, bf16[256,1536]{1,0:T(8,128)(2,1)S(1)}, u32[]{:S(2)}, u32[]{:S(2)}) %collective-permute-start.101) | collective-permute-done | bytes 786464 | tf_op jit(solution)/shard_map/ppermute | solution.py:243
  715.8 33.0 %collective-permute-done.84 = bf16[256,1536]{1,0:T(8,128)(2,1)S(1)} collective-permute-done((bf16[256,1536]{1,0:T(8,128)(2,1)S(1)}, bf16[256,1536]{1,0:T(8,128)(2,1)S(1)}, u32[]{:S(2)}, u32[]{:S(2)}) %collective-permute-start.84) | collective-permute-done | bytes 786464 | tf_op jit(solution)/shard_map/ppermute | solution.py:243
  749.8 32.7 %collective-permute-done.102 = bf16[256,1536]{1,0:T(8,128)(2,1)S(1)} collective-permute-done((bf16[256,1536]{1,0:T(8,128)(2,1)S(1)}, bf16[256,1536]{1,0:T(8,128)(2,1)S(1)}, u32[]{:S(2)}, u32[]{:S(2)}) %collective-permute-start.102) | collective-permute-done | bytes 786464 | tf_op jit(solution)/shard_map/ppermute | solution.py:243
  782.6 16.7 %collective-permute-done.85 = bf16[256,1536]{1,0:T(8,128)(2,1)S(1)} collective-permute-done((bf16[256,1536]{1,0:T(8,128)(2,1)S(1)}, bf16[256,1536]{1,0:T(8,128)(2,1)S(1)}, u32[]{:S(2)}, u32[]{:S(2)}) %collective-permute-start.85) | collective-permute-done | bytes 786464 | tf_op jit(solution)/shard_map/ppermute | solution.py:243
  815.6 9.0 %collective-permute-done.90 = bf16[128,1536]{1,0:T(8,128)(2,1)S(1)} collective-permute-done((bf16[128,1536]{1,0:T(8,128)(2,1)S(1)}, bf16[128,1536]{1,0:T(8,128)(2,1)S(1)}, u32[]{:S(2)}, u32[]{:S(2)}) %collective-permute-start.90) | collective-permute-done | bytes 393248 | tf_op jit(solution)/shard_map/ppermute | solution.py:234
  825.8 5.3 collective-permute-done.108
  831.0 9.4 %collective-permute-done.107 = bf16[128,1536]{1,0:T(8,128)(2,1)S(1)} collective-permute-done((bf16[128,1536]{1,0:T(8,128)(2,1)S(1)}, bf16[128,1536]{1,0:T(8,128)(2,1)S(1)}, u32[]{:S(2)}, u32[]{:S(2)}) %collective-permute-start.107) | collective-permute-done | bytes 393248 | tf_op jit(solution)/shard_map/ppermute | solution.py:234
  842.3 9.7 %collective-permute-done.109 = bf16[128,1536]{1,0:T(8,128)(2,1)S(1)} collective-permute-done((bf16[128,1536]{1,0:T(8,128)(2,1)S(1)}, bf16[128,1536]{1,0:T(8,128)(2,1)S(1)}, u32[]{:S(2)}, u32[]{:S(2)}) %collective-permute-start.109) | collective-permute-done | bytes 393248 | tf_op jit(solution)/shard_map/ppermute | solution.py:239
  (634 shorter events, 273.7 us)
Async XLA Ops:
  2.6 34.3 %collective-permute-start = (bf16[256,768]{1,0:T(8,128)(2,1)}, bf16[256,768]{1,0:T(8,128)(2,1)}, u32[]{:S(2)}, u32[]{:S(2)}) collective-permute-start(bf16[256,768]{1,0:T(8,128)(2,1)} %dynamic-slice_bitcast_fusion.8), channel_id=1, source_target_pairs={{0,1},{1,0},{2,3},{3,2},{4,5},{5,4},{6,7},{7,6},{8,9},{9,8},{10,11... | collective-permute-start | bytes 1179656 | tf_op jit(solution)/shard_map/ppermute | solution.py:239
  13.9 37.1 %collective-permute-start.3 = (bf16[768,1152]{1,0:T(8,128)(2,1)}, bf16[768,1152]{1,0:T(8,128)(2,1)}, u32[]{:S(2)}, u32[]{:S(2)}) collective-permute-start(bf16[768,1152]{1,0:T(8,128)(2,1)} %pad_maximum_fusion.9), channel_id=1, source_target_pairs={{0,16},{1,17},{2,18},{3,19},{4,20},{5,21},{6,22},{7,23},{8,24},{9,... | collective-permute-start | bytes 5308424 | tf_op jit(solution)/shard_map/ppermute | solution.py:314
  50.9 24.7 %collective-permute-start.8 = (bf16[768,1152]{1,0:T(8,128)(2,1)}, bf16[768,1152]{1,0:T(8,128)(2,1)}, u32[]{:S(2)}, u32[]{:S(2)}) collective-permute-start(bf16[768,1152]{1,0:T(8,128)(2,1)} %pad_maximum_fusion.8), channel_id=1, source_target_pairs={{0,1},{1,0},{2,3},{3,2},{4,5},{5,4},{6,7},{7,6},{8,9},{9,8},{10,11... | collective-permute-start | bytes 5308424 | tf_op jit(solution)/shard_map/ppermute | solution.py:311
  75.7 25.4 %collective-permute-start.9 = (bf16[768,1152]{1,0:T(8,128)(2,1)}, bf16[768,1152]{1,0:T(8,128)(2,1)S(1)}, u32[]{:S(2)}, u32[]{:S(2)}) collective-permute-start(bf16[768,1152]{1,0:T(8,128)(2,1)} %collective-permute-done.8), channel_id=1, source_target_pairs={{0,16},{1,17},{2,18},{3,19},{4,20},{5,21},{6,22},{7,23},{8,24},{9,... | collective-permute-start | bytes 5308424 | tf_op jit(solution)/shard_map/ppermute | solution.py:314
  79.0 25.5 %collective-permute-start.13 = (bf16[128,1536]{1,0:T(8,128)(2,1)S(1)}, bf16[128,1536]{1,0:T(8,128)(2,1)S(1)}, u32[]{:S(2)}, u32[]{:S(2)}) collective-permute-start(bf16[128,1536]{1,0:T(8,128)(2,1)S(1)} %fusion.114), channel_id=1, source_target_pairs={{0,12},{4,8},{8,4},{12,0},{1,13},{5,9},{9,5},{13,1},{2,14},{6,10},... | collective-permute-start | bytes 1179656 | tf_op jit(solution)/shard_map/ppermute | solution.py:227
  81.5 23.8 %collective-permute-start.12 = (bf16[128,1536]{1,0:T(8,128)(2,1)S(1)}, bf16[128,1536]{1,0:T(8,128)(2,1)S(1)}, u32[]{:S(2)}, u32[]{:S(2)}) collective-permute-start(bf16[128,1536]{1,0:T(8,128)(2,1)S(1)} %fusion.114), channel_id=1, source_target_pairs={{0,8},{4,12},{8,0},{12,4},{1,9},{5,13},{9,1},{13,5},{2,10},{6,14},... | collective-permute-start | bytes 1179656 | tf_op jit(solution)/shard_map/ppermute | solution.py:227
  98.5 18.4 %collective-permute-start.17 = (bf16[384,768]{1,0:T(8,128)(2,1)}, bf16[384,768]{1,0:T(8,128)(2,1)S(1)}, u32[]{:S(2)}, u32[]{:S(2)}) collective-permute-start(bf16[384,768]{1,0:T(8,128)(2,1)} %pad_maximum_fusion.19), channel_id=1, source_target_pairs={{0,1},{1,0},{2,3},{3,2},{4,5},{5,4},{6,7},{7,6},{8,9},{9,8},{10,11... | collective-permute-start | bytes 1769480 | tf_op jit(solution)/shard_map/ppermute | solution.py:311
  101.1 22.4 %collective-permute-start.7 = (bf16[128,1536]{1,0:T(8,128)(2,1)}, bf16[128,1536]{1,0:T(8,128)(2,1)}, u32[]{:S(2)}, u32[]{:S(2)}) collective-permute-start(bf16[128,1536]{1,0:T(8,128)(2,1)} %fusion.110), channel_id=1, source_target_pairs={{0,12},{4,8},{8,4},{12,0},{1,13},{5,9},{9,5},{13,1},{2,14},{6,10},... | collective-permute-start | bytes 1179656 | tf_op jit(solution)/shard_map/ppermute | solution.py:227
  104.5 19.0 %collective-permute-start.6 = (bf16[128,1536]{1,0:T(8,128)(2,1)}, bf16[128,1536]{1,0:T(8,128)(2,1)S(1)}, u32[]{:S(2)}, u32[]{:S(2)}) collective-permute-start(bf16[128,1536]{1,0:T(8,128)(2,1)} %fusion.110), channel_id=1, source_target_pairs={{0,8},{4,12},{8,0},{12,4},{1,9},{5,13},{9,1},{13,5},{2,10},{6,14},... | collective-permute-start | bytes 1179656 | tf_op jit(solution)/shard_map/ppermute | solution.py:227
  105.3 18.2 %collective-permute-start.5 = (bf16[128,1536]{1,0:T(8,128)(2,1)}, bf16[128,1536]{1,0:T(8,128)(2,1)}, u32[]{:S(2)}, u32[]{:S(2)}) collective-permute-start(bf16[128,1536]{1,0:T(8,128)(2,1)} %fusion.110), channel_id=1, source_target_pairs={{0,4},{4,0},{8,12},{12,8},{1,5},{5,1},{9,13},{13,9},{2,6},{6,2},{1... | collective-permute-start | bytes 1179656 | tf_op jit(solution)/shard_map/ppermute | solution.py:227
  118.8 25.9 %collective-permute-start.18 = (bf16[512,576]{0,1:T(8,128)(2,1)}, bf16[512,576]{0,1:T(8,128)(2,1)S(1)}, u32[]{:S(2)}, u32[]{:S(2)}) collective-permute-start(bf16[512,576]{0,1:T(8,128)(2,1)} %copy.37), channel_id=1, source_target_pairs={{0,2},{1,3},{2,0},{3,1},{4,6},{5,7},{6,4},{7,5},{8,10},{9,11},{10,... | collective-permute-start | bytes 1769480 | tf_op jit(solution)/shard_map/ppermute | solution.py:243
  121.1 38.6 %collective-permute-start.19 = (bf16[384,1536]{1,0:T(8,128)(2,1)}, bf16[384,1536]{1,0:T(8,128)(2,1)}, u32[]{:S(2)}, u32[]{:S(2)}) collective-permute-start(bf16[384,1536]{1,0:T(8,128)(2,1)} %pad_maximum_fusion.10), channel_id=1, source_target_pairs={{0,16},{1,17},{2,18},{3,19},{4,20},{5,21},{6,22},{7,23},{8,24},{9,... | collective-permute-start | bytes 3538952 | tf_op jit(solution)/shard_map/ppermute | solution.py:314
  129.7 21.4 %collective-permute-start.10 = (bf16[512,576]{0,1:T(8,128)(2,1)}, bf16[512,576]{0,1:T(8,128)(2,1)}, u32[]{:S(2)}, u32[]{:S(2)}) collective-permute-start(bf16[512,576]{0,1:T(8,128)(2,1)} %copy.31), channel_id=1, source_target_pairs={{0,2},{1,3},{2,0},{3,1},{4,6},{5,7},{6,4},{7,5},{8,10},{9,11},{10,... | collective-permute-start | bytes 1769480 | tf_op jit(solution)/shard_map/ppermute | solution.py:243
  162.1 52.6 %collective-permute-start.22 = (bf16[768,1536]{1,0:T(8,128)(2,1)}, bf16[768,1536]{1,0:T(8,128)(2,1)}, u32[]{:S(2)}, u32[]{:S(2)}) collective-permute-start(bf16[768,1536]{1,0:T(8,128)(2,1)} %get-tuple-element.89), channel_id=1, source_target_pairs={{0,1},{1,0},{2,3},{3,2},{4,5},{5,4},{6,7},{7,6},{8,9},{9,8},{10,11... | collective-permute-start | bytes 7077896 | tf_op jit(solution)/shard_map/ppermute | solution.py:311
  170.0 33.3 %collective-permute-start.34 = (bf16[512,192]{1,0:T(8,128)(2,1)}, bf16[512,192]{1,0:T(8,128)(2,1)}, u32[]{:S(2)}, u32[]{:S(2)}) collective-permute-start(bf16[512,192]{1,0:T(8,128)(2,1)} %attend.5), channel_id=1, source_target_pairs={{0,2},{1,3},{2,0},{3,1},{4,6},{5,7},{6,4},{7,5},{8,10},{9,11},{10,... | collective-permute-start | bytes 589832 | tf_op jit(solution)/shard_map/ppermute | solution.py:243
  183.5 26.5 %collective-permute-start.21 = (bf16[512,192]{1,0:T(8,128)(2,1)S(1)}, bf16[512,192]{1,0:T(8,128)(2,1)S(1)}, u32[]{:S(2)}, u32[]{:S(2)}) collective-permute-start(bf16[512,192]{1,0:T(8,128)(2,1)S(1)} %attend.4), channel_id=1, source_target_pairs={{0,2},{1,3},{2,0},{3,1},{4,6},{5,7},{6,4},{7,5},{8,10},{9,11},{10,... | collective-permute-start | bytes 589832 | tf_op jit(solution)/shard_map/ppermute | solution.py:243
  210.0 23.6 %collective-permute-start.51 = (bf16[1,3,256,128]{3,2,0,1:T(8,128)(2,1)S(1)}, bf16[1,3,256,128]{3,2,0,1:T(8,128)(2,1)S(1)}, u32[]{:S(2)}, u32[]{:S(2)}) collective-permute-start(bf16[1,3,256,128]{3,2,0,1:T(8,128)(2,1)S(1)} %get-tuple-element.228), channel_id=1, source_target_pairs={{0,1},{1,2},{2,3},{3,0},{4,5},{5,6},{6,7},{7,4},{8,9},{9,10},{10,1... | collective-permute-start | bytes 589832 | tf_op jit(solution)/shard_map/ppermute | solution.py:167
  214.7 21.8 %collective-permute-start.52 = (bf16[1,3,256,128]{3,2,0,1:T(8,128)(2,1)S(1)}, bf16[1,3,256,128]{3,2,0,1:T(8,128)(2,1)S(1)}, u32[]{:S(2)}, u32[]{:S(2)}) collective-permute-start(bf16[1,3,256,128]{3,2,0,1:T(8,128)(2,1)S(1)} %get-tuple-element.227), channel_id=1, source_target_pairs={{0,2},{1,3},{2,0},{3,1},{4,6},{5,7},{6,4},{7,5},{8,10},{9,11},{10,... | collective-permute-start | bytes 589832 | tf_op jit(solution)/shard_map/ppermute | solution.py:167
  227.0 84.2 %collective-permute-start.31 = (bf16[1536,1536]{1,0:T(8,128)(2,1)S(1)}, bf16[1536,1536]{1,0:T(8,128)(2,1)}, u32[]{:S(2)}, u32[]{:S(2)}) collective-permute-start(bf16[1536,1536]{1,0:T(8,128)(2,1)S(1)} %pad_maximum_fusion.1), channel_id=1, source_target_pairs={{0,16},{1,17},{2,18},{3,19},{4,20},{5,21},{6,22},{7,23},{8,24},{9,... | collective-permute-start | bytes 14155784 | tf_op jit(solution)/shard_map/ppermute | solution.py:314
  231.1 14.1 %collective-permute-start.44 = (bf16[128,1536]{1,0:T(8,128)(2,1)S(1)}, bf16[128,1536]{1,0:T(8,128)(2,1)S(1)}, u32[]{:S(2)}, u32[]{:S(2)}) collective-permute-start(bf16[128,1536]{1,0:T(8,128)(2,1)S(1)} %pad_maximum_fusion.23), channel_id=1, source_target_pairs={{0,1},{1,0},{2,3},{3,2},{4,5},{5,4},{6,7},{7,6},{8,9},{9,8},{10,11... | collective-permute-start | bytes 1179656 | tf_op jit(solution)/shard_map/ppermute | solution.py:239
  236.5 69.9 %collective-permute-start.35 = (bf16[1536,768]{1,0:T(8,128)(2,1)S(1)}, bf16[1536,768]{1,0:T(8,128)(2,1)S(1)}, u32[]{:S(2)}, u32[]{:S(2)}) collective-permute-start(bf16[1536,768]{1,0:T(8,128)(2,1)S(1)} %copy-done.41), channel_id=1, source_target_pairs={{0,1},{1,0},{2,3},{3,2},{4,5},{5,4},{6,7},{7,6},{8,9},{9,8},{10,11... | collective-permute-start | bytes 7077896 | tf_op jit(solution)/shard_map/ppermute | solution.py:311
  246.3 43.2 %collective-permute-start.45 = (f32[2,128]{1,0:T(2,128)S(1)}, f32[2,128]{1,0:T(2,128)S(1)}, u32[]{:S(2)}, u32[]{:S(2)}) collective-permute-start(f32[2,128]{1,0:T(2,128)S(1)} %pad_maximum_fusion.38), channel_id=1, source_target_pairs={{0,2},{1,3},{2,0},{3,1},{4,6},{5,7},{6,4},{7,5},{8,10},{9,11},{10,... | collective-permute-start | bytes 3080 | tf_op jit(solution)/shard_map/ppermute | solution.py:243
  248.2 45.5 %collective-permute-start.27 = (f32[2,128]{1,0:T(2,128)S(1)}, f32[2,128]{1,0:T(2,128)S(1)}, u32[]{:S(2)}, u32[]{:S(2)}) collective-permute-start(f32[2,128]{1,0:T(2,128)S(1)} %pad_maximum_fusion.37), channel_id=1, source_target_pairs={{0,2},{1,3},{2,0},{3,1},{4,6},{5,7},{6,4},{7,5},{8,10},{9,11},{10,... | collective-permute-start | bytes 3080 | tf_op jit(solution)/shard_map/ppermute | solution.py:243
  290.5 17.7 %collective-permute-start.48 = (bf16[128,1536]{1,0:T(8,128)(2,1)S(1)}, bf16[128,1536]{1,0:T(8,128)(2,1)S(1)}, u32[]{:S(2)}, u32[]{:S(2)}) collective-permute-start(bf16[128,1536]{1,0:T(8,128)(2,1)S(1)} %add_convert_fusion.8), channel_id=1, source_target_pairs={{0,12},{4,8},{8,4},{12,0},{1,13},{5,9},{9,5},{13,1},{2,14},{6,10},... | collective-permute-start | bytes 1179656 | tf_op jit(solution)/shard_map/ppermute | solution.py:227
  291.6 18.0 %collective-permute-start.47 = (bf16[128,1536]{1,0:T(8,128)(2,1)S(1)}, bf16[128,1536]{1,0:T(8,128)(2,1)S(1)}, u32[]{:S(2)}, u32[]{:S(2)}) collective-permute-start(bf16[128,1536]{1,0:T(8,128)(2,1)S(1)} %add_convert_fusion.8), channel_id=1, source_target_pairs={{0,8},{4,12},{8,0},{12,4},{1,9},{5,13},{9,1},{13,5},{2,10},{6,14},... | collective-permute-start | bytes 1179656 | tf_op jit(solution)/shard_map/ppermute | solution.py:227
  293.7 16.7 %collective-permute-start.46 = (bf16[128,1536]{1,0:T(8,128)(2,1)S(1)}, bf16[128,1536]{1,0:T(8,128)(2,1)}, u32[]{:S(2)}, u32[]{:S(2)}) collective-permute-start(bf16[128,1536]{1,0:T(8,128)(2,1)S(1)} %add_convert_fusion.8), channel_id=1, source_target_pairs={{0,4},{4,0},{8,12},{12,8},{1,5},{5,1},{9,13},{13,9},{2,6},{6,2},{1... | collective-permute-start | bytes 1179656 | tf_op jit(solution)/shard_map/ppermute | solution.py:227
  310.4 73.5 %collective-permute-start.62 = (bf16[768,1152]{1,0:T(8,128)(2,1)}, bf16[768,1152]{1,0:T(8,128)(2,1)S(1)}, u32[]{:S(2)}, u32[]{:S(2)}) collective-permute-start(bf16[768,1152]{1,0:T(8,128)(2,1)} %pad_maximum_fusion.8), channel_id=1, source_target_pairs={{16,17},{17,16},{18,19},{19,18},{20,21},{21,20},{22,23},{23,22},{2... | collective-permute-start | bytes 5308424 | tf_op jit(solution)/shard_map/ppermute | solution.py:311
  311.2 97.4 %collective-permute-start.36 = (bf16[1536,1536]{1,0:T(8,128)(2,1)S(1)}, bf16[1536,1536]{1,0:T(8,128)(2,1)S(1)}, u32[]{:S(2)}, u32[]{:S(2)}) collective-permute-start(bf16[1536,1536]{1,0:T(8,128)(2,1)S(1)} %pad_maximum_fusion.3), channel_id=1, source_target_pairs={{0,16},{1,17},{2,18},{3,19},{4,20},{5,21},{6,22},{7,23},{8,24},{9,... | collective-permute-start | bytes 14155784 | tf_op jit(solution)/shard_map/ppermute | solution.py:314
  317.5 40.5 %collective-permute-start.49 = (bf16[256,1536]{1,0:T(8,128)(2,1)S(1)}, bf16[256,1536]{1,0:T(8,128)(2,1)S(1)}, u32[]{:S(2)}, u32[]{:S(2)}) collective-permute-start(bf16[256,1536]{1,0:T(8,128)(2,1)S(1)} %constant_dynamic-slice_fusion.10), channel_id=1, source_target_pairs={{0,2},{1,3},{2,0},{3,1},{4,6},{5,7},{6,4},{7,5},{8,10},{9,11},{10,... | collective-permute-start | bytes 2359304 | tf_op jit(solution)/shard_map/ppermute | solution.py:243
  323.9 59.3 %collective-permute-start.32 = (bf16[256,1536]{1,0:T(8,128)(2,1)S(1)}, bf16[256,1536]{1,0:T(8,128)(2,1)S(1)}, u32[]{:S(2)}, u32[]{:S(2)}) collective-permute-start(bf16[256,1536]{1,0:T(8,128)(2,1)S(1)} %constant_dynamic-slice_fusion.11), channel_id=1, source_target_pairs={{0,2},{1,3},{2,0},{3,1},{4,6},{5,7},{6,4},{7,5},{8,10},{9,11},{10,... | collective-permute-start | bytes 2359304 | tf_op jit(solution)/shard_map/ppermute | solution.py:243
  358.7 41.4 %collective-permute-start.50 = (bf16[256,1536]{1,0:T(8,128)(2,1)S(1)}, bf16[256,1536]{1,0:T(8,128)(2,1)S(1)}, u32[]{:S(2)}, u32[]{:S(2)}) collective-permute-start(bf16[256,1536]{1,0:T(8,128)(2,1)S(1)} %fusion.19), channel_id=1, source_target_pairs={{0,2},{1,3},{2,0},{3,1},{4,6},{5,7},{6,4},{7,5},{8,10},{9,11},{10,... | collective-permute-start | bytes 2359304 | tf_op jit(solution)/shard_map/ppermute | solution.py:243
  383.9 24.6 %collective-permute-start.33 = (bf16[256,1536]{1,0:T(8,128)(2,1)S(1)}, bf16[256,1536]{1,0:T(8,128)(2,1)S(1)}, u32[]{:S(2)}, u32[]{:S(2)}) collective-permute-start(bf16[256,1536]{1,0:T(8,128)(2,1)S(1)} %fusion.11), channel_id=1, source_target_pairs={{0,2},{1,3},{2,0},{3,1},{4,6},{5,7},{6,4},{7,5},{8,10},{9,11},{10,... | collective-permute-start | bytes 2359304 | tf_op jit(solution)/shard_map/ppermute | solution.py:243
  388.2 75.0 %collective-permute-start.63 = (bf16[1536,1152]{1,0:T(8,128)(2,1)}, bf16[1536,1152]{1,0:T(8,128)(2,1)}, u32[]{:S(2)}, u32[]{:S(2)}) collective-permute-start(bf16[1536,1152]{1,0:T(8,128)(2,1)} %pad_maximum_fusion.5), channel_id=1, source_target_pairs={{16,0},{17,1},{18,2},{19,3},{20,4},{21,5},{22,6},{23,7},{24,8},{25... | collective-permute-start | bytes 10616840 | tf_op jit(solution)/shard_map/ppermute | solution.py:314
  426.2 15.4 %collective-permute-start.70 = (bf16[384,768]{1,0:T(8,128)(2,1)}, bf16[384,768]{1,0:T(8,128)(2,1)}, u32[]{:S(2)}, u32[]{:S(2)}) collective-permute-start(bf16[384,768]{1,0:T(8,128)(2,1)} %pad_maximum_fusion.19), channel_id=1, source_target_pairs={{16,17},{17,16},{18,19},{19,18},{20,21},{21,20},{22,23},{23,22},{2... | collective-permute-start | bytes 1769480 | tf_op jit(solution)/shard_map/ppermute | solution.py:311
  429.1 14.7 %collective-permute-start.40 = (bf16[128,1536]{1,0:T(8,128)(2,1)}, bf16[128,1536]{1,0:T(8,128)(2,1)}, u32[]{:S(2)}, u32[]{:S(2)}) collective-permute-start(bf16[128,1536]{1,0:T(8,128)(2,1)} %pad_maximum_fusion.22), channel_id=1, source_target_pairs={{0,1},{1,0},{2,3},{3,2},{4,5},{5,4},{6,7},{7,6},{8,9},{9,8},{10,11... | collective-permute-start | bytes 1179656 | tf_op jit(solution)/shard_map/ppermute | solution.py:239
  434.9 14.5 %collective-permute-start.57 = (bf16[128,1536]{1,0:T(8,128)(2,1)}, bf16[128,1536]{1,0:T(8,128)(2,1)}, u32[]{:S(2)}, u32[]{:S(2)}) collective-permute-start(bf16[128,1536]{1,0:T(8,128)(2,1)} %pad_maximum_fusion.24), channel_id=1, source_target_pairs={{0,1},{1,0},{2,3},{3,2},{4,5},{5,4},{6,7},{7,6},{8,9},{9,8},{10,11... | collective-permute-start | bytes 1179656 | tf_op jit(solution)/shard_map/ppermute | solution.py:239
  439.5 114.9 %collective-permute-start.82 = (bf16[768,1536]{1,0:T(8,128)(2,1)}, bf16[768,1536]{1,0:T(8,128)(2,1)}, u32[]{:S(2)}, u32[]{:S(2)}) collective-permute-start(bf16[768,1536]{1,0:T(8,128)(2,1)} %get-tuple-element.89), channel_id=1, source_target_pairs={{16,17},{17,16},{18,19},{19,18},{20,21},{21,20},{22,23},{23,22},{2... | collective-permute-start | bytes 7077896 | tf_op jit(solution)/shard_map/ppermute | solution.py:311
  463.2 76.5 %collective-permute-start.71 = (bf16[384,1536]{1,0:T(8,128)(2,1)}, bf16[384,1536]{1,0:T(8,128)(2,1)}, u32[]{:S(2)}, u32[]{:S(2)}) collective-permute-start(bf16[384,1536]{1,0:T(8,128)(2,1)} %pad_maximum_fusion.12), channel_id=1, source_target_pairs={{16,0},{17,1},{18,2},{19,3},{20,4},{21,5},{22,6},{23,7},{24,8},{25... | collective-permute-start | bytes 3538952 | tf_op jit(solution)/shard_map/ppermute | solution.py:314
  470.6 17.5 %collective-permute-start.60 = (bf16[128,1536]{1,0:T(8,128)(2,1)}, bf16[128,1536]{1,0:T(8,128)(2,1)}, u32[]{:S(2)}, u32[]{:S(2)}) collective-permute-start(bf16[128,1536]{1,0:T(8,128)(2,1)} %fusion.120), channel_id=1, source_target_pairs={{0,8},{4,12},{8,0},{12,4},{1,9},{5,13},{9,1},{13,5},{2,10},{6,14},... | collective-permute-start | bytes 1179656 | tf_op jit(solution)/shard_map/ppermute | solution.py:227
  472.0 16.1 %collective-permute-start.59 = (bf16[128,1536]{1,0:T(8,128)(2,1)}, bf16[128,1536]{1,0:T(8,128)(2,1)}, u32[]{:S(2)}, u32[]{:S(2)}) collective-permute-start(bf16[128,1536]{1,0:T(8,128)(2,1)} %fusion.120), channel_id=1, source_target_pairs={{0,4},{4,0},{8,12},{12,8},{1,5},{5,1},{9,13},{13,9},{2,6},{6,2},{1... | collective-permute-start | bytes 1179656 | tf_op jit(solution)/shard_map/ppermute | solution.py:227
  479.8 19.6 %collective-permute-start.69 = (bf16[512,576]{0,1:T(8,128)(2,1)S(1)}, bf16[512,576]{0,1:T(8,128)(2,1)}, u32[]{:S(2)}, u32[]{:S(2)}) collective-permute-start(bf16[512,576]{0,1:T(8,128)(2,1)S(1)} %copy.44), channel_id=1, source_target_pairs={{0,2},{1,3},{2,0},{3,1},{4,6},{5,7},{6,4},{7,5},{8,10},{9,11},{10,... | collective-permute-start | bytes 1769480 | tf_op jit(solution)/shard_map/ppermute | solution.py:243
  496.1 35.7 %collective-permute-start.64 = (bf16[512,576]{0,1:T(8,128)(2,1)}, bf16[512,576]{0,1:T(8,128)(2,1)}, u32[]{:S(2)}, u32[]{:S(2)}) collective-permute-start(bf16[512,576]{0,1:T(8,128)(2,1)} %copy.41), channel_id=1, source_target_pairs={{0,2},{1,3},{2,0},{3,1},{4,6},{5,7},{6,4},{7,5},{8,10},{9,11},{10,... | collective-permute-start | bytes 1769480 | tf_op jit(solution)/shard_map/ppermute | solution.py:243
  554.3 14.1 %collective-permute-start.73 = (bf16[512,192]{1,0:T(8,128)(2,1)S(1)}, bf16[512,192]{1,0:T(8,128)(2,1)S(1)}, u32[]{:S(2)}, u32[]{:S(2)}) collective-permute-start(bf16[512,192]{1,0:T(8,128)(2,1)S(1)} %attend.6), channel_id=1, source_target_pairs={{0,2},{1,3},{2,0},{3,1},{4,6},{5,7},{6,4},{7,5},{8,10},{9,11},{10,... | collective-permute-start | bytes 589832 | tf_op jit(solution)/shard_map/ppermute | solution.py:243
  556.4 86.4 %collective-permute-start.83 = (bf16[1536,1536]{1,0:T(8,128)(2,1)S(1)}, bf16[1536,1536]{1,0:T(8,128)(2,1)}, u32[]{:S(2)}, u32[]{:S(2)}) collective-permute-start(bf16[1536,1536]{1,0:T(8,128)(2,1)S(1)} %pad_maximum_fusion), channel_id=1, source_target_pairs={{16,0},{17,1},{18,2},{19,3},{20,4},{21,5},{22,6},{23,7},{24,8},{25... | collective-permute-start | bytes 14155784 | tf_op jit(solution)/shard_map/ppermute | solution.py:314
  563.0 15.9 %collective-permute-start.86 = (bf16[512,192]{1,0:T(8,128)(2,1)S(1)}, bf16[512,192]{1,0:T(8,128)(2,1)S(1)}, u32[]{:S(2)}, u32[]{:S(2)}) collective-permute-start(bf16[512,192]{1,0:T(8,128)(2,1)S(1)} %attend.7), channel_id=1, source_target_pairs={{0,2},{1,3},{2,0},{3,1},{4,6},{5,7},{6,4},{7,5},{8,10},{9,11},{10,... | collective-permute-start | bytes 589832 | tf_op jit(solution)/shard_map/ppermute | solution.py:243
  572.4 19.8 %collective-permute-start.75 = (bf16[128,1536]{1,0:T(8,128)(2,1)S(1)}, bf16[128,1536]{1,0:T(8,128)(2,1)S(1)}, u32[]{:S(2)}, u32[]{:S(2)}) collective-permute-start(bf16[128,1536]{1,0:T(8,128)(2,1)S(1)} %get-tuple-element.179), channel_id=1, source_target_pairs={{0,8},{4,12},{8,0},{12,4},{1,9},{5,13},{9,1},{13,5},{2,10},{6,14},... | collective-permute-start | bytes 1179656 | tf_op jit(solution)/shard_map/ppermute | solution.py:234
  573.8 19.9 %collective-permute-start.74 = (bf16[128,1536]{1,0:T(8,128)(2,1)S(1)}, bf16[128,1536]{1,0:T(8,128)(2,1)S(1)}, u32[]{:S(2)}, u32[]{:S(2)}) collective-permute-start(bf16[128,1536]{1,0:T(8,128)(2,1)S(1)} %get-tuple-element.177), channel_id=1, source_target_pairs={{0,4},{4,0},{8,12},{12,8},{1,5},{5,1},{9,13},{13,9},{2,6},{6,2},{1... | collective-permute-start | bytes 1179656 | tf_op jit(solution)/shard_map/ppermute | solution.py:234
  581.3 19.3 %collective-permute-start.95 = (bf16[128,1536]{1,0:T(8,128)(2,1)S(1)}, bf16[128,1536]{1,0:T(8,128)(2,1)S(1)}, u32[]{:S(2)}, u32[]{:S(2)}) collective-permute-start(bf16[128,1536]{1,0:T(8,128)(2,1)S(1)} %get-tuple-element.186), channel_id=1, source_target_pairs={{0,12},{4,8},{8,4},{12,0},{1,13},{5,9},{9,5},{13,1},{2,14},{6,10},... | collective-permute-start | bytes 1179656 | tf_op jit(solution)/shard_map/ppermute | solution.py:234
  583.8 24.9 %collective-permute-start.94 = (bf16[128,1536]{1,0:T(8,128)(2,1)S(1)}, bf16[128,1536]{1,0:T(8,128)(2,1)S(1)}, u32[]{:S(2)}, u32[]{:S(2)}) collective-permute-start(bf16[128,1536]{1,0:T(8,128)(2,1)S(1)} %get-tuple-element.187), channel_id=1, source_target_pairs={{0,8},{4,12},{8,0},{12,4},{1,9},{5,13},{9,1},{13,5},{2,10},{6,14},... | collective-permute-start | bytes 1179656 | tf_op jit(solution)/shard_map/ppermute | solution.py:234
  592.2 16.5 %collective-permute-start.93 = (bf16[128,1536]{1,0:T(8,128)(2,1)S(1)}, bf16[128,1536]{1,0:T(8,128)(2,1)S(1)}, u32[]{:S(2)}, u32[]{:S(2)}) collective-permute-start(bf16[128,1536]{1,0:T(8,128)(2,1)S(1)} %get-tuple-element.185), channel_id=1, source_target_pairs={{0,4},{4,0},{8,12},{12,8},{1,5},{5,1},{9,13},{13,9},{2,6},{6,2},{1... | collective-permute-start | bytes 1179656 | tf_op jit(solution)/shard_map/ppermute | solution.py:234
  593.7 38.0 %collective-permute-start.87 = (bf16[1536,768]{1,0:T(8,128)(2,1)S(1)}, bf16[1536,768]{1,0:T(8,128)(2,1)S(1)}, u32[]{:S(2)}, u32[]{:S(2)}) collective-permute-start(bf16[1536,768]{1,0:T(8,128)(2,1)S(1)} %copy-done.42), channel_id=1, source_target_pairs={{16,17},{17,16},{18,19},{19,18},{20,21},{21,20},{22,23},{23,22},{2... | collective-permute-start | bytes 7077896 | tf_op jit(solution)/shard_map/ppermute | solution.py:311
  609.6 51.1 %collective-permute-start.103 = (bf16[1,3,256,128]{3,2,0,1:T(8,128)(2,1)S(1)}, bf16[1,3,256,128]{3,2,0,1:T(8,128)(2,1)S(1)}, u32[]{:S(2)}, u32[]{:S(2)}) collective-permute-start(bf16[1,3,256,128]{3,2,0,1:T(8,128)(2,1)S(1)} %get-tuple-element.220), channel_id=1, source_target_pairs={{0,1},{1,2},{2,3},{3,0},{4,5},{5,6},{6,7},{7,4},{8,9},{9,10},{10,1... | collective-permute-start | bytes 589832 | tf_op jit(solution)/shard_map/ppermute | solution.py:167
  636.6 13.6 %collective-permute-start.81 = (bf16[128,1536]{1,0:T(8,128)(2,1)S(1)}, bf16[128,1536]{1,0:T(8,128)(2,1)S(1)}, u32[]{:S(2)}, u32[]{:S(2)}) collective-permute-start(bf16[128,1536]{1,0:T(8,128)(2,1)S(1)} %add_convert_fusion.4), channel_id=1, source_target_pairs={{0,12},{4,8},{8,4},{12,0},{1,13},{5,9},{9,5},{13,1},{2,14},{6,10},... | collective-permute-start | bytes 1179656 | tf_op jit(solution)/shard_map/ppermute | solution.py:227
  642.8 156.6 %collective-permute-start.88 = (bf16[1536,1536]{1,0:T(8,128)(2,1)S(1)}, bf16[1536,1536]{1,0:T(8,128)(2,1)S(1)}, u32[]{:S(2)}, u32[]{:S(2)}) collective-permute-start(bf16[1536,1536]{1,0:T(8,128)(2,1)S(1)} %pad_maximum_fusion.2), channel_id=1, source_target_pairs={{16,0},{17,1},{18,2},{19,3},{20,4},{21,5},{22,6},{23,7},{24,8},{25... | collective-permute-start | bytes 14155784 | tf_op jit(solution)/shard_map/ppermute | solution.py:314
  652.9 62.2 %collective-permute-start.101 = (bf16[256,1536]{1,0:T(8,128)(2,1)S(1)}, bf16[256,1536]{1,0:T(8,128)(2,1)S(1)}, u32[]{:S(2)}, u32[]{:S(2)}) collective-permute-start(bf16[256,1536]{1,0:T(8,128)(2,1)S(1)} %constant_dynamic-slice_fusion.4), channel_id=1, source_target_pairs={{0,2},{1,3},{2,0},{3,1},{4,6},{5,7},{6,4},{7,5},{8,10},{9,11},{10,... | collective-permute-start | bytes 2359304 | tf_op jit(solution)/shard_map/ppermute | solution.py:243
  660.7 88.1 %collective-permute-start.84 = (bf16[256,1536]{1,0:T(8,128)(2,1)S(1)}, bf16[256,1536]{1,0:T(8,128)(2,1)S(1)}, u32[]{:S(2)}, u32[]{:S(2)}) collective-permute-start(bf16[256,1536]{1,0:T(8,128)(2,1)S(1)} %constant_dynamic-slice_fusion.5), channel_id=1, source_target_pairs={{0,2},{1,3},{2,0},{3,1},{4,6},{5,7},{6,4},{7,5},{8,10},{9,11},{10,... | collective-permute-start | bytes 2359304 | tf_op jit(solution)/shard_map/ppermute | solution.py:243
  715.7 66.8 %collective-permute-start.102 = (bf16[256,1536]{1,0:T(8,128)(2,1)S(1)}, bf16[256,1536]{1,0:T(8,128)(2,1)S(1)}, u32[]{:S(2)}, u32[]{:S(2)}) collective-permute-start(bf16[256,1536]{1,0:T(8,128)(2,1)S(1)} %fusion.35), channel_id=1, source_target_pairs={{0,2},{1,3},{2,0},{3,1},{4,6},{5,7},{6,4},{7,5},{8,10},{9,11},{10,... | collective-permute-start | bytes 2359304 | tf_op jit(solution)/shard_map/ppermute | solution.py:243
  749.4 49.9 %collective-permute-start.85 = (bf16[256,1536]{1,0:T(8,128)(2,1)S(1)}, bf16[256,1536]{1,0:T(8,128)(2,1)S(1)}, u32[]{:S(2)}, u32[]{:S(2)}) collective-permute-start(bf16[256,1536]{1,0:T(8,128)(2,1)S(1)} %fusion.27), channel_id=1, source_target_pairs={{0,2},{1,3},{2,0},{3,1},{4,6},{5,7},{6,4},{7,5},{8,10},{9,11},{10,... | collective-permute-start | bytes 2359304 | tf_op jit(solution)/shard_map/ppermute | solution.py:243
  803.8 20.9 %collective-permute-start.90 = (bf16[128,1536]{1,0:T(8,128)(2,1)S(1)}, bf16[128,1536]{1,0:T(8,128)(2,1)S(1)}, u32[]{:S(2)}, u32[]{:S(2)}) collective-permute-start(bf16[128,1536]{1,0:T(8,128)(2,1)S(1)} %get-tuple-element.174), channel_id=1, source_target_pairs={{0,8},{4,12},{8,0},{12,4},{1,9},{5,13},{9,1},{13,5},{2,10},{6,14},... | collective-permute-start | bytes 1179656 | tf_op jit(solution)/shard_map/ppermute | solution.py:234
  805.3 19.4 %collective-permute-start.89 = (bf16[128,1536]{1,0:T(8,128)(2,1)S(1)}, bf16[128,1536]{1,0:T(8,128)(2,1)S(1)}, u32[]{:S(2)}, u32[]{:S(2)}) collective-permute-start(bf16[128,1536]{1,0:T(8,128)(2,1)S(1)} %get-tuple-element.172), channel_id=1, source_target_pairs={{0,4},{4,0},{8,12},{12,8},{1,5},{5,1},{9,13},{13,9},{2,6},{6,2},{1... | collective-permute-start | bytes 1179656 | tf_op jit(solution)/shard_map/ppermute | solution.py:234
  808.7 22.4 %collective-permute-start.108 = (bf16[128,1536]{1,0:T(8,128)(2,1)S(1)}, bf16[128,1536]{1,0:T(8,128)(2,1)S(1)}, u32[]{:S(2)}, u32[]{:S(2)}) collective-permute-start(bf16[128,1536]{1,0:T(8,128)(2,1)S(1)} %get-tuple-element.181), channel_id=1, source_target_pairs={{0,12},{4,8},{8,4},{12,0},{1,13},{5,9},{9,5},{13,1},{2,14},{6,10},... | collective-permute-start | bytes 1179656 | tf_op jit(solution)/shard_map/ppermute | solution.py:234
  810.2 30.3 %collective-permute-start.107 = (bf16[128,1536]{1,0:T(8,128)(2,1)S(1)}, bf16[128,1536]{1,0:T(8,128)(2,1)S(1)}, u32[]{:S(2)}, u32[]{:S(2)}) collective-permute-start(bf16[128,1536]{1,0:T(8,128)(2,1)S(1)} %get-tuple-element.182), channel_id=1, source_target_pairs={{0,8},{4,12},{8,0},{12,4},{1,9},{5,13},{9,1},{13,5},{2,10},{6,14},... | collective-permute-start | bytes 1179656 | tf_op jit(solution)/shard_map/ppermute | solution.py:234
  814.2 26.3 %collective-permute-start.106 = (bf16[128,1536]{1,0:T(8,128)(2,1)S(1)}, bf16[128,1536]{1,0:T(8,128)(2,1)S(1)}, u32[]{:S(2)}, u32[]{:S(2)}) collective-permute-start(bf16[128,1536]{1,0:T(8,128)(2,1)S(1)} %get-tuple-element.180), channel_id=1, source_target_pairs={{0,4},{4,0},{8,12},{12,8},{1,5},{5,1},{9,13},{13,9},{2,6},{6,2},{1... | collective-permute-start | bytes 1179656 | tf_op jit(solution)/shard_map/ppermute | solution.py:234
  824.9 17.3 %collective-permute-start.92 = (bf16[128,1536]{1,0:T(8,128)(2,1)S(1)}, bf16[128,1536]{1,0:T(8,128)(2,1)S(1)}, u32[]{:S(2)}, u32[]{:S(2)}) collective-permute-start(bf16[128,1536]{1,0:T(8,128)(2,1)S(1)} %pad_maximum_fusion.27), channel_id=1, source_target_pairs={{0,1},{1,0},{2,3},{3,2},{4,5},{5,4},{6,7},{7,6},{8,9},{9,8},{10,11... | collective-permute-start | bytes 1179656 | tf_op jit(solution)/shard_map/ppermute | solution.py:239
  (153 other events, 2473.1 us)

commit v10 on v9

--- a/solution.py
+++ b/solution.py
@@ -329,17 +329,17 @@
 
     size = w_qkv.shape[1] // 4
     qkv_parts = [two_blocks(w_qkv, 1, size, 2 * p + 1 - high, 2 * p + high) for p in (odd, 1 - odd)]
-    size = w_out.shape[0] // 4
-    out_parts = [two_blocks(w_out, 0, size, 2 * p + high, 2 * p + 1 - high) for p in (odd, 1 - odd)]
-    size = w_up.shape[1] // 2
-    up_parts = [lax.dynamic_slice_in_dim(w_up, p * size, size, 1) for p in (odd, 1 - odd)]
-    size = w_down.shape[0] // 2
-    down_parts = [lax.dynamic_slice_in_dim(w_down, p * size, size, 0) for p in (odd, 1 - odd)]
-
     def ordered_parts(value, parts):
         value, sent = ordered(value, parts[1])
         return value, (parts[0], sent)
 
+    def stale_heads(rows_part):
+        blocks = rows_part.reshape(rows_b, n_narrow, heads, pair)
+        blocks = jnp.stack([blocks[:, group] for group in head_group]).transpose(0, 2, 1, 3)
+        got = exchange(blocks, "narrow")
+        return got.transpose(1, 0, 2, 3).reshape(heads, total_rows, pair)
+
+    stale = stale_heads(stale_cache[0, 1])
     layer_in = lax.dynamic_index_in_dim(hidden_in, section, 0, False)
     layer_in = jnp.concatenate([layer_in, to_mate(layer_in)], axis=1)
     layer_in, timesteps = ordered(layer_in, timesteps)
@@ -350,7 +350,9 @@
     modulation = modulation.reshape(2, 4, 3, feat_a)
     modulation = jnp.concatenate([modulation, to_mate(modulation)], axis=-1)
     kept = passed(0, qkv_parts[0])
-    modulation, first_mean, sent, kept = ordered(modulation, first_mean, qkv_parts[1], kept)
+    modulation, first_mean, sent, kept, stale = ordered(
+        modulation, first_mean, qkv_parts[1], kept, stale
+    )
     got = mate_half(0, sent)
     qkv_now = jnp.concatenate(
         [jnp.where(lead, qkv_parts[0], kept), jnp.where(lead, got, passed(0, got))], axis=0
@@ -373,12 +375,6 @@
     places = lax.dynamic_index_in_dim(positions, section, 1, False)
     places = jnp.stack([relative(places[i]) for i in range(3)])
     cosine, sine = rotary_tables(places, head_dim)
-
-    def stale_heads(rows_part):
-        blocks = rows_part.reshape(rows_b, n_narrow, heads, pair)
-        blocks = jnp.stack([blocks[:, group] for group in head_group]).transpose(0, 2, 1, 3)
-        got = exchange(blocks, "narrow")
-        return got.transpose(1, 0, 2, 3).reshape(heads, total_rows, pair)
 
     def to_rows(fresh):
         blocks = [f.reshape(heads, n_wide, part, pair) for f in fresh]
@@ -411,13 +407,17 @@
                 moments = statistics(x_in[h])
             entry = normed(x_in[h], moments, table[0], kinds_h[h])
             if layer == 0 and h == 0:
-                entry, stale = ordered(entry, stale_cache[0, 1])
-                stale = stale_heads(stale)
-                entry, out_sent = ordered(entry, out_parts[1])
-                out_got = mate_half(0, out_sent)
+                entry, w_out, w_up = ordered(entry, w_out, w_up)
+                size = w_out.shape[0] // 4
+                out_parts = [
+                    two_blocks(w_out, 0, size, 2 * p + high, 2 * p + 1 - high) for p in (odd, 1 - odd)
+                ]
+                size = w_up.shape[1] // 2
+                up_parts = [lax.dynamic_slice_in_dim(w_up, p * size, size, 1) for p in (odd, 1 - odd)]
+                out_got = mate_half(0, out_parts[1])
             terms = jnp.dot(gather_wide(entry), qkv_now, preferred_element_type=F32).astype(BF)
             if layer == 0 and h == 1:
-                terms, stale, out_got, up_sent = ordered(terms, stale, out_got, up_parts[1])
+                terms, out_got, up_sent = ordered(terms, out_got, up_parts[1])
                 out_weight = pass_on(0, out_parts[0], out_got, 1)
                 up_got = mate_half(0, up_sent)
             width = terms.shape[1] // 2
@@ -431,6 +431,10 @@
         own = jnp.concatenate(fresh, axis=1)
         own, *out_weight = ordered(own, *out_weight)
         if layer == 0:
+            own, w_down = ordered(own, w_down)
+            size = w_down.shape[0] // 2
+            down_parts = [lax.dynamic_slice_in_dim(w_down, p * size, size, 0) for p in (odd, 1 - odd)]
+        if layer == 0:
             other = jnp.where(lead, stale, lax.ppermute(own, "section", [(0, 1)]))
         else:
             other = swap(jnp.where(lead, own, stale))
@@ -443,28 +447,34 @@
                 terms, up_got = ordered(terms, up_got)
                 up_weight = pass_on(0, up_parts[0], up_got, 0)
             if h == 1:
-                terms, down_sent, *fresh = ordered(terms, down_parts[1], *fresh)
+                terms, *fresh = ordered(terms, *fresh)
                 cache = to_rows(fresh)
-                down_weight = weight_of(layer, (down_parts[0], down_sent), 1)
             after.append(x_in[h] + pick(table[0], kinds_h[h], 2) * summed(terms))
-        inner = []
+        after[0], after[1], cache = ordered(after[0], after[1], cache)
+        caches.append(cache)
+        ups = []
         for h in range(halves):
             entry = normed(after[h], statistics(after[h]), table[1], kinds_h[h])
             if layer == 0 and h == 0:
                 entry, parts = ordered_parts(entry, qkv_parts)
                 qkv_weight = weight_of(1, parts, 0)
             entry = gather_wide(entry)
-            up = jnp.dot(entry, select(layer, up_weight), preferred_element_type=F32).astype(BF)
+            ups.append(
+                jnp.dot(entry, select(layer, up_weight), preferred_element_type=F32).astype(BF)
+            )
+        ups[0], ups[1], down_sent = ordered(ups[0], ups[1], down_parts[1])
+        down_got = mate_half(layer, down_sent)
+        inner = []
+        for h in range(halves):
             size = chunk // 2
-            got = to_partner(lax.dynamic_slice_in_dim(up, (1 - high) * size, size, 0))
-            up = lax.dynamic_slice_in_dim(up, high * size, size, 0).astype(F32) + got.astype(F32)
+            got = to_partner(lax.dynamic_slice_in_dim(ups[h], (1 - high) * size, size, 0))
+            up = lax.dynamic_slice_in_dim(ups[h], high * size, size, 0).astype(F32) + got.astype(F32)
             inner.append(jax.nn.gelu(up, approximate=True).astype(BF))
+        inner[0], inner[1], down_got = ordered(inner[0], inner[1], down_got)
+        down_weight = pass_on(layer, down_parts[0], down_got, 1)
         layer_in = []
         for h in range(halves):
             got = to_partner(inner[h])
-            if h == 1:
-                got, cache = ordered(got, cache)
-                caches.append(cache)
             first = jnp.where(lower, inner[h], got)
             second = jnp.where(lower, got, inner[h])
             whole = jnp.concatenate([first, second], axis=0)

time: 865 us -> 913 us (1.055)
  waiting for transfers between devices: 472 us -> 497 us
  other arithmetic: 66.3 us -> 87.4 us
    ppermute x24, waiting for transfers between devices: 18.5 us -> 44.8 us  [gather_wide(): lax.ppermute(block, 'wide', wide_pairs(step))]
    ppermute x10, waiting for transfers between devices: 27.6 us -> 37 us  [to_mate(): lax.ppermute(value, 'narrow', [(i, i ^ 1) for i in range(lax.axis_size('n...]
  transfers between devices with their start and end apart: 112 -> 112, of which waited for: 54 -> 55; matrix products, arithmetic and copies ran while one was open for 20% -> 20% of each run, Pallas kernels for 4% -> 4%
where the time goes in v10:
time: 913 us; the launch traced here: 903 us
  waiting for transfers between devices  497 us (54%)
  starting transfers between devices  156 us (17%)
  other arithmetic  87.4 us (10%)
  matrix products  67.2 us (7%)
  local copies, waits for them, and re-layouts  54.6 us (6%)
  Pallas kernels  37.2 us (4%)
    ppermute x23, waiting for transfers between devices, to_partner(): lax.ppermute(value, 'narrow', [(i, i ^ 2) for i in range(lax.axis_size('n...  322 us
    ppermute x24, waiting for transfers between devices, scatter_wide(): total += lax.ppermute(terms[step], 'wide', wide_pairs(step)).astype(F32)  58 us
    ppermute x24, waiting for transfers between devices, gather_wide(): lax.ppermute(block, 'wide', wide_pairs(step))  44.8 us
    ppermute x10, waiting for transfers between devices, to_mate(): lax.ppermute(value, 'narrow', [(i, i ^ 1) for i in range(lax.axis_size('n...  37 us
    ppermute x23, starting transfers between devices, to_partner(): lax.ppermute(value, 'narrow', [(i, i ^ 2) for i in range(lax.axis_size('n...  33.4 us
    ppermute x24, starting transfers between devices, gather_wide(): lax.ppermute(block, 'wide', wide_pairs(step))  32.2 us
    ppermute x24, starting transfers between devices, scatter_wide(): total += lax.ppermute(terms[step], 'wide', wide_pairs(step)).astype(F32)  29.3 us
    ppermute x8, waiting for transfers between devices, mate_half(): return lax.ppermute(sent, ('section', 'narrow'), pairs)  21.4 us
  transfers between devices with their start and end apart: 112, of which 55 were waited for; matrix products, arithmetic and copies ran while one was open for 20% of the time, Pallas kernels for 4%

profile of v10, /device:TPU:0, one launch (start us, length us, event | category | flops | bytes accessed | tf_op | source)
XLA Modules:
  0.0 903.4 jit_solution(15182505019801254073)
XLA Ops:
  4.9 5.8 dynamic-slice_bitcast_fusion.1
  42.2 5.0 fusion.104
  52.7 3.9 collective-permute-start.11
  57.0 3.5 broadcast_select_fusion.14
  61.6 15.8 %collective-permute-done.11 = bf16[768,1152]{1,0:T(8,128)(2,1)} collective-permute-done((bf16[768,1152]{1,0:T(8,128)(2,1)}, bf16[768,1152]{1,0:T(8,128)(2,1)}, u32[]{:S(2)}, u32[]{:S(2)}) %collective-permute-start.11) | collective-permute-done | bytes 1769504 | tf_op jit(solution)/shard_map/ppermute | solution.py:311
  87.7 3.9 collective-permute-start.17
  92.2 4.9 constant_dynamic-slice_fusion.10
  111.5 4.2 convolution_convert_fusion.3
  120.7 21.8 %collective-permute-done.18 = bf16[512,576]{0,1:T(8,128)(2,1)} collective-permute-done((bf16[512,576]{0,1:T(8,128)(2,1)S(1)}, bf16[512,576]{0,1:T(8,128)(2,1)}, u32[]{:S(2)}, u32[]{:S(2)}) %collective-permute-start.18) | collective-permute-done | bytes 589856 | tf_op jit(solution)/shard_map/ppermute | solution.py:243
  145.2 4.0 prepare.5
  152.7 4.0 prepare.4
  163.3 5.2 attend.5
  170.6 4.9 constant_dynamic-slice_fusion.9
  175.5 5.2 attend.4
  181.8 21.6 %collective-permute-done.27 = bf16[512,192]{1,0:T(8,128)(2,1)S(1)} collective-permute-done((bf16[512,192]{1,0:T(8,128)(2,1)S(1)}, bf16[512,192]{1,0:T(8,128)(2,1)S(1)}, u32[]{:S(2)}, u32[]{:S(2)}) %collective-permute-start.27) | collective-permute-done | bytes 196640 | tf_op jit(solution)/shard_map/ppermute | solution.py:243
  215.9 3.6 collective-permute-done.32
  229.7 3.6 collective-permute-start.39
  241.5 4.2 collective-permute-done.26
  266.0 3.4 collective-permute-done.37
  270.2 5.6 convolution_convert_fusion.13
  277.8 3.9 convolution_convert_fusion.12
  292.1 28.1 %collective-permute-done.44 = bf16[256,1536]{1,0:T(8,128)(2,1)} collective-permute-done((bf16[256,1536]{1,0:T(8,128)(2,1)}, bf16[256,1536]{1,0:T(8,128)(2,1)}, u32[]{:S(2)}, u32[]{:S(2)}) %collective-permute-start.44) | collective-permute-done | bytes 786464 | tf_op jit(solution)/shard_map/ppermute | solution.py:243
  323.0 13.9 %collective-permute-done.45 = bf16[256,1536]{1,0:T(8,128)(2,1)} collective-permute-done((bf16[256,1536]{1,0:T(8,128)(2,1)}, bf16[256,1536]{1,0:T(8,128)(2,1)}, u32[]{:S(2)}, u32[]{:S(2)}) %collective-permute-start.45) | collective-permute-done | bytes 786464 | tf_op jit(solution)/shard_map/ppermute | solution.py:243
  339.8 5.1 collective-permute-done.46
  344.9 4.2 pad_maximum_fusion.3
  349.1 3.5 collective-permute-start.48
  357.4 4.0 pad_maximum_fusion.5
  363.2 44.3 %collective-permute-done.53 = bf16[256,1536]{1,0:T(8,128)(2,1)} collective-permute-done((bf16[256,1536]{1,0:T(8,128)(2,1)}, bf16[256,1536]{1,0:T(8,128)(2,1)}, u32[]{:S(2)}, u32[]{:S(2)}) %collective-permute-start.53) | collective-permute-done | bytes 786464 | tf_op jit(solution)/shard_map/ppermute | solution.py:243
  409.0 6.8 collective-permute-done.47
  416.0 4.4 convolution_convert_fusion.10
  424.0 4.3 convolution_convert_fusion.11
  433.7 7.2 collective-permute-done.55
  445.3 4.1 collective-permute-done.50
  457.7 8.4 collective-permute-done.52
  484.7 10.7 %collective-permute-done.67 = bf16[128,1536]{1,0:T(8,128)(2,1)S(1)} collective-permute-done((bf16[128,1536]{1,0:T(8,128)(2,1)S(1)}, bf16[128,1536]{1,0:T(8,128)(2,1)S(1)}, u32[]{:S(2)}, u32[]{:S(2)}) %collective-permute-start.67) | collective-permute-done | bytes 393248 | tf_op jit(solution)/shard_map/ppermute | solution.py:227
  498.5 5.4 convolution_convert_fusion
  505.3 5.0 collective-permute-done.60
  510.4 5.8 convolution_convert_fusion.1
  518.5 28.3 %collective-permute-done.69 = bf16[512,576]{0,1:T(8,128)(2,1)} collective-permute-done((bf16[512,576]{0,1:T(8,128)(2,1)S(1)}, bf16[512,576]{0,1:T(8,128)(2,1)}, u32[]{:S(2)}, u32[]{:S(2)}) %collective-permute-start.69) | collective-permute-done | bytes 589856 | tf_op jit(solution)/shard_map/ppermute | solution.py:243
  549.6 4.2 prepare.7
  554.6 4.9 collective-permute-done.64
  562.2 4.0 prepare.6
  571.5 5.2 attend.7
  576.9 4.2 pad_maximum_fusion
  581.0 5.2 attend.6
  597.4 13.1 %collective-permute-done.73 = bf16[512,192]{1,0:T(8,128)(2,1)S(1)} collective-permute-done((bf16[512,192]{1,0:T(8,128)(2,1)S(1)}, bf16[512,192]{1,0:T(8,128)(2,1)S(1)}, u32[]{:S(2)}, u32[]{:S(2)}) %collective-permute-start.73) | collective-permute-done | bytes 196640 | tf_op jit(solution)/shard_map/ppermute | solution.py:243
  614.4 3.8 collective-permute-done.84
  622.1 9.1 %collective-permute-done.76 = bf16[128,1536]{1,0:T(8,128)(2,1)S(1)} collective-permute-done((bf16[128,1536]{1,0:T(8,128)(2,1)S(1)}, bf16[128,1536]{1,0:T(8,128)(2,1)S(1)}, u32[]{:S(2)}, u32[]{:S(2)}) %collective-permute-start.76) | collective-permute-done | bytes 393248 | tf_op jit(solution)/shard_map/ppermute | solution.py:234
  631.2 6.3 collective-permute-done.75
  639.6 8.5 collective-permute-done.77
  667.9 5.2 collective-permute-done.89
  674.7 6.9 collective-permute-done.88
  683.1 5.9 convolution_convert_fusion.7
  689.9 6.4 collective-permute-done.94
  696.4 5.9 convolution_convert_fusion.6
  706.2 34.9 %collective-permute-done.96 = bf16[256,1536]{1,0:T(8,128)(2,1)S(1)} collective-permute-done((bf16[256,1536]{1,0:T(8,128)(2,1)S(1)}, bf16[256,1536]{1,0:T(8,128)(2,1)S(1)}, u32[]{:S(2)}, u32[]{:S(2)}) %collective-permute-start.96) | collective-permute-done | bytes 786464 | tf_op jit(solution)/shard_map/ppermute | solution.py:243
  741.8 31.8 %collective-permute-done.97 = bf16[256,1536]{1,0:T(8,128)(2,1)S(1)} collective-permute-done((bf16[256,1536]{1,0:T(8,128)(2,1)S(1)}, bf16[256,1536]{1,0:T(8,128)(2,1)S(1)}, u32[]{:S(2)}, u32[]{:S(2)}) %collective-permute-start.97) | collective-permute-done | bytes 786464 | tf_op jit(solution)/shard_map/ppermute | solution.py:243
  779.2 51.6 %collective-permute-done.99 = bf16[256,1536]{1,0:T(8,128)(2,1)S(1)} collective-permute-done((bf16[256,1536]{1,0:T(8,128)(2,1)S(1)}, bf16[256,1536]{1,0:T(8,128)(2,1)S(1)}, u32[]{:S(2)}, u32[]{:S(2)}) %collective-permute-start.99) | collective-permute-done | bytes 786464 | tf_op jit(solution)/shard_map/ppermute | solution.py:243
  830.9 16.7 %collective-permute-done.105 = bf16[256,1536]{1,0:T(8,128)(2,1)S(1)} collective-permute-done((bf16[256,1536]{1,0:T(8,128)(2,1)S(1)}, bf16[256,1536]{1,0:T(8,128)(2,1)S(1)}, u32[]{:S(2)}, u32[]{:S(2)}) %collective-permute-start.105) | collective-permute-done | bytes 786464 | tf_op jit(solution)/shard_map/ppermute | solution.py:243
  860.0 3.6 collective-permute-done.103
  865.1 7.0 collective-permute-done.102
  872.5 8.0 collective-permute-done.108
  880.5 7.5 collective-permute-done.107
  889.3 10.2 %collective-permute-done.109 = bf16[128,1536]{1,0:T(8,128)(2,1)S(1)} collective-permute-done((bf16[128,1536]{1,0:T(8,128)(2,1)S(1)}, bf16[128,1536]{1,0:T(8,128)(2,1)S(1)}, u32[]{:S(2)}, u32[]{:S(2)}) %collective-permute-start.109) | collective-permute-done | bytes 393248 | tf_op jit(solution)/shard_map/ppermute | solution.py:239
  (621 shorter events, 297.7 us)
Async XLA Ops:
  1.8 35.3 %collective-permute-start = (bf16[256,768]{1,0:T(8,128)(2,1)S(1)}, bf16[256,768]{1,0:T(8,128)(2,1)}, u32[]{:S(2)}, u32[]{:S(2)}) collective-permute-start(bf16[256,768]{1,0:T(8,128)(2,1)S(1)} %dynamic-slice_bitcast_fusion.4), channel_id=1, source_target_pairs={{0,1},{1,0},{2,3},{3,2},{4,5},{5,4},{6,7},{7,6},{8,9},{9,8},{10,11... | collective-permute-start | bytes 1179656 | tf_op jit(solution)/shard_map/ppermute | solution.py:239
  14.8 37.9 %collective-permute-start.3 = (bf16[768,1152]{1,0:T(8,128)(2,1)}, bf16[768,1152]{1,0:T(8,128)(2,1)}, u32[]{:S(2)}, u32[]{:S(2)}) collective-permute-start(bf16[768,1152]{1,0:T(8,128)(2,1)} %pad_maximum_fusion.9), channel_id=1, source_target_pairs={{0,16},{1,17},{2,18},{3,19},{4,20},{5,21},{6,22},{7,23},{8,24},{9,... | collective-permute-start | bytes 5308424 | tf_op jit(solution)/shard_map/ppermute | solution.py:314
  18.8 15.5 %collective-permute-start.5 = (bf16[1,3,256,128]{3,2,0,1:T(8,128)(2,1)}, bf16[1,3,256,128]{3,2,0,1:T(8,128)(2,1)}, u32[]{:S(2)}, u32[]{:S(2)}) collective-permute-start(bf16[1,3,256,128]{3,2,0,1:T(8,128)(2,1)} %get-tuple-element.249), channel_id=1, source_target_pairs={{0,2},{1,3},{2,0},{3,1},{4,6},{5,7},{6,4},{7,5},{8,10},{9,11},{10,... | collective-permute-start | bytes 589832 | tf_op jit(solution)/shard_map/ppermute | solution.py:167
  52.7 24.7 %collective-permute-start.11 = (bf16[768,1152]{1,0:T(8,128)(2,1)}, bf16[768,1152]{1,0:T(8,128)(2,1)}, u32[]{:S(2)}, u32[]{:S(2)}) collective-permute-start(bf16[768,1152]{1,0:T(8,128)(2,1)} %pad_maximum_fusion.8), channel_id=1, source_target_pairs={{0,1},{1,0},{2,3},{3,2},{4,5},{5,4},{6,7},{7,6},{8,9},{9,8},{10,11... | collective-permute-start | bytes 5308424 | tf_op jit(solution)/shard_map/ppermute | solution.py:311
  77.4 19.6 %collective-permute-start.12 = (bf16[768,1152]{1,0:T(8,128)(2,1)}, bf16[768,1152]{1,0:T(8,128)(2,1)S(1)}, u32[]{:S(2)}, u32[]{:S(2)}) collective-permute-start(bf16[768,1152]{1,0:T(8,128)(2,1)} %collective-permute-done.11), channel_id=1, source_target_pairs={{0,16},{1,17},{2,18},{3,19},{4,20},{5,21},{6,22},{7,23},{8,24},{9,... | collective-permute-start | bytes 5308424 | tf_op jit(solution)/shard_map/ppermute | solution.py:314
  80.1 21.2 %collective-permute-start.16 = (bf16[128,1536]{1,0:T(8,128)(2,1)S(1)}, bf16[128,1536]{1,0:T(8,128)(2,1)S(1)}, u32[]{:S(2)}, u32[]{:S(2)}) collective-permute-start(bf16[128,1536]{1,0:T(8,128)(2,1)S(1)} %fusion.114), channel_id=1, source_target_pairs={{0,12},{4,8},{8,4},{12,0},{1,13},{5,9},{9,5},{13,1},{2,14},{6,10},... | collective-permute-start | bytes 1179656 | tf_op jit(solution)/shard_map/ppermute | solution.py:227
  82.6 19.2 %collective-permute-start.15 = (bf16[128,1536]{1,0:T(8,128)(2,1)S(1)}, bf16[128,1536]{1,0:T(8,128)(2,1)S(1)}, u32[]{:S(2)}, u32[]{:S(2)}) collective-permute-start(bf16[128,1536]{1,0:T(8,128)(2,1)S(1)} %fusion.114), channel_id=1, source_target_pairs={{0,8},{4,12},{8,0},{12,4},{1,9},{5,13},{9,1},{13,5},{2,10},{6,14},... | collective-permute-start | bytes 1179656 | tf_op jit(solution)/shard_map/ppermute | solution.py:227
  83.1 19.8 %collective-permute-start.14 = (bf16[128,1536]{1,0:T(8,128)(2,1)S(1)}, bf16[128,1536]{1,0:T(8,128)(2,1)S(1)}, u32[]{:S(2)}, u32[]{:S(2)}) collective-permute-start(bf16[128,1536]{1,0:T(8,128)(2,1)S(1)} %fusion.114), channel_id=1, source_target_pairs={{0,4},{4,0},{8,12},{12,8},{1,5},{5,1},{9,13},{13,9},{2,6},{6,2},{1... | collective-permute-start | bytes 1179656 | tf_op jit(solution)/shard_map/ppermute | solution.py:227
  87.7 17.9 %collective-permute-start.17 = (bf16[384,768]{1,0:T(8,128)(2,1)}, bf16[384,768]{1,0:T(8,128)(2,1)S(1)}, u32[]{:S(2)}, u32[]{:S(2)}) collective-permute-start(bf16[384,768]{1,0:T(8,128)(2,1)} %pad_maximum_fusion.19), channel_id=1, source_target_pairs={{0,1},{1,0},{2,3},{3,2},{4,5},{5,4},{6,7},{7,6},{8,9},{9,8},{10,11... | collective-permute-start | bytes 1769480 | tf_op jit(solution)/shard_map/ppermute | solution.py:311
  106.7 35.8 %collective-permute-start.18 = (bf16[512,576]{0,1:T(8,128)(2,1)S(1)}, bf16[512,576]{0,1:T(8,128)(2,1)}, u32[]{:S(2)}, u32[]{:S(2)}) collective-permute-start(bf16[512,576]{0,1:T(8,128)(2,1)S(1)} %copy.37), channel_id=1, source_target_pairs={{0,2},{1,3},{2,0},{3,1},{4,6},{5,7},{6,4},{7,5},{8,10},{9,11},{10,... | collective-permute-start | bytes 1769480 | tf_op jit(solution)/shard_map/ppermute | solution.py:243
  109.1 47.8 %collective-permute-start.19 = (bf16[384,1536]{1,0:T(8,128)(2,1)}, bf16[384,1536]{1,0:T(8,128)(2,1)}, u32[]{:S(2)}, u32[]{:S(2)}) collective-permute-start(bf16[384,1536]{1,0:T(8,128)(2,1)} %pad_maximum_fusion.10), channel_id=1, source_target_pairs={{0,16},{1,17},{2,18},{3,19},{4,20},{5,21},{6,22},{7,23},{8,24},{9,... | collective-permute-start | bytes 3538952 | tf_op jit(solution)/shard_map/ppermute | solution.py:314
  117.8 32.2 %collective-permute-start.13 = (bf16[512,576]{0,1:T(8,128)(2,1)}, bf16[512,576]{0,1:T(8,128)(2,1)}, u32[]{:S(2)}, u32[]{:S(2)}) collective-permute-start(bf16[512,576]{0,1:T(8,128)(2,1)} %copy.34), channel_id=1, source_target_pairs={{0,2},{1,3},{2,0},{3,1},{4,6},{5,7},{6,4},{7,5},{8,10},{9,11},{10,... | collective-permute-start | bytes 1769480 | tf_op jit(solution)/shard_map/ppermute | solution.py:243
  160.1 54.5 %collective-permute-start.22 = (bf16[768,1536]{1,0:T(8,128)(2,1)}, bf16[768,1536]{1,0:T(8,128)(2,1)S(1)}, u32[]{:S(2)}, u32[]{:S(2)}) collective-permute-start(bf16[768,1536]{1,0:T(8,128)(2,1)} %get-tuple-element.114), channel_id=1, source_target_pairs={{0,1},{1,0},{2,3},{3,2},{4,5},{5,4},{6,7},{7,6},{8,9},{9,8},{10,11... | collective-permute-start | bytes 7077896 | tf_op jit(solution)/shard_map/ppermute | solution.py:311
  168.6 34.8 %collective-permute-start.27 = (bf16[512,192]{1,0:T(8,128)(2,1)S(1)}, bf16[512,192]{1,0:T(8,128)(2,1)S(1)}, u32[]{:S(2)}, u32[]{:S(2)}) collective-permute-start(bf16[512,192]{1,0:T(8,128)(2,1)S(1)} %attend.5), channel_id=1, source_target_pairs={{0,2},{1,3},{2,0},{3,1},{4,6},{5,7},{6,4},{7,5},{8,10},{9,11},{10,... | collective-permute-start | bytes 589832 | tf_op jit(solution)/shard_map/ppermute | solution.py:243
  180.7 29.2 %collective-permute-start.21 = (bf16[512,192]{1,0:T(8,128)(2,1)S(1)}, bf16[512,192]{1,0:T(8,128)(2,1)S(1)}, u32[]{:S(2)}, u32[]{:S(2)}) collective-permute-start(bf16[512,192]{1,0:T(8,128)(2,1)S(1)} %attend.4), channel_id=1, source_target_pairs={{0,2},{1,3},{2,0},{3,1},{4,6},{5,7},{6,4},{7,5},{8,10},{9,11},{10,... | collective-permute-start | bytes 589832 | tf_op jit(solution)/shard_map/ppermute | solution.py:243
  205.8 21.3 %collective-permute-start.30 = (bf16[128,1536]{1,0:T(8,128)(2,1)S(1)}, bf16[128,1536]{1,0:T(8,128)(2,1)S(1)}, u32[]{:S(2)}, u32[]{:S(2)}) collective-permute-start(bf16[128,1536]{1,0:T(8,128)(2,1)S(1)} %get-tuple-element.217), channel_id=1, source_target_pairs={{0,12},{4,8},{8,4},{12,0},{1,13},{5,9},{9,5},{13,1},{2,14},{6,10},... | collective-permute-start | bytes 1179656 | tf_op jit(solution)/shard_map/ppermute | solution.py:234
  208.7 19.3 %collective-permute-start.29 = (bf16[128,1536]{1,0:T(8,128)(2,1)S(1)}, bf16[128,1536]{1,0:T(8,128)(2,1)S(1)}, u32[]{:S(2)}, u32[]{:S(2)}) collective-permute-start(bf16[128,1536]{1,0:T(8,128)(2,1)S(1)} %get-tuple-element.218), channel_id=1, source_target_pairs={{0,8},{4,12},{8,0},{12,4},{1,9},{5,13},{9,1},{13,5},{2,10},{6,14},... | collective-permute-start | bytes 1179656 | tf_op jit(solution)/shard_map/ppermute | solution.py:234
  208.8 21.0 %collective-permute-start.28 = (bf16[128,1536]{1,0:T(8,128)(2,1)S(1)}, bf16[128,1536]{1,0:T(8,128)(2,1)S(1)}, u32[]{:S(2)}, u32[]{:S(2)}) collective-permute-start(bf16[128,1536]{1,0:T(8,128)(2,1)S(1)} %get-tuple-element.216), channel_id=1, source_target_pairs={{0,4},{4,0},{8,12},{12,8},{1,5},{5,1},{9,13},{13,9},{2,6},{6,2},{1... | collective-permute-start | bytes 1179656 | tf_op jit(solution)/shard_map/ppermute | solution.py:234
  219.5 19.1 %collective-permute-start.34 = (bf16[1,3,256,128]{3,2,0,1:T(8,128)(2,1)S(1)}, bf16[1,3,256,128]{3,2,0,1:T(8,128)(2,1)S(1)}, u32[]{:S(2)}, u32[]{:S(2)}) collective-permute-start(bf16[1,3,256,128]{3,2,0,1:T(8,128)(2,1)S(1)} %get-tuple-element.244), channel_id=1, source_target_pairs={{0,3},{1,0},{2,1},{3,2},{4,7},{5,4},{6,5},{7,6},{8,11},{9,8},{10,9... | collective-permute-start | bytes 589832 | tf_op jit(solution)/shard_map/ppermute | solution.py:167
  229.7 40.5 %collective-permute-start.39 = (bf16[1536,1536]{1,0:T(8,128)(2,1)}, bf16[1536,1536]{1,0:T(8,128)(2,1)}, u32[]{:S(2)}, u32[]{:S(2)}) collective-permute-start(bf16[1536,1536]{1,0:T(8,128)(2,1)} %pad_maximum_fusion.1), channel_id=1, source_target_pairs={{0,16},{1,17},{2,18},{3,19},{4,20},{5,21},{6,22},{7,23},{8,24},{9,... | collective-permute-start | bytes 14155784 | tf_op jit(solution)/shard_map/ppermute | solution.py:314
  281.7 63.1 %collective-permute-start.46 = (bf16[1536,768]{1,0:T(8,128)(2,1)}, bf16[1536,768]{1,0:T(8,128)(2,1)}, u32[]{:S(2)}, u32[]{:S(2)}) collective-permute-start(bf16[1536,768]{1,0:T(8,128)(2,1)} %get-tuple-element.118), channel_id=1, source_target_pairs={{0,1},{1,0},{2,3},{3,2},{4,5},{5,4},{6,7},{7,6},{8,9},{9,8},{10,11... | collective-permute-start | bytes 7077896 | tf_op jit(solution)/shard_map/ppermute | solution.py:311
  287.1 33.0 %collective-permute-start.44 = (bf16[256,1536]{1,0:T(8,128)(2,1)}, bf16[256,1536]{1,0:T(8,128)(2,1)}, u32[]{:S(2)}, u32[]{:S(2)}) collective-permute-start(bf16[256,1536]{1,0:T(8,128)(2,1)} %constant_dynamic-slice_fusion.8), channel_id=1, source_target_pairs={{0,2},{1,3},{2,0},{3,1},{4,6},{5,7},{6,4},{7,5},{8,10},{9,11},{10,... | collective-permute-start | bytes 2359304 | tf_op jit(solution)/shard_map/ppermute | solution.py:243
  289.4 47.5 %collective-permute-start.45 = (bf16[256,1536]{1,0:T(8,128)(2,1)}, bf16[256,1536]{1,0:T(8,128)(2,1)}, u32[]{:S(2)}, u32[]{:S(2)}) collective-permute-start(bf16[256,1536]{1,0:T(8,128)(2,1)} %constant_dynamic-slice_fusion.7), channel_id=1, source_target_pairs={{0,2},{1,3},{2,0},{3,1},{4,6},{5,7},{6,4},{7,5},{8,10},{9,11},{10,... | collective-permute-start | bytes 2359304 | tf_op jit(solution)/shard_map/ppermute | solution.py:243
  349.1 66.9 %collective-permute-start.48 = (bf16[1536,1536]{1,0:T(8,128)(2,1)}, bf16[1536,1536]{1,0:T(8,128)(2,1)}, u32[]{:S(2)}, u32[]{:S(2)}) collective-permute-start(bf16[1536,1536]{1,0:T(8,128)(2,1)} %pad_maximum_fusion.3), channel_id=1, source_target_pairs={{0,16},{1,17},{2,18},{3,19},{4,20},{5,21},{6,22},{7,23},{8,24},{9,... | collective-permute-start | bytes 14155784 | tf_op jit(solution)/shard_map/ppermute | solution.py:314
  354.4 53.1 %collective-permute-start.53 = (bf16[256,1536]{1,0:T(8,128)(2,1)}, bf16[256,1536]{1,0:T(8,128)(2,1)}, u32[]{:S(2)}, u32[]{:S(2)}) collective-permute-start(bf16[256,1536]{1,0:T(8,128)(2,1)} %fusion.19), channel_id=1, source_target_pairs={{0,2},{1,3},{2,0},{3,1},{4,6},{5,7},{6,4},{7,5},{8,10},{9,11},{10,... | collective-permute-start | bytes 2359304 | tf_op jit(solution)/shard_map/ppermute | solution.py:243
  355.1 60.8 %collective-permute-start.47 = (bf16[256,1536]{1,0:T(8,128)(2,1)}, bf16[256,1536]{1,0:T(8,128)(2,1)S(1)}, u32[]{:S(2)}, u32[]{:S(2)}) collective-permute-start(bf16[256,1536]{1,0:T(8,128)(2,1)} %fusion.11), channel_id=1, source_target_pairs={{0,2},{1,3},{2,0},{3,1},{4,6},{5,7},{6,4},{7,5},{8,10},{9,11},{10,... | collective-permute-start | bytes 2359304 | tf_op jit(solution)/shard_map/ppermute | solution.py:243
  361.4 117.8 %collective-permute-start.63 = (bf16[1536,1152]{1,0:T(8,128)(2,1)}, bf16[1536,1152]{1,0:T(8,128)(2,1)}, u32[]{:S(2)}, u32[]{:S(2)}) collective-permute-start(bf16[1536,1152]{1,0:T(8,128)(2,1)} %pad_maximum_fusion.5), channel_id=1, source_target_pairs={{16,0},{17,1},{18,2},{19,3},{20,4},{21,5},{22,6},{23,7},{24,8},{25... | collective-permute-start | bytes 10616840 | tf_op jit(solution)/shard_map/ppermute | solution.py:314
  422.6 18.3 %collective-permute-start.55 = (bf16[128,1536]{1,0:T(8,128)(2,1)S(1)}, bf16[128,1536]{1,0:T(8,128)(2,1)S(1)}, u32[]{:S(2)}, u32[]{:S(2)}) collective-permute-start(bf16[128,1536]{1,0:T(8,128)(2,1)S(1)} %get-tuple-element.208), channel_id=1, source_target_pairs={{0,8},{4,12},{8,0},{12,4},{1,9},{5,13},{9,1},{13,5},{2,10},{6,14},... | collective-permute-start | bytes 1179656 | tf_op jit(solution)/shard_map/ppermute | solution.py:234
  423.8 18.2 %collective-permute-start.54 = (bf16[128,1536]{1,0:T(8,128)(2,1)S(1)}, bf16[128,1536]{1,0:T(8,128)(2,1)S(1)}, u32[]{:S(2)}, u32[]{:S(2)}) collective-permute-start(bf16[128,1536]{1,0:T(8,128)(2,1)S(1)} %get-tuple-element.206), channel_id=1, source_target_pairs={{0,4},{4,0},{8,12},{12,8},{1,5},{5,1},{9,13},{13,9},{2,6},{6,2},{1... | collective-permute-start | bytes 1179656 | tf_op jit(solution)/shard_map/ppermute | solution.py:234
  428.5 16.8 %collective-permute-start.51 = (bf16[128,1536]{1,0:T(8,128)(2,1)S(1)}, bf16[128,1536]{1,0:T(8,128)(2,1)S(1)}, u32[]{:S(2)}, u32[]{:S(2)}) collective-permute-start(bf16[128,1536]{1,0:T(8,128)(2,1)S(1)} %get-tuple-element.212), channel_id=1, source_target_pairs={{0,12},{4,8},{8,4},{12,0},{1,13},{5,9},{9,5},{13,1},{2,14},{6,10},... | collective-permute-start | bytes 1179656 | tf_op jit(solution)/shard_map/ppermute | solution.py:234
  433.4 15.9 %collective-permute-start.50 = (bf16[128,1536]{1,0:T(8,128)(2,1)S(1)}, bf16[128,1536]{1,0:T(8,128)(2,1)S(1)}, u32[]{:S(2)}, u32[]{:S(2)}) collective-permute-start(bf16[128,1536]{1,0:T(8,128)(2,1)S(1)} %get-tuple-element.213), channel_id=1, source_target_pairs={{0,8},{4,12},{8,0},{12,4},{1,9},{5,13},{9,1},{13,5},{2,10},{6,14},... | collective-permute-start | bytes 1179656 | tf_op jit(solution)/shard_map/ppermute | solution.py:234
  451.9 124.9 %collective-permute-start.90 = (bf16[768,1536]{1,0:T(8,128)(2,1)}, bf16[768,1536]{1,0:T(8,128)(2,1)}, u32[]{:S(2)}, u32[]{:S(2)}) collective-permute-start(bf16[768,1536]{1,0:T(8,128)(2,1)} %get-tuple-element.114), channel_id=1, source_target_pairs={{16,17},{17,16},{18,19},{19,18},{20,21},{21,20},{22,23},{23,22},{2... | collective-permute-start | bytes 7077896 | tf_op jit(solution)/shard_map/ppermute | solution.py:311
  475.9 19.4 %collective-permute-start.67 = (bf16[128,1536]{1,0:T(8,128)(2,1)S(1)}, bf16[128,1536]{1,0:T(8,128)(2,1)S(1)}, u32[]{:S(2)}, u32[]{:S(2)}) collective-permute-start(bf16[128,1536]{1,0:T(8,128)(2,1)S(1)} %fusion.126), channel_id=1, source_target_pairs={{0,8},{4,12},{8,0},{12,4},{1,9},{5,13},{9,1},{13,5},{2,10},{6,14},... | collective-permute-start | bytes 1179656 | tf_op jit(solution)/shard_map/ppermute | solution.py:227
  477.1 19.5 %collective-permute-start.66 = (bf16[128,1536]{1,0:T(8,128)(2,1)S(1)}, bf16[128,1536]{1,0:T(8,128)(2,1)S(1)}, u32[]{:S(2)}, u32[]{:S(2)}) collective-permute-start(bf16[128,1536]{1,0:T(8,128)(2,1)S(1)} %fusion.126), channel_id=1, source_target_pairs={{0,4},{4,0},{8,12},{12,8},{1,5},{5,1},{9,13},{13,9},{2,6},{6,2},{1... | collective-permute-start | bytes 1179656 | tf_op jit(solution)/shard_map/ppermute | solution.py:227
  479.2 87.2 %collective-permute-start.71 = (bf16[384,1536]{1,0:T(8,128)(2,1)}, bf16[384,1536]{1,0:T(8,128)(2,1)}, u32[]{:S(2)}, u32[]{:S(2)}) collective-permute-start(bf16[384,1536]{1,0:T(8,128)(2,1)} %pad_maximum_fusion.12), channel_id=1, source_target_pairs={{16,0},{17,1},{18,2},{19,3},{20,4},{21,5},{22,6},{23,7},{24,8},{25... | collective-permute-start | bytes 3538952 | tf_op jit(solution)/shard_map/ppermute | solution.py:314
  482.7 22.6 %collective-permute-start.61 = (bf16[128,1536]{1,0:T(8,128)(2,1)}, bf16[128,1536]{1,0:T(8,128)(2,1)}, u32[]{:S(2)}, u32[]{:S(2)}) collective-permute-start(bf16[128,1536]{1,0:T(8,128)(2,1)} %fusion.120), channel_id=1, source_target_pairs={{0,12},{4,8},{8,4},{12,0},{1,13},{5,9},{9,5},{13,1},{2,14},{6,10},... | collective-permute-start | bytes 1179656 | tf_op jit(solution)/shard_map/ppermute | solution.py:227
  495.3 15.0 %collective-permute-start.60 = (bf16[128,1536]{1,0:T(8,128)(2,1)}, bf16[128,1536]{1,0:T(8,128)(2,1)}, u32[]{:S(2)}, u32[]{:S(2)}) collective-permute-start(bf16[128,1536]{1,0:T(8,128)(2,1)} %fusion.120), channel_id=1, source_target_pairs={{0,8},{4,12},{8,0},{12,4},{1,9},{5,13},{9,1},{13,5},{2,10},{6,14},... | collective-permute-start | bytes 1179656 | tf_op jit(solution)/shard_map/ppermute | solution.py:227
  505.2 41.6 %collective-permute-start.69 = (bf16[512,576]{0,1:T(8,128)(2,1)S(1)}, bf16[512,576]{0,1:T(8,128)(2,1)}, u32[]{:S(2)}, u32[]{:S(2)}) collective-permute-start(bf16[512,576]{0,1:T(8,128)(2,1)S(1)} %copy.44), channel_id=1, source_target_pairs={{0,2},{1,3},{2,0},{3,1},{4,6},{5,7},{6,4},{7,5},{8,10},{9,11},{10,... | collective-permute-start | bytes 1769480 | tf_op jit(solution)/shard_map/ppermute | solution.py:243
  518.3 41.2 %collective-permute-start.64 = (bf16[512,576]{0,1:T(8,128)(2,1)}, bf16[512,576]{0,1:T(8,128)(2,1)}, u32[]{:S(2)}, u32[]{:S(2)}) collective-permute-start(bf16[512,576]{0,1:T(8,128)(2,1)} %copy.41), channel_id=1, source_target_pairs={{0,2},{1,3},{2,0},{3,1},{4,6},{5,7},{6,4},{7,5},{8,10},{9,11},{10,... | collective-permute-start | bytes 1769480 | tf_op jit(solution)/shard_map/ppermute | solution.py:243
  586.3 24.2 %collective-permute-start.73 = (bf16[512,192]{1,0:T(8,128)(2,1)S(1)}, bf16[512,192]{1,0:T(8,128)(2,1)S(1)}, u32[]{:S(2)}, u32[]{:S(2)}) collective-permute-start(bf16[512,192]{1,0:T(8,128)(2,1)S(1)} %attend.6), channel_id=1, source_target_pairs={{0,2},{1,3},{2,0},{3,1},{4,6},{5,7},{6,4},{7,5},{8,10},{9,11},{10,... | collective-permute-start | bytes 589832 | tf_op jit(solution)/shard_map/ppermute | solution.py:243
  593.3 25.0 %collective-permute-start.81 = (bf16[128,1536]{1,0:T(8,128)(2,1)S(1)}, bf16[128,1536]{1,0:T(8,128)(2,1)S(1)}, u32[]{:S(2)}, u32[]{:S(2)}) collective-permute-start(bf16[128,1536]{1,0:T(8,128)(2,1)S(1)} %get-tuple-element.201), channel_id=1, source_target_pairs={{0,12},{4,8},{8,4},{12,0},{1,13},{5,9},{9,5},{13,1},{2,14},{6,10},... | collective-permute-start | bytes 1179656 | tf_op jit(solution)/shard_map/ppermute | solution.py:234
  593.7 26.1 %collective-permute-start.80 = (bf16[128,1536]{1,0:T(8,128)(2,1)S(1)}, bf16[128,1536]{1,0:T(8,128)(2,1)S(1)}, u32[]{:S(2)}, u32[]{:S(2)}) collective-permute-start(bf16[128,1536]{1,0:T(8,128)(2,1)S(1)} %get-tuple-element.202), channel_id=1, source_target_pairs={{0,8},{4,12},{8,0},{12,4},{1,9},{5,13},{9,1},{13,5},{2,10},{6,14},... | collective-permute-start | bytes 1179656 | tf_op jit(solution)/shard_map/ppermute | solution.py:234
  594.9 26.9 %collective-permute-start.79 = (bf16[128,1536]{1,0:T(8,128)(2,1)S(1)}, bf16[128,1536]{1,0:T(8,128)(2,1)S(1)}, u32[]{:S(2)}, u32[]{:S(2)}) collective-permute-start(bf16[128,1536]{1,0:T(8,128)(2,1)S(1)} %get-tuple-element.200), channel_id=1, source_target_pairs={{0,4},{4,0},{8,12},{12,8},{1,5},{5,1},{9,13},{13,9},{2,6},{6,2},{1... | collective-permute-start | bytes 1179656 | tf_op jit(solution)/shard_map/ppermute | solution.py:234
  597.4 15.5 %collective-permute-start.83 = (bf16[1,3,256,128]{3,2,0,1:T(8,128)(2,1)S(1)}, bf16[1,3,256,128]{3,2,0,1:T(8,128)(2,1)S(1)}, u32[]{:S(2)}, u32[]{:S(2)}) collective-permute-start(bf16[1,3,256,128]{3,2,0,1:T(8,128)(2,1)S(1)} %get-tuple-element.238), channel_id=1, source_target_pairs={{0,1},{1,2},{2,3},{3,0},{4,5},{5,6},{6,7},{7,4},{8,9},{9,10},{10,1... | collective-permute-start | bytes 589832 | tf_op jit(solution)/shard_map/ppermute | solution.py:167
  612.9 70.2 %collective-permute-start.91 = (bf16[1536,1536]{1,0:T(8,128)(2,1)}, bf16[1536,1536]{1,0:T(8,128)(2,1)}, u32[]{:S(2)}, u32[]{:S(2)}) collective-permute-start(bf16[1536,1536]{1,0:T(8,128)(2,1)} %pad_maximum_fusion), channel_id=1, source_target_pairs={{16,0},{17,1},{18,2},{19,3},{20,4},{21,5},{22,6},{23,7},{24,8},{25... | collective-permute-start | bytes 14155784 | tf_op jit(solution)/shard_map/ppermute | solution.py:314
  618.3 19.2 %collective-permute-start.75 = (bf16[128,1536]{1,0:T(8,128)(2,1)S(1)}, bf16[128,1536]{1,0:T(8,128)(2,1)S(1)}, u32[]{:S(2)}, u32[]{:S(2)}) collective-permute-start(bf16[128,1536]{1,0:T(8,128)(2,1)S(1)} %get-tuple-element.205), channel_id=1, source_target_pairs={{0,8},{4,12},{8,0},{12,4},{1,9},{5,13},{9,1},{13,5},{2,10},{6,14},... | collective-permute-start | bytes 1179656 | tf_op jit(solution)/shard_map/ppermute | solution.py:234
  619.8 17.7 %collective-permute-start.74 = (bf16[128,1536]{1,0:T(8,128)(2,1)S(1)}, bf16[128,1536]{1,0:T(8,128)(2,1)S(1)}, u32[]{:S(2)}, u32[]{:S(2)}) collective-permute-start(bf16[128,1536]{1,0:T(8,128)(2,1)S(1)} %get-tuple-element.203), channel_id=1, source_target_pairs={{0,4},{4,0},{8,12},{12,8},{1,5},{5,1},{9,13},{13,9},{2,6},{6,2},{1... | collective-permute-start | bytes 1179656 | tf_op jit(solution)/shard_map/ppermute | solution.py:234
  621.8 16.0 %collective-permute-start.85 = (bf16[1,3,256,128]{3,2,0,1:T(8,128)(2,1)S(1)}, bf16[1,3,256,128]{3,2,0,1:T(8,128)(2,1)S(1)}, u32[]{:S(2)}, u32[]{:S(2)}) collective-permute-start(bf16[1,3,256,128]{3,2,0,1:T(8,128)(2,1)S(1)} %get-tuple-element.236), channel_id=1, source_target_pairs={{0,3},{1,0},{2,1},{3,2},{4,7},{5,4},{6,5},{7,6},{8,11},{9,8},{10,9... | collective-permute-start | bytes 589832 | tf_op jit(solution)/shard_map/ppermute | solution.py:167
  661.9 19.6 %collective-permute-start.88 = (bf16[128,1536]{1,0:T(8,128)(2,1)S(1)}, bf16[128,1536]{1,0:T(8,128)(2,1)S(1)}, u32[]{:S(2)}, u32[]{:S(2)}) collective-permute-start(bf16[128,1536]{1,0:T(8,128)(2,1)S(1)} %add_convert_fusion.3), channel_id=1, source_target_pairs={{0,8},{4,12},{8,0},{12,4},{1,9},{5,13},{9,1},{13,5},{2,10},{6,14},... | collective-permute-start | bytes 1179656 | tf_op jit(solution)/shard_map/ppermute | solution.py:227
  663.1 20.0 %collective-permute-start.87 = (bf16[128,1536]{1,0:T(8,128)(2,1)S(1)}, bf16[128,1536]{1,0:T(8,128)(2,1)S(1)}, u32[]{:S(2)}, u32[]{:S(2)}) collective-permute-start(bf16[128,1536]{1,0:T(8,128)(2,1)S(1)} %add_convert_fusion.3), channel_id=1, source_target_pairs={{0,4},{4,0},{8,12},{12,8},{1,5},{5,1},{9,13},{13,9},{2,6},{6,2},{1... | collective-permute-start | bytes 1179656 | tf_op jit(solution)/shard_map/ppermute | solution.py:227
  666.0 23.9 %collective-permute-start.95 = (bf16[128,1536]{1,0:T(8,128)(2,1)S(1)}, bf16[128,1536]{1,0:T(8,128)(2,1)S(1)}, u32[]{:S(2)}, u32[]{:S(2)}) collective-permute-start(bf16[128,1536]{1,0:T(8,128)(2,1)S(1)} %add_convert_fusion.2), channel_id=1, source_target_pairs={{0,12},{4,8},{8,4},{12,0},{1,13},{5,9},{9,5},{13,1},{2,14},{6,10},... | collective-permute-start | bytes 1179656 | tf_op jit(solution)/shard_map/ppermute | solution.py:227
  673.0 23.3 %collective-permute-start.94 = (bf16[128,1536]{1,0:T(8,128)(2,1)S(1)}, bf16[128,1536]{1,0:T(8,128)(2,1)S(1)}, u32[]{:S(2)}, u32[]{:S(2)}) collective-permute-start(bf16[128,1536]{1,0:T(8,128)(2,1)S(1)} %add_convert_fusion.2), channel_id=1, source_target_pairs={{0,8},{4,12},{8,0},{12,4},{1,9},{5,13},{9,1},{13,5},{2,10},{6,14},... | collective-permute-start | bytes 1179656 | tf_op jit(solution)/shard_map/ppermute | solution.py:227
  702.2 72.0 %collective-permute-start.98 = (bf16[1536,768]{1,0:T(8,128)(2,1)}, bf16[1536,768]{1,0:T(8,128)(2,1)S(1)}, u32[]{:S(2)}, u32[]{:S(2)}) collective-permute-start(bf16[1536,768]{1,0:T(8,128)(2,1)} %get-tuple-element.118), channel_id=1, source_target_pairs={{16,17},{17,16},{18,19},{19,18},{20,21},{21,20},{22,23},{23,22},{2... | collective-permute-start | bytes 7077896 | tf_op jit(solution)/shard_map/ppermute | solution.py:311
  703.1 38.0 %collective-permute-start.96 = (bf16[256,1536]{1,0:T(8,128)(2,1)S(1)}, bf16[256,1536]{1,0:T(8,128)(2,1)S(1)}, u32[]{:S(2)}, u32[]{:S(2)}) collective-permute-start(bf16[256,1536]{1,0:T(8,128)(2,1)S(1)} %constant_dynamic-slice_fusion.2), channel_id=1, source_target_pairs={{0,2},{1,3},{2,0},{3,1},{4,6},{5,7},{6,4},{7,5},{8,10},{9,11},{10,... | collective-permute-start | bytes 2359304 | tf_op jit(solution)/shard_map/ppermute | solution.py:243
  705.5 68.1 %collective-permute-start.97 = (bf16[256,1536]{1,0:T(8,128)(2,1)S(1)}, bf16[256,1536]{1,0:T(8,128)(2,1)S(1)}, u32[]{:S(2)}, u32[]{:S(2)}) collective-permute-start(bf16[256,1536]{1,0:T(8,128)(2,1)S(1)} %constant_dynamic-slice_fusion.1), channel_id=1, source_target_pairs={{0,2},{1,3},{2,0},{3,1},{4,6},{5,7},{6,4},{7,5},{8,10},{9,11},{10,... | collective-permute-start | bytes 2359304 | tf_op jit(solution)/shard_map/ppermute | solution.py:243
  774.6 73.1 %collective-permute-start.100 = (bf16[1536,1536]{1,0:T(8,128)(2,1)S(1)}, bf16[1536,1536]{1,0:T(8,128)(2,1)S(1)}, u32[]{:S(2)}, u32[]{:S(2)}) collective-permute-start(bf16[1536,1536]{1,0:T(8,128)(2,1)S(1)} %pad_maximum_fusion.2), channel_id=1, source_target_pairs={{16,0},{17,1},{18,2},{19,3},{20,4},{21,5},{22,6},{23,7},{24,8},{25... | collective-permute-start | bytes 14155784 | tf_op jit(solution)/shard_map/ppermute | solution.py:314
  776.2 54.6 %collective-permute-start.99 = (bf16[256,1536]{1,0:T(8,128)(2,1)S(1)}, bf16[256,1536]{1,0:T(8,128)(2,1)S(1)}, u32[]{:S(2)}, u32[]{:S(2)}) collective-permute-start(bf16[256,1536]{1,0:T(8,128)(2,1)S(1)} %fusion.27), channel_id=1, source_target_pairs={{0,2},{1,3},{2,0},{3,1},{4,6},{5,7},{6,4},{7,5},{8,10},{9,11},{10,... | collective-permute-start | bytes 2359304 | tf_op jit(solution)/shard_map/ppermute | solution.py:243
  776.3 71.4 %collective-permute-start.105 = (bf16[256,1536]{1,0:T(8,128)(2,1)S(1)}, bf16[256,1536]{1,0:T(8,128)(2,1)S(1)}, u32[]{:S(2)}, u32[]{:S(2)}) collective-permute-start(bf16[256,1536]{1,0:T(8,128)(2,1)S(1)} %fusion.35), channel_id=1, source_target_pairs={{0,2},{1,3},{2,0},{3,1},{4,6},{5,7},{6,4},{7,5},{8,10},{9,11},{10,... | collective-permute-start | bytes 2359304 | tf_op jit(solution)/shard_map/ppermute | solution.py:243
  852.6 19.5 %collective-permute-start.102 = (bf16[128,1536]{1,0:T(8,128)(2,1)S(1)}, bf16[128,1536]{1,0:T(8,128)(2,1)S(1)}, u32[]{:S(2)}, u32[]{:S(2)}) collective-permute-start(bf16[128,1536]{1,0:T(8,128)(2,1)S(1)} %get-tuple-element.192), channel_id=1, source_target_pairs={{0,8},{4,12},{8,0},{12,4},{1,9},{5,13},{9,1},{13,5},{2,10},{6,14},... | collective-permute-start | bytes 1179656 | tf_op jit(solution)/shard_map/ppermute | solution.py:234
  853.6 18.5 %collective-permute-start.101 = (bf16[128,1536]{1,0:T(8,128)(2,1)S(1)}, bf16[128,1536]{1,0:T(8,128)(2,1)S(1)}, u32[]{:S(2)}, u32[]{:S(2)}) collective-permute-start(bf16[128,1536]{1,0:T(8,128)(2,1)S(1)} %get-tuple-element.190), channel_id=1, source_target_pairs={{0,4},{4,0},{8,12},{12,8},{1,5},{5,1},{9,13},{13,9},{2,6},{6,2},{1... | collective-permute-start | bytes 1179656 | tf_op jit(solution)/shard_map/ppermute | solution.py:234
  857.0 23.5 %collective-permute-start.108 = (bf16[128,1536]{1,0:T(8,128)(2,1)S(1)}, bf16[128,1536]{1,0:T(8,128)(2,1)S(1)}, u32[]{:S(2)}, u32[]{:S(2)}) collective-permute-start(bf16[128,1536]{1,0:T(8,128)(2,1)S(1)} %get-tuple-element.196), channel_id=1, source_target_pairs={{0,12},{4,8},{8,4},{12,0},{1,13},{5,9},{9,5},{13,1},{2,14},{6,10},... | collective-permute-start | bytes 1179656 | tf_op jit(solution)/shard_map/ppermute | solution.py:234
  858.9 29.1 %collective-permute-start.107 = (bf16[128,1536]{1,0:T(8,128)(2,1)S(1)}, bf16[128,1536]{1,0:T(8,128)(2,1)S(1)}, u32[]{:S(2)}, u32[]{:S(2)}) collective-permute-start(bf16[128,1536]{1,0:T(8,128)(2,1)S(1)} %get-tuple-element.197), channel_id=1, source_target_pairs={{0,8},{4,12},{8,0},{12,4},{1,9},{5,13},{9,1},{13,5},{2,10},{6,14},... | collective-permute-start | bytes 1179656 | tf_op jit(solution)/shard_map/ppermute | solution.py:234
  863.6 24.4 %collective-permute-start.106 = (bf16[128,1536]{1,0:T(8,128)(2,1)S(1)}, bf16[128,1536]{1,0:T(8,128)(2,1)S(1)}, u32[]{:S(2)}, u32[]{:S(2)}) collective-permute-start(bf16[128,1536]{1,0:T(8,128)(2,1)S(1)} %get-tuple-element.195), channel_id=1, source_target_pairs={{0,4},{4,0},{8,12},{12,8},{1,5},{5,1},{9,13},{13,9},{2,6},{6,2},{1... | collective-permute-start | bytes 1179656 | tf_op jit(solution)/shard_map/ppermute | solution.py:234
  872.4 16.9 %collective-permute-start.104 = (bf16[128,1536]{1,0:T(8,128)(2,1)S(1)}, bf16[128,1536]{1,0:T(8,128)(2,1)S(1)}, u32[]{:S(2)}, u32[]{:S(2)}) collective-permute-start(bf16[128,1536]{1,0:T(8,128)(2,1)S(1)} %pad_maximum_fusion.28), channel_id=1, source_target_pairs={{0,1},{1,0},{2,3},{3,2},{4,5},{5,4},{6,7},{7,6},{8,9},{9,8},{10,11... | collective-permute-start | bytes 1179656 | tf_op jit(solution)/shard_map/ppermute | solution.py:239
  (145 other events, 3224.7 us)

commit v11 on v9

--- a/solution.py
+++ b/solution.py
@@ -394,6 +394,10 @@
         total = scatter_wide([terms[r * part : (r + 1) * part] for r in range(n_wide)]).astype(BF)
         far = to_mate(jnp.concatenate([total[:, feat_a:], total[:, :feat_a]], axis=1))
         return total.astype(F32) + far.astype(F32)
+
+    def summed_mine(terms):
+        total = scatter_wide([terms[r * part : (r + 1) * part] for r in range(n_wide)]).astype(BF)
+        return total[:, :feat_a].astype(F32) + to_mate(total[:, feat_a:]).astype(F32)
 
     results = []
     caches = []
@@ -475,7 +479,12 @@
                 terms, parts = ordered_parts(terms, up_parts)
                 up_weight = weight_of(1, parts, 0)
                 qkv_now = select(1, qkv_weight)
-            layer_in.append((after[h] + pick(table[1], kinds_h[h], 2) * summed(terms)).astype(BF))
+            gate = pick(table[1], kinds_h[h], 2)
+            if layer == 1:
+                mine = after[h][:, :feat_a] + gate[:, :feat_a] * summed_mine(terms)
+                layer_in.append(mine.astype(BF))
+            else:
+                layer_in.append((after[h] + gate * summed(terms)).astype(BF))
         results.append(jnp.concatenate([block[:, :feat_a] for block in layer_in], axis=0))
     return (by_layer(results, lead), by_layer(caches, lead))
 

time: 865 us -> 860 us (level)
    ppermute x9, waiting for transfers between devices: 18.1 us -> 37.1 us  [exchange(): block = lax.ppermute(block, axis, [(i, (i + step) % n) for i in range(n)])]
    ppermute x23, waiting for transfers between devices: 316 us -> 300 us  [to_partner(): lax.ppermute(value, 'narrow', [(i, i ^ 2) for i in range(lax.axis_size('n...]
    ppermute x10, waiting for transfers between devices: 27.6 us -> 15.7 us  [to_mate(): lax.ppermute(value, 'narrow', [(i, i ^ 1) for i in range(lax.axis_size('n...]
  transfers between devices with their start and end apart: 112 -> 112, of which waited for: 54 -> 53; matrix products, arithmetic and copies ran while one was open for 20% -> 21% of each run, Pallas kernels for 4% -> 4%
where the time goes in v11:
time: 860 us; the launch traced here: 851 us
  waiting for transfers between devices  467 us (54%)
  starting transfers between devices  151 us (18%)
  matrix products  67.8 us (8%)
  other arithmetic  66.3 us (8%)
  local copies, waits for them, and re-layouts  57 us (7%)
  Pallas kernels  37.7 us (4%)
    ppermute x23, waiting for transfers between devices, to_partner(): lax.ppermute(value, 'narrow', [(i, i ^ 2) for i in range(lax.axis_size('n...  300 us
    ppermute x24, waiting for transfers between devices, scatter_wide(): total += lax.ppermute(terms[step], 'wide', wide_pairs(step)).astype(F32)  60.8 us
    ppermute x9, waiting for transfers between devices, exchange(): block = lax.ppermute(block, axis, [(i, (i + step) % n) for i in range(n)])  37.1 us
    ppermute x8, waiting for transfers between devices, mate_half(): return lax.ppermute(sent, ('section', 'narrow'), pairs)  30.7 us
    ppermute x23, starting transfers between devices, to_partner(): lax.ppermute(value, 'narrow', [(i, i ^ 2) for i in range(lax.axis_size('n...  30 us
    ppermute x24, starting transfers between devices, gather_wide(): lax.ppermute(block, 'wide', wide_pairs(step))  29.7 us
    ppermute x24, starting transfers between devices, scatter_wide(): total += lax.ppermute(terms[step], 'wide', wide_pairs(step)).astype(F32)  28 us
    pallas_call x4, Pallas kernels, attend(): pl.pallas_call(functools.partial(attend_kernel, heads, head_dim), grid=(r...  21.6 us
  transfers between devices with their start and end apart: 112, of which 53 were waited for; matrix products, arithmetic and copies ran while one was open for 21% of the time, Pallas kernels for 4%

profile of v11, /device:TPU:0, one launch (start us, length us, event | category | flops | bytes accessed | tf_op | source)
XLA Modules:
  0.0 850.6 jit_solution(4497613632646813318)
XLA Ops:
  2.5 3.0 collective-permute-start
  5.6 5.5 dynamic-slice_bitcast_fusion.5
  32.0 4.9 dynamic-slice_bitcast_fusion.2
  41.5 5.0 fusion.104
  56.1 3.2 broadcast_select_fusion.14
  64.9 10.8 %collective-permute-done.8 = bf16[768,1152]{1,0:T(8,128)(2,1)} collective-permute-done((bf16[768,1152]{1,0:T(8,128)(2,1)}, bf16[768,1152]{1,0:T(8,128)(2,1)}, u32[]{:S(2)}, u32[]{:S(2)}) %collective-permute-start.8) | collective-permute-done | bytes 1769504 | tf_op jit(solution)/shard_map/ppermute | solution.py:311
  86.5 5.9 collective-permute-done.14
  92.4 4.1 collective-permute-done.15
  108.9 8.1 collective-permute-done.17
  123.5 4.0 convolution_convert_fusion.3
  132.7 12.1 %collective-permute-done.18 = bf16[512,576]{0,1:T(8,128)(2,1)S(1)} collective-permute-done((bf16[512,576]{0,1:T(8,128)(2,1)}, bf16[512,576]{0,1:T(8,128)(2,1)S(1)}, u32[]{:S(2)}, u32[]{:S(2)}) %collective-permute-start.18) | collective-permute-done | bytes 589856 | tf_op jit(solution)/shard_map/ppermute | solution.py:243
  146.5 4.0 prepare.5
  155.0 4.0 prepare.4
  164.0 5.9 attend.5
  171.7 4.8 dynamic-slice_bitcast_fusion.1
  178.2 5.2 attend.4
  184.6 18.6 %collective-permute-done.34 = bf16[512,192]{1,0:T(8,128)(2,1)} collective-permute-done((bf16[512,192]{1,0:T(8,128)(2,1)}, bf16[512,192]{1,0:T(8,128)(2,1)}, u32[]{:S(2)}, u32[]{:S(2)}) %collective-permute-start.34) | collective-permute-done | bytes 196640 | tf_op jit(solution)/shard_map/ppermute | solution.py:243
  222.0 4.9 collective-permute-done.25
  226.9 3.5 collective-permute-start.31
  233.6 2.8 collective-permute-start.53
  238.8 6.3 collective-permute-done.53
  249.5 39.5 %collective-permute-done.45 = f32[2,128]{1,0:T(2,128)S(1)} collective-permute-done((f32[2,128]{1,0:T(2,128)S(1)}, f32[2,128]{1,0:T(2,128)S(1)}, u32[]{:S(2)}, u32[]{:S(2)}) %collective-permute-start.45) | collective-permute-done | bytes 1056 | tf_op jit(solution)/shard_map/ppermute | solution.py:243
  294.6 11.8 %collective-permute-done.35 = bf16[1536,768]{1,0:T(8,128)(2,1)S(1)} collective-permute-done((bf16[1536,768]{1,0:T(8,128)(2,1)S(1)}, bf16[1536,768]{1,0:T(8,128)(2,1)S(1)}, u32[]{:S(2)}, u32[]{:S(2)}) %collective-permute-start.35) | collective-permute-done | bytes 2359328 | tf_op jit(solution)/shard_map/ppermute | solution.py:311
  312.7 4.7 convolution_convert_fusion.11
  319.3 4.6 convolution_convert_fusion.14
  326.3 31.6 %collective-permute-done.49 = bf16[256,1536]{1,0:T(8,128)(2,1)S(1)} collective-permute-done((bf16[256,1536]{1,0:T(8,128)(2,1)S(1)}, bf16[256,1536]{1,0:T(8,128)(2,1)S(1)}, u32[]{:S(2)}, u32[]{:S(2)}) %collective-permute-start.49) | collective-permute-done | bytes 786464 | tf_op jit(solution)/shard_map/ppermute | solution.py:243
  358.6 24.5 %collective-permute-done.32 = bf16[256,1536]{1,0:T(8,128)(2,1)S(1)} collective-permute-done((bf16[256,1536]{1,0:T(8,128)(2,1)S(1)}, bf16[256,1536]{1,0:T(8,128)(2,1)S(1)}, u32[]{:S(2)}, u32[]{:S(2)}) %collective-permute-start.32) | collective-permute-done | bytes 786464 | tf_op jit(solution)/shard_map/ppermute | solution.py:243
  383.8 4.2 pad_maximum_fusion.5
  389.4 10.5 %collective-permute-done.50 = bf16[256,1536]{1,0:T(8,128)(2,1)S(1)} collective-permute-done((bf16[256,1536]{1,0:T(8,128)(2,1)S(1)}, bf16[256,1536]{1,0:T(8,128)(2,1)S(1)}, u32[]{:S(2)}, u32[]{:S(2)}) %collective-permute-start.50) | collective-permute-done | bytes 786464 | tf_op jit(solution)/shard_map/ppermute | solution.py:243
  400.0 8.3 collective-permute-done.33
  442.9 6.2 collective-permute-done.57
  451.4 3.3 collective-permute-start.65
  472.3 4.9 convolution_convert_fusion
  479.3 3.0 collective-permute-start.69
  482.4 5.3 collective-permute-done.60
  487.7 5.8 convolution_convert_fusion.1
  495.7 3.0 collective-permute-start.64
  501.6 4.0 prepare.7
  505.7 25.8 %collective-permute-done.64 = bf16[512,576]{0,1:T(8,128)(2,1)} collective-permute-done((bf16[512,576]{0,1:T(8,128)(2,1)}, bf16[512,576]{0,1:T(8,128)(2,1)}, u32[]{:S(2)}, u32[]{:S(2)}) %collective-permute-start.64) | collective-permute-done | bytes 589856 | tf_op jit(solution)/shard_map/ppermute | solution.py:243
  535.2 4.0 prepare.6
  540.9 4.4 collective-permute-start.72
  548.5 5.2 attend.6
  557.6 5.2 attend.7
  562.9 2.9 collective-permute-start.86
  574.1 4.0 collective-permute-done.86
  584.9 7.0 collective-permute-done.75
  593.6 6.8 collective-permute-done.95
  600.4 8.1 collective-permute-done.94
  613.9 19.2 %collective-permute-done.105 = bf16[1,3,256,128]{3,2,0,1:T(8,128)(2,1)S(1)} collective-permute-done((bf16[1,3,256,128]{3,2,0,1:T(8,128)(2,1)S(1)}, bf16[1,3,256,128]{3,2,0,1:T(8,128)(2,1)S(1)}, u32[]{:S(2)}, u32[]{:S(2)}) %collective-permute-start.105) | collective-permute-done | bytes 196640 | tf_op jit(solution)/shard_map/ppermute | solution.py:167
  655.5 5.9 convolution_convert_fusion.5
  662.0 4.0 collective-permute-done.80
  666.0 5.9 convolution_convert_fusion.8
  672.0 41.7 %collective-permute-done.101 = bf16[256,1536]{1,0:T(8,128)(2,1)S(1)} collective-permute-done((bf16[256,1536]{1,0:T(8,128)(2,1)S(1)}, bf16[256,1536]{1,0:T(8,128)(2,1)S(1)}, u32[]{:S(2)}, u32[]{:S(2)}) %collective-permute-start.101) | collective-permute-done | bytes 786464 | tf_op jit(solution)/shard_map/ppermute | solution.py:243
  714.7 32.7 %collective-permute-done.84 = bf16[256,1536]{1,0:T(8,128)(2,1)S(1)} collective-permute-done((bf16[256,1536]{1,0:T(8,128)(2,1)S(1)}, bf16[256,1536]{1,0:T(8,128)(2,1)S(1)}, u32[]{:S(2)}, u32[]{:S(2)}) %collective-permute-start.84) | collective-permute-done | bytes 786464 | tf_op jit(solution)/shard_map/ppermute | solution.py:243
  748.1 33.0 %collective-permute-done.102 = bf16[256,1536]{1,0:T(8,128)(2,1)S(1)} collective-permute-done((bf16[256,1536]{1,0:T(8,128)(2,1)S(1)}, bf16[256,1536]{1,0:T(8,128)(2,1)S(1)}, u32[]{:S(2)}, u32[]{:S(2)}) %collective-permute-start.102) | collective-permute-done | bytes 786464 | tf_op jit(solution)/shard_map/ppermute | solution.py:243
  781.2 4.1 collective-permute-start.111
  785.4 12.6 %collective-permute-done.85 = bf16[256,1536]{1,0:T(8,128)(2,1)S(1)} collective-permute-done((bf16[256,1536]{1,0:T(8,128)(2,1)S(1)}, bf16[256,1536]{1,0:T(8,128)(2,1)S(1)}, u32[]{:S(2)}, u32[]{:S(2)}) %collective-permute-start.85) | collective-permute-done | bytes 786464 | tf_op jit(solution)/shard_map/ppermute | solution.py:243
  798.1 5.1 convolution_convert_fusion.6
  806.8 5.1 convolution_convert_fusion.4
  813.5 2.8 collective-permute-done.91
  816.3 8.5 collective-permute-done.90
  825.1 8.1 collective-permute-done.108
  833.2 6.8 collective-permute-done.107
  840.4 6.7 collective-permute-done.109
  (596 shorter events, 269.8 us)
Async XLA Ops:
  2.5 34.4 %collective-permute-start = (bf16[256,768]{1,0:T(8,128)(2,1)}, bf16[256,768]{1,0:T(8,128)(2,1)}, u32[]{:S(2)}, u32[]{:S(2)}) collective-permute-start(bf16[256,768]{1,0:T(8,128)(2,1)} %dynamic-slice_bitcast_fusion.8), channel_id=1, source_target_pairs={{0,1},{1,0},{2,3},{3,2},{4,5},{5,4},{6,7},{7,6},{8,9},{9,8},{10,11... | collective-permute-start | bytes 1179656 | tf_op jit(solution)/shard_map/ppermute | solution.py:239
  13.8 37.2 %collective-permute-start.3 = (bf16[768,1152]{1,0:T(8,128)(2,1)}, bf16[768,1152]{1,0:T(8,128)(2,1)}, u32[]{:S(2)}, u32[]{:S(2)}) collective-permute-start(bf16[768,1152]{1,0:T(8,128)(2,1)} %pad_maximum_fusion.9), channel_id=1, source_target_pairs={{0,16},{1,17},{2,18},{3,19},{4,20},{5,21},{6,22},{7,23},{8,24},{9,... | collective-permute-start | bytes 5308424 | tf_op jit(solution)/shard_map/ppermute | solution.py:314
  51.0 24.7 %collective-permute-start.8 = (bf16[768,1152]{1,0:T(8,128)(2,1)}, bf16[768,1152]{1,0:T(8,128)(2,1)}, u32[]{:S(2)}, u32[]{:S(2)}) collective-permute-start(bf16[768,1152]{1,0:T(8,128)(2,1)} %pad_maximum_fusion.8), channel_id=1, source_target_pairs={{0,1},{1,0},{2,3},{3,2},{4,5},{5,4},{6,7},{7,6},{8,9},{9,8},{10,11... | collective-permute-start | bytes 5308424 | tf_op jit(solution)/shard_map/ppermute | solution.py:311
  75.8 25.4 %collective-permute-start.9 = (bf16[768,1152]{1,0:T(8,128)(2,1)}, bf16[768,1152]{1,0:T(8,128)(2,1)S(1)}, u32[]{:S(2)}, u32[]{:S(2)}) collective-permute-start(bf16[768,1152]{1,0:T(8,128)(2,1)} %collective-permute-done.8), channel_id=1, source_target_pairs={{0,16},{1,17},{2,18},{3,19},{4,20},{5,21},{6,22},{7,23},{8,24},{9,... | collective-permute-start | bytes 5308424 | tf_op jit(solution)/shard_map/ppermute | solution.py:314
  79.1 25.5 %collective-permute-start.13 = (bf16[128,1536]{1,0:T(8,128)(2,1)S(1)}, bf16[128,1536]{1,0:T(8,128)(2,1)S(1)}, u32[]{:S(2)}, u32[]{:S(2)}) collective-permute-start(bf16[128,1536]{1,0:T(8,128)(2,1)S(1)} %fusion.114), channel_id=1, source_target_pairs={{0,12},{4,8},{8,4},{12,0},{1,13},{5,9},{9,5},{13,1},{2,14},{6,10},... | collective-permute-start | bytes 1179656 | tf_op jit(solution)/shard_map/ppermute | solution.py:227
  81.6 23.8 %collective-permute-start.12 = (bf16[128,1536]{1,0:T(8,128)(2,1)S(1)}, bf16[128,1536]{1,0:T(8,128)(2,1)S(1)}, u32[]{:S(2)}, u32[]{:S(2)}) collective-permute-start(bf16[128,1536]{1,0:T(8,128)(2,1)S(1)} %fusion.114), channel_id=1, source_target_pairs={{0,8},{4,12},{8,0},{12,4},{1,9},{5,13},{9,1},{13,5},{2,10},{6,14},... | collective-permute-start | bytes 1179656 | tf_op jit(solution)/shard_map/ppermute | solution.py:227
  98.6 18.3 %collective-permute-start.17 = (bf16[384,768]{1,0:T(8,128)(2,1)}, bf16[384,768]{1,0:T(8,128)(2,1)S(1)}, u32[]{:S(2)}, u32[]{:S(2)}) collective-permute-start(bf16[384,768]{1,0:T(8,128)(2,1)} %pad_maximum_fusion.19), channel_id=1, source_target_pairs={{0,1},{1,0},{2,3},{3,2},{4,5},{5,4},{6,7},{7,6},{8,9},{9,8},{10,11... | collective-permute-start | bytes 1769480 | tf_op jit(solution)/shard_map/ppermute | solution.py:311
  101.2 22.3 %collective-permute-start.7 = (bf16[128,1536]{1,0:T(8,128)(2,1)}, bf16[128,1536]{1,0:T(8,128)(2,1)}, u32[]{:S(2)}, u32[]{:S(2)}) collective-permute-start(bf16[128,1536]{1,0:T(8,128)(2,1)} %fusion.110), channel_id=1, source_target_pairs={{0,12},{4,8},{8,4},{12,0},{1,13},{5,9},{9,5},{13,1},{2,14},{6,10},... | collective-permute-start | bytes 1179656 | tf_op jit(solution)/shard_map/ppermute | solution.py:227
  104.6 19.0 %collective-permute-start.6 = (bf16[128,1536]{1,0:T(8,128)(2,1)}, bf16[128,1536]{1,0:T(8,128)(2,1)S(1)}, u32[]{:S(2)}, u32[]{:S(2)}) collective-permute-start(bf16[128,1536]{1,0:T(8,128)(2,1)} %fusion.110), channel_id=1, source_target_pairs={{0,8},{4,12},{8,0},{12,4},{1,9},{5,13},{9,1},{13,5},{2,10},{6,14},... | collective-permute-start | bytes 1179656 | tf_op jit(solution)/shard_map/ppermute | solution.py:227
  105.4 18.1 %collective-permute-start.5 = (bf16[128,1536]{1,0:T(8,128)(2,1)}, bf16[128,1536]{1,0:T(8,128)(2,1)}, u32[]{:S(2)}, u32[]{:S(2)}) collective-permute-start(bf16[128,1536]{1,0:T(8,128)(2,1)} %fusion.110), channel_id=1, source_target_pairs={{0,4},{4,0},{8,12},{12,8},{1,5},{5,1},{9,13},{13,9},{2,6},{6,2},{1... | collective-permute-start | bytes 1179656 | tf_op jit(solution)/shard_map/ppermute | solution.py:227
  118.9 25.9 %collective-permute-start.18 = (bf16[512,576]{0,1:T(8,128)(2,1)}, bf16[512,576]{0,1:T(8,128)(2,1)S(1)}, u32[]{:S(2)}, u32[]{:S(2)}) collective-permute-start(bf16[512,576]{0,1:T(8,128)(2,1)} %copy.37), channel_id=1, source_target_pairs={{0,2},{1,3},{2,0},{3,1},{4,6},{5,7},{6,4},{7,5},{8,10},{9,11},{10,... | collective-permute-start | bytes 1769480 | tf_op jit(solution)/shard_map/ppermute | solution.py:243
  121.2 38.6 %collective-permute-start.19 = (bf16[384,1536]{1,0:T(8,128)(2,1)}, bf16[384,1536]{1,0:T(8,128)(2,1)}, u32[]{:S(2)}, u32[]{:S(2)}) collective-permute-start(bf16[384,1536]{1,0:T(8,128)(2,1)} %pad_maximum_fusion.10), channel_id=1, source_target_pairs={{0,16},{1,17},{2,18},{3,19},{4,20},{5,21},{6,22},{7,23},{8,24},{9,... | collective-permute-start | bytes 3538952 | tf_op jit(solution)/shard_map/ppermute | solution.py:314
  129.8 21.4 %collective-permute-start.10 = (bf16[512,576]{0,1:T(8,128)(2,1)}, bf16[512,576]{0,1:T(8,128)(2,1)}, u32[]{:S(2)}, u32[]{:S(2)}) collective-permute-start(bf16[512,576]{0,1:T(8,128)(2,1)} %copy.31), channel_id=1, source_target_pairs={{0,2},{1,3},{2,0},{3,1},{4,6},{5,7},{6,4},{7,5},{8,10},{9,11},{10,... | collective-permute-start | bytes 1769480 | tf_op jit(solution)/shard_map/ppermute | solution.py:243
  162.0 52.6 %collective-permute-start.22 = (bf16[768,1536]{1,0:T(8,128)(2,1)}, bf16[768,1536]{1,0:T(8,128)(2,1)}, u32[]{:S(2)}, u32[]{:S(2)}) collective-permute-start(bf16[768,1536]{1,0:T(8,128)(2,1)} %get-tuple-element.89), channel_id=1, source_target_pairs={{0,1},{1,0},{2,3},{3,2},{4,5},{5,4},{6,7},{7,6},{8,9},{9,8},{10,11... | collective-permute-start | bytes 7077896 | tf_op jit(solution)/shard_map/ppermute | solution.py:311
  169.9 33.3 %collective-permute-start.34 = (bf16[512,192]{1,0:T(8,128)(2,1)}, bf16[512,192]{1,0:T(8,128)(2,1)}, u32[]{:S(2)}, u32[]{:S(2)}) collective-permute-start(bf16[512,192]{1,0:T(8,128)(2,1)} %attend.5), channel_id=1, source_target_pairs={{0,2},{1,3},{2,0},{3,1},{4,6},{5,7},{6,4},{7,5},{8,10},{9,11},{10,... | collective-permute-start | bytes 589832 | tf_op jit(solution)/shard_map/ppermute | solution.py:243
  183.4 26.5 %collective-permute-start.21 = (bf16[512,192]{1,0:T(8,128)(2,1)S(1)}, bf16[512,192]{1,0:T(8,128)(2,1)S(1)}, u32[]{:S(2)}, u32[]{:S(2)}) collective-permute-start(bf16[512,192]{1,0:T(8,128)(2,1)S(1)} %attend.4), channel_id=1, source_target_pairs={{0,2},{1,3},{2,0},{3,1},{4,6},{5,7},{6,4},{7,5},{8,10},{9,11},{10,... | collective-permute-start | bytes 589832 | tf_op jit(solution)/shard_map/ppermute | solution.py:243
  209.9 23.7 %collective-permute-start.51 = (bf16[1,3,256,128]{3,2,0,1:T(8,128)(2,1)S(1)}, bf16[1,3,256,128]{3,2,0,1:T(8,128)(2,1)S(1)}, u32[]{:S(2)}, u32[]{:S(2)}) collective-permute-start(bf16[1,3,256,128]{3,2,0,1:T(8,128)(2,1)S(1)} %get-tuple-element.228), channel_id=1, source_target_pairs={{0,1},{1,2},{2,3},{3,0},{4,5},{5,6},{6,7},{7,4},{8,9},{9,10},{10,1... | collective-permute-start | bytes 589832 | tf_op jit(solution)/shard_map/ppermute | solution.py:167
  214.5 21.9 %collective-permute-start.52 = (bf16[1,3,256,128]{3,2,0,1:T(8,128)(2,1)S(1)}, bf16[1,3,256,128]{3,2,0,1:T(8,128)(2,1)S(1)}, u32[]{:S(2)}, u32[]{:S(2)}) collective-permute-start(bf16[1,3,256,128]{3,2,0,1:T(8,128)(2,1)S(1)} %get-tuple-element.227), channel_id=1, source_target_pairs={{0,2},{1,3},{2,0},{3,1},{4,6},{5,7},{6,4},{7,5},{8,10},{9,11},{10,... | collective-permute-start | bytes 589832 | tf_op jit(solution)/shard_map/ppermute | solution.py:167
  226.9 84.1 %collective-permute-start.31 = (bf16[1536,1536]{1,0:T(8,128)(2,1)S(1)}, bf16[1536,1536]{1,0:T(8,128)(2,1)}, u32[]{:S(2)}, u32[]{:S(2)}) collective-permute-start(bf16[1536,1536]{1,0:T(8,128)(2,1)S(1)} %pad_maximum_fusion.1), channel_id=1, source_target_pairs={{0,16},{1,17},{2,18},{3,19},{4,20},{5,21},{6,22},{7,23},{8,24},{9,... | collective-permute-start | bytes 14155784 | tf_op jit(solution)/shard_map/ppermute | solution.py:314
  236.5 69.9 %collective-permute-start.35 = (bf16[1536,768]{1,0:T(8,128)(2,1)S(1)}, bf16[1536,768]{1,0:T(8,128)(2,1)S(1)}, u32[]{:S(2)}, u32[]{:S(2)}) collective-permute-start(bf16[1536,768]{1,0:T(8,128)(2,1)S(1)} %copy-done.41), channel_id=1, source_target_pairs={{0,1},{1,0},{2,3},{3,2},{4,5},{5,4},{6,7},{7,6},{8,9},{9,8},{10,11... | collective-permute-start | bytes 7077896 | tf_op jit(solution)/shard_map/ppermute | solution.py:311
  246.2 42.8 %collective-permute-start.45 = (f32[2,128]{1,0:T(2,128)S(1)}, f32[2,128]{1,0:T(2,128)S(1)}, u32[]{:S(2)}, u32[]{:S(2)}) collective-permute-start(f32[2,128]{1,0:T(2,128)S(1)} %pad_maximum_fusion.36), channel_id=1, source_target_pairs={{0,2},{1,3},{2,0},{3,1},{4,6},{5,7},{6,4},{7,5},{8,10},{9,11},{10,... | collective-permute-start | bytes 3080 | tf_op jit(solution)/shard_map/ppermute | solution.py:243
  248.1 45.1 %collective-permute-start.27 = (f32[2,128]{1,0:T(2,128)S(1)}, f32[2,128]{1,0:T(2,128)S(1)}, u32[]{:S(2)}, u32[]{:S(2)}) collective-permute-start(f32[2,128]{1,0:T(2,128)S(1)} %pad_maximum_fusion.35), channel_id=1, source_target_pairs={{0,2},{1,3},{2,0},{3,1},{4,6},{5,7},{6,4},{7,5},{8,10},{9,11},{10,... | collective-permute-start | bytes 3080 | tf_op jit(solution)/shard_map/ppermute | solution.py:243
  290.0 18.1 %collective-permute-start.48 = (bf16[128,1536]{1,0:T(8,128)(2,1)S(1)}, bf16[128,1536]{1,0:T(8,128)(2,1)S(1)}, u32[]{:S(2)}, u32[]{:S(2)}) collective-permute-start(bf16[128,1536]{1,0:T(8,128)(2,1)S(1)} %add_convert_fusion.8), channel_id=1, source_target_pairs={{0,12},{4,8},{8,4},{12,0},{1,13},{5,9},{9,5},{13,1},{2,14},{6,10},... | collective-permute-start | bytes 1179656 | tf_op jit(solution)/shard_map/ppermute | solution.py:227
  291.2 18.4 %collective-permute-start.47 = (bf16[128,1536]{1,0:T(8,128)(2,1)S(1)}, bf16[128,1536]{1,0:T(8,128)(2,1)S(1)}, u32[]{:S(2)}, u32[]{:S(2)}) collective-permute-start(bf16[128,1536]{1,0:T(8,128)(2,1)S(1)} %add_convert_fusion.8), channel_id=1, source_target_pairs={{0,8},{4,12},{8,0},{12,4},{1,9},{5,13},{9,1},{13,5},{2,10},{6,14},... | collective-permute-start | bytes 1179656 | tf_op jit(solution)/shard_map/ppermute | solution.py:227
  293.1 17.2 %collective-permute-start.46 = (bf16[128,1536]{1,0:T(8,128)(2,1)S(1)}, bf16[128,1536]{1,0:T(8,128)(2,1)}, u32[]{:S(2)}, u32[]{:S(2)}) collective-permute-start(bf16[128,1536]{1,0:T(8,128)(2,1)S(1)} %add_convert_fusion.8), channel_id=1, source_target_pairs={{0,4},{4,0},{8,12},{12,8},{1,5},{5,1},{9,13},{13,9},{2,6},{6,2},{1... | collective-permute-start | bytes 1179656 | tf_op jit(solution)/shard_map/ppermute | solution.py:227
  310.3 73.5 %collective-permute-start.62 = (bf16[768,1152]{1,0:T(8,128)(2,1)}, bf16[768,1152]{1,0:T(8,128)(2,1)S(1)}, u32[]{:S(2)}, u32[]{:S(2)}) collective-permute-start(bf16[768,1152]{1,0:T(8,128)(2,1)} %pad_maximum_fusion.8), channel_id=1, source_target_pairs={{16,17},{17,16},{18,19},{19,18},{20,21},{21,20},{22,23},{23,22},{2... | collective-permute-start | bytes 5308424 | tf_op jit(solution)/shard_map/ppermute | solution.py:311
  311.1 97.4 %collective-permute-start.36 = (bf16[1536,1536]{1,0:T(8,128)(2,1)S(1)}, bf16[1536,1536]{1,0:T(8,128)(2,1)S(1)}, u32[]{:S(2)}, u32[]{:S(2)}) collective-permute-start(bf16[1536,1536]{1,0:T(8,128)(2,1)S(1)} %pad_maximum_fusion.3), channel_id=1, source_target_pairs={{0,16},{1,17},{2,18},{3,19},{4,20},{5,21},{6,22},{7,23},{8,24},{9,... | collective-permute-start | bytes 14155784 | tf_op jit(solution)/shard_map/ppermute | solution.py:314
  317.4 40.4 %collective-permute-start.49 = (bf16[256,1536]{1,0:T(8,128)(2,1)S(1)}, bf16[256,1536]{1,0:T(8,128)(2,1)S(1)}, u32[]{:S(2)}, u32[]{:S(2)}) collective-permute-start(bf16[256,1536]{1,0:T(8,128)(2,1)S(1)} %constant_dynamic-slice_fusion.10), channel_id=1, source_target_pairs={{0,2},{1,3},{2,0},{3,1},{4,6},{5,7},{6,4},{7,5},{8,10},{9,11},{10,... | collective-permute-start | bytes 2359304 | tf_op jit(solution)/shard_map/ppermute | solution.py:243
  323.9 59.2 %collective-permute-start.32 = (bf16[256,1536]{1,0:T(8,128)(2,1)S(1)}, bf16[256,1536]{1,0:T(8,128)(2,1)S(1)}, u32[]{:S(2)}, u32[]{:S(2)}) collective-permute-start(bf16[256,1536]{1,0:T(8,128)(2,1)S(1)} %constant_dynamic-slice_fusion.11), channel_id=1, source_target_pairs={{0,2},{1,3},{2,0},{3,1},{4,6},{5,7},{6,4},{7,5},{8,10},{9,11},{10,... | collective-permute-start | bytes 2359304 | tf_op jit(solution)/shard_map/ppermute | solution.py:243
  358.5 41.4 %collective-permute-start.50 = (bf16[256,1536]{1,0:T(8,128)(2,1)S(1)}, bf16[256,1536]{1,0:T(8,128)(2,1)S(1)}, u32[]{:S(2)}, u32[]{:S(2)}) collective-permute-start(bf16[256,1536]{1,0:T(8,128)(2,1)S(1)} %fusion.19), channel_id=1, source_target_pairs={{0,2},{1,3},{2,0},{3,1},{4,6},{5,7},{6,4},{7,5},{8,10},{9,11},{10,... | collective-permute-start | bytes 2359304 | tf_op jit(solution)/shard_map/ppermute | solution.py:243
  383.7 24.6 %collective-permute-start.33 = (bf16[256,1536]{1,0:T(8,128)(2,1)S(1)}, bf16[256,1536]{1,0:T(8,128)(2,1)S(1)}, u32[]{:S(2)}, u32[]{:S(2)}) collective-permute-start(bf16[256,1536]{1,0:T(8,128)(2,1)S(1)} %fusion.11), channel_id=1, source_target_pairs={{0,2},{1,3},{2,0},{3,1},{4,6},{5,7},{6,4},{7,5},{8,10},{9,11},{10,... | collective-permute-start | bytes 2359304 | tf_op jit(solution)/shard_map/ppermute | solution.py:243
  388.0 74.8 %collective-permute-start.63 = (bf16[1536,1152]{1,0:T(8,128)(2,1)}, bf16[1536,1152]{1,0:T(8,128)(2,1)}, u32[]{:S(2)}, u32[]{:S(2)}) collective-permute-start(bf16[1536,1152]{1,0:T(8,128)(2,1)} %pad_maximum_fusion.5), channel_id=1, source_target_pairs={{16,0},{17,1},{18,2},{19,3},{20,4},{21,5},{22,6},{23,7},{24,8},{25... | collective-permute-start | bytes 10616840 | tf_op jit(solution)/shard_map/ppermute | solution.py:314
  438.5 115.3 %collective-permute-start.82 = (bf16[768,1536]{1,0:T(8,128)(2,1)}, bf16[768,1536]{1,0:T(8,128)(2,1)}, u32[]{:S(2)}, u32[]{:S(2)}) collective-permute-start(bf16[768,1536]{1,0:T(8,128)(2,1)} %get-tuple-element.89), channel_id=1, source_target_pairs={{16,17},{17,16},{18,19},{19,18},{20,21},{21,20},{22,23},{23,22},{2... | collective-permute-start | bytes 7077896 | tf_op jit(solution)/shard_map/ppermute | solution.py:311
  462.8 76.5 %collective-permute-start.71 = (bf16[384,1536]{1,0:T(8,128)(2,1)}, bf16[384,1536]{1,0:T(8,128)(2,1)}, u32[]{:S(2)}, u32[]{:S(2)}) collective-permute-start(bf16[384,1536]{1,0:T(8,128)(2,1)} %pad_maximum_fusion.12), channel_id=1, source_target_pairs={{16,0},{17,1},{18,2},{19,3},{20,4},{21,5},{22,6},{23,7},{24,8},{25... | collective-permute-start | bytes 3538952 | tf_op jit(solution)/shard_map/ppermute | solution.py:314
  470.2 17.4 %collective-permute-start.60 = (bf16[128,1536]{1,0:T(8,128)(2,1)}, bf16[128,1536]{1,0:T(8,128)(2,1)}, u32[]{:S(2)}, u32[]{:S(2)}) collective-permute-start(bf16[128,1536]{1,0:T(8,128)(2,1)} %fusion.120), channel_id=1, source_target_pairs={{0,8},{4,12},{8,0},{12,4},{1,9},{5,13},{9,1},{13,5},{2,10},{6,14},... | collective-permute-start | bytes 1179656 | tf_op jit(solution)/shard_map/ppermute | solution.py:227
  471.6 16.1 %collective-permute-start.59 = (bf16[128,1536]{1,0:T(8,128)(2,1)}, bf16[128,1536]{1,0:T(8,128)(2,1)}, u32[]{:S(2)}, u32[]{:S(2)}) collective-permute-start(bf16[128,1536]{1,0:T(8,128)(2,1)} %fusion.120), channel_id=1, source_target_pairs={{0,4},{4,0},{8,12},{12,8},{1,5},{5,1},{9,13},{13,9},{2,6},{6,2},{1... | collective-permute-start | bytes 1179656 | tf_op jit(solution)/shard_map/ppermute | solution.py:227
  479.3 19.6 %collective-permute-start.69 = (bf16[512,576]{0,1:T(8,128)(2,1)S(1)}, bf16[512,576]{0,1:T(8,128)(2,1)}, u32[]{:S(2)}, u32[]{:S(2)}) collective-permute-start(bf16[512,576]{0,1:T(8,128)(2,1)S(1)} %copy.44), channel_id=1, source_target_pairs={{0,2},{1,3},{2,0},{3,1},{4,6},{5,7},{6,4},{7,5},{8,10},{9,11},{10,... | collective-permute-start | bytes 1769480 | tf_op jit(solution)/shard_map/ppermute | solution.py:243
  495.7 35.8 %collective-permute-start.64 = (bf16[512,576]{0,1:T(8,128)(2,1)}, bf16[512,576]{0,1:T(8,128)(2,1)}, u32[]{:S(2)}, u32[]{:S(2)}) collective-permute-start(bf16[512,576]{0,1:T(8,128)(2,1)} %copy.41), channel_id=1, source_target_pairs={{0,2},{1,3},{2,0},{3,1},{4,6},{5,7},{6,4},{7,5},{8,10},{9,11},{10,... | collective-permute-start | bytes 1769480 | tf_op jit(solution)/shard_map/ppermute | solution.py:243
  555.9 99.7 %collective-permute-start.83 = (bf16[1536,1536]{1,0:T(8,128)(2,1)S(1)}, bf16[1536,1536]{1,0:T(8,128)(2,1)}, u32[]{:S(2)}, u32[]{:S(2)}) collective-permute-start(bf16[1536,1536]{1,0:T(8,128)(2,1)S(1)} %pad_maximum_fusion), channel_id=1, source_target_pairs={{16,0},{17,1},{18,2},{19,3},{20,4},{21,5},{22,6},{23,7},{24,8},{25... | collective-permute-start | bytes 14155784 | tf_op jit(solution)/shard_map/ppermute | solution.py:314
  562.9 15.2 %collective-permute-start.86 = (bf16[512,192]{1,0:T(8,128)(2,1)S(1)}, bf16[512,192]{1,0:T(8,128)(2,1)S(1)}, u32[]{:S(2)}, u32[]{:S(2)}) collective-permute-start(bf16[512,192]{1,0:T(8,128)(2,1)S(1)} %attend.7), channel_id=1, source_target_pairs={{0,2},{1,3},{2,0},{3,1},{4,6},{5,7},{6,4},{7,5},{8,10},{9,11},{10,... | collective-permute-start | bytes 589832 | tf_op jit(solution)/shard_map/ppermute | solution.py:243
  572.1 19.8 %collective-permute-start.75 = (bf16[128,1536]{1,0:T(8,128)(2,1)S(1)}, bf16[128,1536]{1,0:T(8,128)(2,1)S(1)}, u32[]{:S(2)}, u32[]{:S(2)}) collective-permute-start(bf16[128,1536]{1,0:T(8,128)(2,1)S(1)} %get-tuple-element.179), channel_id=1, source_target_pairs={{0,8},{4,12},{8,0},{12,4},{1,9},{5,13},{9,1},{13,5},{2,10},{6,14},... | collective-permute-start | bytes 1179656 | tf_op jit(solution)/shard_map/ppermute | solution.py:234
  573.5 19.9 %collective-permute-start.74 = (bf16[128,1536]{1,0:T(8,128)(2,1)S(1)}, bf16[128,1536]{1,0:T(8,128)(2,1)S(1)}, u32[]{:S(2)}, u32[]{:S(2)}) collective-permute-start(bf16[128,1536]{1,0:T(8,128)(2,1)S(1)} %get-tuple-element.177), channel_id=1, source_target_pairs={{0,4},{4,0},{8,12},{12,8},{1,5},{5,1},{9,13},{13,9},{2,6},{6,2},{1... | collective-permute-start | bytes 1179656 | tf_op jit(solution)/shard_map/ppermute | solution.py:234
  580.5 19.9 %collective-permute-start.95 = (bf16[128,1536]{1,0:T(8,128)(2,1)S(1)}, bf16[128,1536]{1,0:T(8,128)(2,1)S(1)}, u32[]{:S(2)}, u32[]{:S(2)}) collective-permute-start(bf16[128,1536]{1,0:T(8,128)(2,1)S(1)} %get-tuple-element.186), channel_id=1, source_target_pairs={{0,12},{4,8},{8,4},{12,0},{1,13},{5,9},{9,5},{13,1},{2,14},{6,10},... | collective-permute-start | bytes 1179656 | tf_op jit(solution)/shard_map/ppermute | solution.py:234
  583.5 25.0 %collective-permute-start.94 = (bf16[128,1536]{1,0:T(8,128)(2,1)S(1)}, bf16[128,1536]{1,0:T(8,128)(2,1)S(1)}, u32[]{:S(2)}, u32[]{:S(2)}) collective-permute-start(bf16[128,1536]{1,0:T(8,128)(2,1)S(1)} %get-tuple-element.187), channel_id=1, source_target_pairs={{0,8},{4,12},{8,0},{12,4},{1,9},{5,13},{9,1},{13,5},{2,10},{6,14},... | collective-permute-start | bytes 1179656 | tf_op jit(solution)/shard_map/ppermute | solution.py:234
  591.9 16.8 %collective-permute-start.93 = (bf16[128,1536]{1,0:T(8,128)(2,1)S(1)}, bf16[128,1536]{1,0:T(8,128)(2,1)S(1)}, u32[]{:S(2)}, u32[]{:S(2)}) collective-permute-start(bf16[128,1536]{1,0:T(8,128)(2,1)S(1)} %get-tuple-element.185), channel_id=1, source_target_pairs={{0,4},{4,0},{8,12},{12,8},{1,5},{5,1},{9,13},{13,9},{2,6},{6,2},{1... | collective-permute-start | bytes 1179656 | tf_op jit(solution)/shard_map/ppermute | solution.py:234
  593.3 17.7 %collective-permute-start.103 = (bf16[1,3,256,128]{3,2,0,1:T(8,128)(2,1)S(1)}, bf16[1,3,256,128]{3,2,0,1:T(8,128)(2,1)S(1)}, u32[]{:S(2)}, u32[]{:S(2)}) collective-permute-start(bf16[1,3,256,128]{3,2,0,1:T(8,128)(2,1)S(1)} %get-tuple-element.220), channel_id=1, source_target_pairs={{0,1},{1,2},{2,3},{3,0},{4,5},{5,6},{6,7},{7,4},{8,9},{9,10},{10,1... | collective-permute-start | bytes 589832 | tf_op jit(solution)/shard_map/ppermute | solution.py:167
  608.5 24.6 %collective-permute-start.77 = (bf16[128,1536]{1,0:T(8,128)(2,1)S(1)}, bf16[128,1536]{1,0:T(8,128)(2,1)S(1)}, u32[]{:S(2)}, u32[]{:S(2)}) collective-permute-start(bf16[128,1536]{1,0:T(8,128)(2,1)S(1)} %pad_maximum_fusion.26), channel_id=1, source_target_pairs={{0,1},{1,0},{2,3},{3,2},{4,5},{5,4},{6,7},{7,6},{8,9},{9,8},{10,11... | collective-permute-start | bytes 1179656 | tf_op jit(solution)/shard_map/ppermute | solution.py:239
  609.0 24.2 %collective-permute-start.96 = (bf16[128,1536]{1,0:T(8,128)(2,1)S(1)}, bf16[128,1536]{1,0:T(8,128)(2,1)S(1)}, u32[]{:S(2)}, u32[]{:S(2)}) collective-permute-start(bf16[128,1536]{1,0:T(8,128)(2,1)S(1)} %pad_maximum_fusion.27), channel_id=1, source_target_pairs={{0,1},{1,0},{2,3},{3,2},{4,5},{5,4},{6,7},{7,6},{8,9},{9,8},{10,11... | collective-permute-start | bytes 1179656 | tf_op jit(solution)/shard_map/ppermute | solution.py:239
  611.1 22.0 %collective-permute-start.105 = (bf16[1,3,256,128]{3,2,0,1:T(8,128)(2,1)S(1)}, bf16[1,3,256,128]{3,2,0,1:T(8,128)(2,1)S(1)}, u32[]{:S(2)}, u32[]{:S(2)}) collective-permute-start(bf16[1,3,256,128]{3,2,0,1:T(8,128)(2,1)S(1)} %get-tuple-element.218), channel_id=1, source_target_pairs={{0,3},{1,0},{2,1},{3,2},{4,7},{5,4},{6,5},{7,6},{8,11},{9,8},{10,9... | collective-permute-start | bytes 589832 | tf_op jit(solution)/shard_map/ppermute | solution.py:167
  613.0 31.2 %collective-permute-start.87 = (bf16[1536,768]{1,0:T(8,128)(2,1)S(1)}, bf16[1536,768]{1,0:T(8,128)(2,1)S(1)}, u32[]{:S(2)}, u32[]{:S(2)}) collective-permute-start(bf16[1536,768]{1,0:T(8,128)(2,1)S(1)} %copy-done.42), channel_id=1, source_target_pairs={{16,17},{17,16},{18,19},{19,18},{20,21},{21,20},{22,23},{23,22},{2... | collective-permute-start | bytes 7077896 | tf_op jit(solution)/shard_map/ppermute | solution.py:311
  644.2 17.8 %collective-permute-start.81 = (bf16[128,1536]{1,0:T(8,128)(2,1)S(1)}, bf16[128,1536]{1,0:T(8,128)(2,1)S(1)}, u32[]{:S(2)}, u32[]{:S(2)}) collective-permute-start(bf16[128,1536]{1,0:T(8,128)(2,1)S(1)} %add_convert_fusion.4), channel_id=1, source_target_pairs={{0,12},{4,8},{8,4},{12,0},{1,13},{5,9},{9,5},{13,1},{2,14},{6,10},... | collective-permute-start | bytes 1179656 | tf_op jit(solution)/shard_map/ppermute | solution.py:227
  648.5 17.5 %collective-permute-start.80 = (bf16[128,1536]{1,0:T(8,128)(2,1)S(1)}, bf16[128,1536]{1,0:T(8,128)(2,1)S(1)}, u32[]{:S(2)}, u32[]{:S(2)}) collective-permute-start(bf16[128,1536]{1,0:T(8,128)(2,1)S(1)} %add_convert_fusion.4), channel_id=1, source_target_pairs={{0,8},{4,12},{8,0},{12,4},{1,9},{5,13},{9,1},{13,5},{2,10},{6,14},... | collective-permute-start | bytes 1179656 | tf_op jit(solution)/shard_map/ppermute | solution.py:227
  654.1 144.0 %collective-permute-start.88 = (bf16[1536,1536]{1,0:T(8,128)(2,1)S(1)}, bf16[1536,1536]{1,0:T(8,128)(2,1)}, u32[]{:S(2)}, u32[]{:S(2)}) collective-permute-start(bf16[1536,1536]{1,0:T(8,128)(2,1)S(1)} %pad_maximum_fusion.2), channel_id=1, source_target_pairs={{16,0},{17,1},{18,2},{19,3},{20,4},{21,5},{22,6},{23,7},{24,8},{25... | collective-permute-start | bytes 14155784 | tf_op jit(solution)/shard_map/ppermute | solution.py:314
  661.5 52.2 %collective-permute-start.101 = (bf16[256,1536]{1,0:T(8,128)(2,1)S(1)}, bf16[256,1536]{1,0:T(8,128)(2,1)S(1)}, u32[]{:S(2)}, u32[]{:S(2)}) collective-permute-start(bf16[256,1536]{1,0:T(8,128)(2,1)S(1)} %constant_dynamic-slice_fusion.4), channel_id=1, source_target_pairs={{0,2},{1,3},{2,0},{3,1},{4,6},{5,7},{6,4},{7,5},{8,10},{9,11},{10,... | collective-permute-start | bytes 2359304 | tf_op jit(solution)/shard_map/ppermute | solution.py:243
  671.9 75.5 %collective-permute-start.84 = (bf16[256,1536]{1,0:T(8,128)(2,1)S(1)}, bf16[256,1536]{1,0:T(8,128)(2,1)S(1)}, u32[]{:S(2)}, u32[]{:S(2)}) collective-permute-start(bf16[256,1536]{1,0:T(8,128)(2,1)S(1)} %constant_dynamic-slice_fusion.5), channel_id=1, source_target_pairs={{0,2},{1,3},{2,0},{3,1},{4,6},{5,7},{6,4},{7,5},{8,10},{9,11},{10,... | collective-permute-start | bytes 2359304 | tf_op jit(solution)/shard_map/ppermute | solution.py:243
  714.3 66.8 %collective-permute-start.102 = (bf16[256,1536]{1,0:T(8,128)(2,1)S(1)}, bf16[256,1536]{1,0:T(8,128)(2,1)S(1)}, u32[]{:S(2)}, u32[]{:S(2)}) collective-permute-start(bf16[256,1536]{1,0:T(8,128)(2,1)S(1)} %fusion.35), channel_id=1, source_target_pairs={{0,2},{1,3},{2,0},{3,1},{4,6},{5,7},{6,4},{7,5},{8,10},{9,11},{10,... | collective-permute-start | bytes 2359304 | tf_op jit(solution)/shard_map/ppermute | solution.py:243
  748.1 49.9 %collective-permute-start.85 = (bf16[256,1536]{1,0:T(8,128)(2,1)S(1)}, bf16[256,1536]{1,0:T(8,128)(2,1)S(1)}, u32[]{:S(2)}, u32[]{:S(2)}) collective-permute-start(bf16[256,1536]{1,0:T(8,128)(2,1)S(1)} %fusion.27), channel_id=1, source_target_pairs={{0,2},{1,3},{2,0},{3,1},{4,6},{5,7},{6,4},{7,5},{8,10},{9,11},{10,... | collective-permute-start | bytes 2359304 | tf_op jit(solution)/shard_map/ppermute | solution.py:243
  781.2 66.4 %collective-permute-start.111 = (bf16[256,12,128]{2,0,1:T(8,128)(2,1)S(1)}, bf16[256,12,128]{2,0,1:T(8,128)(2,1)S(1)}, u32[]{:S(2)}, u32[]{:S(2)}) collective-permute-start(bf16[256,12,128]{2,0,1:T(8,128)(2,1)S(1)} %broadcast_select_fusion.19), channel_id=1, source_target_pairs={{0,16},{16,0},{1,17},{17,1},{2,18},{18,2},{3,19},{19,3},{4,20},{20... | collective-permute-start | bytes 2359304 | tf_op jit(solution)/shard_map/ppermute | solution.py:205
  804.8 20.0 %collective-permute-start.90 = (bf16[128,1536]{1,0:T(8,128)(2,1)S(1)}, bf16[128,1536]{1,0:T(8,128)(2,1)S(1)}, u32[]{:S(2)}, u32[]{:S(2)}) collective-permute-start(bf16[128,1536]{1,0:T(8,128)(2,1)S(1)} %get-tuple-element.174), channel_id=1, source_target_pairs={{0,8},{4,12},{8,0},{12,4},{1,9},{5,13},{9,1},{13,5},{2,10},{6,14},... | collective-permute-start | bytes 1179656 | tf_op jit(solution)/shard_map/ppermute | solution.py:234
  804.8 20.0 %collective-permute-start.89 = (bf16[128,1536]{1,0:T(8,128)(2,1)S(1)}, bf16[128,1536]{1,0:T(8,128)(2,1)S(1)}, u32[]{:S(2)}, u32[]{:S(2)}) collective-permute-start(bf16[128,1536]{1,0:T(8,128)(2,1)S(1)} %get-tuple-element.172), channel_id=1, source_target_pairs={{0,4},{4,0},{8,12},{12,8},{1,5},{5,1},{9,13},{13,9},{2,6},{6,2},{1... | collective-permute-start | bytes 1179656 | tf_op jit(solution)/shard_map/ppermute | solution.py:234
  812.0 21.3 %collective-permute-start.108 = (bf16[128,1536]{1,0:T(8,128)(2,1)S(1)}, bf16[128,1536]{1,0:T(8,128)(2,1)S(1)}, u32[]{:S(2)}, u32[]{:S(2)}) collective-permute-start(bf16[128,1536]{1,0:T(8,128)(2,1)S(1)} %get-tuple-element.181), channel_id=1, source_target_pairs={{0,12},{4,8},{8,4},{12,0},{1,13},{5,9},{9,5},{13,1},{2,14},{6,10},... | collective-permute-start | bytes 1179656 | tf_op jit(solution)/shard_map/ppermute | solution.py:234
  816.3 23.6 %collective-permute-start.107 = (bf16[128,1536]{1,0:T(8,128)(2,1)S(1)}, bf16[128,1536]{1,0:T(8,128)(2,1)S(1)}, u32[]{:S(2)}, u32[]{:S(2)}) collective-permute-start(bf16[128,1536]{1,0:T(8,128)(2,1)S(1)} %get-tuple-element.182), channel_id=1, source_target_pairs={{0,8},{4,12},{8,0},{12,4},{1,9},{5,13},{9,1},{13,5},{2,10},{6,14},... | collective-permute-start | bytes 1179656 | tf_op jit(solution)/shard_map/ppermute | solution.py:234
  824.8 15.2 %collective-permute-start.106 = (bf16[128,1536]{1,0:T(8,128)(2,1)S(1)}, bf16[128,1536]{1,0:T(8,128)(2,1)S(1)}, u32[]{:S(2)}, u32[]{:S(2)}) collective-permute-start(bf16[128,1536]{1,0:T(8,128)(2,1)S(1)} %get-tuple-element.180), channel_id=1, source_target_pairs={{0,4},{4,0},{8,12},{12,8},{1,5},{5,1},{9,13},{13,9},{2,6},{6,2},{1... | collective-permute-start | bytes 1179656 | tf_op jit(solution)/shard_map/ppermute | solution.py:234
  825.0 15.4 %collective-permute-start.92 = (bf16[128,768]{1,0:T(8,128)(2,1)S(1)}, bf16[128,768]{1,0:T(8,128)(2,1)S(1)}, u32[]{:S(2)}, u32[]{:S(2)}) collective-permute-start(bf16[128,768]{1,0:T(8,128)(2,1)S(1)} %slice.884), channel_id=1, source_target_pairs={{0,1},{1,0},{2,3},{3,2},{4,5},{5,4},{6,7},{7,6},{8,9},{9,8},{10,11... | collective-permute-start | bytes 589832 | tf_op jit(solution)/shard_map/ppermute | solution.py:239
  (135 other events, 1550.5 us)
